TPU v7x, 32 devices: a whole 2x2x4 slice. The times are simulated.
32 devices in a mesh: fsdp: 16 (over z, y, x), ctx: 2 (over core).
Axes of the slice: x: 2, y: 2, z: 4, core: 2. Of those that a mesh axis runs over, the one named last changes fastest.
Arguments:
- token_ids: int32 [256], P('ctx'), may hold values from 0 to 511
- embed: bfloat16 [512, 8192], P(None, 'fsdp'), may hold values from -6 to 6
- w_in: bfloat16 [8192, 3, 8192], P('ctx', None, 'fsdp'), may hold values from -0.09375 to 0.09375
- taps: float32 [7, 3, 8192], P(None, None, 'fsdp'), may hold values from -2 to 2
- rates: float32 [16, 8192], P(None, 'fsdp'), may hold values from 0.000390625 to 0.08, as said below
- residues: float32 [16, 8192], P(None, 'fsdp'), may hold values from -0.15 to 0.15
- cotangent: bfloat16 [256, 8192], P('ctx', 'fsdp'), may hold values from -6 to 6
Outputs:
- mixed: bfloat16 [256, 8192], P('ctx', 'fsdp')
- input_grad: bfloat16 [256, 8192], P('ctx', 'fsdp')
Inputs may be any that keep to these rules, and one draw needn't show every extreme that they name: `rates`: every rate lies between 0.1 / 256 and 0.08.
All inputs are finite; a program needn't handle non-finite values.
Results may differ from a plain program's by a relative error of at most 0.0064.
Values may be sent and summed in bfloat16 or wider, within the bound.
No kernel may reach another device: no remote copies, remote signals or barrier semaphores. Data moves between devices by JAX's collectives and lax.ppermute only.
A program may use at most 128 MiB of HBM per device.

v0:
```python
import functools

import jax
import jax.numpy as jnp
from jax import lax
from jax.experimental import pallas as pl
from jax.experimental.pallas import tpu as pltpu
from jax.sharding import PartitionSpec as P

BOTH = ("fsdp", "ctx")
CHUNKS = 8
f32 = jnp.float32
bf16 = jnp.bfloat16


def from_behind(shard, axis, by):
    count = lax.axis_size(axis)
    pairs = [(i, i + by) for i in range(count) if 0 <= i + by < count]
    return lax.ppermute(shard, axis, pairs)


def pair_combine(earlier, later):
    return (earlier[0] * later[0], later[0] * earlier[1] + later[1])


def modal_states(drive, step_decay):
    tok_count = drive.shape[0]
    factors = jnp.broadcast_to(step_decay[None], (tok_count,) + step_decay.shape)
    inputs = jnp.broadcast_to(drive[:, None, :], factors.shape)
    return lax.associative_scan(pair_combine, (factors, inputs), axis=0)[1]


def short_filter(extended, taps, tok_count):
    rim_width = taps.shape[0] - 1
    filtered = taps[0] * extended[rim_width : rim_width + tok_count]
    for shift_lag in range(1, rim_width + 1):
        filtered = (
            filtered
            + taps[shift_lag] * extended[rim_width - shift_lag : rim_width - shift_lag + tok_count]
        )
    return filtered


def short_adjoint(extended, taps, tok_count):
    rim_width = taps.shape[0] - 1
    result = taps[0] * extended[:tok_count]
    for shift_lag in range(1, rim_width + 1):
        result = result + taps[shift_lag] * extended[shift_lag : shift_lag + tok_count]
    return result


def carry(block_decay, leaving, by):
    def relay_step(turn_index, incoming):
        return from_behind(block_decay * incoming + leaving, "ctx", by)

    return lax.fori_loop(0, lax.axis_size("ctx") - 1, relay_step, jnp.zeros_like(leaving))


def general_plan(token_ids, embed, w_in, taps, rates, residues, cotangent):
    tok_count = token_ids.shape[0]
    vocab_size = embed.shape[0]
    chan_width = embed.shape[1]
    rim_width = taps.shape[0] - 1
    onehot = (
        token_ids[:, None] == lax.broadcasted_iota(jnp.int32, (tok_count, vocab_size), 1)
    ).astype(bf16)
    embedded = jnp.dot(onehot, embed, preferred_element_type=f32).astype(bf16)
    features = lax.all_gather(embedded, "fsdp", axis=1, tiled=True)
    feat_width = features.shape[1]
    whole_w = lax.all_gather(w_in, "ctx", axis=0, tiled=True).reshape(feat_width, 3 * chan_width)
    projected = jnp.dot(features, whole_w, preferred_element_type=f32)
    stored = lax.optimization_barrier(projected.astype(bf16).reshape(tok_count, 3, chan_width))
    before = from_behind(stored[tok_count - rim_width :], "ctx", 1)
    extended = jnp.concatenate([before, stored], axis=0).astype(f32)
    filtered = short_filter(extended, taps, tok_count)
    query_part = filtered[:, 0]
    key_part = filtered[:, 1]
    value_part = filtered[:, 2]
    drive = key_part * value_part
    step_decay = jnp.exp(-rates)
    block_decay = jnp.exp(-rates * tok_count)
    local_states = modal_states(drive, step_decay)
    entering = carry(block_decay, local_states[tok_count - 1], 1)
    offsets = lax.broadcasted_iota(f32, (tok_count, 1, 1), 0)
    states = local_states + jnp.exp(-rates[None] * (offsets + 1.0)) * entering[None]
    long_out = jnp.sum(residues[None] * states, axis=1)
    mixed = (query_part * long_out).astype(bf16)
    incoming = cotangent.astype(f32)
    grad_long = incoming * query_part
    grad_query = incoming * long_out
    back_states = jnp.flip(modal_states(jnp.flip(grad_long, 0), step_decay), 0)
    beyond = carry(block_decay, back_states[0], -1)
    adjoint = back_states + jnp.exp(-rates[None] * (tok_count - offsets)) * beyond[None]
    grad_drive = jnp.sum(residues[None] * adjoint, axis=1)
    grad_filtered = jnp.stack([grad_query, grad_drive * value_part, grad_drive * key_part], axis=1)
    after = from_behind(grad_filtered[:rim_width], "ctx", -1)
    ext_grad = jnp.concatenate([grad_filtered, after], axis=0)
    grad_stored = short_adjoint(ext_grad, taps, tok_count).astype(bf16)
    grad_rows = grad_stored.reshape(tok_count, 3 * chan_width)
    own_rows = lax.psum_scatter(
        lax.dot_general(whole_w, grad_rows, (((1,), (1,)), ((), ())), preferred_element_type=f32),
        "fsdp",
        scatter_dimension=0,
        tiled=True,
    )
    return (mixed, own_rows.T.astype(bf16))


def device_at(z, y, x, core):
    return ((z * 2 + y) * 2 + x) * 2 + core


def everywhere(move):
    pairs = []
    for z in range(4):
        for y in range(2):
            for x in range(2):
                for core in range(2):
                    pairs.append((device_at(z, y, x, core), device_at(*move(z, y, x, core))))
    return pairs


OTHER_CORE = everywhere(lambda z, y, x, core: (z, y, x, 1 - core))
OVER_X = everywhere(lambda z, y, x, core: (z, y, 1 - x, core))
OVER_Y = everywhere(lambda z, y, x, core: (z, 1 - y, x, core))


def along_z(moves):
    pairs = []
    for core in range(2):
        for (place, other), (to_place, to_other) in moves:
            z, to_z = (place, to_place) if core == 0 else (3 - place, 3 - to_place)
            for y in range(2):
                for x in range(2):
                    pairs.append(
                        (
                            device_at(z, y, x, core ^ other),
                            device_at(to_z, y, x, core ^ to_other),
                        )
                    )
    return pairs


GATHER_Z = (
    along_z([((0, 0), (1, 0)), ((1, 0), (0, 0)), ((0, 1), (2, 0)), ((1, 1), (3, 0))]),
    along_z([((1, 0), (2, 0)), ((2, 0), (3, 0))]),
)
SCATTER_Z = (
    along_z([((0, 0), (1, 0)), ((1, 0), (0, 0)), ((2, 0), (1, 1)), ((3, 0), (0, 1))]),
    along_z([((0, 0), (1, 1)), ((1, 0), (0, 1)), ((2, 0), (1, 0)), ((3, 0), (0, 0))]),
    along_z([((0, 0), (0, 1)), ((1, 0), (1, 1)), ((2, 0), (0, 0)), ((3, 0), (1, 0))]),
    along_z([((2, 0), (0, 1)), ((3, 0), (1, 1))]),
)

IN_VMEM = pl.BlockSpec(memory_space=pltpu.VMEM)
IN_SMEM = pl.BlockSpec(memory_space=pltpu.SMEM)


def small_call(kernel, out_shape, operands, name, flops=0, scratch=(), limit=8):
    sizes = [o.size * o.dtype.itemsize for o in operands]
    return pl.pallas_call(
        kernel,
        in_specs=[IN_SMEM] + [IN_VMEM] * (len(operands) - 1),
        out_specs=jax.tree.map(lambda _: IN_VMEM, out_shape),
        out_shape=out_shape,
        scratch_shapes=list(scratch),
        compiler_params=pltpu.CompilerParams(vmem_limit_bytes=limit * 1024 * 1024),
        cost_estimate=pl.CostEstimate(
            flops=flops, bytes_accessed=min(sum(sizes), 8 * 1024 * 1024), transcendentals=0
        ),
        name=name,
    )(*operands)


def load_kernel(w_ref, out_ref, sem):
    copy = pltpu.make_async_copy(w_ref, out_ref, sem)
    copy.start()
    copy.wait()


def load(w):
    return pl.pallas_call(
        load_kernel,
        in_specs=[pl.BlockSpec(memory_space=pltpu.HBM)],
        out_specs=IN_VMEM,
        out_shape=pltpu.VMEM(w.shape, w.dtype),
        scratch_shapes=[pltpu.SemaphoreType.DMA],
        compiler_params=pltpu.CompilerParams(vmem_limit_bytes=2 * 1024 * 1024),
        cost_estimate=pl.CostEstimate(
            flops=0, bytes_accessed=2 * w.size * w.dtype.itemsize, transcendentals=0
        ),
        name="load",
    )(pltpu.with_memory_space_constraint(w, pltpu.HBM))


def project_kernel(rows, has_base, last, index_ref, w_ref, *refs):
    count = len(rows)
    acts = refs[:count]
    groups, _, chans = w_ref.shape
    width = acts[0].shape[1]
    if last:
        keep_ref, send_ref, total_ref = refs[-3:]
    else:
        total_ref = refs[-1]
    toks = total_ref.shape[1]
    for g in range(groups):
        for low in range(0, toks, toks // 2):
            high = low + toks // 2
            total = refs[count][g, low:high] if has_base else None
            for n, ((first, end), act) in enumerate(zip(rows, acts)):
                if first > low or end < high:
                    continue
                start = pl.multiple_of(index_ref[n] * width, width)
                term = jnp.dot(
                    act[low - first : high - first],
                    w_ref[g, pl.ds(start, width), :],
                    preferred_element_type=f32,
                )
                total = term if total is None else total + term
            total_ref[g, low:high] = total
    if last:
        half = chans // 2
        for core in range(2):

            @pl.when(index_ref[count] == core)
            def _():
                keep_ref[...] = total_ref[:, :, core * half : (core + 1) * half]
                send_ref[...] = total_ref[:, :, (1 - core) * half : (2 - core) * half].astype(
                    send_ref.dtype
                )


def project(index, acts, rows, w, base, last):
    groups, _, chans = w.shape
    width = acts[0].shape[1]
    toks = max(high for _, high in rows)
    total = jax.ShapeDtypeStruct((groups, toks, chans), f32)
    scratch = []
    if last:
        out_shape = [
            jax.ShapeDtypeStruct((groups, toks, chans // 2), f32),
            jax.ShapeDtypeStruct((groups, toks, chans // 2), bf16),
        ]
        scratch = [pltpu.VMEM(total.shape, f32)]
    else:
        out_shape = total
    operands = [index, w] + list(acts) + ([] if base is None else [base])
    flops = 2 * groups * width * chans * sum(high - low for low, high in rows)
    return small_call(
        functools.partial(project_kernel, rows, base is not None, last),
        out_shape,
        operands,
        "project",
        flops,
        scratch,
        16,
    )


def shifted(values, by):
    place = lax.broadcasted_iota(jnp.int32, values.shape, 0)
    moved = pltpu.roll(values, by % CHUNKS, 0)
    inside = place >= by if by > 0 else place < CHUNKS + by
    return jnp.where(inside, moved, 0.0)


def mixer_kernel(
    core_ref,
    keep_ref,
    other_ref,
    taps_ref,
    rates_ref,
    residues_ref,
    cot_own_ref,
    cot_other_ref,
    mixed_own_ref,
    mixed_send_ref,
    grad_ref,
    flat,
    flat_cot,
    ext,
    filt,
    drive,
    back,
    grad_ext,
):
    groups, toks, chans = keep_ref.shape
    modes = rates_ref.shape[0]
    short = taps_ref.shape[0] // groups
    rim = short - 1
    length = toks // CHUNKS
    lanes = flat.shape[-1]
    wide = (CHUNKS, lanes)
    half = toks // 2
    core = core_ref[0]

    def row(array, at):
        return jnp.broadcast_to(array[at : at + 1, :], wide)

    def column(c, _):
        here = pl.ds(pl.multiple_of(c * lanes, lanes), lanes)
        whole = pl.ds(pl.multiple_of(core * chans + c * lanes, lanes), lanes)
        own_rows = pl.ds(pl.multiple_of(core * half, half), half)
        other_rows = pl.ds(pl.multiple_of((1 - core) * half, half), half)

        for g in range(groups):
            flat[g] = (keep_ref[g, :, here] + other_ref[g, :, here].astype(f32)).astype(bf16).astype(f32)
        flat_cot[own_rows] = cot_own_ref[:, whole].astype(f32)
        flat_cot[other_rows] = cot_other_ref[:, here].astype(f32)

        for g in range(groups):
            for k in range(length):
                ext[g, rim + k] = flat[g, pl.ds(k, CHUNKS, stride=length), :]
            for k in range(rim):
                ext[g, k] = shifted(ext[g, length + k], 1)

        taps = taps_ref[:, whole]
        tap = [[row(taps, j * groups + g) for g in range(groups)] for j in range(short)]

        def filter_step(k, _):
            parts = []
            for g in range(groups):
                total = tap[0][g] * ext[g, k + rim]
                for j in range(1, short):
                    total = total + tap[j][g] * ext[g, k + rim - j]
                parts.append(total)
                filt[g, k] = total
            drive[k] = parts[1] * parts[2]
            back[k] = parts[0] * flat_cot[pl.ds(k, CHUNKS, stride=length), :]
            return _

        lax.fori_loop(0, length, filter_step, 0, unroll=4)

        rates = rates_ref[:, whole]
        decay_rows = jnp.exp(-rates)
        jump_rows = [jnp.exp(-rates * (length * n)) for n in (1, 2, 4)]
        residue_rows = residues_ref[:, whole]

        def long_filter(source, forward, finish):
            decay = [row(decay_rows, m) for m in range(modes)]

            def place(k):
                return k if forward else length - 1 - k

            def end_step(k, states):
                value = source[place(k)]
                return tuple(decay[m] * states[m] + value for m in range(modes))

            zero = jnp.zeros(wide, f32)
            ends = lax.fori_loop(0, length, end_step, (zero,) * modes, unroll=8)
            entering = []
            sign = 1 if forward else -1
            for m in range(modes):
                carried = ends[m]
                for jump, by in zip(jump_rows, (1, 2, 4)):
                    carried = carried + row(jump, m) * shifted(carried, sign * by)
                entering.append(shifted(carried, sign))

            def out_step(k, states):
                value = source[place(k)]
                states = tuple(decay[m] * states[m] + value for m in range(modes))
                terms = [row(residue_rows, m) * states[m] for m in range(modes)]
                while len(terms) > 1:
                    terms = [a + b for a, b in zip(terms[::2], terms[1::2])]
                finish(place(k), terms[0])
                return states

            lax.fori_loop(0, length, out_step, tuple(entering), unroll=4)

        def finish_forward(k, total):
            flat[0, pl.ds(k, CHUNKS, stride=length), :] = filt[0, k] * total
            grad_ext[0, k] = flat_cot[pl.ds(k, CHUNKS, stride=length), :] * total

        def finish_backward(k, total):
            grad_ext[1, k] = total * filt[2, k]
            grad_ext[2, k] = total * filt[1, k]

        long_filter(drive, True, finish_forward)
        mixed_own_ref[:, here] = flat[0, own_rows].astype(bf16)
        mixed_send_ref[:, here] = flat[0, other_rows].astype(bf16)
        long_filter(back, False, finish_backward)

        for g in range(groups):
            for k in range(rim):
                grad_ext[g, length + k] = shifted(grad_ext[g, k], -1)

        def adjoint_step(k, _):
            for g in range(groups):
                total = tap[0][g] * grad_ext[g, k]
                for j in range(1, short):
                    total = total + tap[j][g] * grad_ext[g, k + j]
                flat[g, pl.ds(k, CHUNKS, stride=length), :] = total
            return _

        lax.fori_loop(0, length, adjoint_step, 0, unroll=4)
        for g in range(groups):
            grad_ref[g, here, :] = flat[g].T.astype(bf16)
        return _

    lax.fori_loop(0, chans // lanes, column, 0)


def mixer(core, keep, other, taps, rates, residues, cot_own, cot_other):
    groups, toks, chans = keep.shape
    modes = rates.shape[0]
    rim = taps.shape[0] // groups - 1
    lanes = 128
    length = toks // CHUNKS
    return small_call(
        mixer_kernel,
        [
            jax.ShapeDtypeStruct((toks // 2, chans), bf16),
            jax.ShapeDtypeStruct((toks // 2, chans), bf16),
            jax.ShapeDtypeStruct((groups, chans, toks), bf16),
        ],
        [core, keep, other, taps, rates, residues, cot_own, cot_other],
        "mixer",
        12 * modes * toks * chans,
        [
            pltpu.VMEM((groups, toks, lanes), f32),
            pltpu.VMEM((toks, lanes), f32),
            pltpu.VMEM((groups, length + rim, CHUNKS, lanes), f32),
            pltpu.VMEM((groups, length, CHUNKS, lanes), f32),
            pltpu.VMEM((length, CHUNKS, lanes), f32),
            pltpu.VMEM((length, CHUNKS, lanes), f32),
            pltpu.VMEM((groups, length + rim, CHUNKS, lanes), f32),
        ],
    )


def back_kernel(split, index_ref, w_ref, own_ref, other_ref, *out_refs):
    groups, half, toks = own_ref.shape
    per = 2 if split else 1
    width = out_refs[0].shape[0]
    count = len(out_refs) // per
    core = index_ref[count]
    own_at = pl.multiple_of(core * half, half)
    other_at = pl.multiple_of((1 - core) * half, half)
    for n in range(count):
        start = pl.multiple_of(index_ref[n] * width, width)
        total = None
        for g in range(groups):
            for ref, at in ((own_ref, own_at), (other_ref, other_at)):
                term = jnp.dot(
                    w_ref[g, pl.ds(start, width), pl.ds(at, half)],
                    ref[g],
                    preferred_element_type=f32,
                )
                total = term if total is None else total + term
        part = toks // per
        for p in range(per):
            out = out_refs[n * per + p]
            out[...] = total[:, p * part : (p + 1) * part].astype(out.dtype)


def back_project(index, w, own, other, width, split, dtype):
    groups, half, toks = own.shape
    count = index.shape[0] - 1
    per = 2 if split else 1
    return small_call(
        functools.partial(back_kernel, split),
        [jax.ShapeDtypeStruct((width, toks // per), dtype) for _ in range(count * per)],
        [index, w, own, other],
        "back_project",
        4 * count * groups * width * half * toks,
        (),
        16,
    )


def merge_kernel(core_ref, x_ref, y_ref, from_y_ref, from_x_ref, x_out, y_out):
    half = x_ref.shape[1] // 2
    x_out[:, :half] = (x_ref[:, :half] + from_y_ref[...].astype(f32)).astype(bf16)
    x_out[:, half:] = x_ref[:, half:].astype(bf16)
    y_out[:, :half] = y_ref[:, :half].astype(bf16)
    y_out[:, half:] = (y_ref[:, half:] + from_x_ref[...].astype(f32)).astype(bf16)


def merge(core, x_part, y_part, from_y, from_x):
    shape = jax.ShapeDtypeStruct(x_part.shape, bf16)
    return small_call(merge_kernel, [shape, shape], [core, x_part, y_part, from_y, from_x], "merge")


def column_kernel(flag_ref, own_ref, x_ref, y_ref, total_ref, one_ref, two_ref):
    half = own_ref.shape[1] // 2
    total_ref[...] = own_ref[...] + x_ref[...].astype(f32) + y_ref[...].astype(f32)
    first = pl.ds(pl.multiple_of(flag_ref[0] * half, half), half)
    second = pl.ds(pl.multiple_of((1 - flag_ref[0]) * half, half), half)
    one_ref[...] = total_ref[:, first].astype(bf16)
    two_ref[...] = total_ref[:, second].astype(bf16)


def column(flag, own, from_x, from_y):
    shape = jax.ShapeDtypeStruct((own.shape[0], own.shape[1] // 2), bf16)
    return small_call(
        column_kernel,
        [jax.ShapeDtypeStruct(own.shape, f32), shape, shape],
        [flag, own, from_x, from_y],
        "column",
    )


def finish_kernel(flag_ref, own_ref, a_ref, b_ref, c_ref, d_ref, out_ref):
    half = own_ref.shape[1] // 2
    mine = own_ref[:, pl.ds(pl.multiple_of(flag_ref[0] * half, half), half)]
    total = jnp.where(flag_ref[1] == 1, mine, 0.0)
    for ref in (a_ref, b_ref, c_ref, d_ref):
        total = total + ref[...].astype(f32)
    out_ref[...] = total.T.astype(bf16)


def finish(flags, own, received):
    shape = jax.ShapeDtypeStruct((own.shape[1] // 2, own.shape[0]), bf16)
    return small_call(finish_kernel, shape, [flags, own] + received, "finish")


def pair_kernel(core_ref, own_ref, other_ref, out_ref):
    half = own_ref.shape[1]
    out_ref[:, pl.ds(pl.multiple_of(core_ref[0] * half, half), half)] = own_ref[...]
    out_ref[:, pl.ds(pl.multiple_of((1 - core_ref[0]) * half, half), half)] = other_ref[...]


def pair(core, own, other):
    shape = jax.ShapeDtypeStruct((own.shape[0], 2 * own.shape[1]), own.dtype)
    return small_call(pair_kernel, shape, [core, own, other], "pair")


def chip_plan(token_ids, embed, w_in, taps, rates, residues, cotangent):
    vocab_size, width = embed.shape
    tok_half = token_ids.shape[0]
    toks = 2 * tok_half
    chan_half = width // 2
    spot = lax.axis_index("fsdp")
    core = lax.axis_index("ctx")
    z, y, x = spot // 4, (spot // 2) % 2, spot % 2
    first = core == 0
    place = jnp.where(first, z, 3 - z)
    inner = place < 2

    def table(*entries):
        return jnp.stack([jnp.asarray(e, jnp.int32) for e in entries])

    def swap(array):
        return lax.ppermute(array, BOTH, OTHER_CORE)

    def over_x(array):
        return lax.ppermute(array, BOTH, OVER_X)

    def over_y(array):
        return lax.ppermute(array, BOTH, OVER_Y)

    me = table(core)
    other_ids = swap(token_ids)
    cot_other = swap(lax.dynamic_slice_in_dim(cotangent, (1 - core) * chan_half, chan_half, 1))
    ids = jnp.where(
        first,
        jnp.concatenate([token_ids, other_ids]),
        jnp.concatenate([other_ids, token_ids]),
    )
    onehot = (ids[:, None] == lax.broadcasted_iota(jnp.int32, (toks, vocab_size), 1)).astype(bf16)
    embedded = jnp.dot(onehot, embed, preferred_element_type=f32).astype(bf16)

    got_1 = lax.ppermute(embedded, BOTH, GATHER_Z[0])
    w = load(jnp.transpose(w_in, (1, 0, 2)))
    w = pltpu.with_memory_space_constraint(w, pltpu.VMEM)
    got_1, w = lax.optimization_barrier((got_1, w))
    slot_1 = jnp.where(inner, embedded, got_1)
    got_2 = lax.ppermute(slot_1, BOTH, GATHER_Z[1])
    x_1, y_1 = over_x(slot_1), over_y(slot_1)
    far, near = core * 4, (1 - core) * 4
    base_1 = jnp.where(place % 2 == 0, far, near)
    base_2 = jnp.where(place % 2 == 0, near, far)

    def at(base, y_at, x_at):
        return base + y_at * 2 + x_at

    whole, upper, lower = (0, toks), (0, tok_half), (tok_half, toks)
    slot_2 = jnp.where(inner, got_1, got_2)
    x_2, y_2 = over_x(slot_2), over_y(slot_2)
    sums = project(
        table(at(base_1, y, x), at(base_2, y, x)), [slot_1, slot_2], [whole, whole], w, None, False
    )
    x_1, y_1, sums = lax.optimization_barrier((x_1, y_1, sums))
    d_1a, d_1b = over_y(x_1[:tok_half]), over_x(y_1[tok_half:])
    sums = project(
        table(at(base_1, y, 1 - x), at(base_1, 1 - y, x)), [x_1, y_1], [whole, whole], w, sums, False
    )
    x_2, y_2, sums = lax.optimization_barrier((x_2, y_2, sums))
    d_2a, d_2b = over_y(x_2[:tok_half]), over_x(y_2[tok_half:])
    sums = project(
        table(at(base_2, y, 1 - x), at(base_2, 1 - y, x)), [x_2, y_2], [whole, whole], w, sums, False
    )
    d_2a, d_2b, sums = lax.optimization_barrier((d_2a, d_2b, sums))
    diag_1, diag_2 = at(base_1, 1 - y, 1 - x), at(base_2, 1 - y, 1 - x)
    keep, send = project(
        table(diag_1, diag_1, diag_2, diag_2, core),
        [d_1a, d_1b, d_2a, d_2b],
        [upper, lower, upper, lower],
        w,
        sums,
        True,
    )

    groups = w.shape[0]
    mixed_own, mixed_send, grad_own = mixer(
        me,
        keep,
        swap(send),
        taps.reshape(taps.shape[0] * groups, width),
        rates,
        residues,
        cotangent,
        cot_other,
    )
    grad_other = swap(grad_own)
    mixed_other = swap(mixed_send)

    d_2a, d_2b, d_1a, d_1b = back_project(
        table(diag_2, diag_1, core), w, grad_own, grad_other, width, True, bf16
    )
    y_d2, x_d2 = over_y(d_2a), over_x(d_2b)
    y_d1, x_d1 = over_y(d_1a), over_x(d_1b)
    x_2, y_2, x_1, y_1, own_2, own_1 = back_project(
        table(
            at(base_2, y, 1 - x),
            at(base_2, 1 - y, x),
            at(base_1, y, 1 - x),
            at(base_1, 1 - y, x),
            at(base_2, y, x),
            at(base_1, y, x),
            core,
        ),
        w,
        grad_own,
        grad_other,
        width,
        False,
        f32,
    )
    x_2, y_2 = merge(me, x_2, y_2, y_d2, x_d2)
    x_2, y_2 = over_x(x_2), over_y(y_2)
    x_1, y_1 = merge(me, x_1, y_1, y_d1, x_d1)
    x_1, y_1 = over_x(x_1), over_y(y_1)

    half_2 = jnp.where(inner, core, 1 - core)
    _, send_1, send_2 = column(table(half_2), own_2, x_2, y_2)
    received = [
        lax.ppermute(send_1, BOTH, SCATTER_Z[0]),
        lax.ppermute(send_2, BOTH, SCATTER_Z[1]),
    ]
    mixed = pair(me, mixed_own, mixed_other)
    own, send_1, send_2 = column(table(1 - half_2), own_1, x_1, y_1)
    received += [
        lax.ppermute(send_1, BOTH, SCATTER_Z[2]),
        lax.ppermute(send_2, BOTH, SCATTER_Z[3]),
    ]
    return (mixed, finish(table(core, inner), own, received))


def solution(mesh):
    in_specs = (
        P("ctx"),
        P(None, "fsdp"),
        P("ctx", None, "fsdp"),
        P(None, None, "fsdp"),
        P(None, "fsdp"),
        P(None, "fsdp"),
        P("ctx", "fsdp"),
    )
    out_specs = (P("ctx", "fsdp"), P("ctx", "fsdp"))
    chips = mesh.shape["fsdp"] == 16 and mesh.shape["ctx"] == 2
    return jax.shard_map(
        chip_plan if chips else general_plan,
        mesh=mesh,
        in_specs=in_specs,
        out_specs=out_specs,
        check_vma=False,
    )
```

profile of v0, /device:TPU:0, one launch (start us, length us, event | category | flops | bytes accessed | tf_op | source)
XLA Modules:
  0.0 94.5 jit_solution(1523422890302111537)
XLA Ops:
  3.2 2.9 %collective-permute-start.1 = (bf16[256,512]{1,0:T(8,128)(2,1)S(1)}, bf16[256,512]{1,0:T(8,128)(2,1)S(1)}, u32[]{:S(2)}, u32[]{:S(2)}) collective-permute-start(bf16[256,512]{1,0:T(8,128)(2,1)S(1)} %convolution_convert_fusion), channel_id=1, source_target_pairs={{0,8},{2,10},{4,12},{6,14},{8,0},{10,2},{12,4},{14,6},{1,16},{3,18... | collective-permute-start | bytes 786440 | tf_op jit(solution)/shard_map/ppermute | solution.py:563
  6.2 4.6 %load.1.w_ref = bf16[3,4096,512]{2,1,0:T(8,128)(2,1)S(1)} custom-call(bf16[3,4096,512]{2,1,0:T(8,128)(2,1)} %bitcast.14), custom_call_target="tpu_custom_call" | custom-call | bytes 25165824 | tf_op jit(solution)/shard_map/load/pallas_call | solution.py:182
  10.8 4.5 %copy-done.1 = bf16[3,4096,512]{2,1,0:T(8,128)(2,1)} copy-done((bf16[3,4096,512]{2,1,0:T(8,128)(2,1)}, bf16[3,4096,512]{2,1,0:T(8,128)(2,1)S(1)}, u32[]{:S(2)}) %copy-start.1) | copy-done | bytes 12582936
  17.6 1.5 %collective-permute-start.3 = (bf16[256,512]{1,0:T(8,128)(2,1)S(1)}, bf16[256,512]{1,0:T(8,128)(2,1)S(1)}, u32[]{:S(2)}, u32[]{:S(2)}) collective-permute-start(bf16[256,512]{1,0:T(8,128)(2,1)S(1)} %broadcast_select_fusion.1.refs_0_), channel_id=1, source_target_pairs={{0,4},{1,5},{2,6},{3,7},{4,0},{5,1},{6,2},{7,3},{8,12},{9,13},{10,... | collective-permute-start | bytes 786440 | tf_op jit(solution)/shard_map/ppermute | solution.py:550
  20.4 4.6 %copy-done.2 = bf16[3,4096,512]{2,1,0:T(8,128)(2,1)S(1)} copy-done((bf16[3,4096,512]{2,1,0:T(8,128)(2,1)S(1)}, bf16[3,4096,512]{2,1,0:T(8,128)(2,1)}, u32[]{:S(2)}) %copy-start.2) | copy-done | bytes 12582936
  25.0 1.5 %project.4.refs_2_ = f32[3,256,512]{2,1,0:T(8,128)S(1)} custom-call(s32[2]{0:T(128)S(1)} %pad_add_fusion.index_ref, bf16[3,4096,512]{2,1,0:T(8,128)(2,1)S(1)} %copy-done.2, bf16[256,512]{1,0:T(8,128)(2,1)S(1)} %broadcast_select_fusion.1.refs_0_, bf16[256,512]{1,0:T(8,128)(2,1)S(1)} %broadcast_select_fusion.refs_1_), custom_call_target="tpu_custom_call" | custom-call | flops 805306368 | bytes 8388608 | tf_op jit(solution)/shard_map/project/pallas_call | solution.py:161
  26.5 1.6 %collective-permute-start.5 = (bf16[128,512]{1,0:T(8,128)(2,1)S(1)}, bf16[128,512]{1,0:T(8,128)(2,1)S(1)}, u32[]{:S(2)}, u32[]{:S(2)}) collective-permute-start(bf16[128,512]{1,0:T(8,128)(2,1)S(1)} %slice.12), channel_id=1, source_target_pairs={{0,4},{1,5},{2,6},{3,7},{4,0},{5,1},{6,2},{7,3},{8,12},{9,13},{10,... | collective-permute-start | bytes 393224 | tf_op jit(solution)/shard_map/ppermute | solution.py:550
  28.1 1.6 %collective-permute-start.6 = (bf16[128,512]{1,0:T(8,128)(2,1)S(1)}, bf16[128,512]{1,0:T(8,128)(2,1)S(1)}, u32[]{:S(2)}, u32[]{:S(2)}) collective-permute-start(bf16[128,512]{1,0:T(8,128)(2,1)S(1)} %slice.13), channel_id=1, source_target_pairs={{0,2},{1,3},{2,0},{3,1},{4,6},{5,7},{6,4},{7,5},{8,10},{9,11},{10,... | collective-permute-start | bytes 393224 | tf_op jit(solution)/shard_map/ppermute | solution.py:547
  29.7 1.6 %project.5.refs_2_ = f32[3,256,512]{2,1,0:T(8,128)S(1)} custom-call(s32[2]{0:T(128)S(1)} %pad_add_fusion.1.index_ref, bf16[3,4096,512]{2,1,0:T(8,128)(2,1)S(1)} %copy-done.2, bf16[256,512]{1,0:T(8,128)(2,1)S(1)} %collective-permute-done.2.refs_0_, bf16[256,512]{1,0:T(8,128)(2,1)S(1)} %collective-permute-done.3.refs_1_, f32[3,256,512]{2,1,0:T(8,128)S(1)} %project.4.refs_2_), custom_call_target="tpu_custom_call" | custom-call | flops 805306368 | bytes 8388608 | tf_op jit(solution)/shard_map/project/pallas_call | solution.py:161
  32.7 1.5 %collective-permute-start.9 = (bf16[128,512]{1,0:T(8,128)(2,1)}, bf16[128,512]{1,0:T(8,128)(2,1)S(1)}, u32[]{:S(2)}, u32[]{:S(2)}) collective-permute-start(bf16[128,512]{1,0:T(8,128)(2,1)} %slice.14), channel_id=1, source_target_pairs={{0,4},{1,5},{2,6},{3,7},{4,0},{5,1},{6,2},{7,3},{8,12},{9,13},{10,... | collective-permute-start | bytes 393224 | tf_op jit(solution)/shard_map/ppermute | solution.py:550
  34.4 4.6 %copy-done.3 = bf16[3,4096,512]{2,1,0:T(8,128)(2,1)S(1)} copy-done((bf16[3,4096,512]{2,1,0:T(8,128)(2,1)S(1)}, bf16[3,4096,512]{2,1,0:T(8,128)(2,1)}, u32[]{:S(2)}) %copy-start.3) | copy-done | bytes 12582936
  39.0 1.5 %project.6.refs_4_ = f32[3,256,512]{2,1,0:T(8,128)S(1)} custom-call(s32[2]{0:T(128)S(1)} %pad_add_fusion.2.index_ref, bf16[3,4096,512]{2,1,0:T(8,128)(2,1)S(1)} %copy-done.3, bf16[256,512]{1,0:T(8,128)(2,1)S(1)} %collective-permute-done.7.refs_0_, bf16[256,512]{1,0:T(8,128)(2,1)S(1)} %collective-permute-done.8.refs_1_, f32[3,256,512]{2,1,0:T(8,128)S(1)} %project.5.refs_2_), custom_call_target="tpu_custom_call" | custom-call | flops 805306368 | bytes 8388608 | tf_op jit(solution)/shard_map/project/pallas_call | solution.py:161
  40.6 1.6 %project.7 = (f32[3,256,256]{2,1,0:T(8,128)S(1)}, bf16[3,256,256]{2,1,0:T(8,128)(2,1)S(1)}) custom-call(s32[5]{0:T(128)S(1)} %stack.77.index_ref, bf16[3,4096,512]{2,1,0:T(8,128)(2,1)S(1)} %copy-done.3, bf16[128,512]{1,0:T(8,128)(2,1)S(1)} %collective-permute-done.5.refs_0_, bf16[128,512]{1,0:T(8,128)(2,1)S(1)} %collective-permute-done.6.refs_1_, ...), custom_call_target="tpu_custom_call" | custom-call | flops 805306368 | bytes 8388608 | tf_op jit(solution)/shard_map/project/pallas_call | solution.py:161
  42.3 3.9 %collective-permute-start.11 = (bf16[3,256,256]{2,1,0:T(8,128)(2,1)S(1)}, bf16[3,256,256]{2,1,0:T(8,128)(2,1)S(1)}, u32[]{:S(2)}, u32[]{:S(2)}) collective-permute-start(bf16[3,256,256]{2,1,0:T(8,128)(2,1)S(1)} %get-tuple-element.49), channel_id=1, source_target_pairs={{0,1},{1,0},{2,3},{3,2},{4,5},{5,4},{6,7},{7,6},{8,9},{9,8},{10,11... | collective-permute-start | bytes 1179656 | tf_op jit(solution)/shard_map/ppermute | solution.py:544
  47.6 4.6 %mixer.1 = (bf16[128,256]{1,0:T(8,128)(2,1)S(1)}, bf16[128,256]{1,0:T(8,128)(2,1)S(1)}, bf16[3,256,256]{2,1,0:T(8,128)(2,1)S(1)}) custom-call(s32[1]{0:T(128)} %bitcast.core_ref, f32[3,256,256]{2,1,0:T(8,128)S(1)} %get-tuple-element.48.keep_ref, bf16[3,256,256]{2,1,0:T(8,128)(2,1)S(1)} %collective-permute-done.11.other_ref, f32[21,512]{1,0:T(8,128)S(1)} %reshape.36.taps_ref, ...), custom_call_target="tpu_custom_call" | custom-call | flops 12582912 | bytes 1484804 | tf_op jit(solution)/shard_map/mixer/pallas_call | solution.py:161
  54.0 4.6 %copy-done.4 = bf16[3,4096,512]{2,1,0:T(8,128)(2,1)S(1)} copy-done((bf16[3,4096,512]{2,1,0:T(8,128)(2,1)S(1)}, bf16[3,4096,512]{2,1,0:T(8,128)(2,1)}, u32[]{:S(2)}) %copy-start.4) | copy-done | bytes 12582936
  58.6 1.5 %back_project.3 = (bf16[512,128]{1,0:T(8,128)(2,1)S(1)}, bf16[512,128]{1,0:T(8,128)(2,1)S(1)}, bf16[512,128]{1,0:T(8,128)(2,1)S(1)}, bf16[512,128]{1,0:T(8,128)(2,1)S(1)}) custom-call(s32[3]{0:T(128)S(1)} %pad_add_fusion.4.index_ref, bf16[3,4096,512]{2,1,0:T(8,128)(2,1)S(1)} %copy-done.4, bf16[3,256,256]{2,1,0:T(8,128)(2,1)S(1)} %get-tuple-element.52.own_ref, ...), custom_call_target="tpu_custom_call" | custom-call | flops 805306368 | bytes 8388608 | tf_op jit(solution)/shard_map/back_project/pallas_call | solution.py:161
  64.3 3.1 %back_project.2 = (f32[512,256]{1,0:T(8,128)S(1)}, f32[512,256]{1,0:T(8,128)S(1)}, f32[512,256]{1,0:T(8,128)S(1)}, f32[512,256]{1,0:T(8,128)S(1)}, f32[512,256]{1,0:T(8,128)S(1)}, /*index=5*/f32[512,256]{1,0:T(8,128)S(1)}) custom-call(s32[7]{0:T(128)S(1)} %stack.91.index_ref, bf16[3,4096,512]{2,1,0:T(8,128)(2,1)S(1)} %copy-done.4, ...), custom_call_target="tpu_custom_call" | custom-call | flops 2415919104 | bytes 8388608 | tf_op jit(solution)/shard_map/back_project/pallas_call | solution.py:161
  70.0 1.6 %collective-permute-start.17 = (bf16[512,256]{1,0:T(8,128)(2,1)S(1)}, bf16[512,256]{1,0:T(8,128)(2,1)S(1)}, u32[]{:S(2)}, u32[]{:S(2)}) collective-permute-start(bf16[512,256]{1,0:T(8,128)(2,1)S(1)} %get-tuple-element.58), channel_id=1, source_target_pairs={{0,2},{1,3},{2,0},{3,1},{4,6},{5,7},{6,4},{7,5},{8,10},{9,11},{10,... | collective-permute-start | bytes 786440 | tf_op jit(solution)/shard_map/ppermute | solution.py:547
  72.4 5.2 %collective-permute-done.21.x_ref = bf16[512,256]{1,0:T(8,128)(2,1)S(1)} collective-permute-done((bf16[512,256]{1,0:T(8,128)(2,1)}, bf16[512,256]{1,0:T(8,128)(2,1)S(1)}, u32[]{:S(2)}, u32[]{:S(2)}) %collective-permute-start.21) | collective-permute-done | bytes 262176 | tf_op jit(solution)/shard_map/ppermute | solution.py:547
  78.9 1.6 %collective-permute-start.23 = (bf16[512,128]{1,0:T(8,128)(2,1)S(1)}, bf16[512,128]{1,0:T(8,128)(2,1)S(1)}, u32[]{:S(2)}, u32[]{:S(2)}) collective-permute-start(bf16[512,128]{1,0:T(8,128)(2,1)S(1)} %get-tuple-element.68), channel_id=1, source_target_pairs={{0,8},{2,10},{4,12},{6,14},{8,0},{10,2},{12,4},{14,6},{16,9},{18,1... | collective-permute-start | bytes 393224 | tf_op jit(solution)/shard_map/ppermute | solution.py:648
  80.4 1.6 %collective-permute-start.24 = (bf16[512,128]{1,0:T(8,128)(2,1)S(1)}, bf16[512,128]{1,0:T(8,128)(2,1)S(1)}, u32[]{:S(2)}, u32[]{:S(2)}) collective-permute-start(bf16[512,128]{1,0:T(8,128)(2,1)S(1)} %get-tuple-element.69), channel_id=1, source_target_pairs={{0,9},{2,11},{4,13},{6,15},{8,1},{10,3},{12,5},{14,7},{16,8},{18,1... | collective-permute-start | bytes 393224 | tf_op jit(solution)/shard_map/ppermute | solution.py:649
  84.0 3.4 %collective-permute-start.13 = (bf16[128,256]{1,0:T(8,128)(2,1)S(1)}, bf16[128,256]{1,0:T(8,128)(2,1)S(1)}, u32[]{:S(2)}, u32[]{:S(2)}) collective-permute-start(bf16[128,256]{1,0:T(8,128)(2,1)S(1)} %get-tuple-element.51), channel_id=1, source_target_pairs={{0,1},{1,0},{2,3},{3,2},{4,5},{5,4},{6,7},{7,6},{8,9},{9,8},{10,11... | collective-permute-start | bytes 196616 | tf_op jit(solution)/shard_map/ppermute | solution.py:544
  88.9 4.3 %collective-permute-done.25.c_ref = bf16[512,128]{1,0:T(8,128)(2,1)S(1)} collective-permute-done((bf16[512,128]{1,0:T(8,128)(2,1)S(1)}, bf16[512,128]{1,0:T(8,128)(2,1)S(1)}, u32[]{:S(2)}, u32[]{:S(2)}) %collective-permute-start.25) | collective-permute-done | bytes 131104 | tf_op jit(solution)/shard_map/ppermute | solution.py:654
  (80 shorter events, 24.5 us)
Async XLA Ops:
  3.2 12.1 %collective-permute-start.1 = (bf16[256,512]{1,0:T(8,128)(2,1)S(1)}, bf16[256,512]{1,0:T(8,128)(2,1)S(1)}, u32[]{:S(2)}, u32[]{:S(2)}) collective-permute-start(bf16[256,512]{1,0:T(8,128)(2,1)S(1)} %convolution_convert_fusion), channel_id=1, source_target_pairs={{0,8},{2,10},{4,12},{6,14},{8,0},{10,2},{12,4},{14,6},{1,16},{3,18... | collective-permute-start | bytes 786440 | tf_op jit(solution)/shard_map/ppermute | solution.py:563
  15.3 3.9 %collective-permute-start.4 = (bf16[256,512]{1,0:T(8,128)(2,1)S(1)}, bf16[256,512]{1,0:T(8,128)(2,1)S(1)}, u32[]{:S(2)}, u32[]{:S(2)}) collective-permute-start(bf16[256,512]{1,0:T(8,128)(2,1)S(1)} %broadcast_select_fusion.1.refs_0_), channel_id=1, source_target_pairs={{8,16},{10,18},{12,20},{14,22},{16,24},{18,26},{20,28},{22,30},{17... | collective-permute-start | bytes 786440 | tf_op jit(solution)/shard_map/ppermute | solution.py:568
  16.1 10.4 %collective-permute-start.2 = (bf16[256,512]{1,0:T(8,128)(2,1)S(1)}, bf16[256,512]{1,0:T(8,128)(2,1)S(1)}, u32[]{:S(2)}, u32[]{:S(2)}) collective-permute-start(bf16[256,512]{1,0:T(8,128)(2,1)S(1)} %broadcast_select_fusion.1.refs_0_), channel_id=1, source_target_pairs={{0,2},{1,3},{2,0},{3,1},{4,6},{5,7},{6,4},{7,5},{8,10},{9,11},{10,... | collective-permute-start | bytes 786440 | tf_op jit(solution)/shard_map/ppermute | solution.py:547
  17.6 8.9 %collective-permute-start.3 = (bf16[256,512]{1,0:T(8,128)(2,1)S(1)}, bf16[256,512]{1,0:T(8,128)(2,1)S(1)}, u32[]{:S(2)}, u32[]{:S(2)}) collective-permute-start(bf16[256,512]{1,0:T(8,128)(2,1)S(1)} %broadcast_select_fusion.1.refs_0_), channel_id=1, source_target_pairs={{0,4},{1,5},{2,6},{3,7},{4,0},{5,1},{6,2},{7,3},{8,12},{9,13},{10,... | collective-permute-start | bytes 786440 | tf_op jit(solution)/shard_map/ppermute | solution.py:550
  19.2 12.1 %collective-permute-start.7 = (bf16[256,512]{1,0:T(8,128)(2,1)S(1)}, bf16[256,512]{1,0:T(8,128)(2,1)S(1)}, u32[]{:S(2)}, u32[]{:S(2)}) collective-permute-start(bf16[256,512]{1,0:T(8,128)(2,1)S(1)} %broadcast_select_fusion.refs_1_), channel_id=1, source_target_pairs={{0,2},{1,3},{2,0},{3,1},{4,6},{5,7},{6,4},{7,5},{8,10},{9,11},{10,... | collective-permute-start | bytes 786440 | tf_op jit(solution)/shard_map/ppermute | solution.py:547
  19.8 11.6 %collective-permute-start.8 = (bf16[256,512]{1,0:T(8,128)(2,1)S(1)}, bf16[256,512]{1,0:T(8,128)(2,1)S(1)}, u32[]{:S(2)}, u32[]{:S(2)}) collective-permute-start(bf16[256,512]{1,0:T(8,128)(2,1)S(1)} %broadcast_select_fusion.refs_1_), channel_id=1, source_target_pairs={{0,4},{1,5},{2,6},{3,7},{4,0},{5,1},{6,2},{7,3},{8,12},{9,13},{10,... | collective-permute-start | bytes 786440 | tf_op jit(solution)/shard_map/ppermute | solution.py:550
  26.5 14.1 %collective-permute-start.5 = (bf16[128,512]{1,0:T(8,128)(2,1)S(1)}, bf16[128,512]{1,0:T(8,128)(2,1)S(1)}, u32[]{:S(2)}, u32[]{:S(2)}) collective-permute-start(bf16[128,512]{1,0:T(8,128)(2,1)S(1)} %slice.12), channel_id=1, source_target_pairs={{0,4},{1,5},{2,6},{3,7},{4,0},{5,1},{6,2},{7,3},{8,12},{9,13},{10,... | collective-permute-start | bytes 393224 | tf_op jit(solution)/shard_map/ppermute | solution.py:550
  28.1 12.5 %collective-permute-start.6 = (bf16[128,512]{1,0:T(8,128)(2,1)S(1)}, bf16[128,512]{1,0:T(8,128)(2,1)S(1)}, u32[]{:S(2)}, u32[]{:S(2)}) collective-permute-start(bf16[128,512]{1,0:T(8,128)(2,1)S(1)} %slice.13), channel_id=1, source_target_pairs={{0,2},{1,3},{2,0},{3,1},{4,6},{5,7},{6,4},{7,5},{8,10},{9,11},{10,... | collective-permute-start | bytes 393224 | tf_op jit(solution)/shard_map/ppermute | solution.py:547
  31.5 9.1 %collective-permute-start.10 = (bf16[128,512]{1,0:T(8,128)(2,1)S(1)}, bf16[128,512]{1,0:T(8,128)(2,1)S(1)}, u32[]{:S(2)}, u32[]{:S(2)}) collective-permute-start(bf16[128,512]{1,0:T(8,128)(2,1)S(1)} %slice.15), channel_id=1, source_target_pairs={{0,2},{1,3},{2,0},{3,1},{4,6},{5,7},{6,4},{7,5},{8,10},{9,11},{10,... | collective-permute-start | bytes 393224 | tf_op jit(solution)/shard_map/ppermute | solution.py:547
  32.7 7.9 %collective-permute-start.9 = (bf16[128,512]{1,0:T(8,128)(2,1)}, bf16[128,512]{1,0:T(8,128)(2,1)S(1)}, u32[]{:S(2)}, u32[]{:S(2)}) collective-permute-start(bf16[128,512]{1,0:T(8,128)(2,1)} %slice.14), channel_id=1, source_target_pairs={{0,4},{1,5},{2,6},{3,7},{4,0},{5,1},{6,2},{7,3},{8,12},{9,13},{10,... | collective-permute-start | bytes 393224 | tf_op jit(solution)/shard_map/ppermute | solution.py:550
  42.3 5.4 %collective-permute-start.11 = (bf16[3,256,256]{2,1,0:T(8,128)(2,1)S(1)}, bf16[3,256,256]{2,1,0:T(8,128)(2,1)S(1)}, u32[]{:S(2)}, u32[]{:S(2)}) collective-permute-start(bf16[3,256,256]{2,1,0:T(8,128)(2,1)S(1)} %get-tuple-element.49), channel_id=1, source_target_pairs={{0,1},{1,0},{2,3},{3,2},{4,5},{5,4},{6,7},{7,6},{8,9},{9,8},{10,11... | collective-permute-start | bytes 1179656 | tf_op jit(solution)/shard_map/ppermute | solution.py:544
  60.1 7.3 %collective-permute-start.19 = (bf16[512,128]{1,0:T(8,128)(2,1)S(1)}, bf16[512,128]{1,0:T(8,128)(2,1)S(1)}, u32[]{:S(2)}, u32[]{:S(2)}) collective-permute-start(bf16[512,128]{1,0:T(8,128)(2,1)S(1)} %get-tuple-element.64), channel_id=1, source_target_pairs={{0,4},{1,5},{2,6},{3,7},{4,0},{5,1},{6,2},{7,3},{8,12},{9,13},{10,... | collective-permute-start | bytes 393224 | tf_op jit(solution)/shard_map/ppermute | solution.py:550
  60.7 6.7 %collective-permute-start.20 = (bf16[512,128]{1,0:T(8,128)(2,1)S(1)}, bf16[512,128]{1,0:T(8,128)(2,1)S(1)}, u32[]{:S(2)}, u32[]{:S(2)}) collective-permute-start(bf16[512,128]{1,0:T(8,128)(2,1)S(1)} %get-tuple-element.65), channel_id=1, source_target_pairs={{0,2},{1,3},{2,0},{3,1},{4,6},{5,7},{6,4},{7,5},{8,10},{9,11},{10,... | collective-permute-start | bytes 393224 | tf_op jit(solution)/shard_map/ppermute | solution.py:547
  61.3 8.6 %collective-permute-start.15 = (bf16[512,128]{1,0:T(8,128)(2,1)S(1)}, bf16[512,128]{1,0:T(8,128)(2,1)S(1)}, u32[]{:S(2)}, u32[]{:S(2)}) collective-permute-start(bf16[512,128]{1,0:T(8,128)(2,1)S(1)} %get-tuple-element.56), channel_id=1, source_target_pairs={{0,4},{1,5},{2,6},{3,7},{4,0},{5,1},{6,2},{7,3},{8,12},{9,13},{10,... | collective-permute-start | bytes 393224 | tf_op jit(solution)/shard_map/ppermute | solution.py:550
  62.8 7.1 %collective-permute-start.16 = (bf16[512,128]{1,0:T(8,128)(2,1)S(1)}, bf16[512,128]{1,0:T(8,128)(2,1)S(1)}, u32[]{:S(2)}, u32[]{:S(2)}) collective-permute-start(bf16[512,128]{1,0:T(8,128)(2,1)S(1)} %get-tuple-element.57), channel_id=1, source_target_pairs={{0,2},{1,3},{2,0},{3,1},{4,6},{5,7},{6,4},{7,5},{8,10},{9,11},{10,... | collective-permute-start | bytes 393224 | tf_op jit(solution)/shard_map/ppermute | solution.py:547
  68.2 9.5 %collective-permute-start.21 = (bf16[512,256]{1,0:T(8,128)(2,1)}, bf16[512,256]{1,0:T(8,128)(2,1)S(1)}, u32[]{:S(2)}, u32[]{:S(2)}) collective-permute-start(bf16[512,256]{1,0:T(8,128)(2,1)} %get-tuple-element.66), channel_id=1, source_target_pairs={{0,2},{1,3},{2,0},{3,1},{4,6},{5,7},{6,4},{7,5},{8,10},{9,11},{10,... | collective-permute-start | bytes 786440 | tf_op jit(solution)/shard_map/ppermute | solution.py:547
  68.7 9.2 %collective-permute-start.22 = (bf16[512,256]{1,0:T(8,128)(2,1)S(1)}, bf16[512,256]{1,0:T(8,128)(2,1)S(1)}, u32[]{:S(2)}, u32[]{:S(2)}) collective-permute-start(bf16[512,256]{1,0:T(8,128)(2,1)S(1)} %get-tuple-element.67), channel_id=1, source_target_pairs={{0,4},{1,5},{2,6},{3,7},{4,0},{5,1},{6,2},{7,3},{8,12},{9,13},{10,... | collective-permute-start | bytes 786440 | tf_op jit(solution)/shard_map/ppermute | solution.py:550
  70.0 12.1 %collective-permute-start.17 = (bf16[512,256]{1,0:T(8,128)(2,1)S(1)}, bf16[512,256]{1,0:T(8,128)(2,1)S(1)}, u32[]{:S(2)}, u32[]{:S(2)}) collective-permute-start(bf16[512,256]{1,0:T(8,128)(2,1)S(1)} %get-tuple-element.58), channel_id=1, source_target_pairs={{0,2},{1,3},{2,0},{3,1},{4,6},{5,7},{6,4},{7,5},{8,10},{9,11},{10,... | collective-permute-start | bytes 786440 | tf_op jit(solution)/shard_map/ppermute | solution.py:547
  71.6 10.5 %collective-permute-start.18 = (bf16[512,256]{1,0:T(8,128)(2,1)S(1)}, bf16[512,256]{1,0:T(8,128)(2,1)S(1)}, u32[]{:S(2)}, u32[]{:S(2)}) collective-permute-start(bf16[512,256]{1,0:T(8,128)(2,1)S(1)} %get-tuple-element.59), channel_id=1, source_target_pairs={{0,4},{1,5},{2,6},{3,7},{4,0},{5,1},{6,2},{7,3},{8,12},{9,13},{10,... | collective-permute-start | bytes 786440 | tf_op jit(solution)/shard_map/ppermute | solution.py:550
  78.9 10.0 %collective-permute-start.23 = (bf16[512,128]{1,0:T(8,128)(2,1)S(1)}, bf16[512,128]{1,0:T(8,128)(2,1)S(1)}, u32[]{:S(2)}, u32[]{:S(2)}) collective-permute-start(bf16[512,128]{1,0:T(8,128)(2,1)S(1)} %get-tuple-element.68), channel_id=1, source_target_pairs={{0,8},{2,10},{4,12},{6,14},{8,0},{10,2},{12,4},{14,6},{16,9},{18,1... | collective-permute-start | bytes 393224 | tf_op jit(solution)/shard_map/ppermute | solution.py:648
  80.4 8.4 %collective-permute-start.24 = (bf16[512,128]{1,0:T(8,128)(2,1)S(1)}, bf16[512,128]{1,0:T(8,128)(2,1)S(1)}, u32[]{:S(2)}, u32[]{:S(2)}) collective-permute-start(bf16[512,128]{1,0:T(8,128)(2,1)S(1)} %get-tuple-element.69), channel_id=1, source_target_pairs={{0,9},{2,11},{4,13},{6,15},{8,1},{10,3},{12,5},{14,7},{16,8},{18,1... | collective-permute-start | bytes 393224 | tf_op jit(solution)/shard_map/ppermute | solution.py:649
  82.2 10.9 %collective-permute-start.25 = (bf16[512,128]{1,0:T(8,128)(2,1)S(1)}, bf16[512,128]{1,0:T(8,128)(2,1)S(1)}, u32[]{:S(2)}, u32[]{:S(2)}) collective-permute-start(bf16[512,128]{1,0:T(8,128)(2,1)S(1)} %get-tuple-element.70), channel_id=1, source_target_pairs={{0,1},{2,3},{4,5},{6,7},{8,9},{10,11},{12,13},{14,15},{16,0},{18,2... | collective-permute-start | bytes 393224 | tf_op jit(solution)/shard_map/ppermute | solution.py:654
  83.3 9.9 %collective-permute-start.26 = (bf16[512,128]{1,0:T(8,128)(2,1)S(1)}, bf16[512,128]{1,0:T(8,128)(2,1)S(1)}, u32[]{:S(2)}, u32[]{:S(2)}) collective-permute-start(bf16[512,128]{1,0:T(8,128)(2,1)S(1)} %get-tuple-element.71), channel_id=1, source_target_pairs={{16,1},{18,3},{20,5},{22,7},{24,9},{26,11},{28,13},{30,15},{9,24},... | collective-permute-start | bytes 393224 | tf_op jit(solution)/shard_map/ppermute | solution.py:655
  84.0 4.3 %collective-permute-start.13 = (bf16[128,256]{1,0:T(8,128)(2,1)S(1)}, bf16[128,256]{1,0:T(8,128)(2,1)S(1)}, u32[]{:S(2)}, u32[]{:S(2)}) collective-permute-start(bf16[128,256]{1,0:T(8,128)(2,1)S(1)} %get-tuple-element.51), channel_id=1, source_target_pairs={{0,1},{1,0},{2,3},{3,2},{4,5},{5,4},{6,7},{7,6},{8,9},{9,8},{10,11... | collective-permute-start | bytes 196616 | tf_op jit(solution)/shard_map/ppermute | solution.py:544
  (12 other events, 50.7 us)
where the time goes:
time: 95.6 us; the launch traced here: 94.5 us
  starting transfers between devices  34.5 us (36%)
  Pallas kernels  24.1 us (25%)
  local copies, waits for them, and re-layouts  19.2 us (20%)
  waiting for transfers between devices  14.2 us (15%)
  other arithmetic  1.17 us (1%)
  between operations  0.99 us (1%)
    pallas_call x13, Pallas kernels, small_call(): pl.pallas_call(kernel, in_specs=[IN_SMEM] + [IN_VMEM] * (len(operands) -...  19.5 us
    unnamed x19, local copies, waits for them, and re-layouts  18.3 us
    ppermute x8, starting transfers between devices, over_y(): return lax.ppermute(array, BOTH, OVER_Y)  9.25 us
    ppermute x8, starting transfers between devices, over_x(): return lax.ppermute(array, BOTH, OVER_X)  8.38 us
    ppermute x5, starting transfers between devices, swap(): return lax.ppermute(array, BOTH, OTHER_CORE)  8.34 us
    ppermute x8, waiting for transfers between devices, over_x(): return lax.ppermute(array, BOTH, OVER_X)  5.25 us
    pallas_call x1, Pallas kernels, load(): pl.pallas_call(load_kernel, in_specs=[pl.BlockSpec(memory_space=pltpu.HBM...  4.58 us
    ppermute x1, waiting for transfers between devices, chip_plan(): lax.ppermute(send_1, BOTH, SCATTER_Z[2])  4.28 us
  transfers between devices with their start and end apart: 27, of which 8 were waited for; matrix products, arithmetic and copies ran while one was open for 1% of the time, Pallas kernels for 16%

commit v1 on v0

--- a/solution.py
+++ b/solution.py
@@ -153,14 +153,13 @@
 )
 
 IN_VMEM = pl.BlockSpec(memory_space=pltpu.VMEM)
-IN_SMEM = pl.BlockSpec(memory_space=pltpu.SMEM)
 
 
 def small_call(kernel, out_shape, operands, name, flops=0, scratch=(), limit=8):
     sizes = [o.size * o.dtype.itemsize for o in operands]
     return pl.pallas_call(
         kernel,
-        in_specs=[IN_SMEM] + [IN_VMEM] * (len(operands) - 1),
+        in_specs=[IN_VMEM] * len(operands),
         out_specs=jax.tree.map(lambda _: IN_VMEM, out_shape),
         out_shape=out_shape,
         scratch_shapes=list(scratch),
@@ -170,6 +169,68 @@
         ),
         name=name,
     )(*operands)
+
+
+def here():
+    spot = lax.axis_index("fsdp")
+    return spot >> 2, (spot >> 1) & 1, spot & 1, lax.axis_index("ctx")
+
+
+def is_inner():
+    z, _, _, core = here()
+    return core == (z >> 1)
+
+
+def block_at(slot, far_y, far_x):
+    z, y, x, _ = here()
+    along = (z & 1) if slot == 1 else 1 - (z & 1)
+    return along * 4 + (1 - y if far_y else y) * 2 + (1 - x if far_x else x)
+
+
+def embed_kernel(own_ref, other_ref, table_ref, cot_ref, out_ref, cot_out_ref):
+    vocab = table_ref.shape[0]
+    half = own_ref.shape[1]
+    chan_half = cot_out_ref.shape[1]
+    _, _, _, core = here()
+    for ref, side in ((own_ref, core), (other_ref, 1 - core)):
+        across = jnp.broadcast_to(ref[...].astype(f32), (half, half)).T
+        lane = lax.broadcasted_iota(jnp.int32, (half, half), 1).astype(f32)
+        picks = [(across == lane + float(first)).astype(f32) for first in range(0, vocab, half)]
+        rows = jnp.dot(
+            jnp.concatenate(picks, axis=1).astype(bf16), table_ref[...], preferred_element_type=f32
+        )
+        out_ref[pl.ds(pl.multiple_of(side * half, half), half), :] = rows.astype(bf16)
+    cot_out_ref[...] = cot_ref[:, pl.ds(pl.multiple_of((1 - core) * chan_half, chan_half), chan_half)]
+
+
+def embed_rows(own_ids, other_ids, table, cotangent):
+    toks, width = 2 * own_ids.shape[1], table.shape[1]
+    return small_call(
+        embed_kernel,
+        [
+            jax.ShapeDtypeStruct((toks, width), bf16),
+            jax.ShapeDtypeStruct((cotangent.shape[0], cotangent.shape[1] // 2), bf16),
+        ],
+        [own_ids, other_ids, table, cotangent],
+        "embed_rows",
+        2 * toks * table.shape[0] * width,
+    )
+
+
+def choose_kernel(inner_ref, outer_ref, out_ref):
+    @pl.when(is_inner())
+    def _():
+        out_ref[...] = inner_ref[...]
+
+    @pl.when(jnp.logical_not(is_inner()))
+    def _():
+        out_ref[...] = outer_ref[...]
+
+
+def choose(inner, outer):
+    return small_call(
+        choose_kernel, jax.ShapeDtypeStruct(inner.shape, inner.dtype), [inner, outer], "choose"
+    )
 
 
 def load_kernel(w_ref, out_ref, sem):
@@ -193,66 +254,41 @@
     )(pltpu.with_memory_space_constraint(w, pltpu.HBM))
 
 
-def project_kernel(rows, has_base, last, index_ref, w_ref, *refs):
-    count = len(rows)
+def project_kernel(blocks, has_base, last, w_ref, *refs):
+    count = len(blocks)
     acts = refs[:count]
     groups, _, chans = w_ref.shape
-    width = acts[0].shape[1]
+    toks, width = acts[0].shape
     if last:
         keep_ref, send_ref, total_ref = refs[-3:]
     else:
         total_ref = refs[-1]
-    toks = total_ref.shape[1]
+    starts = [pl.multiple_of(block_at(*block) * width, width) for block in blocks]
     for g in range(groups):
-        for low in range(0, toks, toks // 2):
-            high = low + toks // 2
-            total = refs[count][g, low:high] if has_base else None
-            for n, ((first, end), act) in enumerate(zip(rows, acts)):
-                if first > low or end < high:
-                    continue
-                start = pl.multiple_of(index_ref[n] * width, width)
-                term = jnp.dot(
-                    act[low - first : high - first],
-                    w_ref[g, pl.ds(start, width), :],
-                    preferred_element_type=f32,
-                )
-                total = term if total is None else total + term
-            total_ref[g, low:high] = total
+        total = refs[count][g] if has_base else None
+        for start, act in zip(starts, acts):
+            term = jnp.dot(act[...], w_ref[g, pl.ds(start, width), :], preferred_element_type=f32)
+            total = term if total is None else total + term
+        total_ref[g] = total
     if last:
         half = chans // 2
-        for core in range(2):
-
-            @pl.when(index_ref[count] == core)
-            def _():
-                keep_ref[...] = total_ref[:, :, core * half : (core + 1) * half]
-                send_ref[...] = total_ref[:, :, (1 - core) * half : (2 - core) * half].astype(
-                    send_ref.dtype
-                )
-
-
-def project(index, acts, rows, w, base, last):
+        _, _, _, core = here()
+        keep_ref[...] = total_ref[:, :, pl.ds(pl.multiple_of(core * half, half), half)]
+        send_ref[...] = total_ref[:, :, pl.ds(pl.multiple_of((1 - core) * half, half), half)]
+
+
+def project(blocks, acts, w, base, last):
     groups, _, chans = w.shape
-    width = acts[0].shape[1]
-    toks = max(high for _, high in rows)
+    toks, width = acts[0].shape
     total = jax.ShapeDtypeStruct((groups, toks, chans), f32)
-    scratch = []
-    if last:
-        out_shape = [
-            jax.ShapeDtypeStruct((groups, toks, chans // 2), f32),
-            jax.ShapeDtypeStruct((groups, toks, chans // 2), bf16),
-        ]
-        scratch = [pltpu.VMEM(total.shape, f32)]
-    else:
-        out_shape = total
-    operands = [index, w] + list(acts) + ([] if base is None else [base])
-    flops = 2 * groups * width * chans * sum(high - low for low, high in rows)
+    half = jax.ShapeDtypeStruct((groups, toks, chans // 2), f32)
     return small_call(
-        functools.partial(project_kernel, rows, base is not None, last),
-        out_shape,
-        operands,
+        functools.partial(project_kernel, blocks, base is not None, last),
+        [half, half] if last else total,
+        [w] + list(acts) + ([] if base is None else [base]),
         "project",
-        flops,
-        scratch,
+        2 * len(acts) * groups * width * chans * toks,
+        [pltpu.VMEM(total.shape, f32)] if last else [],
         16,
     )
 
@@ -265,7 +301,6 @@
 
 
 def mixer_kernel(
-    core_ref,
     keep_ref,
     other_ref,
     taps_ref,
@@ -286,27 +321,27 @@
 ):
     groups, toks, chans = keep_ref.shape
     modes = rates_ref.shape[0]
-    short = taps_ref.shape[0] // groups
+    short = taps_ref.shape[1]
     rim = short - 1
     length = toks // CHUNKS
     lanes = flat.shape[-1]
     wide = (CHUNKS, lanes)
     half = toks // 2
-    core = core_ref[0]
+    _, _, _, core = here()
 
     def row(array, at):
         return jnp.broadcast_to(array[at : at + 1, :], wide)
 
     def column(c, _):
-        here = pl.ds(pl.multiple_of(c * lanes, lanes), lanes)
+        some = pl.ds(pl.multiple_of(c * lanes, lanes), lanes)
         whole = pl.ds(pl.multiple_of(core * chans + c * lanes, lanes), lanes)
         own_rows = pl.ds(pl.multiple_of(core * half, half), half)
         other_rows = pl.ds(pl.multiple_of((1 - core) * half, half), half)
 
         for g in range(groups):
-            flat[g] = (keep_ref[g, :, here] + other_ref[g, :, here].astype(f32)).astype(bf16).astype(f32)
+            flat[g] = (keep_ref[g, :, some] + other_ref[g, :, some].astype(f32)).astype(bf16).astype(f32)
         flat_cot[own_rows] = cot_own_ref[:, whole].astype(f32)
-        flat_cot[other_rows] = cot_other_ref[:, here].astype(f32)
+        flat_cot[other_rows] = cot_other_ref[:, some].astype(f32)
 
         for g in range(groups):
             for k in range(length):
@@ -314,8 +349,8 @@
             for k in range(rim):
                 ext[g, k] = shifted(ext[g, length + k], 1)
 
-        taps = taps_ref[:, whole]
-        tap = [[row(taps, j * groups + g) for g in range(groups)] for j in range(short)]
+        taps = [taps_ref[g, :, whole] for g in range(groups)]
+        tap = [[row(taps[g], j) for g in range(groups)] for j in range(short)]
 
         def filter_step(k, _):
             parts = []
@@ -376,8 +411,8 @@
             grad_ext[2, k] = total * filt[1, k]
 
         long_filter(drive, True, finish_forward)
-        mixed_own_ref[:, here] = flat[0, own_rows].astype(bf16)
-        mixed_send_ref[:, here] = flat[0, other_rows].astype(bf16)
+        mixed_own_ref[:, some] = flat[0, own_rows].astype(bf16)
+        mixed_send_ref[:, some] = flat[0, other_rows].astype(bf16)
         long_filter(back, False, finish_backward)
 
         for g in range(groups):
@@ -394,16 +429,16 @@
 
         lax.fori_loop(0, length, adjoint_step, 0, unroll=4)
         for g in range(groups):
-            grad_ref[g, here, :] = flat[g].T.astype(bf16)
+            grad_ref[g, some, :] = flat[g].T.astype(bf16)
         return _
 
     lax.fori_loop(0, chans // lanes, column, 0)
 
 
-def mixer(core, keep, other, taps, rates, residues, cot_own, cot_other):
+def mixer(keep, other, taps, rates, residues, cot_own, cot_other):
     groups, toks, chans = keep.shape
     modes = rates.shape[0]
-    rim = taps.shape[0] // groups - 1
+    rim = taps.shape[1] - 1
     lanes = 128
     length = toks // CHUNKS
     return small_call(
@@ -413,7 +448,7 @@
             jax.ShapeDtypeStruct((toks // 2, chans), bf16),
             jax.ShapeDtypeStruct((groups, chans, toks), bf16),
         ],
-        [core, keep, other, taps, rates, residues, cot_own, cot_other],
+        [keep, other, taps, rates, residues, cot_own, cot_other],
         "mixer",
         12 * modes * toks * chans,
         [
@@ -428,16 +463,14 @@
     )
 
 
-def back_kernel(split, index_ref, w_ref, own_ref, other_ref, *out_refs):
-    groups, half, toks = own_ref.shape
-    per = 2 if split else 1
+def back_kernel(blocks, w_ref, own_ref, other_ref, *out_refs):
+    groups, half, _ = own_ref.shape
     width = out_refs[0].shape[0]
-    count = len(out_refs) // per
-    core = index_ref[count]
+    _, _, _, core = here()
     own_at = pl.multiple_of(core * half, half)
     other_at = pl.multiple_of((1 - core) * half, half)
-    for n in range(count):
-        start = pl.multiple_of(index_ref[n] * width, width)
+    for block, out in zip(blocks, out_refs):
+        start = pl.multiple_of(block_at(*block) * width, width)
         total = None
         for g in range(groups):
             for ref, at in ((own_ref, own_at), (other_ref, other_at)):
@@ -447,98 +480,78 @@
                     preferred_element_type=f32,
                 )
                 total = term if total is None else total + term
-        part = toks // per
-        for p in range(per):
-            out = out_refs[n * per + p]
-            out[...] = total[:, p * part : (p + 1) * part].astype(out.dtype)
-
-
-def back_project(index, w, own, other, width, split, dtype):
+        out[...] = total.astype(out.dtype)
+
+
+def back_project(blocks, dtypes, w, own, other, width):
     groups, half, toks = own.shape
-    count = index.shape[0] - 1
-    per = 2 if split else 1
     return small_call(
-        functools.partial(back_kernel, split),
-        [jax.ShapeDtypeStruct((width, toks // per), dtype) for _ in range(count * per)],
-        [index, w, own, other],
+        functools.partial(back_kernel, blocks),
+        [jax.ShapeDtypeStruct((width, toks), dtype) for dtype in dtypes],
+        [w, own, other],
         "back_project",
-        4 * count * groups * width * half * toks,
+        4 * len(blocks) * groups * width * half * toks,
         (),
         16,
     )
 
 
-def merge_kernel(core_ref, x_ref, y_ref, from_y_ref, from_x_ref, x_out, y_out):
-    half = x_ref.shape[1] // 2
-    x_out[:, :half] = (x_ref[:, :half] + from_y_ref[...].astype(f32)).astype(bf16)
-    x_out[:, half:] = x_ref[:, half:].astype(bf16)
-    y_out[:, :half] = y_ref[:, :half].astype(bf16)
-    y_out[:, half:] = (y_ref[:, half:] + from_x_ref[...].astype(f32)).astype(bf16)
-
-
-def merge(core, x_part, y_part, from_y, from_x):
-    shape = jax.ShapeDtypeStruct(x_part.shape, bf16)
-    return small_call(merge_kernel, [shape, shape], [core, x_part, y_part, from_y, from_x], "merge")
-
-
-def column_kernel(flag_ref, own_ref, x_ref, y_ref, total_ref, one_ref, two_ref):
+def merge_kernel(part_ref, got_ref, out_ref):
+    out_ref[...] = (part_ref[...] + got_ref[...].astype(f32)).astype(bf16)
+
+
+def merge(part, got):
+    return small_call(merge_kernel, jax.ShapeDtypeStruct(part.shape, bf16), [part, got], "merge")
+
+
+def column_kernel(slot, own_ref, x_ref, y_ref, total_ref, one_ref, two_ref):
     half = own_ref.shape[1] // 2
     total_ref[...] = own_ref[...] + x_ref[...].astype(f32) + y_ref[...].astype(f32)
-    first = pl.ds(pl.multiple_of(flag_ref[0] * half, half), half)
-    second = pl.ds(pl.multiple_of((1 - flag_ref[0]) * half, half), half)
-    one_ref[...] = total_ref[:, first].astype(bf16)
-    two_ref[...] = total_ref[:, second].astype(bf16)
-
-
-def column(flag, own, from_x, from_y):
+    z = here()[0]
+    flag = (z >> 1) if slot == 2 else 1 - (z >> 1)
+    one_ref[...] = total_ref[:, pl.ds(pl.multiple_of(flag * half, half), half)].astype(bf16)
+    two_ref[...] = total_ref[:, pl.ds(pl.multiple_of((1 - flag) * half, half), half)].astype(bf16)
+
+
+def column(slot, own, from_x, from_y):
     shape = jax.ShapeDtypeStruct((own.shape[0], own.shape[1] // 2), bf16)
     return small_call(
-        column_kernel,
+        functools.partial(column_kernel, slot),
         [jax.ShapeDtypeStruct(own.shape, f32), shape, shape],
-        [flag, own, from_x, from_y],
+        [own, from_x, from_y],
         "column",
     )
 
 
-def finish_kernel(flag_ref, own_ref, a_ref, b_ref, c_ref, d_ref, out_ref):
+def finish_kernel(own_ref, a_ref, b_ref, c_ref, d_ref, out_ref):
     half = own_ref.shape[1] // 2
-    mine = own_ref[:, pl.ds(pl.multiple_of(flag_ref[0] * half, half), half)]
-    total = jnp.where(flag_ref[1] == 1, mine, 0.0)
+    core = here()[3]
+    mine = own_ref[:, pl.ds(pl.multiple_of(core * half, half), half)]
+    total = jnp.where(is_inner(), mine, 0.0)
     for ref in (a_ref, b_ref, c_ref, d_ref):
         total = total + ref[...].astype(f32)
     out_ref[...] = total.T.astype(bf16)
 
 
-def finish(flags, own, received):
+def finish(own, received):
     shape = jax.ShapeDtypeStruct((own.shape[1] // 2, own.shape[0]), bf16)
-    return small_call(finish_kernel, shape, [flags, own] + received, "finish")
-
-
-def pair_kernel(core_ref, own_ref, other_ref, out_ref):
+    return small_call(finish_kernel, shape, [own] + received, "finish")
+
+
+def pair_kernel(own_ref, other_ref, out_ref):
     half = own_ref.shape[1]
-    out_ref[:, pl.ds(pl.multiple_of(core_ref[0] * half, half), half)] = own_ref[...]
-    out_ref[:, pl.ds(pl.multiple_of((1 - core_ref[0]) * half, half), half)] = other_ref[...]
-
-
-def pair(core, own, other):
+    core = here()[3]
+    out_ref[:, pl.ds(pl.multiple_of(core * half, half), half)] = own_ref[...]
+    out_ref[:, pl.ds(pl.multiple_of((1 - core) * half, half), half)] = other_ref[...]
+
+
+def pair(own, other):
     shape = jax.ShapeDtypeStruct((own.shape[0], 2 * own.shape[1]), own.dtype)
-    return small_call(pair_kernel, shape, [core, own, other], "pair")
+    return small_call(pair_kernel, shape, [own, other], "pair")
 
 
 def chip_plan(token_ids, embed, w_in, taps, rates, residues, cotangent):
-    vocab_size, width = embed.shape
-    tok_half = token_ids.shape[0]
-    toks = 2 * tok_half
-    chan_half = width // 2
-    spot = lax.axis_index("fsdp")
-    core = lax.axis_index("ctx")
-    z, y, x = spot // 4, (spot // 2) % 2, spot % 2
-    first = core == 0
-    place = jnp.where(first, z, 3 - z)
-    inner = place < 2
-
-    def table(*entries):
-        return jnp.stack([jnp.asarray(e, jnp.int32) for e in entries])
+    width = embed.shape[1]
 
     def swap(array):
         return lax.ppermute(array, BOTH, OTHER_CORE)
@@ -549,112 +562,59 @@
     def over_y(array):
         return lax.ppermute(array, BOTH, OVER_Y)
 
-    me = table(core)
-    other_ids = swap(token_ids)
-    cot_other = swap(lax.dynamic_slice_in_dim(cotangent, (1 - core) * chan_half, chan_half, 1))
-    ids = jnp.where(
-        first,
-        jnp.concatenate([token_ids, other_ids]),
-        jnp.concatenate([other_ids, token_ids]),
-    )
-    onehot = (ids[:, None] == lax.broadcasted_iota(jnp.int32, (toks, vocab_size), 1)).astype(bf16)
-    embedded = jnp.dot(onehot, embed, preferred_element_type=f32).astype(bf16)
+    own_ids = token_ids.reshape(1, -1)
+    embedded, cot_send = embed_rows(own_ids, swap(own_ids), embed, cotangent)
+    cot_other = swap(cot_send)
 
     got_1 = lax.ppermute(embedded, BOTH, GATHER_Z[0])
     w = load(jnp.transpose(w_in, (1, 0, 2)))
     w = pltpu.with_memory_space_constraint(w, pltpu.VMEM)
-    got_1, w = lax.optimization_barrier((got_1, w))
-    slot_1 = jnp.where(inner, embedded, got_1)
+    got_1, cot_other, w = lax.optimization_barrier((got_1, cot_other, w))
+    slot_1 = choose(embedded, got_1)
     got_2 = lax.ppermute(slot_1, BOTH, GATHER_Z[1])
     x_1, y_1 = over_x(slot_1), over_y(slot_1)
-    far, near = core * 4, (1 - core) * 4
-    base_1 = jnp.where(place % 2 == 0, far, near)
-    base_2 = jnp.where(place % 2 == 0, near, far)
-
-    def at(base, y_at, x_at):
-        return base + y_at * 2 + x_at
-
-    whole, upper, lower = (0, toks), (0, tok_half), (tok_half, toks)
-    slot_2 = jnp.where(inner, got_1, got_2)
+    slot_2 = choose(got_1, got_2)
     x_2, y_2 = over_x(slot_2), over_y(slot_2)
-    sums = project(
-        table(at(base_1, y, x), at(base_2, y, x)), [slot_1, slot_2], [whole, whole], w, None, False
-    )
+    sums = project([(1, 0, 0), (2, 0, 0)], [slot_1, slot_2], w, None, False)
     x_1, y_1, sums = lax.optimization_barrier((x_1, y_1, sums))
-    d_1a, d_1b = over_y(x_1[:tok_half]), over_x(y_1[tok_half:])
-    sums = project(
-        table(at(base_1, y, 1 - x), at(base_1, 1 - y, x)), [x_1, y_1], [whole, whole], w, sums, False
-    )
+    d_1 = over_y(x_1)
+    sums = project([(1, 0, 1), (1, 1, 0)], [x_1, y_1], w, sums, False)
     x_2, y_2, sums = lax.optimization_barrier((x_2, y_2, sums))
-    d_2a, d_2b = over_y(x_2[:tok_half]), over_x(y_2[tok_half:])
-    sums = project(
-        table(at(base_2, y, 1 - x), at(base_2, 1 - y, x)), [x_2, y_2], [whole, whole], w, sums, False
-    )
-    d_2a, d_2b, sums = lax.optimization_barrier((d_2a, d_2b, sums))
-    diag_1, diag_2 = at(base_1, 1 - y, 1 - x), at(base_2, 1 - y, 1 - x)
-    keep, send = project(
-        table(diag_1, diag_1, diag_2, diag_2, core),
-        [d_1a, d_1b, d_2a, d_2b],
-        [upper, lower, upper, lower],
-        w,
-        sums,
-        True,
-    )
-
-    groups = w.shape[0]
+    d_2 = over_x(y_2)
+    sums = project([(2, 0, 1), (2, 1, 0)], [x_2, y_2], w, sums, False)
+    d_1, d_2, sums = lax.optimization_barrier((d_1, d_2, sums))
+    keep, send = project([(1, 1, 1), (2, 1, 1)], [d_1, d_2], w, sums, True)
+
     mixed_own, mixed_send, grad_own = mixer(
-        me,
-        keep,
-        swap(send),
-        taps.reshape(taps.shape[0] * groups, width),
-        rates,
-        residues,
-        cotangent,
-        cot_other,
+        keep, swap(send), jnp.transpose(taps, (1, 0, 2)), rates, residues, cotangent, cot_other
     )
     grad_other = swap(grad_own)
     mixed_other = swap(mixed_send)
 
-    d_2a, d_2b, d_1a, d_1b = back_project(
-        table(diag_2, diag_1, core), w, grad_own, grad_other, width, True, bf16
-    )
-    y_d2, x_d2 = over_y(d_2a), over_x(d_2b)
-    y_d1, x_d1 = over_y(d_1a), over_x(d_1b)
+    d_2, d_1 = back_project([(2, 1, 1), (1, 1, 1)], [bf16] * 2, w, grad_own, grad_other, width)
+    d_2, d_1 = over_x(d_2), over_y(d_1)
     x_2, y_2, x_1, y_1, own_2, own_1 = back_project(
-        table(
-            at(base_2, y, 1 - x),
-            at(base_2, 1 - y, x),
-            at(base_1, y, 1 - x),
-            at(base_1, 1 - y, x),
-            at(base_2, y, x),
-            at(base_1, y, x),
-            core,
-        ),
+        [(2, 0, 1), (2, 1, 0), (1, 0, 1), (1, 1, 0), (2, 0, 0), (1, 0, 0)],
+        [bf16, f32, f32, bf16, f32, f32],
         w,
         grad_own,
         grad_other,
         width,
-        False,
-        f32,
-    )
-    x_2, y_2 = merge(me, x_2, y_2, y_d2, x_d2)
-    x_2, y_2 = over_x(x_2), over_y(y_2)
-    x_1, y_1 = merge(me, x_1, y_1, y_d1, x_d1)
-    x_1, y_1 = over_x(x_1), over_y(y_1)
-
-    half_2 = jnp.where(inner, core, 1 - core)
-    _, send_1, send_2 = column(table(half_2), own_2, x_2, y_2)
+    )
+    x_2, y_2 = over_x(x_2), over_y(merge(y_2, d_2))
+    x_1, y_1 = over_x(merge(x_1, d_1)), over_y(y_1)
+    _, send_1, send_2 = column(2, own_2, x_2, y_2)
     received = [
         lax.ppermute(send_1, BOTH, SCATTER_Z[0]),
         lax.ppermute(send_2, BOTH, SCATTER_Z[1]),
     ]
-    mixed = pair(me, mixed_own, mixed_other)
-    own, send_1, send_2 = column(table(1 - half_2), own_1, x_1, y_1)
+    mixed = pair(mixed_own, mixed_other)
+    own, send_1, send_2 = column(1, own_1, x_1, y_1)
     received += [
         lax.ppermute(send_1, BOTH, SCATTER_Z[2]),
         lax.ppermute(send_2, BOTH, SCATTER_Z[3]),
     ]
-    return (mixed, finish(table(core, inner), own, received))
+    return (mixed, finish(own, received))
 
 
 def solution(mesh):

time: 95.6 us -> 86.6 us (0.906)
  waiting for transfers between devices: 14.2 us -> 33.9 us
  local copies, waits for them, and re-layouts: 19.2 us -> 2.62 us
  starting transfers between devices: 34.5 us -> 28.3 us
  Pallas kernels: 24.1 us -> 20 us
  other arithmetic: 1.17 us -> 0 us
    unnamed x19 -> x14, local copies, waits for them, and re-layouts: 18.3 us -> 2.62 us
    ppermute x8 -> x6, waiting for transfers between devices: 0.47 us -> 11.2 us  [over_y(): return lax.ppermute(array, BOTH, OVER_Y)]
    ppermute x8 -> x6, waiting for transfers between devices: 5.25 us -> 13.3 us  [over_x(): return lax.ppermute(array, BOTH, OVER_X)]
    pallas_call x13 -> x16, Pallas kernels: 19.5 us -> 15.4 us  [small_call(): pl.pallas_call(kernel, in_specs=[IN_VMEM] * len(operands), out_specs=jax....]
    ppermute x8 -> x6, starting transfers between devices: 8.38 us -> 4.99 us  [over_x(): return lax.ppermute(array, BOTH, OVER_X)]
    ppermute x8 -> x6, starting transfers between devices: 9.25 us -> 6.91 us  [over_y(): return lax.ppermute(array, BOTH, OVER_Y)]
    ppermute x1, waiting for transfers between devices: 4.28 us -> 2.86 us  [chip_plan(): lax.ppermute(send_1, BOTH, SCATTER_Z[2])]
    ppermute x1, waiting for transfers between devices: 0.01 us -> 1.39 us  [chip_plan(): got_1 = lax.ppermute(embedded, BOTH, GATHER_Z[0])]
  transfers between devices with their start and end apart: 27 -> 23, of which waited for: 8 -> 15; matrix products, arithmetic and copies ran while one was open for 1% -> 0% of each run, Pallas kernels for 16% -> 14%
where the time goes in v1:
time: 86.6 us; the launch traced here: 85.6 us
  waiting for transfers between devices  33.9 us (39%)
  starting transfers between devices  28.3 us (33%)
  Pallas kernels  20 us (23%)
  local copies, waits for them, and re-layouts  2.62 us (3%)
    pallas_call x16, Pallas kernels, small_call(): pl.pallas_call(kernel, in_specs=[IN_VMEM] * len(operands), out_specs=jax....  15.4 us
    ppermute x6, waiting for transfers between devices, over_x(): return lax.ppermute(array, BOTH, OVER_X)  13.3 us
    ppermute x6, waiting for transfers between devices, over_y(): return lax.ppermute(array, BOTH, OVER_Y)  11.2 us
    ppermute x5, starting transfers between devices, swap(): return lax.ppermute(array, BOTH, OTHER_CORE)  7.03 us
    ppermute x6, starting transfers between devices, over_y(): return lax.ppermute(array, BOTH, OVER_Y)  6.91 us
    ppermute x5, waiting for transfers between devices, swap(): return lax.ppermute(array, BOTH, OTHER_CORE)  5.12 us
    ppermute x6, starting transfers between devices, over_x(): return lax.ppermute(array, BOTH, OVER_X)  4.99 us
    pallas_call x1, Pallas kernels, load(): pl.pallas_call(load_kernel, in_specs=[pl.BlockSpec(memory_space=pltpu.HBM...  4.58 us
  transfers between devices with their start and end apart: 23, of which 15 were waited for; matrix products, arithmetic and copies ran while one was open for 0% of the time, Pallas kernels for 14%

profile of v1, /device:TPU:0, one launch (start us, length us, event | category | flops | bytes accessed | tf_op | source)
XLA Modules:
  0.0 85.6 jit_solution(17373316430432243415)
XLA Ops:
  5.1 2.9 %collective-permute-start.1 = (bf16[256,512]{1,0:T(8,128)(2,1)S(1)}, bf16[256,512]{1,0:T(8,128)(2,1)S(1)}, u32[]{:S(2)}, u32[]{:S(2)}) collective-permute-start(bf16[256,512]{1,0:T(8,128)(2,1)S(1)} %get-tuple-element.34.inner_ref), channel_id=1, source_target_pairs={{0,8},{2,10},{4,12},{6,14},{8,0},{10,2},{12,4},{14,6},{1,16},{3,18... | collective-permute-start | bytes 786440 | tf_op jit(solution)/shard_map/ppermute | solution.py:569
  9.1 4.6 %load.1.w_ref = bf16[3,4096,512]{2,1,0:T(8,128)(2,1)S(1)} custom-call(bf16[3,4096,512]{2,1,0:T(8,128)(2,1)} %bitcast.6), custom_call_target="tpu_custom_call" | custom-call | bytes 25165824 | tf_op jit(solution)/shard_map/load/pallas_call | solution.py:243
  13.7 1.4 %collective-permute-done.1.outer_ref.inner_ref = bf16[256,512]{1,0:T(8,128)(2,1)S(1)} collective-permute-done((bf16[256,512]{1,0:T(8,128)(2,1)S(1)}, bf16[256,512]{1,0:T(8,128)(2,1)S(1)}, u32[]{:S(2)}, u32[]{:S(2)}) %collective-permute-start.1) | collective-permute-done | bytes 262176 | tf_op jit(solution)/shard_map/ppermute | solution.py:569
  15.8 2.0 %collective-permute-start.3 = (bf16[256,512]{1,0:T(8,128)(2,1)S(1)}, bf16[256,512]{1,0:T(8,128)(2,1)S(1)}, u32[]{:S(2)}, u32[]{:S(2)}) collective-permute-start(bf16[256,512]{1,0:T(8,128)(2,1)S(1)} %choose.2.refs_0_), channel_id=1, source_target_pairs={{0,2},{1,3},{2,0},{3,1},{4,6},{5,7},{6,4},{7,5},{8,10},{9,11},{10,... | collective-permute-start | bytes 786440 | tf_op jit(solution)/shard_map/ppermute | solution.py:560
  17.9 1.5 %collective-permute-start.4 = (bf16[256,512]{1,0:T(8,128)(2,1)S(1)}, bf16[256,512]{1,0:T(8,128)(2,1)S(1)}, u32[]{:S(2)}, u32[]{:S(2)}) collective-permute-start(bf16[256,512]{1,0:T(8,128)(2,1)S(1)} %choose.2.refs_0_), channel_id=1, source_target_pairs={{0,4},{1,5},{2,6},{3,7},{4,0},{5,1},{6,2},{7,3},{8,12},{9,13},{10,... | collective-permute-start | bytes 786440 | tf_op jit(solution)/shard_map/ppermute | solution.py:563
  21.0 3.6 %collective-permute-done.3.refs_0_ = bf16[256,512]{1,0:T(8,128)(2,1)S(1)} collective-permute-done((bf16[256,512]{1,0:T(8,128)(2,1)S(1)}, bf16[256,512]{1,0:T(8,128)(2,1)S(1)}, u32[]{:S(2)}, u32[]{:S(2)}) %collective-permute-start.3) | collective-permute-done | bytes 262176 | tf_op jit(solution)/shard_map/ppermute | solution.py:560
  24.6 1.5 %collective-permute-done.4.refs_1_ = bf16[256,512]{1,0:T(8,128)(2,1)S(1)} collective-permute-done((bf16[256,512]{1,0:T(8,128)(2,1)S(1)}, bf16[256,512]{1,0:T(8,128)(2,1)S(1)}, u32[]{:S(2)}, u32[]{:S(2)}) %collective-permute-start.4) | collective-permute-done | bytes 262176 | tf_op jit(solution)/shard_map/ppermute | solution.py:563
  26.1 1.5 %collective-permute-start.6 = (bf16[256,512]{1,0:T(8,128)(2,1)S(1)}, bf16[256,512]{1,0:T(8,128)(2,1)S(1)}, u32[]{:S(2)}, u32[]{:S(2)}) collective-permute-start(bf16[256,512]{1,0:T(8,128)(2,1)S(1)} %collective-permute-done.3.refs_0_), channel_id=1, source_target_pairs={{0,4},{1,5},{2,6},{3,7},{4,0},{5,1},{6,2},{7,3},{8,12},{9,13},{10,... | collective-permute-start | bytes 786440 | tf_op jit(solution)/shard_map/ppermute | solution.py:563
  29.2 1.7 %collective-permute-done.8.refs_1_ = bf16[256,512]{1,0:T(8,128)(2,1)S(1)} collective-permute-done((bf16[256,512]{1,0:T(8,128)(2,1)S(1)}, bf16[256,512]{1,0:T(8,128)(2,1)S(1)}, u32[]{:S(2)}, u32[]{:S(2)}) %collective-permute-start.8) | collective-permute-done | bytes 262176 | tf_op jit(solution)/shard_map/ppermute | solution.py:563
  32.2 4.3 %collective-permute-done.6.refs_0_ = bf16[256,512]{1,0:T(8,128)(2,1)S(1)} collective-permute-done((bf16[256,512]{1,0:T(8,128)(2,1)S(1)}, bf16[256,512]{1,0:T(8,128)(2,1)S(1)}, u32[]{:S(2)}, u32[]{:S(2)}) %collective-permute-start.6) | collective-permute-done | bytes 262176 | tf_op jit(solution)/shard_map/ppermute | solution.py:563
  36.5 2.8 %collective-permute-done.9.refs_1_ = bf16[256,512]{1,0:T(8,128)(2,1)S(1)} collective-permute-done((bf16[256,512]{1,0:T(8,128)(2,1)S(1)}, bf16[256,512]{1,0:T(8,128)(2,1)S(1)}, u32[]{:S(2)}, u32[]{:S(2)}) %collective-permute-start.9) | collective-permute-done | bytes 262176 | tf_op jit(solution)/shard_map/ppermute | solution.py:560
  41.3 1.9 %collective-permute-done.10.other_ref = f32[3,256,256]{2,1,0:T(8,128)S(1)} collective-permute-done((f32[3,256,256]{2,1,0:T(8,128)S(1)}, f32[3,256,256]{2,1,0:T(8,128)S(1)}, u32[]{:S(2)}, u32[]{:S(2)}) %collective-permute-start.10) | collective-permute-done | bytes 786464 | tf_op jit(solution)/shard_map/ppermute | solution.py:557
  43.2 4.6 %mixer.1 = (bf16[128,256]{1,0:T(8,128)(2,1)S(1)}, bf16[128,256]{1,0:T(8,128)(2,1)S(1)}, bf16[3,256,256]{2,1,0:T(8,128)(2,1)S(1)}) custom-call(f32[3,256,256]{2,1,0:T(8,128)S(1)} %get-tuple-element.47.keep_ref, f32[3,256,256]{2,1,0:T(8,128)S(1)} %collective-permute-done.10.other_ref, f32[3,7,512]{2,1,0:T(8,128)S(1)} %bitcast.3, f32[16,512]{1,0:T(8,128)S(1)} %copy-done.4, ...), custom_call_target="tpu_custom_call" | custom-call | flops 12582912 | bytes 1878016 | tf_op jit(solution)/shard_map/mixer/pallas_call | solution.py:160
  51.0 1.7 %collective-permute-start.13 = (bf16[512,256]{1,0:T(8,128)(2,1)S(1)}, bf16[512,256]{1,0:T(8,128)(2,1)S(1)}, u32[]{:S(2)}, u32[]{:S(2)}) collective-permute-start(bf16[512,256]{1,0:T(8,128)(2,1)S(1)} %get-tuple-element.55), channel_id=1, source_target_pairs={{0,4},{1,5},{2,6},{3,7},{4,0},{5,1},{6,2},{7,3},{8,12},{9,13},{10,... | collective-permute-start | bytes 786440 | tf_op jit(solution)/shard_map/ppermute | solution.py:563
  52.7 2.6 %back_project.2 = (bf16[512,256]{1,0:T(8,128)(2,1)S(1)}, f32[512,256]{1,0:T(8,128)S(1)}, f32[512,256]{1,0:T(8,128)S(1)}, bf16[512,256]{1,0:T(8,128)(2,1)S(1)}, f...) custom-call(bf16[3,4096,512]{2,1,0:T(8,128)(2,1)S(1)} %load.1.w_ref, bf16[3,256,256]{2,1,0:T(8,128)(2,1)S(1)} %get-tuple-element.52.own_ref, ...), custom_call_target="tpu_custom_call" | custom-call | flops 2415919104 | bytes 8388608 | tf_op jit(solution)/shard_map/back_project/pallas_call | solution.py:160
  55.3 1.6 %collective-permute-start.16 = (bf16[512,256]{1,0:T(8,128)(2,1)S(1)}, bf16[512,256]{1,0:T(8,128)(2,1)S(1)}, u32[]{:S(2)}, u32[]{:S(2)}) collective-permute-start(bf16[512,256]{1,0:T(8,128)(2,1)S(1)} %get-tuple-element.59), channel_id=1, source_target_pairs={{0,2},{1,3},{2,0},{3,1},{4,6},{5,7},{6,4},{7,5},{8,10},{9,11},{10,... | collective-permute-start | bytes 786440 | tf_op jit(solution)/shard_map/ppermute | solution.py:560
  56.9 2.9 %collective-permute-done.17.got_ref = bf16[512,256]{1,0:T(8,128)(2,1)S(1)} collective-permute-done((bf16[512,256]{1,0:T(8,128)(2,1)S(1)}, bf16[512,256]{1,0:T(8,128)(2,1)S(1)}, u32[]{:S(2)}, u32[]{:S(2)}) %collective-permute-start.17) | collective-permute-done | bytes 262176 | tf_op jit(solution)/shard_map/ppermute | solution.py:560
  59.9 1.6 %collective-permute-start.18 = (bf16[512,256]{1,0:T(8,128)(2,1)S(1)}, bf16[512,256]{1,0:T(8,128)(2,1)S(1)}, u32[]{:S(2)}, u32[]{:S(2)}) collective-permute-start(bf16[512,256]{1,0:T(8,128)(2,1)S(1)} %merge.3), channel_id=1, source_target_pairs={{0,4},{1,5},{2,6},{3,7},{4,0},{5,1},{6,2},{7,3},{8,12},{9,13},{10,... | collective-permute-start | bytes 786440 | tf_op jit(solution)/shard_map/ppermute | solution.py:563
  62.1 3.3 %collective-permute-done.16.x_ref = bf16[512,256]{1,0:T(8,128)(2,1)S(1)} collective-permute-done((bf16[512,256]{1,0:T(8,128)(2,1)S(1)}, bf16[512,256]{1,0:T(8,128)(2,1)S(1)}, u32[]{:S(2)}, u32[]{:S(2)}) %collective-permute-start.16) | collective-permute-done | bytes 262176 | tf_op jit(solution)/shard_map/ppermute | solution.py:560
  65.4 3.7 %collective-permute-done.18.y_ref = bf16[512,256]{1,0:T(8,128)(2,1)S(1)} collective-permute-done((bf16[512,256]{1,0:T(8,128)(2,1)S(1)}, bf16[512,256]{1,0:T(8,128)(2,1)S(1)}, u32[]{:S(2)}, u32[]{:S(2)}) %collective-permute-start.18) | collective-permute-done | bytes 262176 | tf_op jit(solution)/shard_map/ppermute | solution.py:563
  70.1 2.2 %collective-permute-start.19 = (bf16[512,128]{1,0:T(8,128)(2,1)S(1)}, bf16[512,128]{1,0:T(8,128)(2,1)S(1)}, u32[]{:S(2)}, u32[]{:S(2)}) collective-permute-start(bf16[512,128]{1,0:T(8,128)(2,1)S(1)} %get-tuple-element.62), channel_id=1, source_target_pairs={{0,8},{2,10},{4,12},{6,14},{8,0},{10,2},{12,4},{14,6},{16,9},{18,1... | collective-permute-start | bytes 393224 | tf_op jit(solution)/shard_map/ppermute | solution.py:608
  72.3 2.8 %collective-permute-start.20 = (bf16[512,128]{1,0:T(8,128)(2,1)S(1)}, bf16[512,128]{1,0:T(8,128)(2,1)S(1)}, u32[]{:S(2)}, u32[]{:S(2)}) collective-permute-start(bf16[512,128]{1,0:T(8,128)(2,1)S(1)} %get-tuple-element.63), channel_id=1, source_target_pairs={{0,9},{2,11},{4,13},{6,15},{8,1},{10,3},{12,5},{14,7},{16,8},{18,1... | collective-permute-start | bytes 393224 | tf_op jit(solution)/shard_map/ppermute | solution.py:609
  76.0 4.3 %collective-permute-start.11 = (bf16[128,256]{1,0:T(8,128)(2,1)S(1)}, bf16[128,256]{1,0:T(8,128)(2,1)S(1)}, u32[]{:S(2)}, u32[]{:S(2)}) collective-permute-start(bf16[128,256]{1,0:T(8,128)(2,1)S(1)} %get-tuple-element.51), channel_id=1, source_target_pairs={{0,1},{1,0},{2,3},{3,2},{4,5},{5,4},{6,7},{7,6},{8,9},{9,8},{10,11... | collective-permute-start | bytes 196616 | tf_op jit(solution)/shard_map/ppermute | solution.py:557
  81.9 2.9 %collective-permute-done.21.c_ref = bf16[512,128]{1,0:T(8,128)(2,1)S(1)} collective-permute-done((bf16[512,128]{1,0:T(8,128)(2,1)S(1)}, bf16[512,128]{1,0:T(8,128)(2,1)S(1)}, u32[]{:S(2)}, u32[]{:S(2)}) %collective-permute-start.21) | collective-permute-done | bytes 131104 | tf_op jit(solution)/shard_map/ppermute | solution.py:614
  (53 shorter events, 20.8 us)
Async XLA Ops:
  0.6 1.5 %collective-permute-start = (s32[1,128]{1,0:T(1,128)}, s32[1,128]{1,0:T(1,128)S(1)}, u32[]{:S(2)}, u32[]{:S(2)}) collective-permute-start(s32[1,128]{1,0:T(1,128)} %bitcast.4), channel_id=1, source_target_pairs={{0,1},{1,0},{2,3},{3,2},{4,5},{5,4},{6,7},{7,6},{8,9},{9,8},{10,11... | collective-permute-start | bytes 1544 | tf_op jit(solution)/shard_map/ppermute | solution.py:557
  5.1 10.1 %collective-permute-start.1 = (bf16[256,512]{1,0:T(8,128)(2,1)S(1)}, bf16[256,512]{1,0:T(8,128)(2,1)S(1)}, u32[]{:S(2)}, u32[]{:S(2)}) collective-permute-start(bf16[256,512]{1,0:T(8,128)(2,1)S(1)} %get-tuple-element.34.inner_ref), channel_id=1, source_target_pairs={{0,8},{2,10},{4,12},{6,14},{8,0},{10,2},{12,4},{14,6},{1,16},{3,18... | collective-permute-start | bytes 786440 | tf_op jit(solution)/shard_map/ppermute | solution.py:569
  8.0 5.7 %collective-permute-start.2 = (bf16[128,256]{1,0:T(8,128)(2,1)S(1)}, bf16[128,256]{1,0:T(8,128)(2,1)S(1)}, u32[]{:S(2)}, u32[]{:S(2)}) collective-permute-start(bf16[128,256]{1,0:T(8,128)(2,1)S(1)} %get-tuple-element.35), channel_id=1, source_target_pairs={{0,1},{1,0},{2,3},{3,2},{4,5},{5,4},{6,7},{7,6},{8,9},{9,8},{10,11... | collective-permute-start | bytes 196616 | tf_op jit(solution)/shard_map/ppermute | solution.py:557
  15.1 4.2 %collective-permute-start.5 = (bf16[256,512]{1,0:T(8,128)(2,1)S(1)}, bf16[256,512]{1,0:T(8,128)(2,1)S(1)}, u32[]{:S(2)}, u32[]{:S(2)}) collective-permute-start(bf16[256,512]{1,0:T(8,128)(2,1)S(1)} %choose.2.refs_0_), channel_id=1, source_target_pairs={{8,16},{10,18},{12,20},{14,22},{16,24},{18,26},{20,28},{22,30},{17... | collective-permute-start | bytes 786440 | tf_op jit(solution)/shard_map/ppermute | solution.py:574
  15.8 8.8 %collective-permute-start.3 = (bf16[256,512]{1,0:T(8,128)(2,1)S(1)}, bf16[256,512]{1,0:T(8,128)(2,1)S(1)}, u32[]{:S(2)}, u32[]{:S(2)}) collective-permute-start(bf16[256,512]{1,0:T(8,128)(2,1)S(1)} %choose.2.refs_0_), channel_id=1, source_target_pairs={{0,2},{1,3},{2,0},{3,1},{4,6},{5,7},{6,4},{7,5},{8,10},{9,11},{10,... | collective-permute-start | bytes 786440 | tf_op jit(solution)/shard_map/ppermute | solution.py:560
  17.9 8.2 %collective-permute-start.4 = (bf16[256,512]{1,0:T(8,128)(2,1)S(1)}, bf16[256,512]{1,0:T(8,128)(2,1)S(1)}, u32[]{:S(2)}, u32[]{:S(2)}) collective-permute-start(bf16[256,512]{1,0:T(8,128)(2,1)S(1)} %choose.2.refs_0_), channel_id=1, source_target_pairs={{0,4},{1,5},{2,6},{3,7},{4,0},{5,1},{6,2},{7,3},{8,12},{9,13},{10,... | collective-permute-start | bytes 786440 | tf_op jit(solution)/shard_map/ppermute | solution.py:563
  19.4 9.8 %collective-permute-start.7 = (bf16[256,512]{1,0:T(8,128)(2,1)S(1)}, bf16[256,512]{1,0:T(8,128)(2,1)S(1)}, u32[]{:S(2)}, u32[]{:S(2)}) collective-permute-start(bf16[256,512]{1,0:T(8,128)(2,1)S(1)} %choose.3.refs_1_), channel_id=1, source_target_pairs={{0,2},{1,3},{2,0},{3,1},{4,6},{5,7},{6,4},{7,5},{8,10},{9,11},{10,... | collective-permute-start | bytes 786440 | tf_op jit(solution)/shard_map/ppermute | solution.py:560
  20.0 10.9 %collective-permute-start.8 = (bf16[256,512]{1,0:T(8,128)(2,1)S(1)}, bf16[256,512]{1,0:T(8,128)(2,1)S(1)}, u32[]{:S(2)}, u32[]{:S(2)}) collective-permute-start(bf16[256,512]{1,0:T(8,128)(2,1)S(1)} %choose.3.refs_1_), channel_id=1, source_target_pairs={{0,4},{1,5},{2,6},{3,7},{4,0},{5,1},{6,2},{7,3},{8,12},{9,13},{10,... | collective-permute-start | bytes 786440 | tf_op jit(solution)/shard_map/ppermute | solution.py:563
  26.1 10.4 %collective-permute-start.6 = (bf16[256,512]{1,0:T(8,128)(2,1)S(1)}, bf16[256,512]{1,0:T(8,128)(2,1)S(1)}, u32[]{:S(2)}, u32[]{:S(2)}) collective-permute-start(bf16[256,512]{1,0:T(8,128)(2,1)S(1)} %collective-permute-done.3.refs_0_), channel_id=1, source_target_pairs={{0,4},{1,5},{2,6},{3,7},{4,0},{5,1},{6,2},{7,3},{8,12},{9,13},{10,... | collective-permute-start | bytes 786440 | tf_op jit(solution)/shard_map/ppermute | solution.py:563
  30.9 8.5 %collective-permute-start.9 = (bf16[256,512]{1,0:T(8,128)(2,1)S(1)}, bf16[256,512]{1,0:T(8,128)(2,1)S(1)}, u32[]{:S(2)}, u32[]{:S(2)}) collective-permute-start(bf16[256,512]{1,0:T(8,128)(2,1)S(1)} %collective-permute-done.8.refs_1_), channel_id=1, source_target_pairs={{0,2},{1,3},{2,0},{3,1},{4,6},{5,7},{6,4},{7,5},{8,10},{9,11},{10,... | collective-permute-start | bytes 786440 | tf_op jit(solution)/shard_map/ppermute | solution.py:560
  32.2 11.0 %copy-start.1 = (bf16[128,512]{1,0:T(8,128)(2,1)S(1)}, bf16[128,512]{1,0:T(8,128)(2,1)}, u32[]{:S(2)}) copy-start(bf16[128,512]{1,0:T(8,128)(2,1)} %cot_own_ref.1) | copy-start | bytes 393220
  40.7 2.5 %collective-permute-start.10 = (f32[3,256,256]{2,1,0:T(8,128)S(1)}, f32[3,256,256]{2,1,0:T(8,128)S(1)}, u32[]{:S(2)}, u32[]{:S(2)}) collective-permute-start(f32[3,256,256]{2,1,0:T(8,128)S(1)} %get-tuple-element.48), channel_id=1, source_target_pairs={{0,1},{1,0},{2,3},{3,2},{4,5},{5,4},{6,7},{7,6},{8,9},{9,8},{10,11... | collective-permute-start | bytes 2359304 | tf_op jit(solution)/shard_map/ppermute | solution.py:557
  47.8 1.8 %collective-permute-start.12 = (bf16[3,256,256]{2,1,0:T(8,128)(2,1)S(1)}, bf16[3,256,256]{2,1,0:T(8,128)(2,1)S(1)}, u32[]{:S(2)}, u32[]{:S(2)}) collective-permute-start(bf16[3,256,256]{2,1,0:T(8,128)(2,1)S(1)} %get-tuple-element.52.own_ref), channel_id=1, source_target_pairs={{0,1},{1,0},{2,3},{3,2},{4,5},{5,4},{6,7},{7,6},{8,9},{9,8},{10,11... | collective-permute-start | bytes 1179656 | tf_op jit(solution)/shard_map/ppermute | solution.py:557
  50.6 9.2 %collective-permute-start.17 = (bf16[512,256]{1,0:T(8,128)(2,1)S(1)}, bf16[512,256]{1,0:T(8,128)(2,1)S(1)}, u32[]{:S(2)}, u32[]{:S(2)}) collective-permute-start(bf16[512,256]{1,0:T(8,128)(2,1)S(1)} %get-tuple-element.61), channel_id=1, source_target_pairs={{0,2},{1,3},{2,0},{3,1},{4,6},{5,7},{6,4},{7,5},{8,10},{9,11},{10,... | collective-permute-start | bytes 786440 | tf_op jit(solution)/shard_map/ppermute | solution.py:560
  51.0 11.0 %collective-permute-start.13 = (bf16[512,256]{1,0:T(8,128)(2,1)S(1)}, bf16[512,256]{1,0:T(8,128)(2,1)S(1)}, u32[]{:S(2)}, u32[]{:S(2)}) collective-permute-start(bf16[512,256]{1,0:T(8,128)(2,1)S(1)} %get-tuple-element.55), channel_id=1, source_target_pairs={{0,4},{1,5},{2,6},{3,7},{4,0},{5,1},{6,2},{7,3},{8,12},{9,13},{10,... | collective-permute-start | bytes 786440 | tf_op jit(solution)/shard_map/ppermute | solution.py:563
  55.3 10.1 %collective-permute-start.16 = (bf16[512,256]{1,0:T(8,128)(2,1)S(1)}, bf16[512,256]{1,0:T(8,128)(2,1)S(1)}, u32[]{:S(2)}, u32[]{:S(2)}) collective-permute-start(bf16[512,256]{1,0:T(8,128)(2,1)S(1)} %get-tuple-element.59), channel_id=1, source_target_pairs={{0,2},{1,3},{2,0},{3,1},{4,6},{5,7},{6,4},{7,5},{8,10},{9,11},{10,... | collective-permute-start | bytes 786440 | tf_op jit(solution)/shard_map/ppermute | solution.py:560
  59.9 9.3 %collective-permute-start.18 = (bf16[512,256]{1,0:T(8,128)(2,1)S(1)}, bf16[512,256]{1,0:T(8,128)(2,1)S(1)}, u32[]{:S(2)}, u32[]{:S(2)}) collective-permute-start(bf16[512,256]{1,0:T(8,128)(2,1)S(1)} %merge.3), channel_id=1, source_target_pairs={{0,4},{1,5},{2,6},{3,7},{4,0},{5,1},{6,2},{7,3},{8,12},{9,13},{10,... | collective-permute-start | bytes 786440 | tf_op jit(solution)/shard_map/ppermute | solution.py:563
  61.4 13.7 %collective-permute-start.15 = (bf16[512,256]{1,0:T(8,128)(2,1)S(1)}, bf16[512,256]{1,0:T(8,128)(2,1)S(1)}, u32[]{:S(2)}, u32[]{:S(2)}) collective-permute-start(bf16[512,256]{1,0:T(8,128)(2,1)S(1)} %get-tuple-element.56), channel_id=1, source_target_pairs={{0,4},{1,5},{2,6},{3,7},{4,0},{5,1},{6,2},{7,3},{8,12},{9,13},{10,... | collective-permute-start | bytes 786440 | tf_op jit(solution)/shard_map/ppermute | solution.py:563
  62.0 13.1 %collective-permute-start.14 = (bf16[512,256]{1,0:T(8,128)(2,1)S(1)}, bf16[512,256]{1,0:T(8,128)(2,1)S(1)}, u32[]{:S(2)}, u32[]{:S(2)}) collective-permute-start(bf16[512,256]{1,0:T(8,128)(2,1)S(1)} %merge.2), channel_id=1, source_target_pairs={{0,2},{1,3},{2,0},{3,1},{4,6},{5,7},{6,4},{7,5},{8,10},{9,11},{10,... | collective-permute-start | bytes 786440 | tf_op jit(solution)/shard_map/ppermute | solution.py:560
  70.1 11.8 %collective-permute-start.19 = (bf16[512,128]{1,0:T(8,128)(2,1)S(1)}, bf16[512,128]{1,0:T(8,128)(2,1)S(1)}, u32[]{:S(2)}, u32[]{:S(2)}) collective-permute-start(bf16[512,128]{1,0:T(8,128)(2,1)S(1)} %get-tuple-element.62), channel_id=1, source_target_pairs={{0,8},{2,10},{4,12},{6,14},{8,0},{10,2},{12,4},{14,6},{16,9},{18,1... | collective-permute-start | bytes 393224 | tf_op jit(solution)/shard_map/ppermute | solution.py:608
  72.3 9.6 %collective-permute-start.20 = (bf16[512,128]{1,0:T(8,128)(2,1)S(1)}, bf16[512,128]{1,0:T(8,128)(2,1)S(1)}, u32[]{:S(2)}, u32[]{:S(2)}) collective-permute-start(bf16[512,128]{1,0:T(8,128)(2,1)S(1)} %get-tuple-element.63), channel_id=1, source_target_pairs={{0,9},{2,11},{4,13},{6,15},{8,1},{10,3},{12,5},{14,7},{16,8},{18,1... | collective-permute-start | bytes 393224 | tf_op jit(solution)/shard_map/ppermute | solution.py:609
  75.2 9.5 %collective-permute-start.21 = (bf16[512,128]{1,0:T(8,128)(2,1)S(1)}, bf16[512,128]{1,0:T(8,128)(2,1)S(1)}, u32[]{:S(2)}, u32[]{:S(2)}) collective-permute-start(bf16[512,128]{1,0:T(8,128)(2,1)S(1)} %get-tuple-element.64), channel_id=1, source_target_pairs={{0,1},{2,3},{4,5},{6,7},{8,9},{10,11},{12,13},{14,15},{16,0},{18,2... | collective-permute-start | bytes 393224 | tf_op jit(solution)/shard_map/ppermute | solution.py:614
  75.3 9.4 %collective-permute-start.22 = (bf16[512,128]{1,0:T(8,128)(2,1)S(1)}, bf16[512,128]{1,0:T(8,128)(2,1)S(1)}, u32[]{:S(2)}, u32[]{:S(2)}) collective-permute-start(bf16[512,128]{1,0:T(8,128)(2,1)S(1)} %get-tuple-element.65), channel_id=1, source_target_pairs={{16,1},{18,3},{20,5},{22,7},{24,9},{26,11},{28,13},{30,15},{9,24},... | collective-permute-start | bytes 393224 | tf_op jit(solution)/shard_map/ppermute | solution.py:615
  76.0 5.2 %collective-permute-start.11 = (bf16[128,256]{1,0:T(8,128)(2,1)S(1)}, bf16[128,256]{1,0:T(8,128)(2,1)S(1)}, u32[]{:S(2)}, u32[]{:S(2)}) collective-permute-start(bf16[128,256]{1,0:T(8,128)(2,1)S(1)} %get-tuple-element.51), channel_id=1, source_target_pairs={{0,1},{1,0},{2,3},{3,2},{4,5},{5,4},{6,7},{7,6},{8,9},{9,8},{10,11... | collective-permute-start | bytes 196616 | tf_op jit(solution)/shard_map/ppermute | solution.py:557
  (6 other events, 35.5 us)

commit v2 on v1

--- a/solution.py
+++ b/solution.py
@@ -141,10 +141,23 @@
     return pairs
 
 
-GATHER_Z = (
-    along_z([((0, 0), (1, 0)), ((1, 0), (0, 0)), ((0, 1), (2, 0)), ((1, 1), (3, 0))]),
-    along_z([((1, 0), (2, 0)), ((2, 0), (3, 0))]),
-)
+def some_cores(move, inner):
+    pairs = []
+    for z in range(4):
+        core = (z >> 1) if inner else 1 - (z >> 1)
+        for y in range(2):
+            for x in range(2):
+                pairs.append((device_at(z, y, x, core), device_at(*move(z, y, x, core))))
+    return pairs
+
+
+OVER_X_INNER = some_cores(lambda z, y, x, core: (z, y, 1 - x, core), True)
+OVER_Y_INNER = some_cores(lambda z, y, x, core: (z, 1 - y, x, core), True)
+OVER_X_OUTER = some_cores(lambda z, y, x, core: (z, y, 1 - x, core), False)
+OVER_Y_OUTER = some_cores(lambda z, y, x, core: (z, 1 - y, x, core), False)
+DIAGONAL = some_cores(lambda z, y, x, core: (z, 1 - y, 1 - x, 1 - core), False)
+GATHER_Z = along_z([((0, 0), (1, 0)), ((1, 0), (0, 0)), ((0, 1), (2, 0)), ((1, 1), (3, 0))])
+GATHER_Z_OUTER = along_z([((1, 1), (2, 0)), ((0, 1), (3, 0))])
 SCATTER_Z = (
     along_z([((0, 0), (1, 0)), ((1, 0), (0, 0)), ((2, 0), (1, 1)), ((3, 0), (0, 1))]),
     along_z([((0, 0), (1, 1)), ((1, 0), (0, 1)), ((2, 0), (1, 0)), ((3, 0), (0, 0))]),
@@ -165,7 +178,7 @@
         scratch_shapes=list(scratch),
         compiler_params=pltpu.CompilerParams(vmem_limit_bytes=limit * 1024 * 1024),
         cost_estimate=pl.CostEstimate(
-            flops=flops, bytes_accessed=min(sum(sizes), 8 * 1024 * 1024), transcendentals=0
+            flops=flops // 64, bytes_accessed=sum(sizes) // 64, transcendentals=0
         ),
         name=name,
     )(*operands)
@@ -217,45 +230,36 @@
     )
 
 
-def choose_kernel(inner_ref, outer_ref, out_ref):
-    @pl.when(is_inner())
-    def _():
-        out_ref[...] = inner_ref[...]
-
-    @pl.when(jnp.logical_not(is_inner()))
-    def _():
-        out_ref[...] = outer_ref[...]
-
-
-def choose(inner, outer):
-    return small_call(
-        choose_kernel, jax.ShapeDtypeStruct(inner.shape, inner.dtype), [inner, outer], "choose"
-    )
-
-
-def load_kernel(w_ref, out_ref, sem):
-    copy = pltpu.make_async_copy(w_ref, out_ref, sem)
-    copy.start()
-    copy.wait()
-
-
-def load(w):
-    return pl.pallas_call(
-        load_kernel,
-        in_specs=[pl.BlockSpec(memory_space=pltpu.HBM)],
-        out_specs=IN_VMEM,
-        out_shape=pltpu.VMEM(w.shape, w.dtype),
-        scratch_shapes=[pltpu.SemaphoreType.DMA],
+def fetch_kernel(count, *refs):
+    copies = [
+        pltpu.make_async_copy(source, target, refs[-1].at[n])
+        for n, (source, target) in enumerate(zip(refs[:count], refs[count : 2 * count]))
+    ]
+    for copy in copies:
+        copy.start()
+    for copy in copies:
+        copy.wait()
+
+
+def fetch(*arrays):
+    out = pl.pallas_call(
+        functools.partial(fetch_kernel, len(arrays)),
+        in_specs=[pl.BlockSpec(memory_space=pltpu.HBM)] * len(arrays),
+        out_specs=[IN_VMEM] * len(arrays),
+        out_shape=[pltpu.VMEM(array.shape, array.dtype) for array in arrays],
+        scratch_shapes=[pltpu.SemaphoreType.DMA((len(arrays),))],
         compiler_params=pltpu.CompilerParams(vmem_limit_bytes=2 * 1024 * 1024),
         cost_estimate=pl.CostEstimate(
-            flops=0, bytes_accessed=2 * w.size * w.dtype.itemsize, transcendentals=0
+            flops=0,
+            bytes_accessed=2 * sum(array.size * array.dtype.itemsize for array in arrays),
+            transcendentals=0,
         ),
-        name="load",
-    )(pltpu.with_memory_space_constraint(w, pltpu.HBM))
-
-
-def project_kernel(blocks, has_base, last, w_ref, *refs):
-    count = len(blocks)
+        name="fetch",
+    )(*[pltpu.with_memory_space_constraint(array, pltpu.HBM) for array in arrays])
+    return [pltpu.with_memory_space_constraint(array, pltpu.VMEM) for array in out]
+
+
+def project_kernel(inner, outer, count, has_base, last, w_ref, *refs):
     acts = refs[:count]
     groups, _, chans = w_ref.shape
     toks, width = acts[0].shape
@@ -263,31 +267,38 @@
         keep_ref, send_ref, total_ref = refs[-3:]
     else:
         total_ref = refs[-1]
-    starts = [pl.multiple_of(block_at(*block) * width, width) for block in blocks]
-    for g in range(groups):
-        total = refs[count][g] if has_base else None
-        for start, act in zip(starts, acts):
-            term = jnp.dot(act[...], w_ref[g, pl.ds(start, width), :], preferred_element_type=f32)
-            total = term if total is None else total + term
-        total_ref[g] = total
+
+    def add(entries):
+        starts = [pl.multiple_of(block_at(*entry[1:]) * width, width) for entry in entries]
+        for g in range(groups):
+            total = refs[count][g] if has_base else None
+            for start, entry in zip(starts, entries):
+                term = jnp.dot(
+                    acts[entry[0]][...], w_ref[g, pl.ds(start, width), :], preferred_element_type=f32
+                )
+                total = term if total is None else total + term
+            total_ref[g] = total
+
+    pl.when(is_inner())(lambda: add(inner))
+    pl.when(jnp.logical_not(is_inner()))(lambda: add(outer))
     if last:
         half = chans // 2
-        _, _, _, core = here()
+        core = here()[3]
         keep_ref[...] = total_ref[:, :, pl.ds(pl.multiple_of(core * half, half), half)]
         send_ref[...] = total_ref[:, :, pl.ds(pl.multiple_of((1 - core) * half, half), half)]
 
 
-def project(blocks, acts, w, base, last):
+def project(acts, inner, outer, w, base, last):
     groups, _, chans = w.shape
     toks, width = acts[0].shape
     total = jax.ShapeDtypeStruct((groups, toks, chans), f32)
     half = jax.ShapeDtypeStruct((groups, toks, chans // 2), f32)
     return small_call(
-        functools.partial(project_kernel, blocks, base is not None, last),
+        functools.partial(project_kernel, inner, outer, len(acts), base is not None, last),
         [half, half] if last else total,
         [w] + list(acts) + ([] if base is None else [base]),
         "project",
-        2 * len(acts) * groups * width * chans * toks,
+        2 * max(len(inner), len(outer)) * groups * width * chans * toks,
         [pltpu.VMEM(total.shape, f32)] if last else [],
         16,
     )
@@ -563,27 +574,43 @@
         return lax.ppermute(array, BOTH, OVER_Y)
 
     own_ids = token_ids.reshape(1, -1)
-    embedded, cot_send = embed_rows(own_ids, swap(own_ids), embed, cotangent)
+    other_ids = swap(own_ids)
+    table, own_ids, cot = fetch(embed, own_ids, cotangent)
+    embedded, cot_send = embed_rows(own_ids, other_ids, table, cot)
+
+    got_1 = lax.ppermute(embedded, BOTH, GATHER_Z)
+    near_x = lax.ppermute(embedded, BOTH, OVER_X_INNER + GATHER_Z_OUTER)
+    near_y = lax.ppermute(embedded, BOTH, OVER_Y_INNER)
+    near_d = lax.ppermute(embedded, BOTH, DIAGONAL)
     cot_other = swap(cot_send)
-
-    got_1 = lax.ppermute(embedded, BOTH, GATHER_Z[0])
-    w = load(jnp.transpose(w_in, (1, 0, 2)))
-    w = pltpu.with_memory_space_constraint(w, pltpu.VMEM)
+    (w,) = fetch(jnp.transpose(w_in, (1, 0, 2)))
     got_1, cot_other, w = lax.optimization_barrier((got_1, cot_other, w))
-    slot_1 = choose(embedded, got_1)
-    got_2 = lax.ppermute(slot_1, BOTH, GATHER_Z[1])
-    x_1, y_1 = over_x(slot_1), over_y(slot_1)
-    slot_2 = choose(got_1, got_2)
-    x_2, y_2 = over_x(slot_2), over_y(slot_2)
-    sums = project([(1, 0, 0), (2, 0, 0)], [slot_1, slot_2], w, None, False)
+    x_1, y_1 = over_x(got_1), over_y(got_1)
+    got_2 = near_x
+    x_2 = lax.ppermute(got_2, BOTH, OVER_X_OUTER)
+    y_2 = lax.ppermute(got_2, BOTH, OVER_Y_OUTER)
+    sums = project(
+        [embedded, near_x, near_y, near_d, got_1],
+        [(0, 1, 0, 0), (1, 1, 0, 1), (2, 1, 1, 0), (3, 1, 1, 1), (4, 2, 0, 0)],
+        [(4, 1, 0, 0), (1, 2, 0, 0)],
+        w,
+        None,
+        False,
+    )
     x_1, y_1, sums = lax.optimization_barrier((x_1, y_1, sums))
-    d_1 = over_y(x_1)
-    sums = project([(1, 0, 1), (1, 1, 0)], [x_1, y_1], w, sums, False)
-    x_2, y_2, sums = lax.optimization_barrier((x_2, y_2, sums))
-    d_2 = over_x(y_2)
-    sums = project([(2, 0, 1), (2, 1, 0)], [x_2, y_2], w, sums, False)
+    d_1 = over_x(y_1)
+    sums = project([x_1, y_1], [(0, 2, 0, 1), (1, 2, 1, 0)], [(0, 1, 0, 1), (1, 1, 1, 0)], w, sums, False)
+    x_2, y_2 = lax.optimization_barrier((x_2, y_2))
+    d_2 = lax.ppermute(x_2, BOTH, OVER_Y_OUTER)
     d_1, d_2, sums = lax.optimization_barrier((d_1, d_2, sums))
-    keep, send = project([(1, 1, 1), (2, 1, 1)], [d_1, d_2], w, sums, True)
+    keep, send = project(
+        [x_2, y_2, d_1, d_2],
+        [(2, 2, 1, 1)],
+        [(0, 2, 0, 1), (1, 2, 1, 0), (2, 1, 1, 1), (3, 2, 1, 1)],
+        w,
+        sums,
+        True,
+    )
 
     mixed_own, mixed_send, grad_own = mixer(
         keep, swap(send), jnp.transpose(taps, (1, 0, 2)), rates, residues, cotangent, cot_other

time: 86.6 us -> 85.9 us (level)
  starting transfers between devices: 28.3 us -> 36.1 us
  waiting for transfers between devices: 33.9 us -> 27.1 us
  local copies, waits for them, and re-layouts: 2.62 us -> 0.03 us
    ppermute x6 -> x4, waiting for transfers between devices: 11.2 us -> 3.75 us  [over_y(): return lax.ppermute(array, BOTH, OVER_Y)]
    ppermute x2 -> x7, starting transfers between devices: 3.61 us -> 11 us  [the longest x1 3.42 us: chip_plan(): near_y = lax.ppermute(embedded, BOTH, OVER_Y_INNER)]
    ppermute x6 -> x4, starting transfers between devices: 6.91 us -> 3.56 us  [over_y(): return lax.ppermute(array, BOTH, OVER_Y)]
    unnamed x14 -> x8, local copies, waits for them, and re-layouts: 2.62 us -> 0.03 us
    ppermute x5, starting transfers between devices: 7.03 us -> 9.24 us  [swap(): return lax.ppermute(array, BOTH, OTHER_CORE)]
    ppermute x6 -> x5, waiting for transfers between devices: 13.3 us -> 14.9 us  [over_x(): return lax.ppermute(array, BOTH, OVER_X)]
    ppermute x1, starting transfers between devices: 2.81 us -> 4.34 us  [chip_plan(): lax.ppermute(send_2, BOTH, SCATTER_Z[1])]
    ppermute x1, waiting for transfers between devices: 2.86 us -> 4.26 us  [chip_plan(): lax.ppermute(send_1, BOTH, SCATTER_Z[2])]
  transfers between devices with their start and end apart: 23 -> 25, of which waited for: 15 -> 9; matrix products, arithmetic and copies ran while one was open for 0% -> 0% of each run, Pallas kernels for 14% -> 16%
where the time goes in v2:
time: 85.9 us; the launch traced here: 84.9 us
  starting transfers between devices  36.1 us (42%)
  waiting for transfers between devices  27.1 us (32%)
  Pallas kernels  20.8 us (24%)
  between operations  0.86 us (1%)
    pallas_call x13, Pallas kernels, small_call(): pl.pallas_call(kernel, in_specs=[IN_VMEM] * len(operands), out_specs=jax....  15.1 us
    ppermute x5, waiting for transfers between devices, over_x(): return lax.ppermute(array, BOTH, OVER_X)  14.9 us
    ppermute x5, starting transfers between devices, swap(): return lax.ppermute(array, BOTH, OTHER_CORE)  9.24 us
    ppermute x5, starting transfers between devices, over_x(): return lax.ppermute(array, BOTH, OVER_X)  6.13 us
    pallas_call x2, Pallas kernels, fetch(): pl.pallas_call(functools.partial(fetch_kernel, len(arrays)), in_specs=[pl...  5.69 us
    ppermute x1, starting transfers between devices, chip_plan(): lax.ppermute(send_2, BOTH, SCATTER_Z[1])  4.34 us
    ppermute x1, waiting for transfers between devices, chip_plan(): lax.ppermute(send_1, BOTH, SCATTER_Z[2])  4.26 us
    ppermute x5, waiting for transfers between devices, swap(): return lax.ppermute(array, BOTH, OTHER_CORE)  4.17 us
  transfers between devices with their start and end apart: 25, of which 9 were waited for; matrix products, arithmetic and copies ran while one was open for 0% of the time, Pallas kernels for 16%

profile of v2, /device:TPU:0, one launch (start us, length us, event | category | flops | bytes accessed | tf_op | source)
XLA Modules:
  0.0 84.9 jit_solution(16165565537468659924)
XLA Ops:
  2.6 2.8 %collective-permute-start.1 = (bf16[256,512]{1,0:T(8,128)(2,1)S(1)}, bf16[256,512]{1,0:T(8,128)(2,1)S(1)}, u32[]{:S(2)}, u32[]{:S(2)}) collective-permute-start(bf16[256,512]{1,0:T(8,128)(2,1)S(1)} %get-tuple-element.39.refs_0_), channel_id=1, source_target_pairs={{0,8},{2,10},{4,12},{6,14},{8,0},{10,2},{12,4},{14,6},{1,16},{3,18... | collective-permute-start | bytes 786440 | tf_op jit(solution)/shard_map/ppermute | solution.py:581
  5.4 1.5 %collective-permute-start.3 = (bf16[256,512]{1,0:T(8,128)(2,1)S(1)}, bf16[256,512]{1,0:T(8,128)(2,1)S(1)}, u32[]{:S(2)}, u32[]{:S(2)}) collective-permute-start(bf16[256,512]{1,0:T(8,128)(2,1)S(1)} %get-tuple-element.39.refs_0_), channel_id=1, source_target_pairs={{0,2},{2,0},{4,6},{6,4},{8,10},{10,8},{12,14},{14,12},{17,19},{19,... | collective-permute-start | bytes 786440 | tf_op jit(solution)/shard_map/ppermute | solution.py:582
  6.9 3.4 %collective-permute-start.8 = (bf16[256,512]{1,0:T(8,128)(2,1)S(1)}, bf16[256,512]{1,0:T(8,128)(2,1)S(1)}, u32[]{:S(2)}, u32[]{:S(2)}) collective-permute-start(bf16[256,512]{1,0:T(8,128)(2,1)S(1)} %get-tuple-element.39.refs_0_), channel_id=1, source_target_pairs={{0,4},{2,6},{4,0},{6,2},{8,12},{10,14},{12,8},{14,10},{17,21},{19,... | collective-permute-start | bytes 786440 | tf_op jit(solution)/shard_map/ppermute | solution.py:583
  10.4 1.3 %collective-permute-start.9 = (bf16[256,512]{1,0:T(8,128)(2,1)S(1)}, bf16[256,512]{1,0:T(8,128)(2,1)S(1)}, u32[]{:S(2)}, u32[]{:S(2)}) collective-permute-start(bf16[256,512]{1,0:T(8,128)(2,1)S(1)} %get-tuple-element.39.refs_0_), channel_id=1, source_target_pairs={{1,6},{3,4},{5,2},{7,0},{9,14},{11,12},{13,10},{15,8},{16,23},{18,... | collective-permute-start | bytes 786440 | tf_op jit(solution)/shard_map/ppermute | solution.py:584
  11.7 4.6 %fetch.3.w_ref = bf16[3,4096,512]{2,1,0:T(8,128)(2,1)S(1)} custom-call(bf16[3,4096,512]{2,1,0:T(8,128)(2,1)} %bitcast.4), custom_call_target="tpu_custom_call" | custom-call | bytes 25165824 | tf_op jit(solution)/shard_map/fetch/pallas_call | solution.py:245
  19.0 2.2 %project.3.refs_2_ = f32[3,256,512]{2,1,0:T(8,128)S(1)} custom-call(bf16[3,4096,512]{2,1,0:T(8,128)(2,1)S(1)} %fetch.3.w_ref, bf16[256,512]{1,0:T(8,128)(2,1)S(1)} %get-tuple-element.39.refs_0_, bf16[256,512]{1,0:T(8,128)(2,1)S(1)} %collective-permute-done.3.refs_1_, bf16[256,512]{1,0:T(8,128)(2,1)S(1)} %collective-permute-done.8.refs_2_, ...), custom_call_target="tpu_custom_call" | custom-call | flops 31457280 | bytes 217088 | tf_op jit(solution)/shard_map/project/pallas_call | solution.py:173
  21.2 4.0 %collective-permute-done.6.refs_0_ = bf16[256,512]{1,0:T(8,128)(2,1)S(1)} collective-permute-done((bf16[256,512]{1,0:T(8,128)(2,1)S(1)}, bf16[256,512]{1,0:T(8,128)(2,1)S(1)}, u32[]{:S(2)}, u32[]{:S(2)}) %collective-permute-start.6) | collective-permute-done | bytes 262176 | tf_op jit(solution)/shard_map/ppermute | solution.py:571
  25.2 2.2 %collective-permute-start.10 = (bf16[256,512]{1,0:T(8,128)(2,1)S(1)}, bf16[256,512]{1,0:T(8,128)(2,1)S(1)}, u32[]{:S(2)}, u32[]{:S(2)}) collective-permute-start(bf16[256,512]{1,0:T(8,128)(2,1)S(1)} %collective-permute-done.7.refs_1_), channel_id=1, source_target_pairs={{0,2},{1,3},{2,0},{3,1},{4,6},{5,7},{6,4},{7,5},{8,10},{9,11},{10,... | collective-permute-start | bytes 786440 | tf_op jit(solution)/shard_map/ppermute | solution.py:571
  29.1 5.0 %collective-permute-done.10.refs_2_ = bf16[256,512]{1,0:T(8,128)(2,1)S(1)} collective-permute-done((bf16[256,512]{1,0:T(8,128)(2,1)S(1)}, bf16[256,512]{1,0:T(8,128)(2,1)S(1)}, u32[]{:S(2)}, u32[]{:S(2)}) %collective-permute-start.10) | collective-permute-done | bytes 262176 | tf_op jit(solution)/shard_map/ppermute | solution.py:571
  34.8 3.9 %collective-permute-start.12 = (f32[3,256,256]{2,1,0:T(8,128)S(1)}, f32[3,256,256]{2,1,0:T(8,128)S(1)}, u32[]{:S(2)}, u32[]{:S(2)}) collective-permute-start(f32[3,256,256]{2,1,0:T(8,128)S(1)} %get-tuple-element.52), channel_id=1, source_target_pairs={{0,1},{1,0},{2,3},{3,2},{4,5},{5,4},{6,7},{7,6},{8,9},{9,8},{10,11... | collective-permute-start | bytes 2359304 | tf_op jit(solution)/shard_map/ppermute | solution.py:568
  38.7 1.9 %collective-permute-done.12.other_ref = f32[3,256,256]{2,1,0:T(8,128)S(1)} collective-permute-done((f32[3,256,256]{2,1,0:T(8,128)S(1)}, f32[3,256,256]{2,1,0:T(8,128)S(1)}, u32[]{:S(2)}, u32[]{:S(2)}) %collective-permute-start.12) | collective-permute-done | bytes 786464 | tf_op jit(solution)/shard_map/ppermute | solution.py:568
  40.6 4.6 %mixer.1 = (bf16[128,256]{1,0:T(8,128)(2,1)S(1)}, bf16[128,256]{1,0:T(8,128)(2,1)S(1)}, bf16[3,256,256]{2,1,0:T(8,128)(2,1)S(1)}) custom-call(f32[3,256,256]{2,1,0:T(8,128)S(1)} %get-tuple-element.51.keep_ref, f32[3,256,256]{2,1,0:T(8,128)S(1)} %collective-permute-done.12.other_ref, f32[3,7,512]{2,1,0:T(8,128)S(1)} %bitcast.3, f32[16,512]{1,0:T(8,128)S(1)} %copy-done.2, ...), custom_call_target="tpu_custom_call" | custom-call | flops 196608 | bytes 29344 | tf_op jit(solution)/shard_map/mixer/pallas_call | solution.py:173
  45.7 1.3 %collective-permute-done.14.other_ref = bf16[3,256,256]{2,1,0:T(8,128)(2,1)S(1)} collective-permute-done((bf16[3,256,256]{2,1,0:T(8,128)(2,1)S(1)}, bf16[3,256,256]{2,1,0:T(8,128)(2,1)S(1)}, u32[]{:S(2)}, u32[]{:S(2)}) %collective-permute-start.14) | collective-permute-done | bytes 393248 | tf_op jit(solution)/shard_map/ppermute | solution.py:568
  48.0 1.3 %collective-permute-start.19 = (bf16[512,256]{1,0:T(8,128)(2,1)S(1)}, bf16[512,256]{1,0:T(8,128)(2,1)S(1)}, u32[]{:S(2)}, u32[]{:S(2)}) collective-permute-start(bf16[512,256]{1,0:T(8,128)(2,1)S(1)} %get-tuple-element.65), channel_id=1, source_target_pairs={{0,2},{1,3},{2,0},{3,1},{4,6},{5,7},{6,4},{7,5},{8,10},{9,11},{10,... | collective-permute-start | bytes 786440 | tf_op jit(solution)/shard_map/ppermute | solution.py:571
  50.1 2.6 %back_project.2 = (bf16[512,256]{1,0:T(8,128)(2,1)S(1)}, f32[512,256]{1,0:T(8,128)S(1)}, f32[512,256]{1,0:T(8,128)S(1)}, bf16[512,256]{1,0:T(8,128)(2,1)S(1)}, f...) custom-call(bf16[3,4096,512]{2,1,0:T(8,128)(2,1)S(1)} %fetch.3.w_ref, bf16[3,256,256]{2,1,0:T(8,128)(2,1)S(1)} %get-tuple-element.56.own_ref, ...), custom_call_target="tpu_custom_call" | custom-call | flops 37748736 | bytes 208896 | tf_op jit(solution)/shard_map/back_project/pallas_call | solution.py:173
  53.5 3.8 %collective-permute-done.19.got_ref = bf16[512,256]{1,0:T(8,128)(2,1)S(1)} collective-permute-done((bf16[512,256]{1,0:T(8,128)(2,1)S(1)}, bf16[512,256]{1,0:T(8,128)(2,1)S(1)}, u32[]{:S(2)}, u32[]{:S(2)}) %collective-permute-start.19) | collective-permute-done | bytes 262176 | tf_op jit(solution)/shard_map/ppermute | solution.py:571
  58.0 1.4 %collective-permute-start.17 = (bf16[512,256]{1,0:T(8,128)(2,1)S(1)}, bf16[512,256]{1,0:T(8,128)(2,1)S(1)}, u32[]{:S(2)}, u32[]{:S(2)}) collective-permute-start(bf16[512,256]{1,0:T(8,128)(2,1)S(1)} %get-tuple-element.60), channel_id=1, source_target_pairs={{0,4},{1,5},{2,6},{3,7},{4,0},{5,1},{6,2},{7,3},{8,12},{9,13},{10,... | collective-permute-start | bytes 786440 | tf_op jit(solution)/shard_map/ppermute | solution.py:574
  59.4 1.3 %collective-permute-start.16 = (bf16[512,256]{1,0:T(8,128)(2,1)S(1)}, bf16[512,256]{1,0:T(8,128)(2,1)S(1)}, u32[]{:S(2)}, u32[]{:S(2)}) collective-permute-start(bf16[512,256]{1,0:T(8,128)(2,1)S(1)} %merge.2), channel_id=1, source_target_pairs={{0,2},{1,3},{2,0},{3,1},{4,6},{5,7},{6,4},{7,5},{8,10},{9,11},{10,... | collective-permute-start | bytes 786440 | tf_op jit(solution)/shard_map/ppermute | solution.py:571
  60.7 2.2 %collective-permute-done.18.x_ref = bf16[512,256]{1,0:T(8,128)(2,1)S(1)} collective-permute-done((bf16[512,256]{1,0:T(8,128)(2,1)S(1)}, bf16[512,256]{1,0:T(8,128)(2,1)S(1)}, u32[]{:S(2)}, u32[]{:S(2)}) %collective-permute-start.18) | collective-permute-done | bytes 262176 | tf_op jit(solution)/shard_map/ppermute | solution.py:571
  62.9 3.7 %collective-permute-done.20.y_ref = bf16[512,256]{1,0:T(8,128)(2,1)S(1)} collective-permute-done((bf16[512,256]{1,0:T(8,128)(2,1)S(1)}, bf16[512,256]{1,0:T(8,128)(2,1)S(1)}, u32[]{:S(2)}, u32[]{:S(2)}) %collective-permute-start.20) | collective-permute-done | bytes 262176 | tf_op jit(solution)/shard_map/ppermute | solution.py:574
  67.5 1.1 %collective-permute-start.21 = (bf16[512,128]{1,0:T(8,128)(2,1)S(1)}, bf16[512,128]{1,0:T(8,128)(2,1)S(1)}, u32[]{:S(2)}, u32[]{:S(2)}) collective-permute-start(bf16[512,128]{1,0:T(8,128)(2,1)S(1)} %get-tuple-element.66), channel_id=1, source_target_pairs={{0,8},{2,10},{4,12},{6,14},{8,0},{10,2},{12,4},{14,6},{16,9},{18,1... | collective-permute-start | bytes 393224 | tf_op jit(solution)/shard_map/ppermute | solution.py:635
  68.7 4.3 %collective-permute-start.22 = (bf16[512,128]{1,0:T(8,128)(2,1)S(1)}, bf16[512,128]{1,0:T(8,128)(2,1)S(1)}, u32[]{:S(2)}, u32[]{:S(2)}) collective-permute-start(bf16[512,128]{1,0:T(8,128)(2,1)S(1)} %get-tuple-element.67), channel_id=1, source_target_pairs={{0,9},{2,11},{4,13},{6,15},{8,1},{10,3},{12,5},{14,7},{16,8},{18,1... | collective-permute-start | bytes 393224 | tf_op jit(solution)/shard_map/ppermute | solution.py:636
  73.9 4.3 %collective-permute-start.13 = (bf16[128,256]{1,0:T(8,128)(2,1)S(1)}, bf16[128,256]{1,0:T(8,128)(2,1)S(1)}, u32[]{:S(2)}, u32[]{:S(2)}) collective-permute-start(bf16[128,256]{1,0:T(8,128)(2,1)S(1)} %get-tuple-element.55), channel_id=1, source_target_pairs={{0,1},{1,0},{2,3},{3,2},{4,5},{5,4},{6,7},{7,6},{8,9},{9,8},{10,11... | collective-permute-start | bytes 196616 | tf_op jit(solution)/shard_map/ppermute | solution.py:568
  79.8 4.3 %collective-permute-done.23.c_ref = bf16[512,128]{1,0:T(8,128)(2,1)S(1)} collective-permute-done((bf16[512,128]{1,0:T(8,128)(2,1)S(1)}, bf16[512,128]{1,0:T(8,128)(2,1)S(1)}, u32[]{:S(2)}, u32[]{:S(2)}) %collective-permute-start.23) | collective-permute-done | bytes 131104 | tf_op jit(solution)/shard_map/ppermute | solution.py:641
  (49 shorter events, 15.1 us)
Async XLA Ops:
  2.6 13.7 %collective-permute-start.1 = (bf16[256,512]{1,0:T(8,128)(2,1)S(1)}, bf16[256,512]{1,0:T(8,128)(2,1)S(1)}, u32[]{:S(2)}, u32[]{:S(2)}) collective-permute-start(bf16[256,512]{1,0:T(8,128)(2,1)S(1)} %get-tuple-element.39.refs_0_), channel_id=1, source_target_pairs={{0,8},{2,10},{4,12},{6,14},{8,0},{10,2},{12,4},{14,6},{1,16},{3,18... | collective-permute-start | bytes 786440 | tf_op jit(solution)/shard_map/ppermute | solution.py:581
  5.4 12.2 %collective-permute-start.3 = (bf16[256,512]{1,0:T(8,128)(2,1)S(1)}, bf16[256,512]{1,0:T(8,128)(2,1)S(1)}, u32[]{:S(2)}, u32[]{:S(2)}) collective-permute-start(bf16[256,512]{1,0:T(8,128)(2,1)S(1)} %get-tuple-element.39.refs_0_), channel_id=1, source_target_pairs={{0,2},{2,0},{4,6},{6,4},{8,10},{10,8},{12,14},{14,12},{17,19},{19,... | collective-permute-start | bytes 786440 | tf_op jit(solution)/shard_map/ppermute | solution.py:582
  6.9 11.4 %collective-permute-start.8 = (bf16[256,512]{1,0:T(8,128)(2,1)S(1)}, bf16[256,512]{1,0:T(8,128)(2,1)S(1)}, u32[]{:S(2)}, u32[]{:S(2)}) collective-permute-start(bf16[256,512]{1,0:T(8,128)(2,1)S(1)} %get-tuple-element.39.refs_0_), channel_id=1, source_target_pairs={{0,4},{2,6},{4,0},{6,2},{8,12},{10,14},{12,8},{14,10},{17,21},{19,... | collective-permute-start | bytes 786440 | tf_op jit(solution)/shard_map/ppermute | solution.py:583
  10.3 6.0 %collective-permute-start.2 = (bf16[128,256]{1,0:T(8,128)(2,1)S(1)}, bf16[128,256]{1,0:T(8,128)(2,1)S(1)}, u32[]{:S(2)}, u32[]{:S(2)}) collective-permute-start(bf16[128,256]{1,0:T(8,128)(2,1)S(1)} %get-tuple-element.40), channel_id=1, source_target_pairs={{0,1},{1,0},{2,3},{3,2},{4,5},{5,4},{6,7},{7,6},{8,9},{9,8},{10,11... | collective-permute-start | bytes 196616 | tf_op jit(solution)/shard_map/ppermute | solution.py:568
  10.4 8.6 %collective-permute-start.9 = (bf16[256,512]{1,0:T(8,128)(2,1)S(1)}, bf16[256,512]{1,0:T(8,128)(2,1)S(1)}, u32[]{:S(2)}, u32[]{:S(2)}) collective-permute-start(bf16[256,512]{1,0:T(8,128)(2,1)S(1)} %get-tuple-element.39.refs_0_), channel_id=1, source_target_pairs={{1,6},{3,4},{5,2},{7,0},{9,14},{11,12},{13,10},{15,8},{16,23},{18,... | collective-permute-start | bytes 786440 | tf_op jit(solution)/shard_map/ppermute | solution.py:584
  16.3 8.9 %collective-permute-start.6 = (bf16[256,512]{1,0:T(8,128)(2,1)S(1)}, bf16[256,512]{1,0:T(8,128)(2,1)S(1)}, u32[]{:S(2)}, u32[]{:S(2)}) collective-permute-start(bf16[256,512]{1,0:T(8,128)(2,1)S(1)} %collective-permute-done.1.refs_4_), channel_id=1, source_target_pairs={{0,2},{1,3},{2,0},{3,1},{4,6},{5,7},{6,4},{7,5},{8,10},{9,11},{10,... | collective-permute-start | bytes 786440 | tf_op jit(solution)/shard_map/ppermute | solution.py:571
  16.9 8.3 %collective-permute-start.7 = (bf16[256,512]{1,0:T(8,128)(2,1)S(1)}, bf16[256,512]{1,0:T(8,128)(2,1)S(1)}, u32[]{:S(2)}, u32[]{:S(2)}) collective-permute-start(bf16[256,512]{1,0:T(8,128)(2,1)S(1)} %collective-permute-done.1.refs_4_), channel_id=1, source_target_pairs={{0,4},{1,5},{2,6},{3,7},{4,0},{5,1},{6,2},{7,3},{8,12},{9,13},{10,... | collective-permute-start | bytes 786440 | tf_op jit(solution)/shard_map/ppermute | solution.py:574
  17.6 9.9 %collective-permute-start.4 = (bf16[256,512]{1,0:T(8,128)(2,1)S(1)}, bf16[256,512]{1,0:T(8,128)(2,1)S(1)}, u32[]{:S(2)}, u32[]{:S(2)}) collective-permute-start(bf16[256,512]{1,0:T(8,128)(2,1)S(1)} %collective-permute-done.3.refs_1_), channel_id=1, source_target_pairs={{1,3},{3,1},{5,7},{7,5},{9,11},{11,9},{13,15},{15,13},{16,18},{18,... | collective-permute-start | bytes 786440 | tf_op jit(solution)/shard_map/ppermute | solution.py:590
  18.3 9.2 %collective-permute-start.5 = (bf16[256,512]{1,0:T(8,128)(2,1)S(1)}, bf16[256,512]{1,0:T(8,128)(2,1)S(1)}, u32[]{:S(2)}, u32[]{:S(2)}) collective-permute-start(bf16[256,512]{1,0:T(8,128)(2,1)S(1)} %collective-permute-done.3.refs_1_), channel_id=1, source_target_pairs={{1,5},{3,7},{5,1},{7,3},{9,13},{11,15},{13,9},{15,11},{16,20},{18,... | collective-permute-start | bytes 786440 | tf_op jit(solution)/shard_map/ppermute | solution.py:591
  25.2 8.9 %collective-permute-start.10 = (bf16[256,512]{1,0:T(8,128)(2,1)S(1)}, bf16[256,512]{1,0:T(8,128)(2,1)S(1)}, u32[]{:S(2)}, u32[]{:S(2)}) collective-permute-start(bf16[256,512]{1,0:T(8,128)(2,1)S(1)} %collective-permute-done.7.refs_1_), channel_id=1, source_target_pairs={{0,2},{1,3},{2,0},{3,1},{4,6},{5,7},{6,4},{7,5},{8,10},{9,11},{10,... | collective-permute-start | bytes 786440 | tf_op jit(solution)/shard_map/ppermute | solution.py:571
  27.4 6.7 %collective-permute-start.11 = (bf16[256,512]{1,0:T(8,128)(2,1)S(1)}, bf16[256,512]{1,0:T(8,128)(2,1)S(1)}, u32[]{:S(2)}, u32[]{:S(2)}) collective-permute-start(bf16[256,512]{1,0:T(8,128)(2,1)S(1)} %collective-permute-done.4.refs_0_), channel_id=1, source_target_pairs={{1,5},{3,7},{5,1},{7,3},{9,13},{11,15},{13,9},{15,11},{16,20},{18,... | collective-permute-start | bytes 786440 | tf_op jit(solution)/shard_map/ppermute | solution.py:604
  34.8 5.8 %collective-permute-start.12 = (f32[3,256,256]{2,1,0:T(8,128)S(1)}, f32[3,256,256]{2,1,0:T(8,128)S(1)}, u32[]{:S(2)}, u32[]{:S(2)}) collective-permute-start(f32[3,256,256]{2,1,0:T(8,128)S(1)} %get-tuple-element.52), channel_id=1, source_target_pairs={{0,1},{1,0},{2,3},{3,2},{4,5},{5,4},{6,7},{7,6},{8,9},{9,8},{10,11... | collective-permute-start | bytes 2359304 | tf_op jit(solution)/shard_map/ppermute | solution.py:568
  45.3 1.8 %collective-permute-start.14 = (bf16[3,256,256]{2,1,0:T(8,128)(2,1)S(1)}, bf16[3,256,256]{2,1,0:T(8,128)(2,1)S(1)}, u32[]{:S(2)}, u32[]{:S(2)}) collective-permute-start(bf16[3,256,256]{2,1,0:T(8,128)(2,1)S(1)} %get-tuple-element.56.own_ref), channel_id=1, source_target_pairs={{0,1},{1,0},{2,3},{3,2},{4,5},{5,4},{6,7},{7,6},{8,9},{9,8},{10,11... | collective-permute-start | bytes 1179656 | tf_op jit(solution)/shard_map/ppermute | solution.py:568
  48.0 9.2 %collective-permute-start.19 = (bf16[512,256]{1,0:T(8,128)(2,1)S(1)}, bf16[512,256]{1,0:T(8,128)(2,1)S(1)}, u32[]{:S(2)}, u32[]{:S(2)}) collective-permute-start(bf16[512,256]{1,0:T(8,128)(2,1)S(1)} %get-tuple-element.65), channel_id=1, source_target_pairs={{0,2},{1,3},{2,0},{3,1},{4,6},{5,7},{6,4},{7,5},{8,10},{9,11},{10,... | collective-permute-start | bytes 786440 | tf_op jit(solution)/shard_map/ppermute | solution.py:571
  49.3 10.1 %collective-permute-start.15 = (bf16[512,256]{1,0:T(8,128)(2,1)S(1)}, bf16[512,256]{1,0:T(8,128)(2,1)S(1)}, u32[]{:S(2)}, u32[]{:S(2)}) collective-permute-start(bf16[512,256]{1,0:T(8,128)(2,1)S(1)} %get-tuple-element.59), channel_id=1, source_target_pairs={{0,4},{1,5},{2,6},{3,7},{4,0},{5,1},{6,2},{7,3},{8,12},{9,13},{10,... | collective-permute-start | bytes 786440 | tf_op jit(solution)/shard_map/ppermute | solution.py:574
  52.7 10.1 %collective-permute-start.18 = (bf16[512,256]{1,0:T(8,128)(2,1)S(1)}, bf16[512,256]{1,0:T(8,128)(2,1)S(1)}, u32[]{:S(2)}, u32[]{:S(2)}) collective-permute-start(bf16[512,256]{1,0:T(8,128)(2,1)S(1)} %get-tuple-element.63), channel_id=1, source_target_pairs={{0,2},{1,3},{2,0},{3,1},{4,6},{5,7},{6,4},{7,5},{8,10},{9,11},{10,... | collective-permute-start | bytes 786440 | tf_op jit(solution)/shard_map/ppermute | solution.py:571
  57.3 9.3 %collective-permute-start.20 = (bf16[512,256]{1,0:T(8,128)(2,1)S(1)}, bf16[512,256]{1,0:T(8,128)(2,1)S(1)}, u32[]{:S(2)}, u32[]{:S(2)}) collective-permute-start(bf16[512,256]{1,0:T(8,128)(2,1)S(1)} %merge.3), channel_id=1, source_target_pairs={{0,4},{1,5},{2,6},{3,7},{4,0},{5,1},{6,2},{7,3},{8,12},{9,13},{10,... | collective-permute-start | bytes 786440 | tf_op jit(solution)/shard_map/ppermute | solution.py:574
  58.0 15.0 %collective-permute-start.17 = (bf16[512,256]{1,0:T(8,128)(2,1)S(1)}, bf16[512,256]{1,0:T(8,128)(2,1)S(1)}, u32[]{:S(2)}, u32[]{:S(2)}) collective-permute-start(bf16[512,256]{1,0:T(8,128)(2,1)S(1)} %get-tuple-element.60), channel_id=1, source_target_pairs={{0,4},{1,5},{2,6},{3,7},{4,0},{5,1},{6,2},{7,3},{8,12},{9,13},{10,... | collective-permute-start | bytes 786440 | tf_op jit(solution)/shard_map/ppermute | solution.py:574
  59.4 13.6 %collective-permute-start.16 = (bf16[512,256]{1,0:T(8,128)(2,1)S(1)}, bf16[512,256]{1,0:T(8,128)(2,1)S(1)}, u32[]{:S(2)}, u32[]{:S(2)}) collective-permute-start(bf16[512,256]{1,0:T(8,128)(2,1)S(1)} %merge.2), channel_id=1, source_target_pairs={{0,2},{1,3},{2,0},{3,1},{4,6},{5,7},{6,4},{7,5},{8,10},{9,11},{10,... | collective-permute-start | bytes 786440 | tf_op jit(solution)/shard_map/ppermute | solution.py:571
  67.5 12.3 %collective-permute-start.21 = (bf16[512,128]{1,0:T(8,128)(2,1)S(1)}, bf16[512,128]{1,0:T(8,128)(2,1)S(1)}, u32[]{:S(2)}, u32[]{:S(2)}) collective-permute-start(bf16[512,128]{1,0:T(8,128)(2,1)S(1)} %get-tuple-element.66), channel_id=1, source_target_pairs={{0,8},{2,10},{4,12},{6,14},{8,0},{10,2},{12,4},{14,6},{16,9},{18,1... | collective-permute-start | bytes 393224 | tf_op jit(solution)/shard_map/ppermute | solution.py:635
  68.7 11.2 %collective-permute-start.22 = (bf16[512,128]{1,0:T(8,128)(2,1)S(1)}, bf16[512,128]{1,0:T(8,128)(2,1)S(1)}, u32[]{:S(2)}, u32[]{:S(2)}) collective-permute-start(bf16[512,128]{1,0:T(8,128)(2,1)S(1)} %get-tuple-element.67), channel_id=1, source_target_pairs={{0,9},{2,11},{4,13},{6,15},{8,1},{10,3},{12,5},{14,7},{16,8},{18,1... | collective-permute-start | bytes 393224 | tf_op jit(solution)/shard_map/ppermute | solution.py:636
  73.2 10.9 %collective-permute-start.23 = (bf16[512,128]{1,0:T(8,128)(2,1)S(1)}, bf16[512,128]{1,0:T(8,128)(2,1)S(1)}, u32[]{:S(2)}, u32[]{:S(2)}) collective-permute-start(bf16[512,128]{1,0:T(8,128)(2,1)S(1)} %get-tuple-element.68), channel_id=1, source_target_pairs={{0,1},{2,3},{4,5},{6,7},{8,9},{10,11},{12,13},{14,15},{16,0},{18,2... | collective-permute-start | bytes 393224 | tf_op jit(solution)/shard_map/ppermute | solution.py:641
  73.2 10.8 %collective-permute-start.24 = (bf16[512,128]{1,0:T(8,128)(2,1)S(1)}, bf16[512,128]{1,0:T(8,128)(2,1)S(1)}, u32[]{:S(2)}, u32[]{:S(2)}) collective-permute-start(bf16[512,128]{1,0:T(8,128)(2,1)S(1)} %get-tuple-element.69), channel_id=1, source_target_pairs={{16,1},{18,3},{20,5},{22,7},{24,9},{26,11},{28,13},{30,15},{9,24},... | collective-permute-start | bytes 393224 | tf_op jit(solution)/shard_map/ppermute | solution.py:642
  73.9 5.2 %collective-permute-start.13 = (bf16[128,256]{1,0:T(8,128)(2,1)S(1)}, bf16[128,256]{1,0:T(8,128)(2,1)S(1)}, u32[]{:S(2)}, u32[]{:S(2)}) collective-permute-start(bf16[128,256]{1,0:T(8,128)(2,1)S(1)} %get-tuple-element.55), channel_id=1, source_target_pairs={{0,1},{1,0},{2,3},{3,2},{4,5},{5,4},{6,7},{7,6},{8,9},{9,8},{10,11... | collective-permute-start | bytes 196616 | tf_op jit(solution)/shard_map/ppermute | solution.py:568
  (5 other events, 79.3 us)

commit v3 on v2

--- a/solution.py
+++ b/solution.py
@@ -123,6 +123,7 @@
 OTHER_CORE = everywhere(lambda z, y, x, core: (z, y, x, 1 - core))
 OVER_X = everywhere(lambda z, y, x, core: (z, y, 1 - x, core))
 OVER_Y = everywhere(lambda z, y, x, core: (z, 1 - y, x, core))
+OVER_XY = everywhere(lambda z, y, x, core: (z, 1 - y, 1 - x, core))
 
 
 def along_z(moves):
@@ -155,6 +156,7 @@
 OVER_Y_INNER = some_cores(lambda z, y, x, core: (z, 1 - y, x, core), True)
 OVER_X_OUTER = some_cores(lambda z, y, x, core: (z, y, 1 - x, core), False)
 OVER_Y_OUTER = some_cores(lambda z, y, x, core: (z, 1 - y, x, core), False)
+OVER_XY_OUTER = some_cores(lambda z, y, x, core: (z, 1 - y, 1 - x, core), False)
 DIAGONAL = some_cores(lambda z, y, x, core: (z, 1 - y, 1 - x, 1 - core), False)
 GATHER_Z = along_z([((0, 0), (1, 0)), ((1, 0), (0, 0)), ((0, 1), (2, 0)), ((1, 1), (3, 0))])
 GATHER_Z_OUTER = along_z([((1, 1), (2, 0)), ((0, 1), (3, 0))])
@@ -200,11 +202,10 @@
     return along * 4 + (1 - y if far_y else y) * 2 + (1 - x if far_x else x)
 
 
-def embed_kernel(own_ref, other_ref, table_ref, cot_ref, out_ref, cot_out_ref):
+def embed_kernel(own_ref, other_ref, table_ref, out_ref):
     vocab = table_ref.shape[0]
     half = own_ref.shape[1]
-    chan_half = cot_out_ref.shape[1]
-    _, _, _, core = here()
+    core = here()[3]
     for ref, side in ((own_ref, core), (other_ref, 1 - core)):
         across = jnp.broadcast_to(ref[...].astype(f32), (half, half)).T
         lane = lax.broadcasted_iota(jnp.int32, (half, half), 1).astype(f32)
@@ -213,27 +214,23 @@
             jnp.concatenate(picks, axis=1).astype(bf16), table_ref[...], preferred_element_type=f32
         )
         out_ref[pl.ds(pl.multiple_of(side * half, half), half), :] = rows.astype(bf16)
-    cot_out_ref[...] = cot_ref[:, pl.ds(pl.multiple_of((1 - core) * chan_half, chan_half), chan_half)]
-
-
-def embed_rows(own_ids, other_ids, table, cotangent):
+
+
+def embed_rows(own_ids, other_ids, table):
     toks, width = 2 * own_ids.shape[1], table.shape[1]
     return small_call(
         embed_kernel,
-        [
-            jax.ShapeDtypeStruct((toks, width), bf16),
-            jax.ShapeDtypeStruct((cotangent.shape[0], cotangent.shape[1] // 2), bf16),
-        ],
-        [own_ids, other_ids, table, cotangent],
+        jax.ShapeDtypeStruct((toks, width), bf16),
+        [own_ids, other_ids, table],
         "embed_rows",
         2 * toks * table.shape[0] * width,
     )
 
 
-def fetch_kernel(count, *refs):
+def fetch_kernel(ids_ref, table_ref, ids_out, table_out, sems):
     copies = [
-        pltpu.make_async_copy(source, target, refs[-1].at[n])
-        for n, (source, target) in enumerate(zip(refs[:count], refs[count : 2 * count]))
+        pltpu.make_async_copy(ids_ref, ids_out, sems.at[0]),
+        pltpu.make_async_copy(table_ref, table_out, sems.at[1]),
     ]
     for copy in copies:
         copy.start()
@@ -241,22 +238,88 @@
         copy.wait()
 
 
-def fetch(*arrays):
+def in_hbm(array):
+    return pltpu.with_memory_space_constraint(array, pltpu.HBM)
+
+
+def in_vmem(array):
+    return pltpu.with_memory_space_constraint(array, pltpu.VMEM)
+
+
+def fetch(ids, table):
     out = pl.pallas_call(
-        functools.partial(fetch_kernel, len(arrays)),
-        in_specs=[pl.BlockSpec(memory_space=pltpu.HBM)] * len(arrays),
-        out_specs=[IN_VMEM] * len(arrays),
-        out_shape=[pltpu.VMEM(array.shape, array.dtype) for array in arrays],
-        scratch_shapes=[pltpu.SemaphoreType.DMA((len(arrays),))],
+        fetch_kernel,
+        in_specs=[pl.BlockSpec(memory_space=pltpu.HBM)] * 2,
+        out_specs=[IN_VMEM] * 2,
+        out_shape=[pltpu.VMEM(ids.shape, ids.dtype), pltpu.VMEM(table.shape, bf16)],
+        scratch_shapes=[pltpu.SemaphoreType.DMA((2,))],
         compiler_params=pltpu.CompilerParams(vmem_limit_bytes=2 * 1024 * 1024),
         cost_estimate=pl.CostEstimate(
-            flops=0,
-            bytes_accessed=2 * sum(array.size * array.dtype.itemsize for array in arrays),
-            transcendentals=0,
+            flops=0, bytes_accessed=4 * table.size, transcendentals=0
         ),
         name="fetch",
-    )(*[pltpu.with_memory_space_constraint(array, pltpu.HBM) for array in arrays])
-    return [pltpu.with_memory_space_constraint(array, pltpu.VMEM) for array in out]
+    )(in_hbm(ids), in_hbm(table))
+    return [in_vmem(array) for array in out]
+
+
+def first_kernel(inner, outer, count, w_ref, *refs):
+    acts = refs[:count]
+    total_ref, w_out, sems = refs[count:]
+    groups, rows, _ = w_out.shape
+    width = acts[0].shape[1]
+    order = [(slot, far_y, far_x) for slot in (1, 2) for far_y in (0, 1) for far_x in (0, 1)]
+    spans = [
+        pl.ds(pl.multiple_of(block_at(*block) * width, width), width) for block in order
+    ]
+    copies = [
+        pltpu.make_async_copy(w_ref.at[:, span, :], w_out.at[:, span, :], sems.at[n])
+        for n, span in enumerate(spans)
+    ]
+    for copy in copies:
+        copy.start()
+
+    def add(entries):
+        met = set()
+        for n, entry in enumerate(entries):
+            block = order.index(entry[1:])
+            if block not in met:
+                copies[block].wait()
+                met.add(block)
+            for g in range(groups):
+                term = jnp.dot(
+                    acts[entry[0]][...], w_out[g, spans[block], :], preferred_element_type=f32
+                )
+                if n == 0:
+                    total_ref[g] = term
+                else:
+                    total_ref[g] += term
+        for block in range(len(order)):
+            if block not in met:
+                copies[block].wait()
+
+    pl.when(is_inner())(lambda: add(inner))
+    pl.when(jnp.logical_not(is_inner()))(lambda: add(outer))
+
+
+def first_project(acts, inner, outer, w):
+    groups, rows, chans = w.shape
+    toks, width = acts[0].shape
+    sums, w = pl.pallas_call(
+        functools.partial(first_kernel, inner, outer, len(acts)),
+        in_specs=[pl.BlockSpec(memory_space=pltpu.HBM)] + [IN_VMEM] * len(acts),
+        out_specs=[IN_VMEM, IN_VMEM],
+        out_shape=[
+            pltpu.VMEM((groups, toks, chans), f32),
+            pltpu.VMEM(w.shape, w.dtype),
+        ],
+        scratch_shapes=[pltpu.SemaphoreType.DMA((rows // width,))],
+        compiler_params=pltpu.CompilerParams(vmem_limit_bytes=16 * 1024 * 1024),
+        cost_estimate=pl.CostEstimate(
+            flops=0, bytes_accessed=2 * w.size * w.dtype.itemsize, transcendentals=0
+        ),
+        name="first_project",
+    )(in_hbm(w), *acts)
+    return in_vmem(sums), in_vmem(w)
 
 
 def project_kernel(inner, outer, count, has_base, last, w_ref, *refs):
@@ -277,7 +340,8 @@
                     acts[entry[0]][...], w_ref[g, pl.ds(start, width), :], preferred_element_type=f32
                 )
                 total = term if total is None else total + term
-            total_ref[g] = total
+            if total is not None:
+                total_ref[g] = total
 
     pl.when(is_inner())(lambda: add(inner))
     pl.when(jnp.logical_not(is_inner()))(lambda: add(outer))
@@ -575,41 +639,40 @@
 
     own_ids = token_ids.reshape(1, -1)
     other_ids = swap(own_ids)
-    table, own_ids, cot = fetch(embed, own_ids, cotangent)
-    embedded, cot_send = embed_rows(own_ids, other_ids, table, cot)
-
+    cot_half = cotangent.shape[1] // 2
+    cot_other = swap(
+        lax.dynamic_slice_in_dim(cotangent, (1 - lax.axis_index("ctx")) * cot_half, cot_half, 1)
+    )
+    own_ids, table = fetch(own_ids, embed)
+    embedded = embed_rows(own_ids, other_ids, table)
+
+    embedded, cot_other = lax.optimization_barrier((embedded, cot_other))
     got_1 = lax.ppermute(embedded, BOTH, GATHER_Z)
     near_x = lax.ppermute(embedded, BOTH, OVER_X_INNER + GATHER_Z_OUTER)
     near_y = lax.ppermute(embedded, BOTH, OVER_Y_INNER)
     near_d = lax.ppermute(embedded, BOTH, DIAGONAL)
-    cot_other = swap(cot_send)
-    (w,) = fetch(jnp.transpose(w_in, (1, 0, 2)))
-    got_1, cot_other, w = lax.optimization_barrier((got_1, cot_other, w))
-    x_1, y_1 = over_x(got_1), over_y(got_1)
-    got_2 = near_x
-    x_2 = lax.ppermute(got_2, BOTH, OVER_X_OUTER)
-    y_2 = lax.ppermute(got_2, BOTH, OVER_Y_OUTER)
-    sums = project(
+    x_1, y_1, d_1 = over_x(got_1), over_y(got_1), lax.ppermute(got_1, BOTH, OVER_XY)
+    sums, w = first_project(
         [embedded, near_x, near_y, near_d, got_1],
         [(0, 1, 0, 0), (1, 1, 0, 1), (2, 1, 1, 0), (3, 1, 1, 1), (4, 2, 0, 0)],
         [(4, 1, 0, 0), (1, 2, 0, 0)],
-        w,
-        None,
-        False,
-    )
-    x_1, y_1, sums = lax.optimization_barrier((x_1, y_1, sums))
-    d_1 = over_x(y_1)
-    sums = project([x_1, y_1], [(0, 2, 0, 1), (1, 2, 1, 0)], [(0, 1, 0, 1), (1, 1, 1, 0)], w, sums, False)
-    x_2, y_2 = lax.optimization_barrier((x_2, y_2))
-    d_2 = lax.ppermute(x_2, BOTH, OVER_Y_OUTER)
-    d_1, d_2, sums = lax.optimization_barrier((d_1, d_2, sums))
-    keep, send = project(
-        [x_2, y_2, d_1, d_2],
-        [(2, 2, 1, 1)],
-        [(0, 2, 0, 1), (1, 2, 1, 0), (2, 1, 1, 1), (3, 2, 1, 1)],
+        jnp.transpose(w_in, (1, 0, 2)),
+    )
+    got_2, sums = lax.optimization_barrier((near_x, sums))
+    x_2 = lax.ppermute(got_2, BOTH, OVER_X_OUTER)
+    y_2 = lax.ppermute(got_2, BOTH, OVER_Y_OUTER)
+    d_2 = lax.ppermute(got_2, BOTH, OVER_XY_OUTER)
+    sums = project(
+        [x_1, y_1, d_1],
+        [(0, 2, 0, 1), (1, 2, 1, 0), (2, 2, 1, 1)],
+        [(0, 1, 0, 1), (1, 1, 1, 0), (2, 1, 1, 1)],
         w,
         sums,
-        True,
+        False,
+    )
+    x_2, y_2, d_2, sums = lax.optimization_barrier((x_2, y_2, d_2, sums))
+    keep, send = project(
+        [x_2, y_2, d_2], [], [(0, 2, 0, 1), (1, 2, 1, 0), (2, 2, 1, 1)], w, sums, True
     )
 
     mixed_own, mixed_send, grad_own = mixer(

time: 85.9 us -> 85.9 us (level)
  Pallas kernels: 20.8 us -> 18.6 us
  starting transfers between devices: 36.1 us -> 37.5 us
    ppermute x5 -> x4, waiting for transfers between devices: 14.9 us -> 7.19 us  [over_x(): return lax.ppermute(array, BOTH, OVER_X)]
    ppermute x4, waiting for transfers between devices: 3.75 us -> 9.15 us  [over_y(): return lax.ppermute(array, BOTH, OVER_Y)]
    ppermute x1, waiting for transfers between devices: 0.01 us -> 5.16 us  [chip_plan(): lax.ppermute(send_2, BOTH, SCATTER_Z[1])]
    ppermute x1, waiting for transfers between devices: 4.26 us -> 0.01 us  [chip_plan(): lax.ppermute(send_1, BOTH, SCATTER_Z[2])]
    ppermute x5 -> x4, starting transfers between devices: 6.13 us -> 3.05 us  [over_x(): return lax.ppermute(array, BOTH, OVER_X)]
    ppermute x1 -> x2, starting transfers between devices: 0.67 us -> 3.65 us  [the longest x1 2.97 us: chip_plan(): lax.ppermute(got_1, BOTH, OVER_XY)]
    pallas_call x13 -> x12, Pallas kernels: 15.1 us -> 12.8 us  [small_call(): pl.pallas_call(kernel, in_specs=[IN_VMEM] * len(operands), out_specs=jax....]
    ppermute x1, starting transfers between devices: 1.13 us -> 2.86 us  [chip_plan(): lax.ppermute(send_1, BOTH, SCATTER_Z[0])]
  transfers between devices with their start and end apart: 25 -> 25, of which waited for: 9 -> 13; matrix products, arithmetic and copies ran while one was open for 0% -> 0% of each run, Pallas kernels for 16% -> 14%
where the time goes in v3:
time: 85.9 us; the launch traced here: 85.6 us
  starting transfers between devices  37.5 us (44%)
  waiting for transfers between devices  27.8 us (32%)
  Pallas kernels  18.6 us (22%)
  local copies, waits for them, and re-layouts  0.86 us (1%)
    pallas_call x12, Pallas kernels, small_call(): pl.pallas_call(kernel, in_specs=[IN_VMEM] * len(operands), out_specs=jax....  12.8 us
    ppermute x4, waiting for transfers between devices, over_y(): return lax.ppermute(array, BOTH, OVER_Y)  9.15 us
    ppermute x5, starting transfers between devices, swap(): return lax.ppermute(array, BOTH, OTHER_CORE)  8.16 us
    ppermute x4, waiting for transfers between devices, over_x(): return lax.ppermute(array, BOTH, OVER_X)  7.19 us
    ppermute x1, waiting for transfers between devices, chip_plan(): lax.ppermute(send_2, BOTH, SCATTER_Z[1])  5.16 us
    pallas_call x1, Pallas kernels, first_project(): pl.pallas_call(functools.partial(first_kernel, inner, outer, len(acts)),...  4.7 us
    ppermute x4, starting transfers between devices, over_y(): return lax.ppermute(array, BOTH, OVER_Y)  4.49 us
    ppermute x5, waiting for transfers between devices, swap(): return lax.ppermute(array, BOTH, OTHER_CORE)  4.28 us
  transfers between devices with their start and end apart: 25, of which 13 were waited for; matrix products, arithmetic and copies ran while one was open for 0% of the time, Pallas kernels for 14%

profile of v3, /device:TPU:0, one launch (start us, length us, event | category | flops | bytes accessed | tf_op | source)
XLA Modules:
  0.0 85.6 jit_solution(774184830958823789)
XLA Ops:
  3.6 3.0 %collective-permute-start.5 = (bf16[256,512]{1,0:T(8,128)(2,1)S(1)}, bf16[256,512]{1,0:T(8,128)(2,1)S(1)}, u32[]{:S(2)}, u32[]{:S(2)}) collective-permute-start(bf16[256,512]{1,0:T(8,128)(2,1)S(1)} %embed_rows.1.refs_0_), channel_id=1, source_target_pairs={{0,8},{2,10},{4,12},{6,14},{8,0},{10,2},{12,4},{14,6},{1,16},{3,18... | collective-permute-start | bytes 786440 | tf_op jit(solution)/shard_map/ppermute | solution.py:650
  6.5 1.3 %collective-permute-start.4 = (bf16[256,512]{1,0:T(8,128)(2,1)S(1)}, bf16[256,512]{1,0:T(8,128)(2,1)S(1)}, u32[]{:S(2)}, u32[]{:S(2)}) collective-permute-start(bf16[256,512]{1,0:T(8,128)(2,1)S(1)} %embed_rows.1.refs_0_), channel_id=1, source_target_pairs={{1,6},{3,4},{5,2},{7,0},{9,14},{11,12},{13,10},{15,8},{16,23},{18,... | collective-permute-start | bytes 786440 | tf_op jit(solution)/shard_map/ppermute | solution.py:653
  7.8 3.4 %collective-permute-start.3 = (bf16[256,512]{1,0:T(8,128)(2,1)S(1)}, bf16[256,512]{1,0:T(8,128)(2,1)S(1)}, u32[]{:S(2)}, u32[]{:S(2)}) collective-permute-start(bf16[256,512]{1,0:T(8,128)(2,1)S(1)} %embed_rows.1.refs_0_), channel_id=1, source_target_pairs={{0,4},{2,6},{4,0},{6,2},{8,12},{10,14},{12,8},{14,10},{17,21},{19,... | collective-permute-start | bytes 786440 | tf_op jit(solution)/shard_map/ppermute | solution.py:652
  11.3 1.6 %collective-permute-start.2 = (bf16[256,512]{1,0:T(8,128)(2,1)S(1)}, bf16[256,512]{1,0:T(8,128)(2,1)S(1)}, u32[]{:S(2)}, u32[]{:S(2)}) collective-permute-start(bf16[256,512]{1,0:T(8,128)(2,1)S(1)} %embed_rows.1.refs_0_), channel_id=1, source_target_pairs={{0,2},{2,0},{4,6},{6,4},{8,10},{10,8},{12,14},{14,12},{17,19},{19,... | collective-permute-start | bytes 786440 | tf_op jit(solution)/shard_map/ppermute | solution.py:651
  13.6 3.0 %collective-permute-start.11 = (bf16[256,512]{1,0:T(8,128)(2,1)S(1)}, bf16[256,512]{1,0:T(8,128)(2,1)S(1)}, u32[]{:S(2)}, u32[]{:S(2)}) collective-permute-start(bf16[256,512]{1,0:T(8,128)(2,1)S(1)} %collective-permute-done.5.refs_4_), channel_id=1, source_target_pairs={{0,6},{1,7},{2,4},{3,5},{4,2},{5,3},{6,0},{7,1},{8,14},{9,15},{10,... | collective-permute-start | bytes 786440 | tf_op jit(solution)/shard_map/ppermute | solution.py:654
  17.2 1.2 %collective-permute-done.3.refs_2_ = bf16[256,512]{1,0:T(8,128)(2,1)S(1)} collective-permute-done((bf16[256,512]{1,0:T(8,128)(2,1)S(1)}, bf16[256,512]{1,0:T(8,128)(2,1)S(1)}, u32[]{:S(2)}, u32[]{:S(2)}) %collective-permute-start.3) | collective-permute-done | bytes 262176 | tf_op jit(solution)/shard_map/ppermute | solution.py:652
  18.4 4.7 %first_project.1 = (f32[3,256,512]{2,1,0:T(8,128)S(1)}, bf16[3,4096,512]{2,1,0:T(8,128)(2,1)S(1)}) custom-call(bf16[3,4096,512]{2,1,0:T(8,128)(2,1)} %bitcast.4, bf16[256,512]{1,0:T(8,128)(2,1)S(1)} %embed_rows.1.refs_0_, bf16[256,512]{1,0:T(8,128)(2,1)S(1)} %collective-permute-done.2.refs_1_, bf16[256,512]{1,0:T(8,128)(2,1)S(1)} %collective-permute-done.3.refs_2_, ...), custom_call_target="tpu_custom_call" | custom-call | bytes 25165824 | tf_op jit(solution)/shard_map/first_project/pallas_call | solution.py:307
  25.2 4.0 %collective-permute-done.10.refs_1_ = bf16[256,512]{1,0:T(8,128)(2,1)S(1)} collective-permute-done((bf16[256,512]{1,0:T(8,128)(2,1)S(1)}, bf16[256,512]{1,0:T(8,128)(2,1)S(1)}, u32[]{:S(2)}, u32[]{:S(2)}) %collective-permute-start.10) | collective-permute-done | bytes 262176 | tf_op jit(solution)/shard_map/ppermute | solution.py:638
  30.0 1.4 %project.2.refs_3_ = f32[3,256,512]{2,1,0:T(8,128)S(1)} custom-call(bf16[3,4096,512]{2,1,0:T(8,128)(2,1)S(1)} %get-tuple-element.35.w_ref, bf16[256,512]{1,0:T(8,128)(2,1)S(1)} %collective-permute-done.9.refs_0_, bf16[256,512]{1,0:T(8,128)(2,1)S(1)} %collective-permute-done.10.refs_1_, bf16[256,512]{1,0:T(8,128)(2,1)S(1)} %collective-permute-done.11.refs_2_, ...), custom_call_target="tpu_custom_call" | custom-call | flops 18874368 | bytes 233472 | tf_op jit(solution)/shard_map/project/pallas_call | solution.py:175
  31.6 6.4 %collective-permute-start.12 = (f32[3,256,256]{2,1,0:T(8,128)S(1)}, f32[3,256,256]{2,1,0:T(8,128)S(1)}, u32[]{:S(2)}, u32[]{:S(2)}) collective-permute-start(f32[3,256,256]{2,1,0:T(8,128)S(1)} %get-tuple-element.44), channel_id=1, source_target_pairs={{0,1},{1,0},{2,3},{3,2},{4,5},{5,4},{6,7},{7,6},{8,9},{9,8},{10,11... | collective-permute-start | bytes 2359304 | tf_op jit(solution)/shard_map/ppermute | solution.py:632
  38.1 1.9 %collective-permute-done.12.other_ref = f32[3,256,256]{2,1,0:T(8,128)S(1)} collective-permute-done((f32[3,256,256]{2,1,0:T(8,128)S(1)}, f32[3,256,256]{2,1,0:T(8,128)S(1)}, u32[]{:S(2)}, u32[]{:S(2)}) %collective-permute-start.12) | collective-permute-done | bytes 786464 | tf_op jit(solution)/shard_map/ppermute | solution.py:632
  40.0 4.6 %mixer.1 = (bf16[128,256]{1,0:T(8,128)(2,1)S(1)}, bf16[128,256]{1,0:T(8,128)(2,1)S(1)}, bf16[3,256,256]{2,1,0:T(8,128)(2,1)S(1)}) custom-call(f32[3,256,256]{2,1,0:T(8,128)S(1)} %get-tuple-element.43.keep_ref, f32[3,256,256]{2,1,0:T(8,128)S(1)} %collective-permute-done.12.other_ref, f32[3,7,512]{2,1,0:T(8,128)S(1)} %bitcast.3, f32[16,512]{1,0:T(8,128)S(1)} %copy-done.2, ...), custom_call_target="tpu_custom_call" | custom-call | flops 196608 | bytes 29344 | tf_op jit(solution)/shard_map/mixer/pallas_call | solution.py:175
  45.1 1.3 %collective-permute-done.14.other_ref = bf16[3,256,256]{2,1,0:T(8,128)(2,1)S(1)} collective-permute-done((bf16[3,256,256]{2,1,0:T(8,128)(2,1)S(1)}, bf16[3,256,256]{2,1,0:T(8,128)(2,1)S(1)}, u32[]{:S(2)}, u32[]{:S(2)}) %collective-permute-start.14) | collective-permute-done | bytes 393248 | tf_op jit(solution)/shard_map/ppermute | solution.py:632
  47.4 1.2 %collective-permute-start.15 = (bf16[512,256]{1,0:T(8,128)(2,1)S(1)}, bf16[512,256]{1,0:T(8,128)(2,1)S(1)}, u32[]{:S(2)}, u32[]{:S(2)}) collective-permute-start(bf16[512,256]{1,0:T(8,128)(2,1)S(1)} %get-tuple-element.51), channel_id=1, source_target_pairs={{0,4},{1,5},{2,6},{3,7},{4,0},{5,1},{6,2},{7,3},{8,12},{9,13},{10,... | collective-permute-start | bytes 786440 | tf_op jit(solution)/shard_map/ppermute | solution.py:638
  49.5 2.6 %back_project.2 = (bf16[512,256]{1,0:T(8,128)(2,1)S(1)}, f32[512,256]{1,0:T(8,128)S(1)}, f32[512,256]{1,0:T(8,128)S(1)}, bf16[512,256]{1,0:T(8,128)(2,1)S(1)}, f...) custom-call(bf16[3,4096,512]{2,1,0:T(8,128)(2,1)S(1)} %get-tuple-element.35.w_ref, ...), custom_call_target="tpu_custom_call" | custom-call | flops 37748736 | bytes 208896 | tf_op jit(solution)/shard_map/back_project/pallas_call | solution.py:175
  52.1 1.6 %collective-permute-start.17 = (bf16[512,256]{1,0:T(8,128)(2,1)S(1)}, bf16[512,256]{1,0:T(8,128)(2,1)S(1)}, u32[]{:S(2)}, u32[]{:S(2)}) collective-permute-start(bf16[512,256]{1,0:T(8,128)(2,1)S(1)} %get-tuple-element.52), channel_id=1, source_target_pairs={{0,4},{1,5},{2,6},{3,7},{4,0},{5,1},{6,2},{7,3},{8,12},{9,13},{10,... | collective-permute-start | bytes 786440 | tf_op jit(solution)/shard_map/ppermute | solution.py:638
  53.7 2.9 %collective-permute-done.15.got_ref = bf16[512,256]{1,0:T(8,128)(2,1)S(1)} collective-permute-done((bf16[512,256]{1,0:T(8,128)(2,1)S(1)}, bf16[512,256]{1,0:T(8,128)(2,1)S(1)}, u32[]{:S(2)}, u32[]{:S(2)}) %collective-permute-start.15) | collective-permute-done | bytes 262176 | tf_op jit(solution)/shard_map/ppermute | solution.py:638
  56.7 1.6 %collective-permute-start.16 = (bf16[512,256]{1,0:T(8,128)(2,1)S(1)}, bf16[512,256]{1,0:T(8,128)(2,1)S(1)}, u32[]{:S(2)}, u32[]{:S(2)}) collective-permute-start(bf16[512,256]{1,0:T(8,128)(2,1)S(1)} %merge.2), channel_id=1, source_target_pairs={{0,2},{1,3},{2,0},{3,1},{4,6},{5,7},{6,4},{7,5},{8,10},{9,11},{10,... | collective-permute-start | bytes 786440 | tf_op jit(solution)/shard_map/ppermute | solution.py:635
  60.0 2.3 %collective-permute-done.17.y_ref = bf16[512,256]{1,0:T(8,128)(2,1)S(1)} collective-permute-done((bf16[512,256]{1,0:T(8,128)(2,1)S(1)}, bf16[512,256]{1,0:T(8,128)(2,1)S(1)}, u32[]{:S(2)}, u32[]{:S(2)}) %collective-permute-start.17) | collective-permute-done | bytes 262176 | tf_op jit(solution)/shard_map/ppermute | solution.py:638
  62.2 3.7 %collective-permute-done.16.x_ref = bf16[512,256]{1,0:T(8,128)(2,1)S(1)} collective-permute-done((bf16[512,256]{1,0:T(8,128)(2,1)S(1)}, bf16[512,256]{1,0:T(8,128)(2,1)S(1)}, u32[]{:S(2)}, u32[]{:S(2)}) %collective-permute-start.16) | collective-permute-done | bytes 262176 | tf_op jit(solution)/shard_map/ppermute | solution.py:635
  66.9 2.7 %collective-permute-done.18.x_ref = bf16[512,256]{1,0:T(8,128)(2,1)S(1)} collective-permute-done((bf16[512,256]{1,0:T(8,128)(2,1)S(1)}, bf16[512,256]{1,0:T(8,128)(2,1)S(1)}, u32[]{:S(2)}, u32[]{:S(2)}) %collective-permute-start.18) | collective-permute-done | bytes 262176 | tf_op jit(solution)/shard_map/ppermute | solution.py:635
  70.5 2.9 %collective-permute-start.21 = (bf16[512,128]{1,0:T(8,128)(2,1)S(1)}, bf16[512,128]{1,0:T(8,128)(2,1)S(1)}, u32[]{:S(2)}, u32[]{:S(2)}) collective-permute-start(bf16[512,128]{1,0:T(8,128)(2,1)S(1)} %get-tuple-element.58), channel_id=1, source_target_pairs={{0,8},{2,10},{4,12},{6,14},{8,0},{10,2},{12,4},{14,6},{16,9},{18,1... | collective-permute-start | bytes 393224 | tf_op jit(solution)/shard_map/ppermute | solution.py:698
  73.4 3.9 %collective-permute-start.22 = (bf16[512,128]{1,0:T(8,128)(2,1)S(1)}, bf16[512,128]{1,0:T(8,128)(2,1)S(1)}, u32[]{:S(2)}, u32[]{:S(2)}) collective-permute-start(bf16[512,128]{1,0:T(8,128)(2,1)S(1)} %get-tuple-element.59), channel_id=1, source_target_pairs={{0,9},{2,11},{4,13},{6,15},{8,1},{10,3},{12,5},{14,7},{16,8},{18,1... | collective-permute-start | bytes 393224 | tf_op jit(solution)/shard_map/ppermute | solution.py:699
  79.6 5.2 %collective-permute-done.22.b_ref = bf16[512,128]{1,0:T(8,128)(2,1)S(1)} collective-permute-done((bf16[512,128]{1,0:T(8,128)(2,1)S(1)}, bf16[512,128]{1,0:T(8,128)(2,1)S(1)}, u32[]{:S(2)}, u32[]{:S(2)}) %collective-permute-start.22) | collective-permute-done | bytes 131104 | tf_op jit(solution)/shard_map/ppermute | solution.py:699
  (49 shorter events, 16.4 us)
Async XLA Ops:
  1.5 2.1 %collective-permute-start.1 = (bf16[128,256]{1,0:T(8,128)(2,1)S(1)}, bf16[128,256]{1,0:T(8,128)(2,1)S(1)}, u32[]{:S(2)}, u32[]{:S(2)}) collective-permute-start(bf16[128,256]{1,0:T(8,128)(2,1)S(1)} %constant_dynamic-slice_fusion), channel_id=1, source_target_pairs={{0,1},{1,0},{2,3},{3,2},{4,5},{5,4},{6,7},{7,6},{8,9},{9,8},{10,11... | collective-permute-start | bytes 196616 | tf_op jit(solution)/shard_map/ppermute | solution.py:632
  3.6 10.1 %collective-permute-start.5 = (bf16[256,512]{1,0:T(8,128)(2,1)S(1)}, bf16[256,512]{1,0:T(8,128)(2,1)S(1)}, u32[]{:S(2)}, u32[]{:S(2)}) collective-permute-start(bf16[256,512]{1,0:T(8,128)(2,1)S(1)} %embed_rows.1.refs_0_), channel_id=1, source_target_pairs={{0,8},{2,10},{4,12},{6,14},{8,0},{10,2},{12,4},{14,6},{1,16},{3,18... | collective-permute-start | bytes 786440 | tf_op jit(solution)/shard_map/ppermute | solution.py:650
  6.5 10.6 %collective-permute-start.4 = (bf16[256,512]{1,0:T(8,128)(2,1)S(1)}, bf16[256,512]{1,0:T(8,128)(2,1)S(1)}, u32[]{:S(2)}, u32[]{:S(2)}) collective-permute-start(bf16[256,512]{1,0:T(8,128)(2,1)S(1)} %embed_rows.1.refs_0_), channel_id=1, source_target_pairs={{1,6},{3,4},{5,2},{7,0},{9,14},{11,12},{13,10},{15,8},{16,23},{18,... | collective-permute-start | bytes 786440 | tf_op jit(solution)/shard_map/ppermute | solution.py:653
  7.8 10.6 %collective-permute-start.3 = (bf16[256,512]{1,0:T(8,128)(2,1)S(1)}, bf16[256,512]{1,0:T(8,128)(2,1)S(1)}, u32[]{:S(2)}, u32[]{:S(2)}) collective-permute-start(bf16[256,512]{1,0:T(8,128)(2,1)S(1)} %embed_rows.1.refs_0_), channel_id=1, source_target_pairs={{0,4},{2,6},{4,0},{6,2},{8,12},{10,14},{12,8},{14,10},{17,21},{19,... | collective-permute-start | bytes 786440 | tf_op jit(solution)/shard_map/ppermute | solution.py:652
  11.3 7.1 %collective-permute-start.2 = (bf16[256,512]{1,0:T(8,128)(2,1)S(1)}, bf16[256,512]{1,0:T(8,128)(2,1)S(1)}, u32[]{:S(2)}, u32[]{:S(2)}) collective-permute-start(bf16[256,512]{1,0:T(8,128)(2,1)S(1)} %embed_rows.1.refs_0_), channel_id=1, source_target_pairs={{0,2},{2,0},{4,6},{6,4},{8,10},{10,8},{12,14},{14,12},{17,19},{19,... | collective-permute-start | bytes 786440 | tf_op jit(solution)/shard_map/ppermute | solution.py:651
  13.6 10.9 %collective-permute-start.11 = (bf16[256,512]{1,0:T(8,128)(2,1)S(1)}, bf16[256,512]{1,0:T(8,128)(2,1)S(1)}, u32[]{:S(2)}, u32[]{:S(2)}) collective-permute-start(bf16[256,512]{1,0:T(8,128)(2,1)S(1)} %collective-permute-done.5.refs_4_), channel_id=1, source_target_pairs={{0,6},{1,7},{2,4},{3,5},{4,2},{5,3},{6,0},{7,1},{8,14},{9,15},{10,... | collective-permute-start | bytes 786440 | tf_op jit(solution)/shard_map/ppermute | solution.py:654
  16.6 12.6 %collective-permute-start.10 = (bf16[256,512]{1,0:T(8,128)(2,1)S(1)}, bf16[256,512]{1,0:T(8,128)(2,1)S(1)}, u32[]{:S(2)}, u32[]{:S(2)}) collective-permute-start(bf16[256,512]{1,0:T(8,128)(2,1)S(1)} %collective-permute-done.5.refs_4_), channel_id=1, source_target_pairs={{0,4},{1,5},{2,6},{3,7},{4,0},{5,1},{6,2},{7,3},{8,12},{9,13},{10,... | collective-permute-start | bytes 786440 | tf_op jit(solution)/shard_map/ppermute | solution.py:638
  17.1 12.8 %collective-permute-start.9 = (bf16[256,512]{1,0:T(8,128)(2,1)S(1)}, bf16[256,512]{1,0:T(8,128)(2,1)S(1)}, u32[]{:S(2)}, u32[]{:S(2)}) collective-permute-start(bf16[256,512]{1,0:T(8,128)(2,1)S(1)} %collective-permute-done.5.refs_4_), channel_id=1, source_target_pairs={{0,2},{1,3},{2,0},{3,1},{4,6},{5,7},{6,4},{7,5},{8,10},{9,11},{10,... | collective-permute-start | bytes 786440 | tf_op jit(solution)/shard_map/ppermute | solution.py:635
  23.1 8.3 %collective-permute-start.8 = (bf16[256,512]{1,0:T(8,128)(2,1)S(1)}, bf16[256,512]{1,0:T(8,128)(2,1)S(1)}, u32[]{:S(2)}, u32[]{:S(2)}) collective-permute-start(bf16[256,512]{1,0:T(8,128)(2,1)S(1)} %collective-permute-done.2.refs_1_), channel_id=1, source_target_pairs={{1,7},{3,5},{5,3},{7,1},{9,15},{11,13},{13,11},{15,9},{16,22},{18,... | collective-permute-start | bytes 786440 | tf_op jit(solution)/shard_map/ppermute | solution.py:664
  23.8 7.6 %collective-permute-start.7 = (bf16[256,512]{1,0:T(8,128)(2,1)S(1)}, bf16[256,512]{1,0:T(8,128)(2,1)S(1)}, u32[]{:S(2)}, u32[]{:S(2)}) collective-permute-start(bf16[256,512]{1,0:T(8,128)(2,1)S(1)} %collective-permute-done.2.refs_1_), channel_id=1, source_target_pairs={{1,5},{3,7},{5,1},{7,3},{9,13},{11,15},{13,9},{15,11},{16,20},{18,... | collective-permute-start | bytes 786440 | tf_op jit(solution)/shard_map/ppermute | solution.py:663
  24.5 6.9 %collective-permute-start.6 = (bf16[256,512]{1,0:T(8,128)(2,1)S(1)}, bf16[256,512]{1,0:T(8,128)(2,1)S(1)}, u32[]{:S(2)}, u32[]{:S(2)}) collective-permute-start(bf16[256,512]{1,0:T(8,128)(2,1)S(1)} %collective-permute-done.2.refs_1_), channel_id=1, source_target_pairs={{1,3},{3,1},{5,7},{7,5},{9,11},{11,9},{13,15},{15,13},{16,18},{18,... | collective-permute-start | bytes 786440 | tf_op jit(solution)/shard_map/ppermute | solution.py:662
  31.6 8.4 %collective-permute-start.12 = (f32[3,256,256]{2,1,0:T(8,128)S(1)}, f32[3,256,256]{2,1,0:T(8,128)S(1)}, u32[]{:S(2)}, u32[]{:S(2)}) collective-permute-start(f32[3,256,256]{2,1,0:T(8,128)S(1)} %get-tuple-element.44), channel_id=1, source_target_pairs={{0,1},{1,0},{2,3},{3,2},{4,5},{5,4},{6,7},{7,6},{8,9},{9,8},{10,11... | collective-permute-start | bytes 2359304 | tf_op jit(solution)/shard_map/ppermute | solution.py:632
  44.6 1.8 %collective-permute-start.14 = (bf16[3,256,256]{2,1,0:T(8,128)(2,1)S(1)}, bf16[3,256,256]{2,1,0:T(8,128)(2,1)S(1)}, u32[]{:S(2)}, u32[]{:S(2)}) collective-permute-start(bf16[3,256,256]{2,1,0:T(8,128)(2,1)S(1)} %get-tuple-element.48.own_ref), channel_id=1, source_target_pairs={{0,1},{1,0},{2,3},{3,2},{4,5},{5,4},{6,7},{7,6},{8,9},{9,8},{10,11... | collective-permute-start | bytes 1179656 | tf_op jit(solution)/shard_map/ppermute | solution.py:632
  47.4 9.2 %collective-permute-start.15 = (bf16[512,256]{1,0:T(8,128)(2,1)S(1)}, bf16[512,256]{1,0:T(8,128)(2,1)S(1)}, u32[]{:S(2)}, u32[]{:S(2)}) collective-permute-start(bf16[512,256]{1,0:T(8,128)(2,1)S(1)} %get-tuple-element.51), channel_id=1, source_target_pairs={{0,4},{1,5},{2,6},{3,7},{4,0},{5,1},{6,2},{7,3},{8,12},{9,13},{10,... | collective-permute-start | bytes 786440 | tf_op jit(solution)/shard_map/ppermute | solution.py:638
  48.6 10.2 %collective-permute-start.19 = (bf16[512,256]{1,0:T(8,128)(2,1)S(1)}, bf16[512,256]{1,0:T(8,128)(2,1)S(1)}, u32[]{:S(2)}, u32[]{:S(2)}) collective-permute-start(bf16[512,256]{1,0:T(8,128)(2,1)S(1)} %get-tuple-element.57), channel_id=1, source_target_pairs={{0,2},{1,3},{2,0},{3,1},{4,6},{5,7},{6,4},{7,5},{8,10},{9,11},{10,... | collective-permute-start | bytes 786440 | tf_op jit(solution)/shard_map/ppermute | solution.py:635
  52.1 10.1 %collective-permute-start.17 = (bf16[512,256]{1,0:T(8,128)(2,1)S(1)}, bf16[512,256]{1,0:T(8,128)(2,1)S(1)}, u32[]{:S(2)}, u32[]{:S(2)}) collective-permute-start(bf16[512,256]{1,0:T(8,128)(2,1)S(1)} %get-tuple-element.52), channel_id=1, source_target_pairs={{0,4},{1,5},{2,6},{3,7},{4,0},{5,1},{6,2},{7,3},{8,12},{9,13},{10,... | collective-permute-start | bytes 786440 | tf_op jit(solution)/shard_map/ppermute | solution.py:638
  56.7 9.3 %collective-permute-start.16 = (bf16[512,256]{1,0:T(8,128)(2,1)S(1)}, bf16[512,256]{1,0:T(8,128)(2,1)S(1)}, u32[]{:S(2)}, u32[]{:S(2)}) collective-permute-start(bf16[512,256]{1,0:T(8,128)(2,1)S(1)} %merge.2), channel_id=1, source_target_pairs={{0,2},{1,3},{2,0},{3,1},{4,6},{5,7},{6,4},{7,5},{8,10},{9,11},{10,... | collective-permute-start | bytes 786440 | tf_op jit(solution)/shard_map/ppermute | solution.py:635
  58.3 11.3 %collective-permute-start.18 = (bf16[512,256]{1,0:T(8,128)(2,1)S(1)}, bf16[512,256]{1,0:T(8,128)(2,1)S(1)}, u32[]{:S(2)}, u32[]{:S(2)}) collective-permute-start(bf16[512,256]{1,0:T(8,128)(2,1)S(1)} %get-tuple-element.55), channel_id=1, source_target_pairs={{0,2},{1,3},{2,0},{3,1},{4,6},{5,7},{6,4},{7,5},{8,10},{9,11},{10,... | collective-permute-start | bytes 786440 | tf_op jit(solution)/shard_map/ppermute | solution.py:635
  58.8 10.8 %collective-permute-start.20 = (bf16[512,256]{1,0:T(8,128)(2,1)S(1)}, bf16[512,256]{1,0:T(8,128)(2,1)S(1)}, u32[]{:S(2)}, u32[]{:S(2)}) collective-permute-start(bf16[512,256]{1,0:T(8,128)(2,1)S(1)} %merge.3), channel_id=1, source_target_pairs={{0,4},{1,5},{2,6},{3,7},{4,0},{5,1},{6,2},{7,3},{8,12},{9,13},{10,... | collective-permute-start | bytes 786440 | tf_op jit(solution)/shard_map/ppermute | solution.py:638
  66.1 13.5 %collective-permute-start.23 = (bf16[512,128]{1,0:T(8,128)(2,1)S(1)}, bf16[512,128]{1,0:T(8,128)(2,1)S(1)}, u32[]{:S(2)}, u32[]{:S(2)}) collective-permute-start(bf16[512,128]{1,0:T(8,128)(2,1)S(1)} %get-tuple-element.60), channel_id=1, source_target_pairs={{0,1},{2,3},{4,5},{6,7},{8,9},{10,11},{12,13},{14,15},{16,0},{18,2... | collective-permute-start | bytes 393224 | tf_op jit(solution)/shard_map/ppermute | solution.py:704
  66.2 13.4 %collective-permute-start.24 = (bf16[512,128]{1,0:T(8,128)(2,1)S(1)}, bf16[512,128]{1,0:T(8,128)(2,1)S(1)}, u32[]{:S(2)}, u32[]{:S(2)}) collective-permute-start(bf16[512,128]{1,0:T(8,128)(2,1)S(1)} %get-tuple-element.61), channel_id=1, source_target_pairs={{16,1},{18,3},{20,5},{22,7},{24,9},{26,11},{28,13},{30,15},{9,24},... | collective-permute-start | bytes 393224 | tf_op jit(solution)/shard_map/ppermute | solution.py:705
  70.5 9.1 %collective-permute-start.21 = (bf16[512,128]{1,0:T(8,128)(2,1)S(1)}, bf16[512,128]{1,0:T(8,128)(2,1)S(1)}, u32[]{:S(2)}, u32[]{:S(2)}) collective-permute-start(bf16[512,128]{1,0:T(8,128)(2,1)S(1)} %get-tuple-element.58), channel_id=1, source_target_pairs={{0,8},{2,10},{4,12},{6,14},{8,0},{10,2},{12,4},{14,6},{16,9},{18,1... | collective-permute-start | bytes 393224 | tf_op jit(solution)/shard_map/ppermute | solution.py:698
  73.4 11.4 %collective-permute-start.22 = (bf16[512,128]{1,0:T(8,128)(2,1)S(1)}, bf16[512,128]{1,0:T(8,128)(2,1)S(1)}, u32[]{:S(2)}, u32[]{:S(2)}) collective-permute-start(bf16[512,128]{1,0:T(8,128)(2,1)S(1)} %get-tuple-element.59), channel_id=1, source_target_pairs={{0,9},{2,11},{4,13},{6,15},{8,1},{10,3},{12,5},{14,7},{16,8},{18,1... | collective-permute-start | bytes 393224 | tf_op jit(solution)/shard_map/ppermute | solution.py:699
  77.3 1.7 %collective-permute-start.13 = (bf16[128,256]{1,0:T(8,128)(2,1)S(1)}, bf16[128,256]{1,0:T(8,128)(2,1)S(1)}, u32[]{:S(2)}, u32[]{:S(2)}) collective-permute-start(bf16[128,256]{1,0:T(8,128)(2,1)S(1)} %get-tuple-element.47), channel_id=1, source_target_pairs={{0,1},{1,0},{2,3},{3,2},{4,5},{5,4},{6,7},{7,6},{8,9},{9,8},{10,11... | collective-permute-start | bytes 196616 | tf_op jit(solution)/shard_map/ppermute | solution.py:632
  (5 other events, 41.5 us)

commit v4 on v1

--- a/solution.py
+++ b/solution.py
@@ -143,7 +143,7 @@
 
 GATHER_Z = (
     along_z([((0, 0), (1, 0)), ((1, 0), (0, 0)), ((0, 1), (2, 0)), ((1, 1), (3, 0))]),
-    along_z([((1, 0), (2, 0)), ((2, 0), (3, 0))]),
+    along_z([((2, 0), (3, 0)), ((3, 0), (2, 0))]),
 )
 SCATTER_Z = (
     along_z([((0, 0), (1, 0)), ((1, 0), (0, 0)), ((2, 0), (1, 1)), ((3, 0), (0, 1))]),
@@ -165,7 +165,7 @@
         scratch_shapes=list(scratch),
         compiler_params=pltpu.CompilerParams(vmem_limit_bytes=limit * 1024 * 1024),
         cost_estimate=pl.CostEstimate(
-            flops=flops, bytes_accessed=min(sum(sizes), 8 * 1024 * 1024), transcendentals=0
+            flops=flops // 64, bytes_accessed=sum(sizes) // 64, transcendentals=0
         ),
         name=name,
     )(*operands)
@@ -187,11 +187,10 @@
     return along * 4 + (1 - y if far_y else y) * 2 + (1 - x if far_x else x)
 
 
-def embed_kernel(own_ref, other_ref, table_ref, cot_ref, out_ref, cot_out_ref):
+def embed_kernel(own_ref, other_ref, table_ref, out_ref):
     vocab = table_ref.shape[0]
     half = own_ref.shape[1]
-    chan_half = cot_out_ref.shape[1]
-    _, _, _, core = here()
+    core = here()[3]
     for ref, side in ((own_ref, core), (other_ref, 1 - core)):
         across = jnp.broadcast_to(ref[...].astype(f32), (half, half)).T
         lane = lax.broadcasted_iota(jnp.int32, (half, half), 1).astype(f32)
@@ -200,37 +199,52 @@
             jnp.concatenate(picks, axis=1).astype(bf16), table_ref[...], preferred_element_type=f32
         )
         out_ref[pl.ds(pl.multiple_of(side * half, half), half), :] = rows.astype(bf16)
-    cot_out_ref[...] = cot_ref[:, pl.ds(pl.multiple_of((1 - core) * chan_half, chan_half), chan_half)]
-
-
-def embed_rows(own_ids, other_ids, table, cotangent):
+
+
+def embed_rows(own_ids, other_ids, table):
     toks, width = 2 * own_ids.shape[1], table.shape[1]
     return small_call(
         embed_kernel,
-        [
-            jax.ShapeDtypeStruct((toks, width), bf16),
-            jax.ShapeDtypeStruct((cotangent.shape[0], cotangent.shape[1] // 2), bf16),
-        ],
-        [own_ids, other_ids, table, cotangent],
+        jax.ShapeDtypeStruct((toks, width), bf16),
+        [own_ids, other_ids, table],
         "embed_rows",
         2 * toks * table.shape[0] * width,
     )
 
 
-def choose_kernel(inner_ref, outer_ref, out_ref):
-    @pl.when(is_inner())
-    def _():
-        out_ref[...] = inner_ref[...]
-
-    @pl.when(jnp.logical_not(is_inner()))
-    def _():
-        out_ref[...] = outer_ref[...]
-
-
-def choose(inner, outer):
-    return small_call(
-        choose_kernel, jax.ShapeDtypeStruct(inner.shape, inner.dtype), [inner, outer], "choose"
-    )
+def fetch_kernel(ids_ref, table_ref, ids_out, table_out, sems):
+    copies = [
+        pltpu.make_async_copy(ids_ref, ids_out, sems.at[0]),
+        pltpu.make_async_copy(table_ref, table_out, sems.at[1]),
+    ]
+    for copy in copies:
+        copy.start()
+    for copy in copies:
+        copy.wait()
+
+
+def in_hbm(array):
+    return pltpu.with_memory_space_constraint(array, pltpu.HBM)
+
+
+def in_vmem(array):
+    return pltpu.with_memory_space_constraint(array, pltpu.VMEM)
+
+
+def fetch(ids, table):
+    out = pl.pallas_call(
+        fetch_kernel,
+        in_specs=[pl.BlockSpec(memory_space=pltpu.HBM)] * 2,
+        out_specs=[IN_VMEM] * 2,
+        out_shape=[pltpu.VMEM(ids.shape, ids.dtype), pltpu.VMEM(table.shape, bf16)],
+        scratch_shapes=[pltpu.SemaphoreType.DMA((2,))],
+        compiler_params=pltpu.CompilerParams(vmem_limit_bytes=2 * 1024 * 1024),
+        cost_estimate=pl.CostEstimate(
+            flops=0, bytes_accessed=4 * table.size, transcendentals=0
+        ),
+        name="fetch",
+    )(in_hbm(ids), in_hbm(table))
+    return [in_vmem(array) for array in out]
 
 
 def load_kernel(w_ref, out_ref, sem):
@@ -240,7 +254,7 @@
 
 
 def load(w):
-    return pl.pallas_call(
+    out = pl.pallas_call(
         load_kernel,
         in_specs=[pl.BlockSpec(memory_space=pltpu.HBM)],
         out_specs=IN_VMEM,
@@ -251,7 +265,24 @@
             flops=0, bytes_accessed=2 * w.size * w.dtype.itemsize, transcendentals=0
         ),
         name="load",
-    )(pltpu.with_memory_space_constraint(w, pltpu.HBM))
+    )(in_hbm(w))
+    return in_vmem(out)
+
+
+def choose_kernel(inner_ref, outer_ref, out_ref):
+    @pl.when(is_inner())
+    def _():
+        out_ref[...] = inner_ref[...]
+
+    @pl.when(jnp.logical_not(is_inner()))
+    def _():
+        out_ref[...] = outer_ref[...]
+
+
+def choose(inner, outer):
+    return small_call(
+        choose_kernel, jax.ShapeDtypeStruct(inner.shape, inner.dtype), [inner, outer], "choose"
+    )
 
 
 def project_kernel(blocks, has_base, last, w_ref, *refs):
@@ -272,7 +303,7 @@
         total_ref[g] = total
     if last:
         half = chans // 2
-        _, _, _, core = here()
+        core = here()[3]
         keep_ref[...] = total_ref[:, :, pl.ds(pl.multiple_of(core * half, half), half)]
         send_ref[...] = total_ref[:, :, pl.ds(pl.multiple_of((1 - core) * half, half), half)]
 
@@ -563,16 +594,21 @@
         return lax.ppermute(array, BOTH, OVER_Y)
 
     own_ids = token_ids.reshape(1, -1)
-    embedded, cot_send = embed_rows(own_ids, swap(own_ids), embed, cotangent)
-    cot_other = swap(cot_send)
-
+    other_ids = swap(own_ids)
+    cot_half = cotangent.shape[1] // 2
+    cot_other = swap(
+        lax.dynamic_slice_in_dim(cotangent, (1 - lax.axis_index("ctx")) * cot_half, cot_half, 1)
+    )
+    own_ids, table = fetch(own_ids, embed)
+    embedded = embed_rows(own_ids, other_ids, table)
+
+    embedded, cot_other = lax.optimization_barrier((embedded, cot_other))
     got_1 = lax.ppermute(embedded, BOTH, GATHER_Z[0])
     w = load(jnp.transpose(w_in, (1, 0, 2)))
-    w = pltpu.with_memory_space_constraint(w, pltpu.VMEM)
-    got_1, cot_other, w = lax.optimization_barrier((got_1, cot_other, w))
+    got_1, w = lax.optimization_barrier((got_1, w))
     slot_1 = choose(embedded, got_1)
-    got_2 = lax.ppermute(slot_1, BOTH, GATHER_Z[1])
     x_1, y_1 = over_x(slot_1), over_y(slot_1)
+    got_2 = lax.ppermute(got_1, BOTH, GATHER_Z[1])
     slot_2 = choose(got_1, got_2)
     x_2, y_2 = over_x(slot_2), over_y(slot_2)
     sums = project([(1, 0, 0), (2, 0, 0)], [slot_1, slot_2], w, None, False)
@@ -601,14 +637,16 @@
         grad_other,
         width,
     )
-    x_2, y_2 = over_x(x_2), over_y(merge(y_2, d_2))
+    mixed = pair(mixed_own, mixed_other)
+    x_2, d_2, mixed = lax.optimization_barrier((x_2, d_2, mixed))
+    x_2, y_2 = lax.optimization_barrier((x_2, merge(y_2, d_2)))
+    x_2, y_2 = over_x(x_2), over_y(y_2)
     x_1, y_1 = over_x(merge(x_1, d_1)), over_y(y_1)
     _, send_1, send_2 = column(2, own_2, x_2, y_2)
     received = [
         lax.ppermute(send_1, BOTH, SCATTER_Z[0]),
         lax.ppermute(send_2, BOTH, SCATTER_Z[1]),
     ]
-    mixed = pair(mixed_own, mixed_other)
     own, send_1, send_2 = column(1, own_1, x_1, y_1)
     received += [
         lax.ppermute(send_1, BOTH, SCATTER_Z[2]),

time: 86.6 us -> 84.3 us (0.973)
  starting transfers between devices: 28.3 us -> 22.1 us
  waiting for transfers between devices: 33.9 us -> 38.4 us
  local copies, waits for them, and re-layouts: 2.62 us -> 0.87 us
  Pallas kernels: 20 us -> 21.1 us
    ppermute x5, starting transfers between devices: 7.03 us -> 2.81 us  [swap(): return lax.ppermute(array, BOTH, OTHER_CORE)]
    ppermute x1, waiting for transfers between devices: 0.01 us -> 3.07 us  [chip_plan(): lax.ppermute(send_2, BOTH, SCATTER_Z[1])]
    ppermute x1, starting transfers between devices: 2.81 us -> 0.05 us  [chip_plan(): lax.ppermute(send_2, BOTH, SCATTER_Z[1])]
    unnamed x14 -> x8, local copies, waits for them, and re-layouts: 2.62 us -> 0.03 us
    ppermute x6, waiting for transfers between devices: 13.3 us -> 11 us  [over_x(): return lax.ppermute(array, BOTH, OVER_X)]
    ppermute x1, waiting for transfers between devices: 0.01 us -> 2.22 us  [chip_plan(): lax.ppermute(send_1, BOTH, SCATTER_Z[0])]
    ppermute x1, waiting for transfers between devices: 2.86 us -> 4.21 us  [chip_plan(): lax.ppermute(send_1, BOTH, SCATTER_Z[2])]
    ppermute x1, waiting for transfers between devices: 1.39 us -> 2.49 us  [chip_plan(): got_1 = lax.ppermute(embedded, BOTH, GATHER_Z[0])]
  transfers between devices with their start and end apart: 23 -> 23, of which waited for: 15 -> 18; matrix products, arithmetic and copies ran while one was open for 0% -> 0% of each run, Pallas kernels for 14% -> 16%
where the time goes in v4:
time: 84.3 us; the launch traced here: 83.3 us
  waiting for transfers between devices  38.4 us (46%)
  starting transfers between devices  22.1 us (26%)
  Pallas kernels  21.1 us (25%)
  local copies, waits for them, and re-layouts  0.87 us (1%)
    pallas_call x16, Pallas kernels, small_call(): pl.pallas_call(kernel, in_specs=[IN_VMEM] * len(operands), out_specs=jax....  15.4 us
    ppermute x6, waiting for transfers between devices, over_x(): return lax.ppermute(array, BOTH, OVER_X)  11 us
    ppermute x6, waiting for transfers between devices, over_y(): return lax.ppermute(array, BOTH, OVER_Y)  10.8 us
    ppermute x6, starting transfers between devices, over_y(): return lax.ppermute(array, BOTH, OVER_Y)  7.22 us
    ppermute x6, starting transfers between devices, over_x(): return lax.ppermute(array, BOTH, OVER_X)  4.92 us
    ppermute x5, waiting for transfers between devices, swap(): return lax.ppermute(array, BOTH, OTHER_CORE)  4.63 us
    pallas_call x1, Pallas kernels, load(): pl.pallas_call(load_kernel, in_specs=[pl.BlockSpec(memory_space=pltpu.HBM...  4.58 us
    ppermute x1, waiting for transfers between devices, chip_plan(): lax.ppermute(send_1, BOTH, SCATTER_Z[2])  4.21 us
  transfers between devices with their start and end apart: 23, of which 18 were waited for; matrix products, arithmetic and copies ran while one was open for 0% of the time, Pallas kernels for 16%

profile of v4, /device:TPU:0, one launch (start us, length us, event | category | flops | bytes accessed | tf_op | source)
XLA Modules:
  0.0 83.3 jit_solution(8136034943046126800)
XLA Ops:
  3.6 3.0 %collective-permute-start.2 = (bf16[256,512]{1,0:T(8,128)(2,1)S(1)}, bf16[256,512]{1,0:T(8,128)(2,1)S(1)}, u32[]{:S(2)}, u32[]{:S(2)}) collective-permute-start(bf16[256,512]{1,0:T(8,128)(2,1)S(1)} %embed_rows.1.inner_ref), channel_id=1, source_target_pairs={{0,8},{2,10},{4,12},{6,14},{8,0},{10,2},{12,4},{14,6},{1,16},{3,18... | collective-permute-start | bytes 786440 | tf_op jit(solution)/shard_map/ppermute | solution.py:606
  6.5 4.6 %load.1.w_ref = bf16[3,4096,512]{2,1,0:T(8,128)(2,1)S(1)} custom-call(bf16[3,4096,512]{2,1,0:T(8,128)(2,1)} %bitcast.4), custom_call_target="tpu_custom_call" | custom-call | bytes 25165824 | tf_op jit(solution)/shard_map/load/pallas_call | solution.py:257
  11.1 2.5 %collective-permute-done.2.outer_ref.inner_ref = bf16[256,512]{1,0:T(8,128)(2,1)S(1)} collective-permute-done((bf16[256,512]{1,0:T(8,128)(2,1)S(1)}, bf16[256,512]{1,0:T(8,128)(2,1)S(1)}, u32[]{:S(2)}, u32[]{:S(2)}) %collective-permute-start.2) | collective-permute-done | bytes 262176 | tf_op jit(solution)/shard_map/ppermute | solution.py:606
  14.3 2.1 %collective-permute-start.3 = (bf16[256,512]{1,0:T(8,128)(2,1)S(1)}, bf16[256,512]{1,0:T(8,128)(2,1)S(1)}, u32[]{:S(2)}, u32[]{:S(2)}) collective-permute-start(bf16[256,512]{1,0:T(8,128)(2,1)S(1)} %choose.2.refs_0_), channel_id=1, source_target_pairs={{0,2},{1,3},{2,0},{3,1},{4,6},{5,7},{6,4},{7,5},{8,10},{9,11},{10,... | collective-permute-start | bytes 786440 | tf_op jit(solution)/shard_map/ppermute | solution.py:591
  16.4 1.5 %collective-permute-start.4 = (bf16[256,512]{1,0:T(8,128)(2,1)S(1)}, bf16[256,512]{1,0:T(8,128)(2,1)S(1)}, u32[]{:S(2)}, u32[]{:S(2)}) collective-permute-start(bf16[256,512]{1,0:T(8,128)(2,1)S(1)} %choose.2.refs_0_), channel_id=1, source_target_pairs={{0,4},{1,5},{2,6},{3,7},{4,0},{5,1},{6,2},{7,3},{8,12},{9,13},{10,... | collective-permute-start | bytes 786440 | tf_op jit(solution)/shard_map/ppermute | solution.py:594
  19.6 1.8 %collective-permute-done.3.refs_0_ = bf16[256,512]{1,0:T(8,128)(2,1)S(1)} collective-permute-done((bf16[256,512]{1,0:T(8,128)(2,1)S(1)}, bf16[256,512]{1,0:T(8,128)(2,1)S(1)}, u32[]{:S(2)}, u32[]{:S(2)}) %collective-permute-start.3) | collective-permute-done | bytes 262176 | tf_op jit(solution)/shard_map/ppermute | solution.py:591
  21.4 2.8 %collective-permute-done.4.refs_1_ = bf16[256,512]{1,0:T(8,128)(2,1)S(1)} collective-permute-done((bf16[256,512]{1,0:T(8,128)(2,1)S(1)}, bf16[256,512]{1,0:T(8,128)(2,1)S(1)}, u32[]{:S(2)}, u32[]{:S(2)}) %collective-permute-start.4) | collective-permute-done | bytes 262176 | tf_op jit(solution)/shard_map/ppermute | solution.py:594
  24.2 1.5 %collective-permute-start.6 = (bf16[256,512]{1,0:T(8,128)(2,1)S(1)}, bf16[256,512]{1,0:T(8,128)(2,1)S(1)}, u32[]{:S(2)}, u32[]{:S(2)}) collective-permute-start(bf16[256,512]{1,0:T(8,128)(2,1)S(1)} %collective-permute-done.3.refs_0_), channel_id=1, source_target_pairs={{0,4},{1,5},{2,6},{3,7},{4,0},{5,1},{6,2},{7,3},{8,12},{9,13},{10,... | collective-permute-start | bytes 786440 | tf_op jit(solution)/shard_map/ppermute | solution.py:594
  27.3 2.6 %collective-permute-done.8.refs_1_ = bf16[256,512]{1,0:T(8,128)(2,1)S(1)} collective-permute-done((bf16[256,512]{1,0:T(8,128)(2,1)S(1)}, bf16[256,512]{1,0:T(8,128)(2,1)S(1)}, u32[]{:S(2)}, u32[]{:S(2)}) %collective-permute-start.8) | collective-permute-done | bytes 262176 | tf_op jit(solution)/shard_map/ppermute | solution.py:594
  30.9 4.6 %collective-permute-done.6.refs_0_ = bf16[256,512]{1,0:T(8,128)(2,1)S(1)} collective-permute-done((bf16[256,512]{1,0:T(8,128)(2,1)S(1)}, bf16[256,512]{1,0:T(8,128)(2,1)S(1)}, u32[]{:S(2)}, u32[]{:S(2)}) %collective-permute-start.6) | collective-permute-done | bytes 262176 | tf_op jit(solution)/shard_map/ppermute | solution.py:594
  35.5 1.6 %collective-permute-done.9.refs_1_ = bf16[256,512]{1,0:T(8,128)(2,1)S(1)} collective-permute-done((bf16[256,512]{1,0:T(8,128)(2,1)S(1)}, bf16[256,512]{1,0:T(8,128)(2,1)S(1)}, u32[]{:S(2)}, u32[]{:S(2)}) %collective-permute-start.9) | collective-permute-done | bytes 262176 | tf_op jit(solution)/shard_map/ppermute | solution.py:591
  38.4 1.8 %collective-permute-start.10 = (f32[3,256,256]{2,1,0:T(8,128)S(1)}, f32[3,256,256]{2,1,0:T(8,128)S(1)}, u32[]{:S(2)}, u32[]{:S(2)}) collective-permute-start(f32[3,256,256]{2,1,0:T(8,128)S(1)} %get-tuple-element.55), channel_id=1, source_target_pairs={{0,1},{1,0},{2,3},{3,2},{4,5},{5,4},{6,7},{7,6},{8,9},{9,8},{10,11... | collective-permute-start | bytes 2359304 | tf_op jit(solution)/shard_map/ppermute | solution.py:588
  40.2 1.9 %collective-permute-done.10.other_ref = f32[3,256,256]{2,1,0:T(8,128)S(1)} collective-permute-done((f32[3,256,256]{2,1,0:T(8,128)S(1)}, f32[3,256,256]{2,1,0:T(8,128)S(1)}, u32[]{:S(2)}, u32[]{:S(2)}) %collective-permute-start.10) | collective-permute-done | bytes 786464 | tf_op jit(solution)/shard_map/ppermute | solution.py:588
  42.1 4.6 %mixer.1 = (bf16[128,256]{1,0:T(8,128)(2,1)S(1)}, bf16[128,256]{1,0:T(8,128)(2,1)S(1)}, bf16[3,256,256]{2,1,0:T(8,128)(2,1)S(1)}) custom-call(f32[3,256,256]{2,1,0:T(8,128)S(1)} %get-tuple-element.54.keep_ref, f32[3,256,256]{2,1,0:T(8,128)S(1)} %collective-permute-done.10.other_ref, f32[3,7,512]{2,1,0:T(8,128)S(1)} %bitcast.3, f32[16,512]{1,0:T(8,128)S(1)} %copy-done.2, ...), custom_call_target="tpu_custom_call" | custom-call | flops 196608 | bytes 29344 | tf_op jit(solution)/shard_map/mixer/pallas_call | solution.py:160
  49.6 2.1 %collective-permute-start.14 = (bf16[512,256]{1,0:T(8,128)(2,1)S(1)}, bf16[512,256]{1,0:T(8,128)(2,1)S(1)}, u32[]{:S(2)}, u32[]{:S(2)}) collective-permute-start(bf16[512,256]{1,0:T(8,128)(2,1)S(1)} %get-tuple-element.65), channel_id=1, source_target_pairs={{0,4},{1,5},{2,6},{3,7},{4,0},{5,1},{6,2},{7,3},{8,12},{9,13},{10,... | collective-permute-start | bytes 786440 | tf_op jit(solution)/shard_map/ppermute | solution.py:594
  53.6 2.6 %back_project.2 = (bf16[512,256]{1,0:T(8,128)(2,1)S(1)}, f32[512,256]{1,0:T(8,128)S(1)}, f32[512,256]{1,0:T(8,128)S(1)}, bf16[512,256]{1,0:T(8,128)(2,1)S(1)}, f...) custom-call(bf16[3,4096,512]{2,1,0:T(8,128)(2,1)S(1)} %load.1.w_ref, bf16[3,256,256]{2,1,0:T(8,128)(2,1)S(1)} %get-tuple-element.57.own_ref, ...), custom_call_target="tpu_custom_call" | custom-call | flops 37748736 | bytes 208896 | tf_op jit(solution)/shard_map/back_project/pallas_call | solution.py:160
  56.2 2.0 %collective-permute-done.12.got_ref = bf16[512,256]{1,0:T(8,128)(2,1)S(1)} collective-permute-done((bf16[512,256]{1,0:T(8,128)(2,1)S(1)}, bf16[512,256]{1,0:T(8,128)(2,1)S(1)}, u32[]{:S(2)}, u32[]{:S(2)}) %collective-permute-start.12) | collective-permute-done | bytes 262176 | tf_op jit(solution)/shard_map/ppermute | solution.py:591
  58.6 1.8 %collective-permute-start.18 = (bf16[512,256]{1,0:T(8,128)(2,1)S(1)}, bf16[512,256]{1,0:T(8,128)(2,1)S(1)}, u32[]{:S(2)}, u32[]{:S(2)}) collective-permute-start(bf16[512,256]{1,0:T(8,128)(2,1)S(1)} %merge.3), channel_id=1, source_target_pairs={{0,4},{1,5},{2,6},{3,7},{4,0},{5,1},{6,2},{7,3},{8,12},{9,13},{10,... | collective-permute-start | bytes 786440 | tf_op jit(solution)/shard_map/ppermute | solution.py:594
  60.7 1.8 %collective-permute-start.15 = (bf16[512,256]{1,0:T(8,128)(2,1)S(1)}, bf16[512,256]{1,0:T(8,128)(2,1)S(1)}, u32[]{:S(2)}, u32[]{:S(2)}) collective-permute-start(bf16[512,256]{1,0:T(8,128)(2,1)S(1)} %merge.2), channel_id=1, source_target_pairs={{0,2},{1,3},{2,0},{3,1},{4,6},{5,7},{6,4},{7,5},{8,10},{9,11},{10,... | collective-permute-start | bytes 786440 | tf_op jit(solution)/shard_map/ppermute | solution.py:591
  62.5 5.1 %collective-permute-done.17.x_ref = bf16[512,256]{1,0:T(8,128)(2,1)S(1)} collective-permute-done((bf16[512,256]{1,0:T(8,128)(2,1)S(1)}, bf16[512,256]{1,0:T(8,128)(2,1)S(1)}, u32[]{:S(2)}, u32[]{:S(2)}) %collective-permute-start.17) | collective-permute-done | bytes 262176 | tf_op jit(solution)/shard_map/ppermute | solution.py:591
  68.7 2.6 %collective-permute-start.19 = (bf16[512,128]{1,0:T(8,128)(2,1)S(1)}, bf16[512,128]{1,0:T(8,128)(2,1)S(1)}, u32[]{:S(2)}, u32[]{:S(2)}) collective-permute-start(bf16[512,128]{1,0:T(8,128)(2,1)S(1)} %get-tuple-element.74), channel_id=1, source_target_pairs={{0,8},{2,10},{4,12},{6,14},{8,0},{10,2},{12,4},{14,6},{16,9},{18,1... | collective-permute-start | bytes 393224 | tf_op jit(solution)/shard_map/ppermute | solution.py:647
  73.0 2.2 %collective-permute-done.19.a_ref = bf16[512,128]{1,0:T(8,128)(2,1)S(1)} collective-permute-done((bf16[512,128]{1,0:T(8,128)(2,1)S(1)}, bf16[512,128]{1,0:T(8,128)(2,1)S(1)}, u32[]{:S(2)}, u32[]{:S(2)}) %collective-permute-start.19) | collective-permute-done | bytes 131104 | tf_op jit(solution)/shard_map/ppermute | solution.py:647
  75.2 3.1 %collective-permute-done.20.b_ref = bf16[512,128]{1,0:T(8,128)(2,1)S(1)} collective-permute-done((bf16[512,128]{1,0:T(8,128)(2,1)S(1)}, bf16[512,128]{1,0:T(8,128)(2,1)S(1)}, u32[]{:S(2)}, u32[]{:S(2)}) %collective-permute-start.20) | collective-permute-done | bytes 131104 | tf_op jit(solution)/shard_map/ppermute | solution.py:648
  78.3 4.2 %collective-permute-done.21.c_ref = bf16[512,128]{1,0:T(8,128)(2,1)S(1)} collective-permute-done((bf16[512,128]{1,0:T(8,128)(2,1)S(1)}, bf16[512,128]{1,0:T(8,128)(2,1)S(1)}, u32[]{:S(2)}, u32[]{:S(2)}) %collective-permute-start.21) | collective-permute-done | bytes 131104 | tf_op jit(solution)/shard_map/ppermute | solution.py:652
  (49 shorter events, 18.1 us)
Async XLA Ops:
  1.5 2.1 %collective-permute-start.1 = (bf16[128,256]{1,0:T(8,128)(2,1)S(1)}, bf16[128,256]{1,0:T(8,128)(2,1)S(1)}, u32[]{:S(2)}, u32[]{:S(2)}) collective-permute-start(bf16[128,256]{1,0:T(8,128)(2,1)S(1)} %constant_dynamic-slice_fusion), channel_id=1, source_target_pairs={{0,1},{1,0},{2,3},{3,2},{4,5},{5,4},{6,7},{7,6},{8,9},{9,8},{10,11... | collective-permute-start | bytes 196616 | tf_op jit(solution)/shard_map/ppermute | solution.py:588
  1.9 1.3 %collective-permute-start = (s32[1,128]{1,0:T(1,128)}, s32[1,128]{1,0:T(1,128)S(1)}, u32[]{:S(2)}, u32[]{:S(2)}) collective-permute-start(s32[1,128]{1,0:T(1,128)} %bitcast.5), channel_id=1, source_target_pairs={{0,1},{1,0},{2,3},{3,2},{4,5},{5,4},{6,7},{7,6},{8,9},{9,8},{10,11... | collective-permute-start | bytes 1544 | tf_op jit(solution)/shard_map/ppermute | solution.py:588
  3.6 10.1 %collective-permute-start.2 = (bf16[256,512]{1,0:T(8,128)(2,1)S(1)}, bf16[256,512]{1,0:T(8,128)(2,1)S(1)}, u32[]{:S(2)}, u32[]{:S(2)}) collective-permute-start(bf16[256,512]{1,0:T(8,128)(2,1)S(1)} %embed_rows.1.inner_ref), channel_id=1, source_target_pairs={{0,8},{2,10},{4,12},{6,14},{8,0},{10,2},{12,4},{14,6},{1,16},{3,18... | collective-permute-start | bytes 786440 | tf_op jit(solution)/shard_map/ppermute | solution.py:606
  13.6 4.3 %collective-permute-start.5 = (bf16[256,512]{1,0:T(8,128)(2,1)S(1)}, bf16[256,512]{1,0:T(8,128)(2,1)S(1)}, u32[]{:S(2)}, u32[]{:S(2)}) collective-permute-start(bf16[256,512]{1,0:T(8,128)(2,1)S(1)} %collective-permute-done.2.outer_ref.inner_ref), channel_id=1, source_target_pairs={{16,24},{18,26},{20,28},{22,30},{24,16},{26,18},{28,20},{30,22},{9... | collective-permute-start | bytes 786440 | tf_op jit(solution)/shard_map/ppermute | solution.py:611
  14.3 7.1 %collective-permute-start.3 = (bf16[256,512]{1,0:T(8,128)(2,1)S(1)}, bf16[256,512]{1,0:T(8,128)(2,1)S(1)}, u32[]{:S(2)}, u32[]{:S(2)}) collective-permute-start(bf16[256,512]{1,0:T(8,128)(2,1)S(1)} %choose.2.refs_0_), channel_id=1, source_target_pairs={{0,2},{1,3},{2,0},{3,1},{4,6},{5,7},{6,4},{7,5},{8,10},{9,11},{10,... | collective-permute-start | bytes 786440 | tf_op jit(solution)/shard_map/ppermute | solution.py:591
  16.4 7.8 %collective-permute-start.4 = (bf16[256,512]{1,0:T(8,128)(2,1)S(1)}, bf16[256,512]{1,0:T(8,128)(2,1)S(1)}, u32[]{:S(2)}, u32[]{:S(2)}) collective-permute-start(bf16[256,512]{1,0:T(8,128)(2,1)S(1)} %choose.2.refs_0_), channel_id=1, source_target_pairs={{0,4},{1,5},{2,6},{3,7},{4,0},{5,1},{6,2},{7,3},{8,12},{9,13},{10,... | collective-permute-start | bytes 786440 | tf_op jit(solution)/shard_map/ppermute | solution.py:594
  18.0 9.3 %collective-permute-start.7 = (bf16[256,512]{1,0:T(8,128)(2,1)S(1)}, bf16[256,512]{1,0:T(8,128)(2,1)S(1)}, u32[]{:S(2)}, u32[]{:S(2)}) collective-permute-start(bf16[256,512]{1,0:T(8,128)(2,1)S(1)} %choose.3.refs_1_), channel_id=1, source_target_pairs={{0,2},{1,3},{2,0},{3,1},{4,6},{5,7},{6,4},{7,5},{8,10},{9,11},{10,... | collective-permute-start | bytes 786440 | tf_op jit(solution)/shard_map/ppermute | solution.py:591
  18.6 11.3 %collective-permute-start.8 = (bf16[256,512]{1,0:T(8,128)(2,1)S(1)}, bf16[256,512]{1,0:T(8,128)(2,1)S(1)}, u32[]{:S(2)}, u32[]{:S(2)}) collective-permute-start(bf16[256,512]{1,0:T(8,128)(2,1)S(1)} %choose.3.refs_1_), channel_id=1, source_target_pairs={{0,4},{1,5},{2,6},{3,7},{4,0},{5,1},{6,2},{7,3},{8,12},{9,13},{10,... | collective-permute-start | bytes 786440 | tf_op jit(solution)/shard_map/ppermute | solution.py:594
  24.2 11.2 %collective-permute-start.6 = (bf16[256,512]{1,0:T(8,128)(2,1)S(1)}, bf16[256,512]{1,0:T(8,128)(2,1)S(1)}, u32[]{:S(2)}, u32[]{:S(2)}) collective-permute-start(bf16[256,512]{1,0:T(8,128)(2,1)S(1)} %collective-permute-done.3.refs_0_), channel_id=1, source_target_pairs={{0,4},{1,5},{2,6},{3,7},{4,0},{5,1},{6,2},{7,3},{8,12},{9,13},{10,... | collective-permute-start | bytes 786440 | tf_op jit(solution)/shard_map/ppermute | solution.py:594
  29.8 7.2 %collective-permute-start.9 = (bf16[256,512]{1,0:T(8,128)(2,1)S(1)}, bf16[256,512]{1,0:T(8,128)(2,1)S(1)}, u32[]{:S(2)}, u32[]{:S(2)}) collective-permute-start(bf16[256,512]{1,0:T(8,128)(2,1)S(1)} %collective-permute-done.8.refs_1_), channel_id=1, source_target_pairs={{0,2},{1,3},{2,0},{3,1},{4,6},{5,7},{6,4},{7,5},{8,10},{9,11},{10,... | collective-permute-start | bytes 786440 | tf_op jit(solution)/shard_map/ppermute | solution.py:591
  30.8 11.3 %copy-start = (bf16[128,512]{1,0:T(8,128)(2,1)S(1)}, bf16[128,512]{1,0:T(8,128)(2,1)}, u32[]{:S(2)}) copy-start(bf16[128,512]{1,0:T(8,128)(2,1)} %cot_own_ref.1) | copy-start | bytes 393220
  38.4 3.8 %collective-permute-start.10 = (f32[3,256,256]{2,1,0:T(8,128)S(1)}, f32[3,256,256]{2,1,0:T(8,128)S(1)}, u32[]{:S(2)}, u32[]{:S(2)}) collective-permute-start(f32[3,256,256]{2,1,0:T(8,128)S(1)} %get-tuple-element.55), channel_id=1, source_target_pairs={{0,1},{1,0},{2,3},{3,2},{4,5},{5,4},{6,7},{7,6},{8,9},{9,8},{10,11... | collective-permute-start | bytes 2359304 | tf_op jit(solution)/shard_map/ppermute | solution.py:588
  46.8 1.8 %collective-permute-start.11 = (bf16[3,256,256]{2,1,0:T(8,128)(2,1)S(1)}, bf16[3,256,256]{2,1,0:T(8,128)(2,1)S(1)}, u32[]{:S(2)}, u32[]{:S(2)}) collective-permute-start(bf16[3,256,256]{2,1,0:T(8,128)(2,1)S(1)} %get-tuple-element.57.own_ref), channel_id=1, source_target_pairs={{0,1},{1,0},{2,3},{3,2},{4,5},{5,4},{6,7},{7,6},{8,9},{9,8},{10,11... | collective-permute-start | bytes 1179656 | tf_op jit(solution)/shard_map/ppermute | solution.py:588
  49.5 8.7 %collective-permute-start.12 = (bf16[512,256]{1,0:T(8,128)(2,1)S(1)}, bf16[512,256]{1,0:T(8,128)(2,1)S(1)}, u32[]{:S(2)}, u32[]{:S(2)}) collective-permute-start(bf16[512,256]{1,0:T(8,128)(2,1)S(1)} %get-tuple-element.59), channel_id=1, source_target_pairs={{0,2},{1,3},{2,0},{3,1},{4,6},{5,7},{6,4},{7,5},{8,10},{9,11},{10,... | collective-permute-start | bytes 786440 | tf_op jit(solution)/shard_map/ppermute | solution.py:591
  49.6 11.0 %collective-permute-start.14 = (bf16[512,256]{1,0:T(8,128)(2,1)S(1)}, bf16[512,256]{1,0:T(8,128)(2,1)S(1)}, u32[]{:S(2)}, u32[]{:S(2)}) collective-permute-start(bf16[512,256]{1,0:T(8,128)(2,1)S(1)} %get-tuple-element.65), channel_id=1, source_target_pairs={{0,4},{1,5},{2,6},{3,7},{4,0},{5,1},{6,2},{7,3},{8,12},{9,13},{10,... | collective-permute-start | bytes 786440 | tf_op jit(solution)/shard_map/ppermute | solution.py:594
  51.7 1.3 %collective-permute-start.13 = (bf16[128,256]{1,0:T(8,128)(2,1)S(1)}, bf16[128,256]{1,0:T(8,128)(2,1)S(1)}, u32[]{:S(2)}, u32[]{:S(2)}) collective-permute-start(bf16[128,256]{1,0:T(8,128)(2,1)S(1)} %get-tuple-element.61), channel_id=1, source_target_pairs={{0,1},{1,0},{2,3},{3,2},{4,5},{5,4},{6,7},{7,6},{8,9},{9,8},{10,11... | collective-permute-start | bytes 196616 | tf_op jit(solution)/shard_map/ppermute | solution.py:588
  58.2 9.3 %collective-permute-start.17 = (bf16[512,256]{1,0:T(8,128)(2,1)S(1)}, bf16[512,256]{1,0:T(8,128)(2,1)S(1)}, u32[]{:S(2)}, u32[]{:S(2)}) collective-permute-start(bf16[512,256]{1,0:T(8,128)(2,1)S(1)} %get-tuple-element.72), channel_id=1, source_target_pairs={{0,2},{1,3},{2,0},{3,1},{4,6},{5,7},{6,4},{7,5},{8,10},{9,11},{10,... | collective-permute-start | bytes 786440 | tf_op jit(solution)/shard_map/ppermute | solution.py:591
  58.6 9.2 %collective-permute-start.18 = (bf16[512,256]{1,0:T(8,128)(2,1)S(1)}, bf16[512,256]{1,0:T(8,128)(2,1)S(1)}, u32[]{:S(2)}, u32[]{:S(2)}) collective-permute-start(bf16[512,256]{1,0:T(8,128)(2,1)S(1)} %merge.3), channel_id=1, source_target_pairs={{0,4},{1,5},{2,6},{3,7},{4,0},{5,1},{6,2},{7,3},{8,12},{9,13},{10,... | collective-permute-start | bytes 786440 | tf_op jit(solution)/shard_map/ppermute | solution.py:594
  60.4 11.5 %collective-permute-start.16 = (bf16[512,256]{1,0:T(8,128)(2,1)S(1)}, bf16[512,256]{1,0:T(8,128)(2,1)S(1)}, u32[]{:S(2)}, u32[]{:S(2)}) collective-permute-start(bf16[512,256]{1,0:T(8,128)(2,1)S(1)} %get-tuple-element.66), channel_id=1, source_target_pairs={{0,4},{1,5},{2,6},{3,7},{4,0},{5,1},{6,2},{7,3},{8,12},{9,13},{10,... | collective-permute-start | bytes 786440 | tf_op jit(solution)/shard_map/ppermute | solution.py:594
  60.7 11.3 %collective-permute-start.15 = (bf16[512,256]{1,0:T(8,128)(2,1)S(1)}, bf16[512,256]{1,0:T(8,128)(2,1)S(1)}, u32[]{:S(2)}, u32[]{:S(2)}) collective-permute-start(bf16[512,256]{1,0:T(8,128)(2,1)S(1)} %merge.2), channel_id=1, source_target_pairs={{0,2},{1,3},{2,0},{3,1},{4,6},{5,7},{6,4},{7,5},{8,10},{9,11},{10,... | collective-permute-start | bytes 786440 | tf_op jit(solution)/shard_map/ppermute | solution.py:591
  68.7 6.4 %collective-permute-start.19 = (bf16[512,128]{1,0:T(8,128)(2,1)S(1)}, bf16[512,128]{1,0:T(8,128)(2,1)S(1)}, u32[]{:S(2)}, u32[]{:S(2)}) collective-permute-start(bf16[512,128]{1,0:T(8,128)(2,1)S(1)} %get-tuple-element.74), channel_id=1, source_target_pairs={{0,8},{2,10},{4,12},{6,14},{8,0},{10,2},{12,4},{14,6},{16,9},{18,1... | collective-permute-start | bytes 393224 | tf_op jit(solution)/shard_map/ppermute | solution.py:647
  71.3 6.9 %collective-permute-start.20 = (bf16[512,128]{1,0:T(8,128)(2,1)S(1)}, bf16[512,128]{1,0:T(8,128)(2,1)S(1)}, u32[]{:S(2)}, u32[]{:S(2)}) collective-permute-start(bf16[512,128]{1,0:T(8,128)(2,1)S(1)} %get-tuple-element.75), channel_id=1, source_target_pairs={{0,9},{2,11},{4,13},{6,15},{8,1},{10,3},{12,5},{14,7},{16,8},{18,1... | collective-permute-start | bytes 393224 | tf_op jit(solution)/shard_map/ppermute | solution.py:648
  72.1 10.4 %collective-permute-start.21 = (bf16[512,128]{1,0:T(8,128)(2,1)S(1)}, bf16[512,128]{1,0:T(8,128)(2,1)S(1)}, u32[]{:S(2)}, u32[]{:S(2)}) collective-permute-start(bf16[512,128]{1,0:T(8,128)(2,1)S(1)} %get-tuple-element.76), channel_id=1, source_target_pairs={{0,1},{2,3},{4,5},{6,7},{8,9},{10,11},{12,13},{14,15},{16,0},{18,2... | collective-permute-start | bytes 393224 | tf_op jit(solution)/shard_map/ppermute | solution.py:652
  72.3 10.2 %collective-permute-start.22 = (bf16[512,128]{1,0:T(8,128)(2,1)S(1)}, bf16[512,128]{1,0:T(8,128)(2,1)S(1)}, u32[]{:S(2)}, u32[]{:S(2)}) collective-permute-start(bf16[512,128]{1,0:T(8,128)(2,1)S(1)} %get-tuple-element.77), channel_id=1, source_target_pairs={{16,1},{18,3},{20,5},{22,7},{24,9},{26,11},{28,13},{30,15},{9,24},... | collective-permute-start | bytes 393224 | tf_op jit(solution)/shard_map/ppermute | solution.py:653
  (3 other events, 33.8 us)

commit v5 on v4

--- a/solution.py
+++ b/solution.py
@@ -141,9 +141,11 @@
     return pairs
 
 
+FIRST_WAY = everywhere(lambda z, y, x, core: (z, y, 1 - x, core) if core == 0 else (z, 1 - y, x, core))
+OTHER_WAY = everywhere(lambda z, y, x, core: (z, 1 - y, x, core) if core == 0 else (z, y, 1 - x, core))
 GATHER_Z = (
     along_z([((0, 0), (1, 0)), ((1, 0), (0, 0)), ((0, 1), (2, 0)), ((1, 1), (3, 0))]),
-    along_z([((2, 0), (3, 0)), ((3, 0), (2, 0))]),
+    along_z([((1, 1), (2, 0)), ((0, 1), (3, 0))]),
 )
 SCATTER_Z = (
     along_z([((0, 0), (1, 0)), ((1, 0), (0, 0)), ((2, 0), (1, 1)), ((3, 0), (0, 1))]),
@@ -187,7 +189,15 @@
     return along * 4 + (1 - y if far_y else y) * 2 + (1 - x if far_x else x)
 
 
-def embed_kernel(own_ref, other_ref, table_ref, out_ref):
+def way_at(slot, way):
+    core = here()[3]
+    far = ((core, 1 - core), (1 - core, core), (1, 1))[way]
+    z, y, x, _ = here()
+    along = (z & 1) if slot == 1 else 1 - (z & 1)
+    return along * 4 + (y ^ far[0]) * 2 + (x ^ far[1])
+
+
+def embed_kernel(own_ref, other_ref, table_ref, *out_refs):
     vocab = table_ref.shape[0]
     half = own_ref.shape[1]
     core = here()[3]
@@ -198,14 +208,18 @@
         rows = jnp.dot(
             jnp.concatenate(picks, axis=1).astype(bf16), table_ref[...], preferred_element_type=f32
         )
-        out_ref[pl.ds(pl.multiple_of(side * half, half), half), :] = rows.astype(bf16)
+        for n, out_ref in enumerate(out_refs):
+
+            @pl.when(side == n)
+            def _():
+                out_ref[...] = rows.astype(bf16)
 
 
 def embed_rows(own_ids, other_ids, table):
     toks, width = 2 * own_ids.shape[1], table.shape[1]
     return small_call(
         embed_kernel,
-        jax.ShapeDtypeStruct((toks, width), bf16),
+        [jax.ShapeDtypeStruct((toks // 2, width), bf16)] * 2,
         [own_ids, other_ids, table],
         "embed_rows",
         2 * toks * table.shape[0] * width,
@@ -269,56 +283,64 @@
     return in_vmem(out)
 
 
-def choose_kernel(inner_ref, outer_ref, out_ref):
+def slots_kernel(own_ref, one_ref, two_ref, out_ref):
+    rows = own_ref.shape[0]
+
     @pl.when(is_inner())
     def _():
-        out_ref[...] = inner_ref[...]
+        out_ref[:rows] = own_ref[...]
+        out_ref[rows:] = one_ref[...]
 
     @pl.when(jnp.logical_not(is_inner()))
     def _():
-        out_ref[...] = outer_ref[...]
-
-
-def choose(inner, outer):
-    return small_call(
-        choose_kernel, jax.ShapeDtypeStruct(inner.shape, inner.dtype), [inner, outer], "choose"
-    )
-
-
-def project_kernel(blocks, has_base, last, w_ref, *refs):
-    count = len(blocks)
+        out_ref[:rows] = one_ref[...]
+        out_ref[rows:] = two_ref[...]
+
+
+def slots(own, one, two):
+    shape = jax.ShapeDtypeStruct((2 * own.shape[0], own.shape[1]), own.dtype)
+    return small_call(slots_kernel, shape, [own, one, two], "slots")
+
+
+def project_kernel(ways, last, w_ref, *refs):
+    count = len(ways)
     acts = refs[:count]
     groups, _, chans = w_ref.shape
-    toks, width = acts[0].shape
-    if last:
-        keep_ref, send_ref, total_ref = refs[-3:]
-    else:
-        total_ref = refs[-1]
-    starts = [pl.multiple_of(block_at(*block) * width, width) for block in blocks]
+    rows, width = acts[0].shape
+    rows //= 2
+    total_ref = refs[-1]
+    parts = []
+    for way, act in zip(ways, acts):
+        for slot in (1, 2):
+            block = block_at(slot, 0, 0) if way is None else way_at(slot, way)
+            start = pl.multiple_of(block * width, width)
+            parts.append((act, pl.ds((slot - 1) * rows, rows), pl.ds(start, width)))
     for g in range(groups):
-        total = refs[count][g] if has_base else None
-        for start, act in zip(starts, acts):
-            term = jnp.dot(act[...], w_ref[g, pl.ds(start, width), :], preferred_element_type=f32)
+        total = refs[count][g] if last else None
+        for act, span, block in parts:
+            term = jnp.dot(act[span, :], w_ref[g, block, :], preferred_element_type=f32)
             total = term if total is None else total + term
         total_ref[g] = total
     if last:
+        keep_ref, send_ref = refs[-3:-1]
         half = chans // 2
         core = here()[3]
         keep_ref[...] = total_ref[:, :, pl.ds(pl.multiple_of(core * half, half), half)]
         send_ref[...] = total_ref[:, :, pl.ds(pl.multiple_of((1 - core) * half, half), half)]
 
 
-def project(blocks, acts, w, base, last):
+def project(ways, acts, w, base=None):
     groups, _, chans = w.shape
-    toks, width = acts[0].shape
-    total = jax.ShapeDtypeStruct((groups, toks, chans), f32)
-    half = jax.ShapeDtypeStruct((groups, toks, chans // 2), f32)
+    rows, width = acts[0].shape
+    total = jax.ShapeDtypeStruct((groups, rows // 2, chans), f32)
+    half = jax.ShapeDtypeStruct((groups, rows // 2, chans // 2), f32)
+    last = base is not None
     return small_call(
-        functools.partial(project_kernel, blocks, base is not None, last),
+        functools.partial(project_kernel, ways, last),
         [half, half] if last else total,
-        [w] + list(acts) + ([] if base is None else [base]),
+        [w] + list(acts) + ([base] if last else []),
         "project",
-        2 * len(acts) * groups * width * chans * toks,
+        2 * len(acts) * groups * width * chans * rows,
         [pltpu.VMEM(total.shape, f32)] if last else [],
         16,
     )
@@ -332,8 +354,8 @@
 
 
 def mixer_kernel(
-    keep_ref,
-    other_ref,
+    keep_refs,
+    other_refs,
     taps_ref,
     rates_ref,
     residues_ref,
@@ -350,14 +372,14 @@
     back,
     grad_ext,
 ):
-    groups, toks, chans = keep_ref.shape
+    groups, half, chans = keep_refs[0].shape
+    toks = 2 * half
     modes = rates_ref.shape[0]
     short = taps_ref.shape[1]
     rim = short - 1
     length = toks // CHUNKS
     lanes = flat.shape[-1]
     wide = (CHUNKS, lanes)
-    half = toks // 2
     _, _, _, core = here()
 
     def row(array, at):
@@ -370,7 +392,9 @@
         other_rows = pl.ds(pl.multiple_of((1 - core) * half, half), half)
 
         for g in range(groups):
-            flat[g] = (keep_ref[g, :, some] + other_ref[g, :, some].astype(f32)).astype(bf16).astype(f32)
+            for n, (keep_ref, other_ref) in enumerate(zip(keep_refs, other_refs)):
+                total = keep_ref[g, :, some] + other_ref[g, :, some]
+                flat[g, n * half : (n + 1) * half] = total.astype(bf16).astype(f32)
         flat_cot[own_rows] = cot_own_ref[:, whole].astype(f32)
         flat_cot[other_rows] = cot_other_ref[:, some].astype(f32)
 
@@ -467,19 +491,20 @@
 
 
 def mixer(keep, other, taps, rates, residues, cot_own, cot_other):
-    groups, toks, chans = keep.shape
+    groups, toks, chans = keep[0].shape
+    toks *= 2
     modes = rates.shape[0]
     rim = taps.shape[1] - 1
     lanes = 128
     length = toks // CHUNKS
     return small_call(
-        mixer_kernel,
+        lambda *refs: mixer_kernel(refs[:2], refs[2:4], *refs[4:]),
         [
             jax.ShapeDtypeStruct((toks // 2, chans), bf16),
             jax.ShapeDtypeStruct((toks // 2, chans), bf16),
             jax.ShapeDtypeStruct((groups, chans, toks), bf16),
         ],
-        [keep, other, taps, rates, residues, cot_own, cot_other],
+        list(keep) + list(other) + [taps, rates, residues, cot_own, cot_other],
         "mixer",
         12 * modes * toks * chans,
         [
@@ -600,29 +625,41 @@
         lax.dynamic_slice_in_dim(cotangent, (1 - lax.axis_index("ctx")) * cot_half, cot_half, 1)
     )
     own_ids, table = fetch(own_ids, embed)
-    embedded = embed_rows(own_ids, other_ids, table)
-
-    embedded, cot_other = lax.optimization_barrier((embedded, cot_other))
-    got_1 = lax.ppermute(embedded, BOTH, GATHER_Z[0])
+    upper, lower = embed_rows(own_ids, other_ids, table)
+    upper, lower, cot_other = lax.optimization_barrier((upper, lower, cot_other))
+
+    def z_stage(rows):
+        return [lax.ppermute(rows, BOTH, pairs) for pairs in GATHER_Z]
+
+    def plane_stage(held):
+        first, other = lax.ppermute(held, BOTH, FIRST_WAY), lax.ppermute(held, BOTH, OTHER_WAY)
+        return first, other, lax.ppermute(first, BOTH, OTHER_WAY)
+
+    came = z_stage(upper)
     w = load(jnp.transpose(w_in, (1, 0, 2)))
-    got_1, w = lax.optimization_barrier((got_1, w))
-    slot_1 = choose(embedded, got_1)
-    x_1, y_1 = over_x(slot_1), over_y(slot_1)
-    got_2 = lax.ppermute(got_1, BOTH, GATHER_Z[1])
-    slot_2 = choose(got_1, got_2)
-    x_2, y_2 = over_x(slot_2), over_y(slot_2)
-    sums = project([(1, 0, 0), (2, 0, 0)], [slot_1, slot_2], w, None, False)
-    x_1, y_1, sums = lax.optimization_barrier((x_1, y_1, sums))
-    d_1 = over_y(x_1)
-    sums = project([(1, 0, 1), (1, 1, 0)], [x_1, y_1], w, sums, False)
-    x_2, y_2, sums = lax.optimization_barrier((x_2, y_2, sums))
-    d_2 = over_x(y_2)
-    sums = project([(2, 0, 1), (2, 1, 0)], [x_2, y_2], w, sums, False)
-    d_1, d_2, sums = lax.optimization_barrier((d_1, d_2, sums))
-    keep, send = project([(1, 1, 1), (2, 1, 1)], [d_1, d_2], w, sums, True)
-
+    *came, w = lax.optimization_barrier((*came, w))
+    held_1 = slots(upper, *came)
+    held_1, lower = lax.optimization_barrier((held_1, lower))
+    came = z_stage(lower)
+    first_1, other_1, both_1 = plane_stage(held_1)
+    sums = project([None, 0, 1], [held_1, first_1, other_1], w)
+    *came, sums = lax.optimization_barrier((*came, sums))
+    held_2 = slots(lower, *came)
+    first_2, other_2, both_2 = plane_stage(held_2)
+    keep_1, send_1 = project([2], [both_1], w, sums)
+    got_1 = swap(send_1)
+    first_2, other_2, send_1 = lax.optimization_barrier((first_2, other_2, send_1))
+    sums = project([None, 0, 1], [held_2, first_2, other_2], w)
+    keep_2, send_2 = project([2], [both_2], w, sums)
+    got_2 = swap(send_2)
     mixed_own, mixed_send, grad_own = mixer(
-        keep, swap(send), jnp.transpose(taps, (1, 0, 2)), rates, residues, cotangent, cot_other
+        (keep_1, keep_2),
+        (got_1, got_2),
+        jnp.transpose(taps, (1, 0, 2)),
+        rates,
+        residues,
+        cotangent,
+        cot_other,
     )
     grad_other = swap(grad_own)
     mixed_other = swap(mixed_send)

time: 84.3 us -> 87.8 us (1.042)
  starting transfers between devices: 22.1 us -> 30.9 us
  waiting for transfers between devices: 38.4 us -> 32.7 us
    ppermute x5 -> x6, starting transfers between devices: 2.81 us -> 12.5 us  [swap(): return lax.ppermute(array, BOTH, OTHER_CORE)]
    ppermute x6 -> x3, waiting for transfers between devices: 10.8 us -> 2.64 us  [over_y(): return lax.ppermute(array, BOTH, OVER_Y)]
    ppermute x2 -> x10, starting transfers between devices: 3.65 us -> 11.5 us  [the longest x4 4.82 us: z_stage(): return [lax.ppermute(rows, BOTH, pairs) for pairs in GATHER_Z]]
    ppermute x2 -> x10, waiting for transfers between devices: 2.5 us -> 8.56 us  [the longest x2 4.88 us: plane_stage(): lax.ppermute(held, BOTH, FIRST_WAY)]
    ppermute x6 -> x3, starting transfers between devices: 7.22 us -> 2.03 us  [over_y(): return lax.ppermute(array, BOTH, OVER_Y)]
    ppermute x1, waiting for transfers between devices: 3.07 us -> 0.01 us  [chip_plan(): lax.ppermute(send_2, BOTH, SCATTER_Z[1])]
    ppermute x6 -> x3, waiting for transfers between devices: 11 us -> 8.25 us  [over_x(): return lax.ppermute(array, BOTH, OVER_X)]
    ppermute x1, starting transfers between devices: 2.58 us -> 0.04 us  [chip_plan(): lax.ppermute(send_1, BOTH, SCATTER_Z[0])]
  transfers between devices with their start and end apart: 23 -> 26, of which waited for: 18 -> 14; matrix products, arithmetic and copies ran while one was open for 0% -> 0% of each run, Pallas kernels for 16% -> 17%
where the time goes in v5:
time: 87.8 us; the launch traced here: 86.7 us
  waiting for transfers between devices  32.7 us (37%)
  starting transfers between devices  30.9 us (35%)
  Pallas kernels  21.4 us (24%)
    pallas_call x16, Pallas kernels, small_call(): pl.pallas_call(kernel, in_specs=[IN_VMEM] * len(operands), out_specs=jax....  15.7 us
    ppermute x6, starting transfers between devices, swap(): return lax.ppermute(array, BOTH, OTHER_CORE)  12.5 us
    ppermute x3, waiting for transfers between devices, over_x(): return lax.ppermute(array, BOTH, OVER_X)  8.25 us
    ppermute x1, waiting for transfers between devices, chip_plan(): lax.ppermute(send_1, BOTH, SCATTER_Z[2])  5.29 us
    ppermute x2, waiting for transfers between devices, plane_stage(): lax.ppermute(held, BOTH, FIRST_WAY)  4.88 us
    ppermute x4, starting transfers between devices, z_stage(): return [lax.ppermute(rows, BOTH, pairs) for pairs in GATHER_Z]  4.82 us
    pallas_call x1, Pallas kernels, load(): pl.pallas_call(load_kernel, in_specs=[pl.BlockSpec(memory_space=pltpu.HBM...  4.58 us
    ppermute x6, waiting for transfers between devices, swap(): return lax.ppermute(array, BOTH, OTHER_CORE)  3.99 us
  transfers between devices with their start and end apart: 26, of which 14 were waited for; matrix products, arithmetic and copies ran while one was open for 0% of the time, Pallas kernels for 17%

profile of v5, /device:TPU:0, one launch (start us, length us, event | category | flops | bytes accessed | tf_op | source)
XLA Modules:
  0.0 86.7 jit_solution(13716521472935364803)
XLA Ops:
  4.5 3.0 %collective-permute-start.2 = (bf16[128,512]{1,0:T(8,128)(2,1)S(1)}, bf16[128,512]{1,0:T(8,128)(2,1)S(1)}, u32[]{:S(2)}, u32[]{:S(2)}) collective-permute-start(bf16[128,512]{1,0:T(8,128)(2,1)S(1)} %get-tuple-element.48.own_ref), channel_id=1, source_target_pairs={{0,8},{2,10},{4,12},{6,14},{8,0},{10,2},{12,4},{14,6},{1,16},{3,18... | collective-permute-start | bytes 393224 | tf_op jit(solution)/shard_map/ppermute | solution.py:632
  7.4 4.6 %load.1.w_ref = bf16[3,4096,512]{2,1,0:T(8,128)(2,1)S(1)} custom-call(bf16[3,4096,512]{2,1,0:T(8,128)(2,1)} %bitcast.4), custom_call_target="tpu_custom_call" | custom-call | bytes 25165824 | tf_op jit(solution)/shard_map/load/pallas_call | solution.py:271
  12.1 1.6 %collective-permute-start.8 = (bf16[256,512]{1,0:T(8,128)(2,1)S(1)}, bf16[256,512]{1,0:T(8,128)(2,1)S(1)}, u32[]{:S(2)}, u32[]{:S(2)}) collective-permute-start(bf16[256,512]{1,0:T(8,128)(2,1)S(1)} %slots.2.refs_0_), channel_id=1, source_target_pairs={{0,4},{1,3},{2,6},{3,1},{4,0},{5,7},{6,2},{7,5},{8,12},{9,11},{10,... | collective-permute-start | bytes 786440 | tf_op jit(solution)/shard_map/ppermute | solution.py:635
  13.7 1.5 %collective-permute-start.4 = (bf16[256,512]{1,0:T(8,128)(2,1)S(1)}, bf16[256,512]{1,0:T(8,128)(2,1)S(1)}, u32[]{:S(2)}, u32[]{:S(2)}) collective-permute-start(bf16[256,512]{1,0:T(8,128)(2,1)S(1)} %slots.2.refs_0_), channel_id=1, source_target_pairs={{0,2},{1,5},{2,0},{3,7},{4,6},{5,1},{6,4},{7,3},{8,10},{9,13},{10,... | collective-permute-start | bytes 786440 | tf_op jit(solution)/shard_map/ppermute | solution.py:635
  16.3 2.2 %collective-permute-done.8.refs_2_ = bf16[256,512]{1,0:T(8,128)(2,1)S(1)} collective-permute-done((bf16[256,512]{1,0:T(8,128)(2,1)S(1)}, bf16[256,512]{1,0:T(8,128)(2,1)S(1)}, u32[]{:S(2)}, u32[]{:S(2)}) %collective-permute-start.8) | collective-permute-done | bytes 262176 | tf_op jit(solution)/shard_map/ppermute | solution.py:635
  18.5 2.0 %collective-permute-done.4.refs_1_ = bf16[256,512]{1,0:T(8,128)(2,1)S(1)} collective-permute-done((bf16[256,512]{1,0:T(8,128)(2,1)S(1)}, bf16[256,512]{1,0:T(8,128)(2,1)S(1)}, u32[]{:S(2)}, u32[]{:S(2)}) %collective-permute-start.4) | collective-permute-done | bytes 262176 | tf_op jit(solution)/shard_map/ppermute | solution.py:635
  20.6 1.4 %project.4.refs_1_ = f32[3,128,512]{2,1,0:T(8,128)S(1)} custom-call(bf16[3,4096,512]{2,1,0:T(8,128)(2,1)S(1)} %load.1.w_ref, bf16[256,512]{1,0:T(8,128)(2,1)S(1)} %slots.2.refs_0_, bf16[256,512]{1,0:T(8,128)(2,1)S(1)} %collective-permute-done.4.refs_1_, bf16[256,512]{1,0:T(8,128)(2,1)S(1)} %collective-permute-done.8.refs_2_), custom_call_target="tpu_custom_call" | custom-call | flops 18874368 | bytes 208896 | tf_op jit(solution)/shard_map/project/pallas_call | solution.py:162
  22.0 1.6 %collective-permute-start.9 = (bf16[256,512]{1,0:T(8,128)(2,1)S(1)}, bf16[256,512]{1,0:T(8,128)(2,1)S(1)}, u32[]{:S(2)}, u32[]{:S(2)}) collective-permute-start(bf16[256,512]{1,0:T(8,128)(2,1)S(1)} %slots.3.refs_0_), channel_id=1, source_target_pairs={{0,2},{1,5},{2,0},{3,7},{4,6},{5,1},{6,4},{7,3},{8,10},{9,13},{10,... | collective-permute-start | bytes 786440 | tf_op jit(solution)/shard_map/ppermute | solution.py:635
  23.6 2.0 %collective-permute-start.11 = (bf16[256,512]{1,0:T(8,128)(2,1)S(1)}, bf16[256,512]{1,0:T(8,128)(2,1)S(1)}, u32[]{:S(2)}, u32[]{:S(2)}) collective-permute-start(bf16[256,512]{1,0:T(8,128)(2,1)S(1)} %slots.3.refs_0_), channel_id=1, source_target_pairs={{0,4},{1,3},{2,6},{3,1},{4,0},{5,7},{6,2},{7,5},{8,12},{9,11},{10,... | collective-permute-start | bytes 786440 | tf_op jit(solution)/shard_map/ppermute | solution.py:635
  25.6 2.9 %collective-permute-done.9.refs_1_ = bf16[256,512]{1,0:T(8,128)(2,1)S(1)} collective-permute-done((bf16[256,512]{1,0:T(8,128)(2,1)S(1)}, bf16[256,512]{1,0:T(8,128)(2,1)S(1)}, u32[]{:S(2)}, u32[]{:S(2)}) %collective-permute-start.9) | collective-permute-done | bytes 262176 | tf_op jit(solution)/shard_map/ppermute | solution.py:635
  28.5 1.5 %collective-permute-done.5.refs_0_ = bf16[256,512]{1,0:T(8,128)(2,1)S(1)} collective-permute-done((bf16[256,512]{1,0:T(8,128)(2,1)S(1)}, bf16[256,512]{1,0:T(8,128)(2,1)S(1)}, u32[]{:S(2)}, u32[]{:S(2)}) %collective-permute-start.5) | collective-permute-done | bytes 262176 | tf_op jit(solution)/shard_map/ppermute | solution.py:636
  30.7 8.9 %collective-permute-start.12 = (f32[3,128,256]{2,1,0:T(8,128)S(1)}, f32[3,128,256]{2,1,0:T(8,128)S(1)}, u32[]{:S(2)}, u32[]{:S(2)}) collective-permute-start(f32[3,128,256]{2,1,0:T(8,128)S(1)} %get-tuple-element.59), channel_id=1, source_target_pairs={{0,1},{1,0},{2,3},{3,2},{4,5},{5,4},{6,7},{7,6},{8,9},{9,8},{10,11... | collective-permute-start | bytes 1179656 | tf_op jit(solution)/shard_map/ppermute | solution.py:613
  39.7 1.4 %project.6.refs_1_ = f32[3,128,512]{2,1,0:T(8,128)S(1)} custom-call(bf16[3,4096,512]{2,1,0:T(8,128)(2,1)S(1)} %load.1.w_ref, bf16[256,512]{1,0:T(8,128)(2,1)S(1)} %slots.3.refs_0_, bf16[256,512]{1,0:T(8,128)(2,1)S(1)} %collective-permute-done.9.refs_1_, bf16[256,512]{1,0:T(8,128)(2,1)S(1)} %collective-permute-done.11.refs_2_), custom_call_target="tpu_custom_call" | custom-call | flops 18874368 | bytes 208896 | tf_op jit(solution)/shard_map/project/pallas_call | solution.py:162
  41.8 2.5 %collective-permute-start.13 = (f32[3,128,256]{2,1,0:T(8,128)S(1)}, f32[3,128,256]{2,1,0:T(8,128)S(1)}, u32[]{:S(2)}, u32[]{:S(2)}) collective-permute-start(f32[3,128,256]{2,1,0:T(8,128)S(1)} %get-tuple-element.63), channel_id=1, source_target_pairs={{0,1},{1,0},{2,3},{3,2},{4,5},{5,4},{6,7},{7,6},{8,9},{9,8},{10,11... | collective-permute-start | bytes 1179656 | tf_op jit(solution)/shard_map/ppermute | solution.py:613
  44.3 1.3 %collective-permute-done.13.refs_3_ = f32[3,128,256]{2,1,0:T(8,128)S(1)} collective-permute-done((f32[3,128,256]{2,1,0:T(8,128)S(1)}, f32[3,128,256]{2,1,0:T(8,128)S(1)}, u32[]{:S(2)}, u32[]{:S(2)}) %collective-permute-start.13) | collective-permute-done | bytes 393248 | tf_op jit(solution)/shard_map/ppermute | solution.py:613
  45.6 4.6 %mixer.1 = (bf16[128,256]{1,0:T(8,128)(2,1)S(1)}, bf16[128,256]{1,0:T(8,128)(2,1)S(1)}, bf16[3,256,256]{2,1,0:T(8,128)(2,1)S(1)}) custom-call(f32[3,128,256]{2,1,0:T(8,128)S(1)} %get-tuple-element.56.refs_0_, f32[3,128,256]{2,1,0:T(8,128)S(1)} %get-tuple-element.62.refs_1_, f32[3,128,256]{2,1,0:T(8,128)S(1)} %collective-permute-done.12.refs_2_, ...), custom_call_target="tpu_custom_call" | custom-call | flops 196608 | bytes 29344 | tf_op jit(solution)/shard_map/mixer/pallas_call | solution.py:162
  50.7 1.3 %collective-permute-done.14.other_ref = bf16[3,256,256]{2,1,0:T(8,128)(2,1)S(1)} collective-permute-done((bf16[3,256,256]{2,1,0:T(8,128)(2,1)S(1)}, bf16[3,256,256]{2,1,0:T(8,128)(2,1)S(1)}, u32[]{:S(2)}, u32[]{:S(2)}) %collective-permute-start.14) | collective-permute-done | bytes 393248 | tf_op jit(solution)/shard_map/ppermute | solution.py:613
  55.9 2.6 %back_project.2 = (bf16[512,256]{1,0:T(8,128)(2,1)S(1)}, f32[512,256]{1,0:T(8,128)S(1)}, f32[512,256]{1,0:T(8,128)S(1)}, bf16[512,256]{1,0:T(8,128)(2,1)S(1)}, f...) custom-call(bf16[3,4096,512]{2,1,0:T(8,128)(2,1)S(1)} %load.1.w_ref, bf16[3,256,256]{2,1,0:T(8,128)(2,1)S(1)} %get-tuple-element.65.own_ref, ...), custom_call_target="tpu_custom_call" | custom-call | flops 37748736 | bytes 208896 | tf_op jit(solution)/shard_map/back_project/pallas_call | solution.py:162
  58.5 3.2 %collective-permute-done.15.got_ref = bf16[512,256]{1,0:T(8,128)(2,1)S(1)} collective-permute-done((bf16[512,256]{1,0:T(8,128)(2,1)S(1)}, bf16[512,256]{1,0:T(8,128)(2,1)S(1)}, u32[]{:S(2)}, u32[]{:S(2)}) %collective-permute-start.15) | collective-permute-done | bytes 262176 | tf_op jit(solution)/shard_map/ppermute | solution.py:616
  62.7 2.0 %collective-permute-start.19 = (bf16[512,256]{1,0:T(8,128)(2,1)S(1)}, bf16[512,256]{1,0:T(8,128)(2,1)S(1)}, u32[]{:S(2)}, u32[]{:S(2)}) collective-permute-start(bf16[512,256]{1,0:T(8,128)(2,1)S(1)} %get-tuple-element.74), channel_id=1, source_target_pairs={{0,4},{1,5},{2,6},{3,7},{4,0},{5,1},{6,2},{7,3},{8,12},{9,13},{10,... | collective-permute-start | bytes 786440 | tf_op jit(solution)/shard_map/ppermute | solution.py:619
  66.0 5.1 %collective-permute-done.20.x_ref = bf16[512,256]{1,0:T(8,128)(2,1)S(1)} collective-permute-done((bf16[512,256]{1,0:T(8,128)(2,1)S(1)}, bf16[512,256]{1,0:T(8,128)(2,1)S(1)}, u32[]{:S(2)}, u32[]{:S(2)}) %collective-permute-start.20) | collective-permute-done | bytes 262176 | tf_op jit(solution)/shard_map/ppermute | solution.py:616
  74.0 1.8 %collective-permute-done.19.y_ref = bf16[512,256]{1,0:T(8,128)(2,1)S(1)} collective-permute-done((bf16[512,256]{1,0:T(8,128)(2,1)S(1)}, bf16[512,256]{1,0:T(8,128)(2,1)S(1)}, u32[]{:S(2)}, u32[]{:S(2)}) %collective-permute-start.19) | collective-permute-done | bytes 262176 | tf_op jit(solution)/shard_map/ppermute | solution.py:619
  76.7 3.9 %collective-permute-done.22.a_ref = bf16[512,128]{1,0:T(8,128)(2,1)S(1)} collective-permute-done((bf16[512,128]{1,0:T(8,128)(2,1)S(1)}, bf16[512,128]{1,0:T(8,128)(2,1)S(1)}, u32[]{:S(2)}, u32[]{:S(2)}) %collective-permute-start.22) | collective-permute-done | bytes 131104 | tf_op jit(solution)/shard_map/ppermute | solution.py:684
  80.6 5.3 %collective-permute-done.24.c_ref = bf16[512,128]{1,0:T(8,128)(2,1)S(1)} collective-permute-done((bf16[512,128]{1,0:T(8,128)(2,1)S(1)}, bf16[512,128]{1,0:T(8,128)(2,1)S(1)}, u32[]{:S(2)}, u32[]{:S(2)}) %collective-permute-start.24) | collective-permute-done | bytes 131104 | tf_op jit(solution)/shard_map/ppermute | solution.py:689
  (55 shorter events, 17.7 us)
Async XLA Ops:
  1.5 2.3 %collective-permute-start.1 = (bf16[128,256]{1,0:T(8,128)(2,1)S(1)}, bf16[128,256]{1,0:T(8,128)(2,1)S(1)}, u32[]{:S(2)}, u32[]{:S(2)}) collective-permute-start(bf16[128,256]{1,0:T(8,128)(2,1)S(1)} %constant_dynamic-slice_fusion), channel_id=1, source_target_pairs={{0,1},{1,0},{2,3},{3,2},{4,5},{5,4},{6,7},{7,6},{8,9},{9,8},{10,11... | collective-permute-start | bytes 196616 | tf_op jit(solution)/shard_map/ppermute | solution.py:613
  3.8 8.3 %collective-permute-start.3 = (bf16[128,512]{1,0:T(8,128)(2,1)S(1)}, bf16[128,512]{1,0:T(8,128)(2,1)S(1)}, u32[]{:S(2)}, u32[]{:S(2)}) collective-permute-start(bf16[128,512]{1,0:T(8,128)(2,1)S(1)} %get-tuple-element.48.own_ref), channel_id=1, source_target_pairs={{9,16},{11,18},{13,20},{15,22},{1,24},{3,26},{5,28},{7,30},{16,9},... | collective-permute-start | bytes 393224 | tf_op jit(solution)/shard_map/ppermute | solution.py:632
  4.5 7.6 %collective-permute-start.2 = (bf16[128,512]{1,0:T(8,128)(2,1)S(1)}, bf16[128,512]{1,0:T(8,128)(2,1)S(1)}, u32[]{:S(2)}, u32[]{:S(2)}) collective-permute-start(bf16[128,512]{1,0:T(8,128)(2,1)S(1)} %get-tuple-element.48.own_ref), channel_id=1, source_target_pairs={{0,8},{2,10},{4,12},{6,14},{8,0},{10,2},{12,4},{14,6},{1,16},{3,18... | collective-permute-start | bytes 393224 | tf_op jit(solution)/shard_map/ppermute | solution.py:632
  12.1 6.4 %collective-permute-start.8 = (bf16[256,512]{1,0:T(8,128)(2,1)S(1)}, bf16[256,512]{1,0:T(8,128)(2,1)S(1)}, u32[]{:S(2)}, u32[]{:S(2)}) collective-permute-start(bf16[256,512]{1,0:T(8,128)(2,1)S(1)} %slots.2.refs_0_), channel_id=1, source_target_pairs={{0,4},{1,3},{2,6},{3,1},{4,0},{5,7},{6,2},{7,5},{8,12},{9,11},{10,... | collective-permute-start | bytes 786440 | tf_op jit(solution)/shard_map/ppermute | solution.py:635
  13.7 6.9 %collective-permute-start.4 = (bf16[256,512]{1,0:T(8,128)(2,1)S(1)}, bf16[256,512]{1,0:T(8,128)(2,1)S(1)}, u32[]{:S(2)}, u32[]{:S(2)}) collective-permute-start(bf16[256,512]{1,0:T(8,128)(2,1)S(1)} %slots.2.refs_0_), channel_id=1, source_target_pairs={{0,2},{1,5},{2,0},{3,7},{4,6},{5,1},{6,4},{7,3},{8,10},{9,13},{10,... | collective-permute-start | bytes 786440 | tf_op jit(solution)/shard_map/ppermute | solution.py:635
  15.2 6.8 %collective-permute-start.7 = (bf16[128,512]{1,0:T(8,128)(2,1)S(1)}, bf16[128,512]{1,0:T(8,128)(2,1)S(1)}, u32[]{:S(2)}, u32[]{:S(2)}) collective-permute-start(bf16[128,512]{1,0:T(8,128)(2,1)S(1)} %get-tuple-element.54.own_ref), channel_id=1, source_target_pairs={{9,16},{11,18},{13,20},{15,22},{1,24},{3,26},{5,28},{7,30},{16,9},... | collective-permute-start | bytes 393224 | tf_op jit(solution)/shard_map/ppermute | solution.py:632
  15.8 6.1 %collective-permute-start.6 = (bf16[128,512]{1,0:T(8,128)(2,1)S(1)}, bf16[128,512]{1,0:T(8,128)(2,1)S(1)}, u32[]{:S(2)}, u32[]{:S(2)}) collective-permute-start(bf16[128,512]{1,0:T(8,128)(2,1)S(1)} %get-tuple-element.54.own_ref), channel_id=1, source_target_pairs={{0,8},{2,10},{4,12},{6,14},{8,0},{10,2},{12,4},{14,6},{1,16},{3,18... | collective-permute-start | bytes 393224 | tf_op jit(solution)/shard_map/ppermute | solution.py:632
  22.0 6.4 %collective-permute-start.9 = (bf16[256,512]{1,0:T(8,128)(2,1)S(1)}, bf16[256,512]{1,0:T(8,128)(2,1)S(1)}, u32[]{:S(2)}, u32[]{:S(2)}) collective-permute-start(bf16[256,512]{1,0:T(8,128)(2,1)S(1)} %slots.3.refs_0_), channel_id=1, source_target_pairs={{0,2},{1,5},{2,0},{3,7},{4,6},{5,1},{6,4},{7,3},{8,10},{9,13},{10,... | collective-permute-start | bytes 786440 | tf_op jit(solution)/shard_map/ppermute | solution.py:635
  23.6 6.4 %collective-permute-start.5 = (bf16[256,512]{1,0:T(8,128)(2,1)S(1)}, bf16[256,512]{1,0:T(8,128)(2,1)S(1)}, u32[]{:S(2)}, u32[]{:S(2)}) collective-permute-start(bf16[256,512]{1,0:T(8,128)(2,1)S(1)} %collective-permute-done.4.refs_1_), channel_id=1, source_target_pairs={{0,4},{1,3},{2,6},{3,1},{4,0},{5,7},{6,2},{7,5},{8,12},{9,11},{10,... | collective-permute-start | bytes 786440 | tf_op jit(solution)/shard_map/ppermute | solution.py:636
  23.6 16.1 %collective-permute-start.11 = (bf16[256,512]{1,0:T(8,128)(2,1)S(1)}, bf16[256,512]{1,0:T(8,128)(2,1)S(1)}, u32[]{:S(2)}, u32[]{:S(2)}) collective-permute-start(bf16[256,512]{1,0:T(8,128)(2,1)S(1)} %slots.3.refs_0_), channel_id=1, source_target_pairs={{0,4},{1,3},{2,6},{3,1},{4,0},{5,7},{6,2},{7,5},{8,12},{9,11},{10,... | collective-permute-start | bytes 786440 | tf_op jit(solution)/shard_map/ppermute | solution.py:635
  28.5 12.6 %collective-permute-start.10 = (bf16[256,512]{1,0:T(8,128)(2,1)S(1)}, bf16[256,512]{1,0:T(8,128)(2,1)S(1)}, u32[]{:S(2)}, u32[]{:S(2)}) collective-permute-start(bf16[256,512]{1,0:T(8,128)(2,1)S(1)} %collective-permute-done.9.refs_1_), channel_id=1, source_target_pairs={{0,4},{1,3},{2,6},{3,1},{4,0},{5,7},{6,2},{7,5},{8,12},{9,11},{10,... | collective-permute-start | bytes 786440 | tf_op jit(solution)/shard_map/ppermute | solution.py:636
  30.7 13.6 %collective-permute-start.12 = (f32[3,128,256]{2,1,0:T(8,128)S(1)}, f32[3,128,256]{2,1,0:T(8,128)S(1)}, u32[]{:S(2)}, u32[]{:S(2)}) collective-permute-start(f32[3,128,256]{2,1,0:T(8,128)S(1)} %get-tuple-element.59), channel_id=1, source_target_pairs={{0,1},{1,0},{2,3},{3,2},{4,5},{5,4},{6,7},{7,6},{8,9},{9,8},{10,11... | collective-permute-start | bytes 1179656 | tf_op jit(solution)/shard_map/ppermute | solution.py:613
  41.8 3.8 %collective-permute-start.13 = (f32[3,128,256]{2,1,0:T(8,128)S(1)}, f32[3,128,256]{2,1,0:T(8,128)S(1)}, u32[]{:S(2)}, u32[]{:S(2)}) collective-permute-start(f32[3,128,256]{2,1,0:T(8,128)S(1)} %get-tuple-element.63), channel_id=1, source_target_pairs={{0,1},{1,0},{2,3},{3,2},{4,5},{5,4},{6,7},{7,6},{8,9},{9,8},{10,11... | collective-permute-start | bytes 1179656 | tf_op jit(solution)/shard_map/ppermute | solution.py:613
  50.3 1.8 %collective-permute-start.14 = (bf16[3,256,256]{2,1,0:T(8,128)(2,1)S(1)}, bf16[3,256,256]{2,1,0:T(8,128)(2,1)S(1)}, u32[]{:S(2)}, u32[]{:S(2)}) collective-permute-start(bf16[3,256,256]{2,1,0:T(8,128)(2,1)S(1)} %get-tuple-element.65.own_ref), channel_id=1, source_target_pairs={{0,1},{1,0},{2,3},{3,2},{4,5},{5,4},{6,7},{7,6},{8,9},{9,8},{10,11... | collective-permute-start | bytes 1179656 | tf_op jit(solution)/shard_map/ppermute | solution.py:613
  53.0 8.7 %collective-permute-start.15 = (bf16[512,256]{1,0:T(8,128)(2,1)S(1)}, bf16[512,256]{1,0:T(8,128)(2,1)S(1)}, u32[]{:S(2)}, u32[]{:S(2)}) collective-permute-start(bf16[512,256]{1,0:T(8,128)(2,1)S(1)} %get-tuple-element.67), channel_id=1, source_target_pairs={{0,2},{1,3},{2,0},{3,1},{4,6},{5,7},{6,4},{7,5},{8,10},{9,11},{10,... | collective-permute-start | bytes 786440 | tf_op jit(solution)/shard_map/ppermute | solution.py:616
  54.0 10.7 %collective-permute-start.17 = (bf16[512,256]{1,0:T(8,128)(2,1)S(1)}, bf16[512,256]{1,0:T(8,128)(2,1)S(1)}, u32[]{:S(2)}, u32[]{:S(2)}) collective-permute-start(bf16[512,256]{1,0:T(8,128)(2,1)S(1)} %get-tuple-element.73), channel_id=1, source_target_pairs={{0,4},{1,5},{2,6},{3,7},{4,0},{5,1},{6,2},{7,3},{8,12},{9,13},{10,... | collective-permute-start | bytes 786440 | tf_op jit(solution)/shard_map/ppermute | solution.py:619
  61.7 9.3 %collective-permute-start.20 = (bf16[512,256]{1,0:T(8,128)(2,1)S(1)}, bf16[512,256]{1,0:T(8,128)(2,1)S(1)}, u32[]{:S(2)}, u32[]{:S(2)}) collective-permute-start(bf16[512,256]{1,0:T(8,128)(2,1)S(1)} %get-tuple-element.80), channel_id=1, source_target_pairs={{0,2},{1,3},{2,0},{3,1},{4,6},{5,7},{6,4},{7,5},{8,10},{9,11},{10,... | collective-permute-start | bytes 786440 | tf_op jit(solution)/shard_map/ppermute | solution.py:616
  62.7 9.2 %collective-permute-start.21 = (bf16[512,256]{1,0:T(8,128)(2,1)S(1)}, bf16[512,256]{1,0:T(8,128)(2,1)S(1)}, u32[]{:S(2)}, u32[]{:S(2)}) collective-permute-start(bf16[512,256]{1,0:T(8,128)(2,1)S(1)} %merge.3), channel_id=1, source_target_pairs={{0,4},{1,5},{2,6},{3,7},{4,0},{5,1},{6,2},{7,3},{8,12},{9,13},{10,... | collective-permute-start | bytes 786440 | tf_op jit(solution)/shard_map/ppermute | solution.py:619
  62.7 13.1 %collective-permute-start.19 = (bf16[512,256]{1,0:T(8,128)(2,1)S(1)}, bf16[512,256]{1,0:T(8,128)(2,1)S(1)}, u32[]{:S(2)}, u32[]{:S(2)}) collective-permute-start(bf16[512,256]{1,0:T(8,128)(2,1)S(1)} %get-tuple-element.74), channel_id=1, source_target_pairs={{0,4},{1,5},{2,6},{3,7},{4,0},{5,1},{6,2},{7,3},{8,12},{9,13},{10,... | collective-permute-start | bytes 786440 | tf_op jit(solution)/shard_map/ppermute | solution.py:619
  64.7 11.0 %collective-permute-start.18 = (bf16[512,256]{1,0:T(8,128)(2,1)S(1)}, bf16[512,256]{1,0:T(8,128)(2,1)S(1)}, u32[]{:S(2)}, u32[]{:S(2)}) collective-permute-start(bf16[512,256]{1,0:T(8,128)(2,1)S(1)} %merge.2), channel_id=1, source_target_pairs={{0,2},{1,3},{2,0},{3,1},{4,6},{5,7},{6,4},{7,5},{8,10},{9,11},{10,... | collective-permute-start | bytes 786440 | tf_op jit(solution)/shard_map/ppermute | solution.py:616
  72.8 7.8 %collective-permute-start.22 = (bf16[512,128]{1,0:T(8,128)(2,1)S(1)}, bf16[512,128]{1,0:T(8,128)(2,1)S(1)}, u32[]{:S(2)}, u32[]{:S(2)}) collective-permute-start(bf16[512,128]{1,0:T(8,128)(2,1)S(1)} %get-tuple-element.82), channel_id=1, source_target_pairs={{0,8},{2,10},{4,12},{6,14},{8,0},{10,2},{12,4},{14,6},{16,9},{18,1... | collective-permute-start | bytes 393224 | tf_op jit(solution)/shard_map/ppermute | solution.py:684
  72.9 7.7 %collective-permute-start.23 = (bf16[512,128]{1,0:T(8,128)(2,1)S(1)}, bf16[512,128]{1,0:T(8,128)(2,1)S(1)}, u32[]{:S(2)}, u32[]{:S(2)}) collective-permute-start(bf16[512,128]{1,0:T(8,128)(2,1)S(1)} %get-tuple-element.83), channel_id=1, source_target_pairs={{0,9},{2,11},{4,13},{6,15},{8,1},{10,3},{12,5},{14,7},{16,8},{18,1... | collective-permute-start | bytes 393224 | tf_op jit(solution)/shard_map/ppermute | solution.py:685
  75.9 10.0 %collective-permute-start.24 = (bf16[512,128]{1,0:T(8,128)(2,1)S(1)}, bf16[512,128]{1,0:T(8,128)(2,1)S(1)}, u32[]{:S(2)}, u32[]{:S(2)}) collective-permute-start(bf16[512,128]{1,0:T(8,128)(2,1)S(1)} %get-tuple-element.84), channel_id=1, source_target_pairs={{0,1},{2,3},{4,5},{6,7},{8,9},{10,11},{12,13},{14,15},{16,0},{18,2... | collective-permute-start | bytes 393224 | tf_op jit(solution)/shard_map/ppermute | solution.py:689
  76.0 9.9 %collective-permute-start.25 = (bf16[512,128]{1,0:T(8,128)(2,1)S(1)}, bf16[512,128]{1,0:T(8,128)(2,1)S(1)}, u32[]{:S(2)}, u32[]{:S(2)}) collective-permute-start(bf16[512,128]{1,0:T(8,128)(2,1)S(1)} %get-tuple-element.85), channel_id=1, source_target_pairs={{16,1},{18,3},{20,5},{22,7},{24,9},{26,11},{28,13},{30,15},{9,24},... | collective-permute-start | bytes 393224 | tf_op jit(solution)/shard_map/ppermute | solution.py:690
  (6 other events, 62.3 us)

commit v6 on v4

--- a/solution.py
+++ b/solution.py
@@ -121,8 +121,6 @@
 
 
 OTHER_CORE = everywhere(lambda z, y, x, core: (z, y, x, 1 - core))
-OVER_X = everywhere(lambda z, y, x, core: (z, y, 1 - x, core))
-OVER_Y = everywhere(lambda z, y, x, core: (z, 1 - y, x, core))
 
 
 def along_z(moves):
@@ -141,9 +139,11 @@
     return pairs
 
 
+FIRST_WAY = everywhere(lambda z, y, x, core: (z, y, 1 - x, core) if core == 0 else (z, 1 - y, x, core))
+OTHER_WAY = everywhere(lambda z, y, x, core: (z, 1 - y, x, core) if core == 0 else (z, y, 1 - x, core))
 GATHER_Z = (
     along_z([((0, 0), (1, 0)), ((1, 0), (0, 0)), ((0, 1), (2, 0)), ((1, 1), (3, 0))]),
-    along_z([((2, 0), (3, 0)), ((3, 0), (2, 0))]),
+    along_z([((1, 1), (2, 0)), ((0, 1), (3, 0))]),
 )
 SCATTER_Z = (
     along_z([((0, 0), (1, 0)), ((1, 0), (0, 0)), ((2, 0), (1, 1)), ((3, 0), (0, 1))]),
@@ -181,10 +181,13 @@
     return core == (z >> 1)
 
 
-def block_at(slot, far_y, far_x):
-    z, y, x, _ = here()
+def block_at(slot, way):
+    z, y, x, core = here()
     along = (z & 1) if slot == 1 else 1 - (z & 1)
-    return along * 4 + (1 - y if far_y else y) * 2 + (1 - x if far_x else x)
+    if way is not None:
+        far_y, far_x = ((core, 1 - core), (1 - core, core), (1, 1))[way]
+        y, x = y ^ far_y, x ^ far_x
+    return along * 4 + y * 2 + x
 
 
 def embed_kernel(own_ref, other_ref, table_ref, out_ref):
@@ -269,56 +272,62 @@
     return in_vmem(out)
 
 
-def choose_kernel(inner_ref, outer_ref, out_ref):
+def slots_kernel(own_ref, one_ref, two_ref, out_ref):
+    rows = own_ref.shape[0]
+
     @pl.when(is_inner())
     def _():
-        out_ref[...] = inner_ref[...]
+        out_ref[:rows] = own_ref[...]
+        out_ref[rows:] = one_ref[...]
 
     @pl.when(jnp.logical_not(is_inner()))
     def _():
-        out_ref[...] = outer_ref[...]
-
-
-def choose(inner, outer):
-    return small_call(
-        choose_kernel, jax.ShapeDtypeStruct(inner.shape, inner.dtype), [inner, outer], "choose"
-    )
-
-
-def project_kernel(blocks, has_base, last, w_ref, *refs):
-    count = len(blocks)
+        out_ref[:rows] = one_ref[...]
+        out_ref[rows:] = two_ref[...]
+
+
+def slots(own, one, two):
+    shape = jax.ShapeDtypeStruct((2 * own.shape[0], own.shape[1]), own.dtype)
+    return small_call(slots_kernel, shape, [own, one, two], "slots")
+
+
+def project_kernel(ways, has_base, last, w_ref, *refs):
+    count = len(ways)
     acts = refs[:count]
     groups, _, chans = w_ref.shape
-    toks, width = acts[0].shape
-    if last:
-        keep_ref, send_ref, total_ref = refs[-3:]
-    else:
-        total_ref = refs[-1]
-    starts = [pl.multiple_of(block_at(*block) * width, width) for block in blocks]
+    rows, width = acts[0].shape
+    rows //= 2
+    total_ref = refs[-1]
+    parts = []
+    for way, act in zip(ways, acts):
+        for slot in (1, 2):
+            start = pl.multiple_of(block_at(slot, way) * width, width)
+            parts.append((act, pl.ds((slot - 1) * rows, rows), pl.ds(start, width)))
     for g in range(groups):
         total = refs[count][g] if has_base else None
-        for start, act in zip(starts, acts):
-            term = jnp.dot(act[...], w_ref[g, pl.ds(start, width), :], preferred_element_type=f32)
+        for act, span, block in parts:
+            term = jnp.dot(act[span, :], w_ref[g, block, :], preferred_element_type=f32)
             total = term if total is None else total + term
         total_ref[g] = total
     if last:
+        keep_ref, send_ref = refs[-3:-1]
         half = chans // 2
         core = here()[3]
         keep_ref[...] = total_ref[:, :, pl.ds(pl.multiple_of(core * half, half), half)]
         send_ref[...] = total_ref[:, :, pl.ds(pl.multiple_of((1 - core) * half, half), half)]
 
 
-def project(blocks, acts, w, base, last):
+def project(ways, acts, w, base, last):
     groups, _, chans = w.shape
-    toks, width = acts[0].shape
-    total = jax.ShapeDtypeStruct((groups, toks, chans), f32)
-    half = jax.ShapeDtypeStruct((groups, toks, chans // 2), f32)
+    rows, width = acts[0].shape
+    total = jax.ShapeDtypeStruct((groups, rows // 2, chans), f32)
+    half = jax.ShapeDtypeStruct((groups, rows // 2, chans // 2), f32)
     return small_call(
-        functools.partial(project_kernel, blocks, base is not None, last),
+        functools.partial(project_kernel, ways, base is not None, last),
         [half, half] if last else total,
         [w] + list(acts) + ([] if base is None else [base]),
         "project",
-        2 * len(acts) * groups * width * chans * toks,
+        2 * len(acts) * groups * width * chans * rows,
         [pltpu.VMEM(total.shape, f32)] if last else [],
         16,
     )
@@ -351,13 +360,13 @@
     grad_ext,
 ):
     groups, toks, chans = keep_ref.shape
+    half = toks // 2
     modes = rates_ref.shape[0]
     short = taps_ref.shape[1]
     rim = short - 1
     length = toks // CHUNKS
     lanes = flat.shape[-1]
     wide = (CHUNKS, lanes)
-    half = toks // 2
     _, _, _, core = here()
 
     def row(array, at):
@@ -370,7 +379,7 @@
         other_rows = pl.ds(pl.multiple_of((1 - core) * half, half), half)
 
         for g in range(groups):
-            flat[g] = (keep_ref[g, :, some] + other_ref[g, :, some].astype(f32)).astype(bf16).astype(f32)
+            flat[g] = (keep_ref[g, :, some] + other_ref[g, :, some]).astype(bf16).astype(f32)
         flat_cot[own_rows] = cot_own_ref[:, whole].astype(f32)
         flat_cot[other_rows] = cot_other_ref[:, some].astype(f32)
 
@@ -494,78 +503,100 @@
     )
 
 
-def back_kernel(blocks, w_ref, own_ref, other_ref, *out_refs):
+def back_kernel(outs, w_ref, own_ref, other_ref, *out_refs):
     groups, half, _ = own_ref.shape
-    width = out_refs[0].shape[0]
-    _, _, _, core = here()
+    core = here()[3]
     own_at = pl.multiple_of(core * half, half)
     other_at = pl.multiple_of((1 - core) * half, half)
-    for block, out in zip(blocks, out_refs):
-        start = pl.multiple_of(block_at(*block) * width, width)
-        total = None
-        for g in range(groups):
-            for ref, at in ((own_ref, own_at), (other_ref, other_at)):
-                term = jnp.dot(
-                    w_ref[g, pl.ds(start, width), pl.ds(at, half)],
-                    ref[g],
-                    preferred_element_type=f32,
-                )
-                total = term if total is None else total + term
-        out[...] = total.astype(out.dtype)
-
-
-def back_project(blocks, dtypes, w, own, other, width):
+    for blocks, out in zip(outs, out_refs):
+        width = out.shape[0] // len(blocks)
+        for n, block in enumerate(blocks):
+            start = pl.multiple_of(block_at(*block) * width, width)
+            total = None
+            for g in range(groups):
+                for ref, at in ((own_ref, own_at), (other_ref, other_at)):
+                    term = jnp.dot(
+                        w_ref[g, pl.ds(start, width), pl.ds(at, half)],
+                        ref[g],
+                        preferred_element_type=f32,
+                    )
+                    total = term if total is None else total + term
+            out[n * width : (n + 1) * width] = total.astype(out.dtype)
+
+
+def back_project(outs, dtypes, w, own, other, width):
     groups, half, toks = own.shape
     return small_call(
-        functools.partial(back_kernel, blocks),
-        [jax.ShapeDtypeStruct((width, toks), dtype) for dtype in dtypes],
+        functools.partial(back_kernel, outs),
+        [
+            jax.ShapeDtypeStruct((width * len(blocks), toks), dtype)
+            for blocks, dtype in zip(outs, dtypes)
+        ],
         [w, own, other],
         "back_project",
-        4 * len(blocks) * groups * width * half * toks,
+        4 * sum(len(blocks) for blocks in outs) * groups * width * half * toks,
         (),
         16,
     )
 
 
-def merge_kernel(part_ref, got_ref, out_ref):
-    out_ref[...] = (part_ref[...] + got_ref[...].astype(f32)).astype(bf16)
-
-
-def merge(part, got):
-    return small_call(merge_kernel, jax.ShapeDtypeStruct(part.shape, bf16), [part, got], "merge")
-
-
-def column_kernel(slot, own_ref, x_ref, y_ref, total_ref, one_ref, two_ref):
-    half = own_ref.shape[1] // 2
-    total_ref[...] = own_ref[...] + x_ref[...].astype(f32) + y_ref[...].astype(f32)
-    z = here()[0]
-    flag = (z >> 1) if slot == 2 else 1 - (z >> 1)
-    one_ref[...] = total_ref[:, pl.ds(pl.multiple_of(flag * half, half), half)].astype(bf16)
-    two_ref[...] = total_ref[:, pl.ds(pl.multiple_of((1 - flag) * half, half), half)].astype(bf16)
-
-
-def column(slot, own, from_x, from_y):
-    shape = jax.ShapeDtypeStruct((own.shape[0], own.shape[1] // 2), bf16)
+def merge_kernel(two_ref, one_ref, got_ref, two_out, one_out):
+    width = one_ref.shape[0]
+    one_out[...] = (one_ref[...] + got_ref[:width].astype(f32)).astype(bf16)
+    two_out[...] = (two_ref[...] + got_ref[width:].astype(f32)).astype(bf16)
+
+
+def merge(two, one, got):
+    shape = jax.ShapeDtypeStruct(one.shape, bf16)
+    return small_call(merge_kernel, [shape, shape], [two, one, got], "merge")
+
+
+def column_kernel(slot, own_ref, other_ref, first_ref, *out_refs):
+    width, toks = own_ref.shape
+    half = toks // 2
+    total = (
+        own_ref[...]
+        + other_ref[(slot - 1) * width : slot * width].astype(f32)
+        + first_ref[...].astype(f32)
+    )
+    z, _, _, core = here()
+    side = (z >> 1) if slot == 2 else 1 - (z >> 1)
+    low, high = total[:, :half], total[:, half:]
+    send_low, send_high = out_refs[0], out_refs[1]
+
+    @pl.when(side == 0)
+    def _():
+        send_low[...] = low.astype(bf16)
+        send_high[...] = high.astype(bf16)
+
+    @pl.when(side == 1)
+    def _():
+        send_low[...] = high.astype(bf16)
+        send_high[...] = low.astype(bf16)
+
+    if len(out_refs) == 3:
+        inner = is_inner()
+        out_refs[2][...] = jnp.where(inner, jnp.where(core == 0, low, high), 0.0)
+
+
+def column(slot, own, other, first):
+    width, toks = own.shape
+    half = jax.ShapeDtypeStruct((width, toks // 2), bf16)
+    kept = [jax.ShapeDtypeStruct((width, toks // 2), f32)] if slot == 1 else []
     return small_call(
-        functools.partial(column_kernel, slot),
-        [jax.ShapeDtypeStruct(own.shape, f32), shape, shape],
-        [own, from_x, from_y],
-        "column",
+        functools.partial(column_kernel, slot), [half, half] + kept, [own, other, first], "column"
     )
 
 
 def finish_kernel(own_ref, a_ref, b_ref, c_ref, d_ref, out_ref):
-    half = own_ref.shape[1] // 2
-    core = here()[3]
-    mine = own_ref[:, pl.ds(pl.multiple_of(core * half, half), half)]
-    total = jnp.where(is_inner(), mine, 0.0)
+    total = own_ref[...]
     for ref in (a_ref, b_ref, c_ref, d_ref):
         total = total + ref[...].astype(f32)
     out_ref[...] = total.T.astype(bf16)
 
 
 def finish(own, received):
-    shape = jax.ShapeDtypeStruct((own.shape[1] // 2, own.shape[0]), bf16)
+    shape = jax.ShapeDtypeStruct((own.shape[1], own.shape[0]), bf16)
     return small_call(finish_kernel, shape, [own] + received, "finish")
 
 
@@ -587,11 +618,11 @@
     def swap(array):
         return lax.ppermute(array, BOTH, OTHER_CORE)
 
-    def over_x(array):
-        return lax.ppermute(array, BOTH, OVER_X)
-
-    def over_y(array):
-        return lax.ppermute(array, BOTH, OVER_Y)
+    def first_way(array):
+        return lax.ppermute(array, BOTH, FIRST_WAY)
+
+    def other_way(array):
+        return lax.ppermute(array, BOTH, OTHER_WAY)
 
     own_ids = token_ids.reshape(1, -1)
     other_ids = swap(own_ids)
@@ -601,57 +632,39 @@
     )
     own_ids, table = fetch(own_ids, embed)
     embedded = embed_rows(own_ids, other_ids, table)
-
     embedded, cot_other = lax.optimization_barrier((embedded, cot_other))
-    got_1 = lax.ppermute(embedded, BOTH, GATHER_Z[0])
+
+    came = [lax.ppermute(embedded, BOTH, pairs) for pairs in GATHER_Z]
     w = load(jnp.transpose(w_in, (1, 0, 2)))
-    got_1, w = lax.optimization_barrier((got_1, w))
-    slot_1 = choose(embedded, got_1)
-    x_1, y_1 = over_x(slot_1), over_y(slot_1)
-    got_2 = lax.ppermute(got_1, BOTH, GATHER_Z[1])
-    slot_2 = choose(got_1, got_2)
-    x_2, y_2 = over_x(slot_2), over_y(slot_2)
-    sums = project([(1, 0, 0), (2, 0, 0)], [slot_1, slot_2], w, None, False)
-    x_1, y_1, sums = lax.optimization_barrier((x_1, y_1, sums))
-    d_1 = over_y(x_1)
-    sums = project([(1, 0, 1), (1, 1, 0)], [x_1, y_1], w, sums, False)
-    x_2, y_2, sums = lax.optimization_barrier((x_2, y_2, sums))
-    d_2 = over_x(y_2)
-    sums = project([(2, 0, 1), (2, 1, 0)], [x_2, y_2], w, sums, False)
-    d_1, d_2, sums = lax.optimization_barrier((d_1, d_2, sums))
-    keep, send = project([(1, 1, 1), (2, 1, 1)], [d_1, d_2], w, sums, True)
-
+    *came, w = lax.optimization_barrier((*came, w))
+    held = slots(embedded, *came)
+    first, other = first_way(held), other_way(held)
+    sums = project([None], [held], w, None, False)
+    first, sums = lax.optimization_barrier((first, sums))
+    both = other_way(first)
+    sums = project([0, 1], [first, other], w, sums, False)
+    keep, send = project([2], [both], w, sums, True)
     mixed_own, mixed_send, grad_own = mixer(
         keep, swap(send), jnp.transpose(taps, (1, 0, 2)), rates, residues, cotangent, cot_other
     )
     grad_other = swap(grad_own)
     mixed_other = swap(mixed_send)
 
-    d_2, d_1 = back_project([(2, 1, 1), (1, 1, 1)], [bf16] * 2, w, grad_own, grad_other, width)
-    d_2, d_1 = over_x(d_2), over_y(d_1)
-    x_2, y_2, x_1, y_1, own_2, own_1 = back_project(
-        [(2, 0, 1), (2, 1, 0), (1, 0, 1), (1, 1, 0), (2, 0, 0), (1, 0, 0)],
-        [bf16, f32, f32, bf16, f32, f32],
-        w,
-        grad_own,
-        grad_other,
-        width,
+    (across,) = back_project([[(1, 2), (2, 2)]], [bf16], w, grad_own, grad_other, width)
+    across = other_way(across)
+    (other,) = back_project([[(1, 1), (2, 1)]], [bf16], w, grad_own, grad_other, width)
+    other = other_way(other)
+    first_2, first_1, own_2, own_1 = back_project(
+        [[(2, 0)], [(1, 0)], [(2, None)], [(1, None)]], [f32] * 4, w, grad_own, grad_other, width
     )
     mixed = pair(mixed_own, mixed_other)
-    x_2, d_2, mixed = lax.optimization_barrier((x_2, d_2, mixed))
-    x_2, y_2 = lax.optimization_barrier((x_2, merge(y_2, d_2)))
-    x_2, y_2 = over_x(x_2), over_y(y_2)
-    x_1, y_1 = over_x(merge(x_1, d_1)), over_y(y_1)
-    _, send_1, send_2 = column(2, own_2, x_2, y_2)
-    received = [
-        lax.ppermute(send_1, BOTH, SCATTER_Z[0]),
-        lax.ppermute(send_2, BOTH, SCATTER_Z[1]),
-    ]
-    own, send_1, send_2 = column(1, own_1, x_1, y_1)
-    received += [
-        lax.ppermute(send_1, BOTH, SCATTER_Z[2]),
-        lax.ppermute(send_2, BOTH, SCATTER_Z[3]),
-    ]
+    across, mixed = lax.optimization_barrier((across, mixed))
+    first_2, first_1 = merge(first_2, first_1, across)
+    first_2, first_1 = first_way(first_2), first_way(first_1)
+    sends = column(2, own_2, other, first_2)
+    received = [lax.ppermute(a, BOTH, pairs) for a, pairs in zip(sends, SCATTER_Z[:2])]
+    *sends, own = column(1, own_1, other, first_1)
+    received += [lax.ppermute(a, BOTH, pairs) for a, pairs in zip(sends, SCATTER_Z[2:])]
     return (mixed, finish(own, received))
 
 

time: 84.3 us -> 88.5 us (1.050)
  starting transfers between devices: 22.1 us -> 25.7 us
  waiting for transfers between devices: 38.4 us -> 39.8 us
    ppermute x5, starting transfers between devices: 2.81 us -> 9.28 us  [swap(): return lax.ppermute(array, BOTH, OTHER_CORE)]
    ppermute x18 -> x13, starting transfers between devices: 19.3 us -> 16.4 us  [the longest x4 5.36 us: other_way(): return lax.ppermute(array, BOTH, OTHER_WAY)]
    ppermute x18 -> x13, waiting for transfers between devices: 33.8 us -> 35.2 us  [the longest x4 20.2 us: other_way(): return lax.ppermute(array, BOTH, OTHER_WAY)]
    pallas_call x16 -> x14, Pallas kernels: 15.4 us -> 14.7 us  [small_call(): pl.pallas_call(kernel, in_specs=[IN_VMEM] * len(operands), out_specs=jax....]
  transfers between devices with their start and end apart: 23 -> 18, of which waited for: 18 -> 11; matrix products, arithmetic and copies ran while one was open for 0% -> 0% of each run, Pallas kernels for 16% -> 14%
where the time goes in v6:
time: 88.5 us; the launch traced here: 87.5 us
  waiting for transfers between devices  39.8 us (45%)
  starting transfers between devices  25.7 us (29%)
  Pallas kernels  20.3 us (23%)
    ppermute x4, waiting for transfers between devices, other_way(): return lax.ppermute(array, BOTH, OTHER_WAY)  20.2 us
    pallas_call x14, Pallas kernels, small_call(): pl.pallas_call(kernel, in_specs=[IN_VMEM] * len(operands), out_specs=jax....  14.7 us
    ppermute x4, waiting for transfers between devices, chip_plan(): lax.ppermute(a, BOTH, pairs)  9.98 us
    ppermute x5, starting transfers between devices, swap(): return lax.ppermute(array, BOTH, OTHER_CORE)  9.28 us
    ppermute x4, starting transfers between devices, other_way(): return lax.ppermute(array, BOTH, OTHER_WAY)  5.36 us
    ppermute x3, waiting for transfers between devices, first_way(): return lax.ppermute(array, BOTH, FIRST_WAY)  4.98 us
    ppermute x5, waiting for transfers between devices, swap(): return lax.ppermute(array, BOTH, OTHER_CORE)  4.63 us
    pallas_call x1, Pallas kernels, load(): pl.pallas_call(load_kernel, in_specs=[pl.BlockSpec(memory_space=pltpu.HBM...  4.58 us
  transfers between devices with their start and end apart: 18, of which 11 were waited for; matrix products, arithmetic and copies ran while one was open for 0% of the time, Pallas kernels for 14%

profile of v6, /device:TPU:0, one launch (start us, length us, event | category | flops | bytes accessed | tf_op | source)
XLA Modules:
  0.0 87.5 jit_solution(11265192362215888888)
XLA Ops:
  2.0 1.1 %fetch.1 = (s32[1,128]{1,0:T(1,128)S(1)}, bf16[512,512]{1,0:T(8,128)(2,1)S(1)}) custom-call(s32[1,128]{1,0:T(1,128)} %bitcast.6, bf16[512,512]{1,0:T(8,128)(2,1)} %table_ref.1), custom_call_target="tpu_custom_call" | custom-call | bytes 1048576 | tf_op jit(solution)/shard_map/fetch/pallas_call | solution.py:238
  4.2 3.0 %collective-permute-start.2 = (bf16[256,512]{1,0:T(8,128)(2,1)S(1)}, bf16[256,512]{1,0:T(8,128)(2,1)S(1)}, u32[]{:S(2)}, u32[]{:S(2)}) collective-permute-start(bf16[256,512]{1,0:T(8,128)(2,1)S(1)} %embed_rows.1.own_ref), channel_id=1, source_target_pairs={{0,8},{2,10},{4,12},{6,14},{8,0},{10,2},{12,4},{14,6},{1,16},{3,18... | collective-permute-start | bytes 786440 | tf_op jit(solution)/shard_map/ppermute | solution.py:637
  7.2 4.6 %load.1.w_ref = bf16[3,4096,512]{2,1,0:T(8,128)(2,1)S(1)} custom-call(bf16[3,4096,512]{2,1,0:T(8,128)(2,1)} %bitcast.4), custom_call_target="tpu_custom_call" | custom-call | bytes 25165824 | tf_op jit(solution)/shard_map/load/pallas_call | solution.py:260
  11.9 1.7 %collective-permute-start.4 = (bf16[512,512]{1,0:T(8,128)(2,1)S(1)}, bf16[512,512]{1,0:T(8,128)(2,1)S(1)}, u32[]{:S(2)}, u32[]{:S(2)}) collective-permute-start(bf16[512,512]{1,0:T(8,128)(2,1)S(1)} %slots.1.refs_0_), channel_id=1, source_target_pairs={{0,2},{1,5},{2,0},{3,7},{4,6},{5,1},{6,4},{7,3},{8,10},{9,13},{10,... | collective-permute-start | bytes 1572872 | tf_op jit(solution)/shard_map/ppermute | solution.py:622
  13.6 1.5 %collective-permute-start.6 = (bf16[512,512]{1,0:T(8,128)(2,1)S(1)}, bf16[512,512]{1,0:T(8,128)(2,1)S(1)}, u32[]{:S(2)}, u32[]{:S(2)}) collective-permute-start(bf16[512,512]{1,0:T(8,128)(2,1)S(1)} %slots.1.refs_0_), channel_id=1, source_target_pairs={{0,4},{1,3},{2,6},{3,1},{4,0},{5,7},{6,2},{7,5},{8,12},{9,11},{10,... | collective-permute-start | bytes 1572872 | tf_op jit(solution)/shard_map/ppermute | solution.py:625
  16.2 5.0 %collective-permute-done.4.refs_0_ = bf16[512,512]{1,0:T(8,128)(2,1)S(1)} collective-permute-done((bf16[512,512]{1,0:T(8,128)(2,1)S(1)}, bf16[512,512]{1,0:T(8,128)(2,1)S(1)}, u32[]{:S(2)}, u32[]{:S(2)}) %collective-permute-start.4) | collective-permute-done | bytes 524320 | tf_op jit(solution)/shard_map/ppermute | solution.py:622
  21.1 1.7 %collective-permute-start.5 = (bf16[512,512]{1,0:T(8,128)(2,1)S(1)}, bf16[512,512]{1,0:T(8,128)(2,1)S(1)}, u32[]{:S(2)}, u32[]{:S(2)}) collective-permute-start(bf16[512,512]{1,0:T(8,128)(2,1)S(1)} %collective-permute-done.4.refs_0_), channel_id=1, source_target_pairs={{0,4},{1,3},{2,6},{3,1},{4,0},{5,7},{6,2},{7,5},{8,12},{9,11},{10,... | collective-permute-start | bytes 1572872 | tf_op jit(solution)/shard_map/ppermute | solution.py:625
  22.8 1.8 %project.4.refs_1_ = f32[3,256,512]{2,1,0:T(8,128)S(1)} custom-call(bf16[3,4096,512]{2,1,0:T(8,128)(2,1)S(1)} %load.1.w_ref, bf16[512,512]{1,0:T(8,128)(2,1)S(1)} %collective-permute-done.4.refs_0_, bf16[512,512]{1,0:T(8,128)(2,1)S(1)} %collective-permute-done.6.refs_1_, f32[3,256,512]{2,1,0:T(8,128)S(1)} %project.3.refs_2_), custom_call_target="tpu_custom_call" | custom-call | flops 25165824 | bytes 237568 | tf_op jit(solution)/shard_map/project/pallas_call | solution.py:160
  24.6 11.1 %collective-permute-done.5.refs_0_ = bf16[512,512]{1,0:T(8,128)(2,1)S(1)} collective-permute-done((bf16[512,512]{1,0:T(8,128)(2,1)S(1)}, bf16[512,512]{1,0:T(8,128)(2,1)S(1)}, u32[]{:S(2)}, u32[]{:S(2)}) %collective-permute-start.5) | collective-permute-done | bytes 524320 | tf_op jit(solution)/shard_map/ppermute | solution.py:625
  35.8 1.3 %project.5 = (f32[3,256,256]{2,1,0:T(8,128)S(1)}, f32[3,256,256]{2,1,0:T(8,128)S(1)}) custom-call(bf16[3,4096,512]{2,1,0:T(8,128)(2,1)S(1)} %load.1.w_ref, bf16[512,512]{1,0:T(8,128)(2,1)S(1)} %collective-permute-done.5.refs_0_, f32[3,256,512]{2,1,0:T(8,128)S(1)} %project.4.refs_1_), custom_call_target="tpu_custom_call" | custom-call | flops 12582912 | bytes 229376 | tf_op jit(solution)/shard_map/project/pallas_call | solution.py:160
  37.0 8.3 %collective-permute-start.7 = (f32[3,256,256]{2,1,0:T(8,128)S(1)}, f32[3,256,256]{2,1,0:T(8,128)S(1)}, u32[]{:S(2)}, u32[]{:S(2)}) collective-permute-start(f32[3,256,256]{2,1,0:T(8,128)S(1)} %get-tuple-element.38), channel_id=1, source_target_pairs={{0,1},{1,0},{2,3},{3,2},{4,5},{5,4},{6,7},{7,6},{8,9},{9,8},{10,11... | collective-permute-start | bytes 2359304 | tf_op jit(solution)/shard_map/ppermute | solution.py:619
  45.4 1.9 %collective-permute-done.7.other_ref = f32[3,256,256]{2,1,0:T(8,128)S(1)} collective-permute-done((f32[3,256,256]{2,1,0:T(8,128)S(1)}, f32[3,256,256]{2,1,0:T(8,128)S(1)}, u32[]{:S(2)}, u32[]{:S(2)}) %collective-permute-start.7) | collective-permute-done | bytes 786464 | tf_op jit(solution)/shard_map/ppermute | solution.py:619
  47.3 4.6 %mixer.1 = (bf16[128,256]{1,0:T(8,128)(2,1)S(1)}, bf16[128,256]{1,0:T(8,128)(2,1)S(1)}, bf16[3,256,256]{2,1,0:T(8,128)(2,1)S(1)}) custom-call(f32[3,256,256]{2,1,0:T(8,128)S(1)} %get-tuple-element.37.keep_ref, f32[3,256,256]{2,1,0:T(8,128)S(1)} %collective-permute-done.7.other_ref, f32[3,7,512]{2,1,0:T(8,128)S(1)} %bitcast.3, f32[16,512]{1,0:T(8,128)S(1)} %copy-done.2, ...), custom_call_target="tpu_custom_call" | custom-call | flops 196608 | bytes 29344 | tf_op jit(solution)/shard_map/mixer/pallas_call | solution.py:160
  52.4 1.3 %collective-permute-done.8.other_ref = bf16[3,256,256]{2,1,0:T(8,128)(2,1)S(1)} collective-permute-done((bf16[3,256,256]{2,1,0:T(8,128)(2,1)S(1)}, bf16[3,256,256]{2,1,0:T(8,128)(2,1)S(1)}, u32[]{:S(2)}, u32[]{:S(2)}) %collective-permute-start.8) | collective-permute-done | bytes 393248 | tf_op jit(solution)/shard_map/ppermute | solution.py:619
  54.7 1.8 %collective-permute-start.9 = (bf16[1024,256]{1,0:T(8,128)(2,1)S(1)}, bf16[1024,256]{1,0:T(8,128)(2,1)S(1)}, u32[]{:S(2)}, u32[]{:S(2)}) collective-permute-start(bf16[1024,256]{1,0:T(8,128)(2,1)S(1)} %back_project.3), channel_id=1, source_target_pairs={{0,4},{1,3},{2,6},{3,1},{4,0},{5,7},{6,2},{7,5},{8,12},{9,11},{10,... | collective-permute-start | bytes 1572872 | tf_op jit(solution)/shard_map/ppermute | solution.py:625
  57.8 1.3 %collective-permute-done.10.other_ref = bf16[128,256]{1,0:T(8,128)(2,1)S(1)} collective-permute-done((bf16[128,256]{1,0:T(8,128)(2,1)S(1)}, bf16[128,256]{1,0:T(8,128)(2,1)S(1)}, u32[]{:S(2)}, u32[]{:S(2)}) %collective-permute-start.10) | collective-permute-done | bytes 65568 | tf_op jit(solution)/shard_map/ppermute | solution.py:619
  59.8 1.8 %back_project.4 = (f32[512,256]{1,0:T(8,128)S(1)}, f32[512,256]{1,0:T(8,128)S(1)}, f32[512,256]{1,0:T(8,128)S(1)}, f32[512,256]{1,0:T(8,128)S(1)}) custom-call(bf16[3,4096,512]{2,1,0:T(8,128)(2,1)S(1)} %load.1.w_ref, bf16[3,256,256]{2,1,0:T(8,128)(2,1)S(1)} %get-tuple-element.40.own_ref, bf16[3,256,256]{2,1,0:T(8,128)(2,1)S(1)} %collective-permute-done.8.other_ref), custom_call_target="tpu_custom_call" | custom-call | flops 25165824 | bytes 208896 | tf_op jit(solution)/shard_map/back_project/pallas_call | solution.py:160
  61.5 2.4 %collective-permute-done.9.got_ref = bf16[1024,256]{1,0:T(8,128)(2,1)S(1)} collective-permute-done((bf16[1024,256]{1,0:T(8,128)(2,1)S(1)}, bf16[1024,256]{1,0:T(8,128)(2,1)S(1)}, u32[]{:S(2)}, u32[]{:S(2)}) %collective-permute-start.9) | collective-permute-done | bytes 524320 | tf_op jit(solution)/shard_map/ppermute | solution.py:625
  64.0 1.8 %collective-permute-start.13 = (bf16[512,256]{1,0:T(8,128)(2,1)S(1)}, bf16[512,256]{1,0:T(8,128)(2,1)S(1)}, u32[]{:S(2)}, u32[]{:S(2)}) collective-permute-start(bf16[512,256]{1,0:T(8,128)(2,1)S(1)} %get-tuple-element.51), channel_id=1, source_target_pairs={{0,2},{1,5},{2,0},{3,7},{4,6},{5,1},{6,4},{7,3},{8,10},{9,13},{10,... | collective-permute-start | bytes 786440 | tf_op jit(solution)/shard_map/ppermute | solution.py:622
  66.1 6.7 %collective-permute-done.11.other_ref = bf16[1024,256]{1,0:T(8,128)(2,1)S(1)} collective-permute-done((bf16[1024,256]{1,0:T(8,128)(2,1)S(1)}, bf16[1024,256]{1,0:T(8,128)(2,1)S(1)}, u32[]{:S(2)}, u32[]{:S(2)}) %collective-permute-start.11) | collective-permute-done | bytes 524320 | tf_op jit(solution)/shard_map/ppermute | solution.py:625
  73.1 2.6 %collective-permute-start.15 = (bf16[512,128]{1,0:T(8,128)(2,1)S(1)}, bf16[512,128]{1,0:T(8,128)(2,1)S(1)}, u32[]{:S(2)}, u32[]{:S(2)}) collective-permute-start(bf16[512,128]{1,0:T(8,128)(2,1)S(1)} %get-tuple-element.53), channel_id=1, source_target_pairs={{0,9},{2,11},{4,13},{6,15},{8,1},{10,3},{12,5},{14,7},{16,8},{18,1... | collective-permute-start | bytes 393224 | tf_op jit(solution)/shard_map/ppermute | solution.py:665
  76.7 2.1 %collective-permute-done.14.a_ref = bf16[512,128]{1,0:T(8,128)(2,1)S(1)} collective-permute-done((bf16[512,128]{1,0:T(8,128)(2,1)S(1)}, bf16[512,128]{1,0:T(8,128)(2,1)S(1)}, u32[]{:S(2)}, u32[]{:S(2)}) %collective-permute-start.14) | collective-permute-done | bytes 131104 | tf_op jit(solution)/shard_map/ppermute | solution.py:665
  78.9 2.9 %collective-permute-done.15.b_ref = bf16[512,128]{1,0:T(8,128)(2,1)S(1)} collective-permute-done((bf16[512,128]{1,0:T(8,128)(2,1)S(1)}, bf16[512,128]{1,0:T(8,128)(2,1)S(1)}, u32[]{:S(2)}, u32[]{:S(2)}) %collective-permute-start.15) | collective-permute-done | bytes 131104 | tf_op jit(solution)/shard_map/ppermute | solution.py:665
  81.8 4.9 %collective-permute-done.16.c_ref = bf16[512,128]{1,0:T(8,128)(2,1)S(1)} collective-permute-done((bf16[512,128]{1,0:T(8,128)(2,1)S(1)}, bf16[512,128]{1,0:T(8,128)(2,1)S(1)}, u32[]{:S(2)}, u32[]{:S(2)}) %collective-permute-start.16) | collective-permute-done | bytes 131104 | tf_op jit(solution)/shard_map/ppermute | solution.py:667
  (37 shorter events, 9.5 us)
Async XLA Ops:
  1.5 2.1 %collective-permute-start.1 = (bf16[128,256]{1,0:T(8,128)(2,1)S(1)}, bf16[128,256]{1,0:T(8,128)(2,1)S(1)}, u32[]{:S(2)}, u32[]{:S(2)}) collective-permute-start(bf16[128,256]{1,0:T(8,128)(2,1)S(1)} %constant_dynamic-slice_fusion), channel_id=1, source_target_pairs={{0,1},{1,0},{2,3},{3,2},{4,5},{5,4},{6,7},{7,6},{8,9},{9,8},{10,11... | collective-permute-start | bytes 196616 | tf_op jit(solution)/shard_map/ppermute | solution.py:619
  1.9 1.3 %collective-permute-start = (s32[1,128]{1,0:T(1,128)}, s32[1,128]{1,0:T(1,128)S(1)}, u32[]{:S(2)}, u32[]{:S(2)}) collective-permute-start(s32[1,128]{1,0:T(1,128)} %bitcast.5), channel_id=1, source_target_pairs={{0,1},{1,0},{2,3},{3,2},{4,5},{5,4},{6,7},{7,6},{8,9},{9,8},{10,11... | collective-permute-start | bytes 1544 | tf_op jit(solution)/shard_map/ppermute | solution.py:619
  3.6 8.3 %collective-permute-start.3 = (bf16[256,512]{1,0:T(8,128)(2,1)S(1)}, bf16[256,512]{1,0:T(8,128)(2,1)S(1)}, u32[]{:S(2)}, u32[]{:S(2)}) collective-permute-start(bf16[256,512]{1,0:T(8,128)(2,1)S(1)} %embed_rows.1.own_ref), channel_id=1, source_target_pairs={{9,16},{11,18},{13,20},{15,22},{1,24},{3,26},{5,28},{7,30},{16,9},... | collective-permute-start | bytes 786440 | tf_op jit(solution)/shard_map/ppermute | solution.py:637
  4.2 7.6 %collective-permute-start.2 = (bf16[256,512]{1,0:T(8,128)(2,1)S(1)}, bf16[256,512]{1,0:T(8,128)(2,1)S(1)}, u32[]{:S(2)}, u32[]{:S(2)}) collective-permute-start(bf16[256,512]{1,0:T(8,128)(2,1)S(1)} %embed_rows.1.own_ref), channel_id=1, source_target_pairs={{0,8},{2,10},{4,12},{6,14},{8,0},{10,2},{12,4},{14,6},{1,16},{3,18... | collective-permute-start | bytes 786440 | tf_op jit(solution)/shard_map/ppermute | solution.py:637
  11.9 9.2 %collective-permute-start.4 = (bf16[512,512]{1,0:T(8,128)(2,1)S(1)}, bf16[512,512]{1,0:T(8,128)(2,1)S(1)}, u32[]{:S(2)}, u32[]{:S(2)}) collective-permute-start(bf16[512,512]{1,0:T(8,128)(2,1)S(1)} %slots.1.refs_0_), channel_id=1, source_target_pairs={{0,2},{1,5},{2,0},{3,7},{4,6},{5,1},{6,4},{7,3},{8,10},{9,13},{10,... | collective-permute-start | bytes 1572872 | tf_op jit(solution)/shard_map/ppermute | solution.py:622
  13.6 9.2 %collective-permute-start.6 = (bf16[512,512]{1,0:T(8,128)(2,1)S(1)}, bf16[512,512]{1,0:T(8,128)(2,1)S(1)}, u32[]{:S(2)}, u32[]{:S(2)}) collective-permute-start(bf16[512,512]{1,0:T(8,128)(2,1)S(1)} %slots.1.refs_0_), channel_id=1, source_target_pairs={{0,4},{1,3},{2,6},{3,1},{4,0},{5,7},{6,2},{7,5},{8,12},{9,11},{10,... | collective-permute-start | bytes 1572872 | tf_op jit(solution)/shard_map/ppermute | solution.py:625
  16.1 31.2 %copy-start = (bf16[128,512]{1,0:T(8,128)(2,1)S(1)}, bf16[128,512]{1,0:T(8,128)(2,1)}, u32[]{:S(2)}) copy-start(bf16[128,512]{1,0:T(8,128)(2,1)} %cot_own_ref.1) | copy-start | bytes 393220
  16.1 31.1 %copy-start.1 = (f32[7,3,512]{2,0,1:T(8,128)S(1)}, f32[7,3,512]{2,0,1:T(8,128)}, u32[]{:S(2)}) copy-start(f32[7,3,512]{2,0,1:T(8,128)} %param.10) | copy-start | bytes 129028
  16.1 31.1 %copy-start.2 = (f32[16,512]{1,0:T(8,128)S(1)}, f32[16,512]{1,0:T(8,128)}, u32[]{:S(2)}) copy-start(f32[16,512]{1,0:T(8,128)} %rates_ref.1) | copy-start | bytes 98308
  16.2 31.1 %copy-start.3 = (f32[16,512]{1,0:T(8,128)S(1)}, f32[16,512]{1,0:T(8,128)}, u32[]{:S(2)}) copy-start(f32[16,512]{1,0:T(8,128)} %residues_ref.1) | copy-start | bytes 98308
  21.1 14.6 %collective-permute-start.5 = (bf16[512,512]{1,0:T(8,128)(2,1)S(1)}, bf16[512,512]{1,0:T(8,128)(2,1)S(1)}, u32[]{:S(2)}, u32[]{:S(2)}) collective-permute-start(bf16[512,512]{1,0:T(8,128)(2,1)S(1)} %collective-permute-done.4.refs_0_), channel_id=1, source_target_pairs={{0,4},{1,3},{2,6},{3,1},{4,0},{5,7},{6,2},{7,5},{8,12},{9,11},{10,... | collective-permute-start | bytes 1572872 | tf_op jit(solution)/shard_map/ppermute | solution.py:625
  37.0 10.2 %collective-permute-start.7 = (f32[3,256,256]{2,1,0:T(8,128)S(1)}, f32[3,256,256]{2,1,0:T(8,128)S(1)}, u32[]{:S(2)}, u32[]{:S(2)}) collective-permute-start(f32[3,256,256]{2,1,0:T(8,128)S(1)} %get-tuple-element.38), channel_id=1, source_target_pairs={{0,1},{1,0},{2,3},{3,2},{4,5},{5,4},{6,7},{7,6},{8,9},{9,8},{10,11... | collective-permute-start | bytes 2359304 | tf_op jit(solution)/shard_map/ppermute | solution.py:619
  51.9 1.8 %collective-permute-start.8 = (bf16[3,256,256]{2,1,0:T(8,128)(2,1)S(1)}, bf16[3,256,256]{2,1,0:T(8,128)(2,1)S(1)}, u32[]{:S(2)}, u32[]{:S(2)}) collective-permute-start(bf16[3,256,256]{2,1,0:T(8,128)(2,1)S(1)} %get-tuple-element.40.own_ref), channel_id=1, source_target_pairs={{0,1},{1,0},{2,3},{3,2},{4,5},{5,4},{6,7},{7,6},{8,9},{9,8},{10,11... | collective-permute-start | bytes 1179656 | tf_op jit(solution)/shard_map/ppermute | solution.py:619
  54.7 9.2 %collective-permute-start.9 = (bf16[1024,256]{1,0:T(8,128)(2,1)S(1)}, bf16[1024,256]{1,0:T(8,128)(2,1)S(1)}, u32[]{:S(2)}, u32[]{:S(2)}) collective-permute-start(bf16[1024,256]{1,0:T(8,128)(2,1)S(1)} %back_project.3), channel_id=1, source_target_pairs={{0,4},{1,3},{2,6},{3,1},{4,0},{5,7},{6,2},{7,5},{8,12},{9,11},{10,... | collective-permute-start | bytes 1572872 | tf_op jit(solution)/shard_map/ppermute | solution.py:625
  57.5 15.4 %collective-permute-start.11 = (bf16[1024,256]{1,0:T(8,128)(2,1)S(1)}, bf16[1024,256]{1,0:T(8,128)(2,1)S(1)}, u32[]{:S(2)}, u32[]{:S(2)}) collective-permute-start(bf16[1024,256]{1,0:T(8,128)(2,1)S(1)} %back_project.5), channel_id=1, source_target_pairs={{0,4},{1,3},{2,6},{3,1},{4,0},{5,7},{6,2},{7,5},{8,12},{9,11},{10,... | collective-permute-start | bytes 1572872 | tf_op jit(solution)/shard_map/ppermute | solution.py:625
  57.8 1.3 %collective-permute-start.10 = (bf16[128,256]{1,0:T(8,128)(2,1)S(1)}, bf16[128,256]{1,0:T(8,128)(2,1)S(1)}, u32[]{:S(2)}, u32[]{:S(2)}) collective-permute-start(bf16[128,256]{1,0:T(8,128)(2,1)S(1)} %get-tuple-element.42), channel_id=1, source_target_pairs={{0,1},{1,0},{2,3},{3,2},{4,5},{5,4},{6,7},{7,6},{8,9},{9,8},{10,11... | collective-permute-start | bytes 196616 | tf_op jit(solution)/shard_map/ppermute | solution.py:619
  64.0 8.8 %collective-permute-start.13 = (bf16[512,256]{1,0:T(8,128)(2,1)S(1)}, bf16[512,256]{1,0:T(8,128)(2,1)S(1)}, u32[]{:S(2)}, u32[]{:S(2)}) collective-permute-start(bf16[512,256]{1,0:T(8,128)(2,1)S(1)} %get-tuple-element.51), channel_id=1, source_target_pairs={{0,2},{1,5},{2,0},{3,7},{4,6},{5,1},{6,4},{7,3},{8,10},{9,13},{10,... | collective-permute-start | bytes 786440 | tf_op jit(solution)/shard_map/ppermute | solution.py:622
  65.8 9.8 %collective-permute-start.12 = (bf16[512,256]{1,0:T(8,128)(2,1)S(1)}, bf16[512,256]{1,0:T(8,128)(2,1)S(1)}, u32[]{:S(2)}, u32[]{:S(2)}) collective-permute-start(bf16[512,256]{1,0:T(8,128)(2,1)S(1)} %get-tuple-element.48), channel_id=1, source_target_pairs={{0,2},{1,5},{2,0},{3,7},{4,6},{5,1},{6,4},{7,3},{8,10},{9,13},{10,... | collective-permute-start | bytes 786440 | tf_op jit(solution)/shard_map/ppermute | solution.py:622
  73.0 5.9 %collective-permute-start.14 = (bf16[512,128]{1,0:T(8,128)(2,1)S(1)}, bf16[512,128]{1,0:T(8,128)(2,1)S(1)}, u32[]{:S(2)}, u32[]{:S(2)}) collective-permute-start(bf16[512,128]{1,0:T(8,128)(2,1)S(1)} %get-tuple-element.52), channel_id=1, source_target_pairs={{0,8},{2,10},{4,12},{6,14},{8,0},{10,2},{12,4},{14,6},{16,9},{18,1... | collective-permute-start | bytes 393224 | tf_op jit(solution)/shard_map/ppermute | solution.py:665
  73.1 8.7 %collective-permute-start.15 = (bf16[512,128]{1,0:T(8,128)(2,1)S(1)}, bf16[512,128]{1,0:T(8,128)(2,1)S(1)}, u32[]{:S(2)}, u32[]{:S(2)}) collective-permute-start(bf16[512,128]{1,0:T(8,128)(2,1)S(1)} %get-tuple-element.53), channel_id=1, source_target_pairs={{0,9},{2,11},{4,13},{6,15},{8,1},{10,3},{12,5},{14,7},{16,8},{18,1... | collective-permute-start | bytes 393224 | tf_op jit(solution)/shard_map/ppermute | solution.py:665
  75.8 10.9 %collective-permute-start.16 = (bf16[512,128]{1,0:T(8,128)(2,1)S(1)}, bf16[512,128]{1,0:T(8,128)(2,1)S(1)}, u32[]{:S(2)}, u32[]{:S(2)}) collective-permute-start(bf16[512,128]{1,0:T(8,128)(2,1)S(1)} %get-tuple-element.54), channel_id=1, source_target_pairs={{0,1},{2,3},{4,5},{6,7},{8,9},{10,11},{12,13},{14,15},{16,0},{18,2... | collective-permute-start | bytes 393224 | tf_op jit(solution)/shard_map/ppermute | solution.py:667
  76.1 10.6 %collective-permute-start.17 = (bf16[512,128]{1,0:T(8,128)(2,1)S(1)}, bf16[512,128]{1,0:T(8,128)(2,1)S(1)}, u32[]{:S(2)}, u32[]{:S(2)}) collective-permute-start(bf16[512,128]{1,0:T(8,128)(2,1)S(1)} %get-tuple-element.55), channel_id=1, source_target_pairs={{16,1},{18,3},{20,5},{22,7},{24,9},{26,11},{28,13},{30,15},{9,24},... | collective-permute-start | bytes 393224 | tf_op jit(solution)/shard_map/ppermute | solution.py:667

commit v7 on v6

--- a/solution.py
+++ b/solution.py
@@ -141,10 +141,24 @@
 
 FIRST_WAY = everywhere(lambda z, y, x, core: (z, y, 1 - x, core) if core == 0 else (z, 1 - y, x, core))
 OTHER_WAY = everywhere(lambda z, y, x, core: (z, 1 - y, x, core) if core == 0 else (z, y, 1 - x, core))
-GATHER_Z = (
-    along_z([((0, 0), (1, 0)), ((1, 0), (0, 0)), ((0, 1), (2, 0)), ((1, 1), (3, 0))]),
-    along_z([((1, 1), (2, 0)), ((0, 1), (3, 0))]),
-)
+def some_move(move, inner):
+    def target(z, y, x, core):
+        return move(z, y, x, core) if (core == z >> 1) == inner else (z, y, x, core)
+
+    return everywhere(target)
+
+
+INNER_Y = some_move(lambda z, y, x, core: (z, 1 - y, x, core), True)
+INNER_XY = some_move(lambda z, y, x, core: (z, 1 - y, 1 - x, core), True)
+OUTER_X = some_move(lambda z, y, x, core: (z, y, 1 - x, core), False)
+OUTER_Y = some_move(lambda z, y, x, core: (z, 1 - y, x, core), False)
+OUTER_XY = some_move(lambda z, y, x, core: (z, 1 - y, 1 - x, core), False)
+GATHER_Z = along_z([((0, 0), (1, 0)), ((1, 0), (0, 0)), ((0, 1), (2, 0)), ((1, 1), (3, 0))])
+OUTER_Z_INNER_X = along_z([((1, 1), (2, 0)), ((0, 1), (3, 0))]) + [
+    pair
+    for pair in everywhere(lambda z, y, x, core: (z, y, 1 - x, core))
+    if (pair[0] & 1) == pair[0] >> 4
+]
 SCATTER_Z = (
     along_z([((0, 0), (1, 0)), ((1, 0), (0, 0)), ((2, 0), (1, 1)), ((3, 0), (0, 1))]),
     along_z([((0, 0), (1, 1)), ((1, 0), (0, 1)), ((2, 0), (1, 0)), ((3, 0), (0, 0))]),
@@ -184,10 +198,9 @@
 def block_at(slot, way):
     z, y, x, core = here()
     along = (z & 1) if slot == 1 else 1 - (z & 1)
-    if way is not None:
-        far_y, far_x = ((core, 1 - core), (1 - core, core), (1, 1))[way]
-        y, x = y ^ far_y, x ^ far_x
-    return along * 4 + y * 2 + x
+    far = {None: (0, 0), 0: (core, 1 - core), 1: (1 - core, core), 2: (1, 1), "x": (0, 1), "y": (1, 0)}
+    far_y, far_x = far[way]
+    return along * 4 + (y ^ far_y) * 2 + (x ^ far_x)
 
 
 def embed_kernel(own_ref, other_ref, table_ref, out_ref):
@@ -272,62 +285,47 @@
     return in_vmem(out)
 
 
-def slots_kernel(own_ref, one_ref, two_ref, out_ref):
-    rows = own_ref.shape[0]
-
-    @pl.when(is_inner())
-    def _():
-        out_ref[:rows] = own_ref[...]
-        out_ref[rows:] = one_ref[...]
-
-    @pl.when(jnp.logical_not(is_inner()))
-    def _():
-        out_ref[:rows] = one_ref[...]
-        out_ref[rows:] = two_ref[...]
-
-
-def slots(own, one, two):
-    shape = jax.ShapeDtypeStruct((2 * own.shape[0], own.shape[1]), own.dtype)
-    return small_call(slots_kernel, shape, [own, one, two], "slots")
-
-
-def project_kernel(ways, has_base, last, w_ref, *refs):
-    count = len(ways)
+def project_kernel(inner, outer, count, has_base, last, w_ref, *refs):
     acts = refs[:count]
     groups, _, chans = w_ref.shape
-    rows, width = acts[0].shape
-    rows //= 2
-    total_ref = refs[-1]
-    parts = []
-    for way, act in zip(ways, acts):
-        for slot in (1, 2):
-            start = pl.multiple_of(block_at(slot, way) * width, width)
-            parts.append((act, pl.ds((slot - 1) * rows, rows), pl.ds(start, width)))
-    for g in range(groups):
-        total = refs[count][g] if has_base else None
-        for act, span, block in parts:
-            term = jnp.dot(act[span, :], w_ref[g, block, :], preferred_element_type=f32)
-            total = term if total is None else total + term
-        total_ref[g] = total
+    width = acts[0].shape[1]
     if last:
-        keep_ref, send_ref = refs[-3:-1]
+        keep_ref, send_ref, total_ref = refs[-3:]
+    else:
+        total_ref = refs[-1]
+
+    def add(entries):
+        spans = [
+            pl.ds(pl.multiple_of(block_at(slot, way) * width, width), width)
+            for _, slot, way in entries
+        ]
+        for g in range(groups):
+            total = refs[count][g] if has_base else None
+            for (which, _, _), span in zip(entries, spans):
+                term = jnp.dot(acts[which][...], w_ref[g, span, :], preferred_element_type=f32)
+                total = term if total is None else total + term
+            total_ref[g] = total
+
+    pl.when(is_inner())(lambda: add(inner))
+    pl.when(jnp.logical_not(is_inner()))(lambda: add(outer))
+    if last:
         half = chans // 2
         core = here()[3]
         keep_ref[...] = total_ref[:, :, pl.ds(pl.multiple_of(core * half, half), half)]
         send_ref[...] = total_ref[:, :, pl.ds(pl.multiple_of((1 - core) * half, half), half)]
 
 
-def project(ways, acts, w, base, last):
+def project(acts, inner, outer, w, base, last):
     groups, _, chans = w.shape
-    rows, width = acts[0].shape
-    total = jax.ShapeDtypeStruct((groups, rows // 2, chans), f32)
-    half = jax.ShapeDtypeStruct((groups, rows // 2, chans // 2), f32)
+    toks, width = acts[0].shape
+    total = jax.ShapeDtypeStruct((groups, toks, chans), f32)
+    half = jax.ShapeDtypeStruct((groups, toks, chans // 2), f32)
     return small_call(
-        functools.partial(project_kernel, ways, base is not None, last),
+        functools.partial(project_kernel, inner, outer, len(acts), base is not None, last),
         [half, half] if last else total,
         [w] + list(acts) + ([] if base is None else [base]),
         "project",
-        2 * len(acts) * groups * width * chans * rows,
+        2 * max(len(inner), len(outer)) * groups * width * chans * toks,
         [pltpu.VMEM(total.shape, f32)] if last else [],
         16,
     )
@@ -381,7 +379,7 @@
         for g in range(groups):
             flat[g] = (keep_ref[g, :, some] + other_ref[g, :, some]).astype(bf16).astype(f32)
         flat_cot[own_rows] = cot_own_ref[:, whole].astype(f32)
-        flat_cot[other_rows] = cot_other_ref[:, some].astype(f32)
+        flat_cot[other_rows] = cot_other_ref[:, whole].astype(f32)
 
         for g in range(groups):
             for k in range(length):
@@ -626,24 +624,43 @@
 
     own_ids = token_ids.reshape(1, -1)
     other_ids = swap(own_ids)
-    cot_half = cotangent.shape[1] // 2
-    cot_other = swap(
-        lax.dynamic_slice_in_dim(cotangent, (1 - lax.axis_index("ctx")) * cot_half, cot_half, 1)
-    )
+    cot_other = swap(cotangent)
     own_ids, table = fetch(own_ids, embed)
     embedded = embed_rows(own_ids, other_ids, table)
     embedded, cot_other = lax.optimization_barrier((embedded, cot_other))
 
-    came = [lax.ppermute(embedded, BOTH, pairs) for pairs in GATHER_Z]
+    came = lax.ppermute(embedded, BOTH, GATHER_Z)
+    more = lax.ppermute(embedded, BOTH, OUTER_Z_INNER_X)
+    near_y = lax.ppermute(embedded, BOTH, INNER_Y)
+    near_d = lax.ppermute(embedded, BOTH, INNER_XY)
     w = load(jnp.transpose(w_in, (1, 0, 2)))
-    *came, w = lax.optimization_barrier((*came, w))
-    held = slots(embedded, *came)
-    first, other = first_way(held), other_way(held)
-    sums = project([None], [held], w, None, False)
-    first, sums = lax.optimization_barrier((first, sums))
+    came, w = lax.optimization_barrier((came, w))
+    first, other = first_way(came), other_way(came)
+    x_2 = lax.ppermute(more, BOTH, OUTER_X)
+    y_2 = lax.ppermute(more, BOTH, OUTER_Y)
+    d_2 = lax.ppermute(more, BOTH, OUTER_XY)
+    sums = project(
+        [embedded, more, near_y, near_d, came],
+        [(0, 1, None), (1, 1, "x"), (2, 1, "y"), (3, 1, 2), (4, 2, None)],
+        [(4, 1, None), (1, 2, None)],
+        w,
+        None,
+        False,
+    )
+    first, other, sums = lax.optimization_barrier((first, other, sums))
     both = other_way(first)
-    sums = project([0, 1], [first, other], w, sums, False)
-    keep, send = project([2], [both], w, sums, True)
+    sums = project(
+        [first, other], [(0, 2, 0), (1, 2, 1)], [(0, 1, 0), (1, 1, 1)], w, sums, False
+    )
+    both, x_2, y_2, d_2, sums = lax.optimization_barrier((both, x_2, y_2, d_2, sums))
+    keep, send = project(
+        [both, x_2, y_2, d_2],
+        [(0, 2, 2)],
+        [(0, 1, 2), (1, 2, "x"), (2, 2, "y"), (3, 2, 2)],
+        w,
+        sums,
+        True,
+    )
     mixed_own, mixed_send, grad_own = mixer(
         keep, swap(send), jnp.transpose(taps, (1, 0, 2)), rates, residues, cotangent, cot_other
     )

time: 88.5 us -> 82.1 us (0.928)
  waiting for transfers between devices: 39.8 us -> 33.7 us
    ppermute x2 -> x7, starting transfers between devices: 3.66 us -> 12.3 us  [the longest x1 3.42 us: chip_plan(): near_y = lax.ppermute(embedded, BOTH, INNER_Y)]
    ppermute x5, starting transfers between devices: 9.28 us -> 0.87 us  [swap(): return lax.ppermute(array, BOTH, OTHER_CORE)]
    ppermute x3, waiting for transfers between devices: 4.98 us -> 0.01 us  [first_way(): return lax.ppermute(array, BOTH, FIRST_WAY)]
    ppermute x4, starting transfers between devices: 3.58 us -> 4.83 us  [chip_plan(): lax.ppermute(a, BOTH, pairs)]
    ppermute x4, waiting for transfers between devices: 20.2 us -> 19.3 us  [other_way(): return lax.ppermute(array, BOTH, OTHER_WAY)]
    pallas_call x14 -> x13, Pallas kernels: 14.7 us -> 14.4 us  [small_call(): pl.pallas_call(kernel, in_specs=[IN_VMEM] * len(operands), out_specs=jax....]
  transfers between devices with their start and end apart: 18 -> 23, of which waited for: 11 -> 10; matrix products, arithmetic and copies ran while one was open for 0% -> 0% of each run, Pallas kernels for 14% -> 16%
where the time goes in v7:
time: 82.1 us; the launch traced here: 81.1 us
  waiting for transfers between devices  33.7 us (41%)
  starting transfers between devices  26.3 us (32%)
  Pallas kernels  20.1 us (24%)
  between operations  0.9 us (1%)
    ppermute x4, waiting for transfers between devices, other_way(): return lax.ppermute(array, BOTH, OTHER_WAY)  19.3 us
    pallas_call x13, Pallas kernels, small_call(): pl.pallas_call(kernel, in_specs=[IN_VMEM] * len(operands), out_specs=jax....  14.4 us
    ppermute x4, waiting for transfers between devices, chip_plan(): lax.ppermute(a, BOTH, pairs)  9.25 us
    ppermute x5, waiting for transfers between devices, swap(): return lax.ppermute(array, BOTH, OTHER_CORE)  5.21 us
    ppermute x4, starting transfers between devices, chip_plan(): lax.ppermute(a, BOTH, pairs)  4.83 us
    ppermute x4, starting transfers between devices, other_way(): return lax.ppermute(array, BOTH, OTHER_WAY)  4.69 us
    pallas_call x1, Pallas kernels, load(): pl.pallas_call(load_kernel, in_specs=[pl.BlockSpec(memory_space=pltpu.HBM...  4.59 us
    ppermute x3, starting transfers between devices, first_way(): return lax.ppermute(array, BOTH, FIRST_WAY)  3.65 us
  transfers between devices with their start and end apart: 23, of which 10 were waited for; matrix products, arithmetic and copies ran while one was open for 0% of the time, Pallas kernels for 16%

profile of v7, /device:TPU:0, one launch (start us, length us, event | category | flops | bytes accessed | tf_op | source)
XLA Modules:
  0.0 81.1 jit_solution(10810558301121316620)
XLA Ops:
  1.2 1.1 %fetch.1 = (s32[1,128]{1,0:T(1,128)S(1)}, bf16[512,512]{1,0:T(8,128)(2,1)S(1)}) custom-call(s32[1,128]{1,0:T(1,128)} %bitcast.6, bf16[512,512]{1,0:T(8,128)(2,1)} %table_ref.1), custom_call_target="tpu_custom_call" | custom-call | bytes 1048576 | tf_op jit(solution)/shard_map/fetch/pallas_call | solution.py:251
  2.8 3.0 %collective-permute-start.2 = (bf16[256,512]{1,0:T(8,128)(2,1)S(1)}, bf16[256,512]{1,0:T(8,128)(2,1)S(1)}, u32[]{:S(2)}, u32[]{:S(2)}) collective-permute-start(bf16[256,512]{1,0:T(8,128)(2,1)S(1)} %embed_rows.1.refs_0_), channel_id=1, source_target_pairs={{0,8},{2,10},{4,12},{6,14},{8,0},{10,2},{12,4},{14,6},{1,16},{3,18... | collective-permute-start | bytes 786440 | tf_op jit(solution)/shard_map/ppermute | solution.py:632
  5.7 1.5 %collective-permute-start.5 = (bf16[256,512]{1,0:T(8,128)(2,1)S(1)}, bf16[256,512]{1,0:T(8,128)(2,1)S(1)}, u32[]{:S(2)}, u32[]{:S(2)}) collective-permute-start(bf16[256,512]{1,0:T(8,128)(2,1)S(1)} %embed_rows.1.refs_0_), channel_id=1, source_target_pairs={{9,16},{11,18},{13,20},{15,22},{1,24},{3,26},{5,28},{7,30},{16,9},... | collective-permute-start | bytes 786440 | tf_op jit(solution)/shard_map/ppermute | solution.py:633
  7.2 3.4 %collective-permute-start.6 = (bf16[256,512]{1,0:T(8,128)(2,1)S(1)}, bf16[256,512]{1,0:T(8,128)(2,1)S(1)}, u32[]{:S(2)}, u32[]{:S(2)}) collective-permute-start(bf16[256,512]{1,0:T(8,128)(2,1)S(1)} %embed_rows.1.refs_0_), channel_id=1, source_target_pairs={{0,4},{1,1},{2,6},{3,3},{4,0},{5,5},{6,2},{7,7},{8,12},{9,9},{10,1... | collective-permute-start | bytes 786440 | tf_op jit(solution)/shard_map/ppermute | solution.py:634
  10.7 2.4 %collective-permute-start.7 = (bf16[256,512]{1,0:T(8,128)(2,1)S(1)}, bf16[256,512]{1,0:T(8,128)(2,1)S(1)}, u32[]{:S(2)}, u32[]{:S(2)}) collective-permute-start(bf16[256,512]{1,0:T(8,128)(2,1)S(1)} %embed_rows.1.refs_0_), channel_id=1, source_target_pairs={{0,6},{1,1},{2,4},{3,3},{4,2},{5,5},{6,0},{7,7},{8,14},{9,9},{10,1... | collective-permute-start | bytes 786440 | tf_op jit(solution)/shard_map/ppermute | solution.py:635
  13.1 4.6 %load.1.w_ref = bf16[3,4096,512]{2,1,0:T(8,128)(2,1)S(1)} custom-call(bf16[3,4096,512]{2,1,0:T(8,128)(2,1)} %bitcast.4), custom_call_target="tpu_custom_call" | custom-call | bytes 25165824 | tf_op jit(solution)/shard_map/load/pallas_call | solution.py:273
  17.7 1.6 %collective-permute-start.3 = (bf16[256,512]{1,0:T(8,128)(2,1)S(1)}, bf16[256,512]{1,0:T(8,128)(2,1)S(1)}, u32[]{:S(2)}, u32[]{:S(2)}) collective-permute-start(bf16[256,512]{1,0:T(8,128)(2,1)S(1)} %collective-permute-done.2.refs_4_), channel_id=1, source_target_pairs={{0,2},{1,5},{2,0},{3,7},{4,6},{5,1},{6,4},{7,3},{8,10},{9,13},{10,... | collective-permute-start | bytes 786440 | tf_op jit(solution)/shard_map/ppermute | solution.py:620
  19.2 1.5 %collective-permute-start.4 = (bf16[256,512]{1,0:T(8,128)(2,1)S(1)}, bf16[256,512]{1,0:T(8,128)(2,1)S(1)}, u32[]{:S(2)}, u32[]{:S(2)}) collective-permute-start(bf16[256,512]{1,0:T(8,128)(2,1)S(1)} %collective-permute-done.2.refs_4_), channel_id=1, source_target_pairs={{0,4},{1,3},{2,6},{3,1},{4,0},{5,7},{6,2},{7,5},{8,12},{9,11},{10,... | collective-permute-start | bytes 786440 | tf_op jit(solution)/shard_map/ppermute | solution.py:623
  22.8 2.2 %project.3.refs_2_ = f32[3,256,512]{2,1,0:T(8,128)S(1)} custom-call(bf16[3,4096,512]{2,1,0:T(8,128)(2,1)S(1)} %load.1.w_ref, bf16[256,512]{1,0:T(8,128)(2,1)S(1)} %embed_rows.1.refs_0_, bf16[256,512]{1,0:T(8,128)(2,1)S(1)} %collective-permute-done.5.refs_1_, bf16[256,512]{1,0:T(8,128)(2,1)S(1)} %collective-permute-done.6.refs_2_, ...), custom_call_target="tpu_custom_call" | custom-call | flops 31457280 | bytes 217088 | tf_op jit(solution)/shard_map/project/pallas_call | solution.py:174
  25.1 5.6 %collective-permute-done.4.refs_1_ = bf16[256,512]{1,0:T(8,128)(2,1)S(1)} collective-permute-done((bf16[256,512]{1,0:T(8,128)(2,1)S(1)}, bf16[256,512]{1,0:T(8,128)(2,1)S(1)}, u32[]{:S(2)}, u32[]{:S(2)}) %collective-permute-start.4) | collective-permute-done | bytes 262176 | tf_op jit(solution)/shard_map/ppermute | solution.py:623
  32.7 4.3 %collective-permute-done.8.refs_0_ = bf16[256,512]{1,0:T(8,128)(2,1)S(1)} collective-permute-done((bf16[256,512]{1,0:T(8,128)(2,1)S(1)}, bf16[256,512]{1,0:T(8,128)(2,1)S(1)}, u32[]{:S(2)}, u32[]{:S(2)}) %collective-permute-start.8) | collective-permute-done | bytes 262176 | tf_op jit(solution)/shard_map/ppermute | solution.py:623
  37.8 2.3 %collective-permute-done.12.other_ref = f32[3,256,256]{2,1,0:T(8,128)S(1)} collective-permute-done((f32[3,256,256]{2,1,0:T(8,128)S(1)}, f32[3,256,256]{2,1,0:T(8,128)S(1)}, u32[]{:S(2)}, u32[]{:S(2)}) %collective-permute-start.12) | collective-permute-done | bytes 786464 | tf_op jit(solution)/shard_map/ppermute | solution.py:617
  40.1 4.6 %mixer.1 = (bf16[128,256]{1,0:T(8,128)(2,1)S(1)}, bf16[128,256]{1,0:T(8,128)(2,1)S(1)}, bf16[3,256,256]{2,1,0:T(8,128)(2,1)S(1)}) custom-call(f32[3,256,256]{2,1,0:T(8,128)S(1)} %get-tuple-element.47.keep_ref, f32[3,256,256]{2,1,0:T(8,128)S(1)} %collective-permute-done.12.other_ref, f32[3,7,512]{2,1,0:T(8,128)S(1)} %bitcast.3, f32[16,512]{1,0:T(8,128)S(1)} %copy-done.2, ...), custom_call_target="tpu_custom_call" | custom-call | flops 196608 | bytes 30368 | tf_op jit(solution)/shard_map/mixer/pallas_call | solution.py:174
  44.9 1.6 %collective-permute-done.13.other_ref = bf16[3,256,256]{2,1,0:T(8,128)(2,1)S(1)} collective-permute-done((bf16[3,256,256]{2,1,0:T(8,128)(2,1)S(1)}, bf16[3,256,256]{2,1,0:T(8,128)(2,1)S(1)}, u32[]{:S(2)}, u32[]{:S(2)}) %collective-permute-start.13) | collective-permute-done | bytes 393248 | tf_op jit(solution)/shard_map/ppermute | solution.py:617
  47.5 1.1 %collective-permute-start.14 = (bf16[1024,256]{1,0:T(8,128)(2,1)S(1)}, bf16[1024,256]{1,0:T(8,128)(2,1)S(1)}, u32[]{:S(2)}, u32[]{:S(2)}) collective-permute-start(bf16[1024,256]{1,0:T(8,128)(2,1)S(1)} %back_project.3), channel_id=1, source_target_pairs={{0,4},{1,3},{2,6},{3,1},{4,0},{5,7},{6,2},{7,5},{8,12},{9,11},{10,... | collective-permute-start | bytes 1572872 | tf_op jit(solution)/shard_map/ppermute | solution.py:623
  49.6 1.1 %collective-permute-start.16 = (bf16[1024,256]{1,0:T(8,128)(2,1)S(1)}, bf16[1024,256]{1,0:T(8,128)(2,1)S(1)}, u32[]{:S(2)}, u32[]{:S(2)}) collective-permute-start(bf16[1024,256]{1,0:T(8,128)(2,1)S(1)} %back_project.5), channel_id=1, source_target_pairs={{0,4},{1,3},{2,6},{3,1},{4,0},{5,7},{6,2},{7,5},{8,12},{9,11},{10,... | collective-permute-start | bytes 1572872 | tf_op jit(solution)/shard_map/ppermute | solution.py:623
  50.6 1.3 %collective-permute-done.15.other_ref = bf16[128,256]{1,0:T(8,128)(2,1)S(1)} collective-permute-done((bf16[128,256]{1,0:T(8,128)(2,1)S(1)}, bf16[128,256]{1,0:T(8,128)(2,1)S(1)}, u32[]{:S(2)}, u32[]{:S(2)}) %collective-permute-start.15) | collective-permute-done | bytes 65568 | tf_op jit(solution)/shard_map/ppermute | solution.py:617
  52.6 1.8 %back_project.4 = (f32[512,256]{1,0:T(8,128)S(1)}, f32[512,256]{1,0:T(8,128)S(1)}, f32[512,256]{1,0:T(8,128)S(1)}, f32[512,256]{1,0:T(8,128)S(1)}) custom-call(bf16[3,4096,512]{2,1,0:T(8,128)(2,1)S(1)} %load.1.w_ref, bf16[3,256,256]{2,1,0:T(8,128)(2,1)S(1)} %get-tuple-element.50.own_ref, bf16[3,256,256]{2,1,0:T(8,128)(2,1)S(1)} %collective-permute-done.13.other_ref), custom_call_target="tpu_custom_call" | custom-call | flops 25165824 | bytes 208896 | tf_op jit(solution)/shard_map/back_project/pallas_call | solution.py:174
  54.3 2.4 %collective-permute-done.14.got_ref = bf16[1024,256]{1,0:T(8,128)(2,1)S(1)} collective-permute-done((bf16[1024,256]{1,0:T(8,128)(2,1)S(1)}, bf16[1024,256]{1,0:T(8,128)(2,1)S(1)}, u32[]{:S(2)}, u32[]{:S(2)}) %collective-permute-start.14) | collective-permute-done | bytes 524320 | tf_op jit(solution)/shard_map/ppermute | solution.py:623
  56.8 1.1 %collective-permute-start.18 = (bf16[512,256]{1,0:T(8,128)(2,1)S(1)}, bf16[512,256]{1,0:T(8,128)(2,1)S(1)}, u32[]{:S(2)}, u32[]{:S(2)}) collective-permute-start(bf16[512,256]{1,0:T(8,128)(2,1)S(1)} %get-tuple-element.61), channel_id=1, source_target_pairs={{0,2},{1,5},{2,0},{3,7},{4,6},{5,1},{6,4},{7,3},{8,10},{9,13},{10,... | collective-permute-start | bytes 786440 | tf_op jit(solution)/shard_map/ppermute | solution.py:620
  58.9 6.9 %collective-permute-done.16.other_ref = bf16[1024,256]{1,0:T(8,128)(2,1)S(1)} collective-permute-done((bf16[1024,256]{1,0:T(8,128)(2,1)S(1)}, bf16[1024,256]{1,0:T(8,128)(2,1)S(1)}, u32[]{:S(2)}, u32[]{:S(2)}) %collective-permute-start.16) | collective-permute-done | bytes 524320 | tf_op jit(solution)/shard_map/ppermute | solution.py:623
  66.1 3.1 %collective-permute-start.20 = (bf16[512,128]{1,0:T(8,128)(2,1)S(1)}, bf16[512,128]{1,0:T(8,128)(2,1)S(1)}, u32[]{:S(2)}, u32[]{:S(2)}) collective-permute-start(bf16[512,128]{1,0:T(8,128)(2,1)S(1)} %get-tuple-element.63), channel_id=1, source_target_pairs={{0,9},{2,11},{4,13},{6,15},{8,1},{10,3},{12,5},{14,7},{16,8},{18,1... | collective-permute-start | bytes 393224 | tf_op jit(solution)/shard_map/ppermute | solution.py:682
  71.1 4.7 %collective-permute-done.20.b_ref = bf16[512,128]{1,0:T(8,128)(2,1)S(1)} collective-permute-done((bf16[512,128]{1,0:T(8,128)(2,1)S(1)}, bf16[512,128]{1,0:T(8,128)(2,1)S(1)}, u32[]{:S(2)}, u32[]{:S(2)}) %collective-permute-start.20) | collective-permute-done | bytes 131104 | tf_op jit(solution)/shard_map/ppermute | solution.py:682
  75.8 4.5 %collective-permute-done.21.c_ref = bf16[512,128]{1,0:T(8,128)(2,1)S(1)} collective-permute-done((bf16[512,128]{1,0:T(8,128)(2,1)S(1)}, bf16[512,128]{1,0:T(8,128)(2,1)S(1)}, u32[]{:S(2)}, u32[]{:S(2)}) %collective-permute-start.21) | collective-permute-done | bytes 131104 | tf_op jit(solution)/shard_map/ppermute | solution.py:684
  (45 shorter events, 12.6 us)
Async XLA Ops:
  0.6 2.1 %collective-permute-start.1 = (bf16[128,512]{1,0:T(8,128)(2,1)}, bf16[128,512]{1,0:T(8,128)(2,1)S(1)}, u32[]{:S(2)}, u32[]{:S(2)}) collective-permute-start(bf16[128,512]{1,0:T(8,128)(2,1)} %cot_own_ref.1), channel_id=1, source_target_pairs={{0,1},{1,0},{2,3},{3,2},{4,5},{5,4},{6,7},{7,6},{8,9},{9,8},{10,11... | collective-permute-start | bytes 393224 | tf_op jit(solution)/shard_map/ppermute | solution.py:617
  1.1 1.3 %collective-permute-start = (s32[1,128]{1,0:T(1,128)}, s32[1,128]{1,0:T(1,128)S(1)}, u32[]{:S(2)}, u32[]{:S(2)}) collective-permute-start(s32[1,128]{1,0:T(1,128)} %bitcast.5), channel_id=1, source_target_pairs={{0,1},{1,0},{2,3},{3,2},{4,5},{5,4},{6,7},{7,6},{8,9},{9,8},{10,11... | collective-permute-start | bytes 1544 | tf_op jit(solution)/shard_map/ppermute | solution.py:617
  2.8 14.9 %collective-permute-start.2 = (bf16[256,512]{1,0:T(8,128)(2,1)S(1)}, bf16[256,512]{1,0:T(8,128)(2,1)S(1)}, u32[]{:S(2)}, u32[]{:S(2)}) collective-permute-start(bf16[256,512]{1,0:T(8,128)(2,1)S(1)} %embed_rows.1.refs_0_), channel_id=1, source_target_pairs={{0,8},{2,10},{4,12},{6,14},{8,0},{10,2},{12,4},{14,6},{1,16},{3,18... | collective-permute-start | bytes 786440 | tf_op jit(solution)/shard_map/ppermute | solution.py:632
  5.7 15.0 %collective-permute-start.5 = (bf16[256,512]{1,0:T(8,128)(2,1)S(1)}, bf16[256,512]{1,0:T(8,128)(2,1)S(1)}, u32[]{:S(2)}, u32[]{:S(2)}) collective-permute-start(bf16[256,512]{1,0:T(8,128)(2,1)S(1)} %embed_rows.1.refs_0_), channel_id=1, source_target_pairs={{9,16},{11,18},{13,20},{15,22},{1,24},{3,26},{5,28},{7,30},{16,9},... | collective-permute-start | bytes 786440 | tf_op jit(solution)/shard_map/ppermute | solution.py:633
  7.2 14.2 %collective-permute-start.6 = (bf16[256,512]{1,0:T(8,128)(2,1)S(1)}, bf16[256,512]{1,0:T(8,128)(2,1)S(1)}, u32[]{:S(2)}, u32[]{:S(2)}) collective-permute-start(bf16[256,512]{1,0:T(8,128)(2,1)S(1)} %embed_rows.1.refs_0_), channel_id=1, source_target_pairs={{0,4},{1,1},{2,6},{3,3},{4,0},{5,5},{6,2},{7,7},{8,12},{9,9},{10,1... | collective-permute-start | bytes 786440 | tf_op jit(solution)/shard_map/ppermute | solution.py:634
  10.7 11.5 %collective-permute-start.7 = (bf16[256,512]{1,0:T(8,128)(2,1)S(1)}, bf16[256,512]{1,0:T(8,128)(2,1)S(1)}, u32[]{:S(2)}, u32[]{:S(2)}) collective-permute-start(bf16[256,512]{1,0:T(8,128)(2,1)S(1)} %embed_rows.1.refs_0_), channel_id=1, source_target_pairs={{0,6},{1,1},{2,4},{3,3},{4,2},{5,5},{6,0},{7,7},{8,14},{9,9},{10,1... | collective-permute-start | bytes 786440 | tf_op jit(solution)/shard_map/ppermute | solution.py:635
  17.7 7.4 %collective-permute-start.3 = (bf16[256,512]{1,0:T(8,128)(2,1)S(1)}, bf16[256,512]{1,0:T(8,128)(2,1)S(1)}, u32[]{:S(2)}, u32[]{:S(2)}) collective-permute-start(bf16[256,512]{1,0:T(8,128)(2,1)S(1)} %collective-permute-done.2.refs_4_), channel_id=1, source_target_pairs={{0,2},{1,5},{2,0},{3,7},{4,6},{5,1},{6,4},{7,3},{8,10},{9,13},{10,... | collective-permute-start | bytes 786440 | tf_op jit(solution)/shard_map/ppermute | solution.py:620
  19.2 11.4 %collective-permute-start.4 = (bf16[256,512]{1,0:T(8,128)(2,1)S(1)}, bf16[256,512]{1,0:T(8,128)(2,1)S(1)}, u32[]{:S(2)}, u32[]{:S(2)}) collective-permute-start(bf16[256,512]{1,0:T(8,128)(2,1)S(1)} %collective-permute-done.2.refs_4_), channel_id=1, source_target_pairs={{0,4},{1,3},{2,6},{3,1},{4,0},{5,7},{6,2},{7,5},{8,12},{9,11},{10,... | collective-permute-start | bytes 786440 | tf_op jit(solution)/shard_map/ppermute | solution.py:623
  20.7 11.9 %collective-permute-start.10 = (bf16[256,512]{1,0:T(8,128)(2,1)S(1)}, bf16[256,512]{1,0:T(8,128)(2,1)S(1)}, u32[]{:S(2)}, u32[]{:S(2)}) collective-permute-start(bf16[256,512]{1,0:T(8,128)(2,1)S(1)} %collective-permute-done.5.refs_1_), channel_id=1, source_target_pairs={{0,0},{1,5},{2,2},{3,7},{4,4},{5,1},{6,6},{7,3},{8,8},{9,13},{10,1... | collective-permute-start | bytes 786440 | tf_op jit(solution)/shard_map/ppermute | solution.py:640
  21.4 11.3 %collective-permute-start.11 = (bf16[256,512]{1,0:T(8,128)(2,1)S(1)}, bf16[256,512]{1,0:T(8,128)(2,1)S(1)}, u32[]{:S(2)}, u32[]{:S(2)}) collective-permute-start(bf16[256,512]{1,0:T(8,128)(2,1)S(1)} %collective-permute-done.5.refs_1_), channel_id=1, source_target_pairs={{0,0},{1,7},{2,2},{3,5},{4,4},{5,3},{6,6},{7,1},{8,8},{9,15},{10,1... | collective-permute-start | bytes 786440 | tf_op jit(solution)/shard_map/ppermute | solution.py:641
  22.1 10.6 %collective-permute-start.9 = (bf16[256,512]{1,0:T(8,128)(2,1)S(1)}, bf16[256,512]{1,0:T(8,128)(2,1)S(1)}, u32[]{:S(2)}, u32[]{:S(2)}) collective-permute-start(bf16[256,512]{1,0:T(8,128)(2,1)S(1)} %collective-permute-done.5.refs_1_), channel_id=1, source_target_pairs={{0,0},{1,3},{2,2},{3,1},{4,4},{5,7},{6,6},{7,5},{8,8},{9,11},{10,1... | collective-permute-start | bytes 786440 | tf_op jit(solution)/shard_map/ppermute | solution.py:639
  25.0 15.1 %copy-start = (bf16[128,512]{1,0:T(8,128)(2,1)S(1)}, bf16[128,512]{1,0:T(8,128)(2,1)}, u32[]{:S(2)}) copy-start(bf16[128,512]{1,0:T(8,128)(2,1)} %cot_own_ref.1) | copy-start | bytes 393220
  30.7 6.4 %collective-permute-start.8 = (bf16[256,512]{1,0:T(8,128)(2,1)S(1)}, bf16[256,512]{1,0:T(8,128)(2,1)S(1)}, u32[]{:S(2)}, u32[]{:S(2)}) collective-permute-start(bf16[256,512]{1,0:T(8,128)(2,1)S(1)} %collective-permute-done.3.refs_0_), channel_id=1, source_target_pairs={{0,4},{1,3},{2,6},{3,1},{4,0},{5,7},{6,2},{7,5},{8,12},{9,11},{10,... | collective-permute-start | bytes 786440 | tf_op jit(solution)/shard_map/ppermute | solution.py:623
  37.7 2.4 %collective-permute-start.12 = (f32[3,256,256]{2,1,0:T(8,128)S(1)}, f32[3,256,256]{2,1,0:T(8,128)S(1)}, u32[]{:S(2)}, u32[]{:S(2)}) collective-permute-start(f32[3,256,256]{2,1,0:T(8,128)S(1)} %get-tuple-element.48), channel_id=1, source_target_pairs={{0,1},{1,0},{2,3},{3,2},{4,5},{5,4},{6,7},{7,6},{8,9},{9,8},{10,11... | collective-permute-start | bytes 2359304 | tf_op jit(solution)/shard_map/ppermute | solution.py:617
  44.7 1.8 %collective-permute-start.13 = (bf16[3,256,256]{2,1,0:T(8,128)(2,1)S(1)}, bf16[3,256,256]{2,1,0:T(8,128)(2,1)S(1)}, u32[]{:S(2)}, u32[]{:S(2)}) collective-permute-start(bf16[3,256,256]{2,1,0:T(8,128)(2,1)S(1)} %get-tuple-element.50.own_ref), channel_id=1, source_target_pairs={{0,1},{1,0},{2,3},{3,2},{4,5},{5,4},{6,7},{7,6},{8,9},{9,8},{10,11... | collective-permute-start | bytes 1179656 | tf_op jit(solution)/shard_map/ppermute | solution.py:617
  47.5 9.2 %collective-permute-start.14 = (bf16[1024,256]{1,0:T(8,128)(2,1)S(1)}, bf16[1024,256]{1,0:T(8,128)(2,1)S(1)}, u32[]{:S(2)}, u32[]{:S(2)}) collective-permute-start(bf16[1024,256]{1,0:T(8,128)(2,1)S(1)} %back_project.3), channel_id=1, source_target_pairs={{0,4},{1,3},{2,6},{3,1},{4,0},{5,7},{6,2},{7,5},{8,12},{9,11},{10,... | collective-permute-start | bytes 1572872 | tf_op jit(solution)/shard_map/ppermute | solution.py:623
  49.6 16.3 %collective-permute-start.16 = (bf16[1024,256]{1,0:T(8,128)(2,1)S(1)}, bf16[1024,256]{1,0:T(8,128)(2,1)S(1)}, u32[]{:S(2)}, u32[]{:S(2)}) collective-permute-start(bf16[1024,256]{1,0:T(8,128)(2,1)S(1)} %back_project.5), channel_id=1, source_target_pairs={{0,4},{1,3},{2,6},{3,1},{4,0},{5,7},{6,2},{7,5},{8,12},{9,11},{10,... | collective-permute-start | bytes 1572872 | tf_op jit(solution)/shard_map/ppermute | solution.py:623
  50.6 1.3 %collective-permute-start.15 = (bf16[128,256]{1,0:T(8,128)(2,1)S(1)}, bf16[128,256]{1,0:T(8,128)(2,1)S(1)}, u32[]{:S(2)}, u32[]{:S(2)}) collective-permute-start(bf16[128,256]{1,0:T(8,128)(2,1)S(1)} %get-tuple-element.52), channel_id=1, source_target_pairs={{0,1},{1,0},{2,3},{3,2},{4,5},{5,4},{6,7},{7,6},{8,9},{9,8},{10,11... | collective-permute-start | bytes 196616 | tf_op jit(solution)/shard_map/ppermute | solution.py:617
  56.8 9.0 %collective-permute-start.18 = (bf16[512,256]{1,0:T(8,128)(2,1)S(1)}, bf16[512,256]{1,0:T(8,128)(2,1)S(1)}, u32[]{:S(2)}, u32[]{:S(2)}) collective-permute-start(bf16[512,256]{1,0:T(8,128)(2,1)S(1)} %get-tuple-element.61), channel_id=1, source_target_pairs={{0,2},{1,5},{2,0},{3,7},{4,6},{5,1},{6,4},{7,3},{8,10},{9,13},{10,... | collective-permute-start | bytes 786440 | tf_op jit(solution)/shard_map/ppermute | solution.py:620
  57.9 11.3 %collective-permute-start.17 = (bf16[512,256]{1,0:T(8,128)(2,1)S(1)}, bf16[512,256]{1,0:T(8,128)(2,1)S(1)}, u32[]{:S(2)}, u32[]{:S(2)}) collective-permute-start(bf16[512,256]{1,0:T(8,128)(2,1)S(1)} %get-tuple-element.58), channel_id=1, source_target_pairs={{0,2},{1,5},{2,0},{3,7},{4,6},{5,1},{6,4},{7,3},{8,10},{9,13},{10,... | collective-permute-start | bytes 786440 | tf_op jit(solution)/shard_map/ppermute | solution.py:620
  66.0 5.0 %collective-permute-start.19 = (bf16[512,128]{1,0:T(8,128)(2,1)S(1)}, bf16[512,128]{1,0:T(8,128)(2,1)S(1)}, u32[]{:S(2)}, u32[]{:S(2)}) collective-permute-start(bf16[512,128]{1,0:T(8,128)(2,1)S(1)} %get-tuple-element.62), channel_id=1, source_target_pairs={{0,8},{2,10},{4,12},{6,14},{8,0},{10,2},{12,4},{14,6},{16,9},{18,1... | collective-permute-start | bytes 393224 | tf_op jit(solution)/shard_map/ppermute | solution.py:682
  66.1 9.7 %collective-permute-start.20 = (bf16[512,128]{1,0:T(8,128)(2,1)S(1)}, bf16[512,128]{1,0:T(8,128)(2,1)S(1)}, u32[]{:S(2)}, u32[]{:S(2)}) collective-permute-start(bf16[512,128]{1,0:T(8,128)(2,1)S(1)} %get-tuple-element.63), channel_id=1, source_target_pairs={{0,9},{2,11},{4,13},{6,15},{8,1},{10,3},{12,5},{14,7},{16,8},{18,1... | collective-permute-start | bytes 393224 | tf_op jit(solution)/shard_map/ppermute | solution.py:682
  69.4 10.9 %collective-permute-start.21 = (bf16[512,128]{1,0:T(8,128)(2,1)S(1)}, bf16[512,128]{1,0:T(8,128)(2,1)S(1)}, u32[]{:S(2)}, u32[]{:S(2)}) collective-permute-start(bf16[512,128]{1,0:T(8,128)(2,1)S(1)} %get-tuple-element.64), channel_id=1, source_target_pairs={{0,1},{2,3},{4,5},{6,7},{8,9},{10,11},{12,13},{14,15},{16,0},{18,2... | collective-permute-start | bytes 393224 | tf_op jit(solution)/shard_map/ppermute | solution.py:684
  70.4 9.9 %collective-permute-start.22 = (bf16[512,128]{1,0:T(8,128)(2,1)S(1)}, bf16[512,128]{1,0:T(8,128)(2,1)S(1)}, u32[]{:S(2)}, u32[]{:S(2)}) collective-permute-start(bf16[512,128]{1,0:T(8,128)(2,1)S(1)} %get-tuple-element.65), channel_id=1, source_target_pairs={{16,1},{18,3},{20,5},{22,7},{24,9},{26,11},{28,13},{30,15},{9,24},... | collective-permute-start | bytes 393224 | tf_op jit(solution)/shard_map/ppermute | solution.py:684
  (3 other events, 45.1 us)

commit v8 on v7

--- a/solution.py
+++ b/solution.py
@@ -356,6 +356,8 @@
     drive,
     back,
     grad_ext,
+    decays,
+    residues,
 ):
     groups, toks, chans = keep_ref.shape
     half = toks // 2
@@ -363,27 +365,33 @@
     short = taps_ref.shape[1]
     rim = short - 1
     length = toks // CHUNKS
+    apart = flat.shape[1] // CHUNKS
     lanes = flat.shape[-1]
     wide = (CHUNKS, lanes)
     _, _, _, core = here()
 
+    def spread(ref, at, values):
+        for s in range(CHUNKS):
+            ref[(*at, slice(s * apart, s * apart + length))] = values[s * length : (s + 1) * length]
+
     def row(array, at):
         return jnp.broadcast_to(array[at : at + 1, :], wide)
 
     def column(c, _):
         some = pl.ds(pl.multiple_of(c * lanes, lanes), lanes)
         whole = pl.ds(pl.multiple_of(core * chans + c * lanes, lanes), lanes)
-        own_rows = pl.ds(pl.multiple_of(core * half, half), half)
-        other_rows = pl.ds(pl.multiple_of((1 - core) * half, half), half)
-
         for g in range(groups):
-            flat[g] = (keep_ref[g, :, some] + other_ref[g, :, some]).astype(bf16).astype(f32)
-        flat_cot[own_rows] = cot_own_ref[:, whole].astype(f32)
-        flat_cot[other_rows] = cot_other_ref[:, whole].astype(f32)
+            spread(flat, (g,), (keep_ref[g, :, some] + other_ref[g, :, some]).astype(bf16).astype(f32))
+        for s in range(CHUNKS // 2):
+            rows = slice(s * length, (s + 1) * length)
+            own_at = pl.multiple_of((core * (CHUNKS // 2) + s) * apart, 8)
+            other_at = pl.multiple_of(((1 - core) * (CHUNKS // 2) + s) * apart, 8)
+            flat_cot[pl.ds(own_at, length)] = cot_own_ref[rows, whole].astype(f32)
+            flat_cot[pl.ds(other_at, length)] = cot_other_ref[rows, whole].astype(f32)
 
         for g in range(groups):
             for k in range(length):
-                ext[g, rim + k] = flat[g, pl.ds(k, CHUNKS, stride=length), :]
+                ext[g, rim + k] = flat[g, pl.ds(k, CHUNKS, stride=apart), :]
             for k in range(rim):
                 ext[g, k] = shifted(ext[g, length + k], 1)
 
@@ -399,7 +407,7 @@
                 parts.append(total)
                 filt[g, k] = total
             drive[k] = parts[1] * parts[2]
-            back[k] = parts[0] * flat_cot[pl.ds(k, CHUNKS, stride=length), :]
+            back[k] = parts[0] * flat_cot[pl.ds(k, CHUNKS, stride=apart), :]
             return _
 
         lax.fori_loop(0, length, filter_step, 0, unroll=4)
@@ -408,9 +416,12 @@
         decay_rows = jnp.exp(-rates)
         jump_rows = [jnp.exp(-rates * (length * n)) for n in (1, 2, 4)]
         residue_rows = residues_ref[:, whole]
+        for m in range(modes):
+            decays[m] = row(decay_rows, m)
+            residues[m] = row(residue_rows, m)
 
         def long_filter(source, forward, finish):
-            decay = [row(decay_rows, m) for m in range(modes)]
+            decay = [decays[m] for m in range(modes)]
 
             def place(k):
                 return k if forward else length - 1 - k
@@ -432,7 +443,7 @@
             def out_step(k, states):
                 value = source[place(k)]
                 states = tuple(decay[m] * states[m] + value for m in range(modes))
-                terms = [row(residue_rows, m) * states[m] for m in range(modes)]
+                terms = [residues[m] * states[m] for m in range(modes)]
                 while len(terms) > 1:
                     terms = [a + b for a, b in zip(terms[::2], terms[1::2])]
                 finish(place(k), terms[0])
@@ -441,16 +452,20 @@
             lax.fori_loop(0, length, out_step, tuple(entering), unroll=4)
 
         def finish_forward(k, total):
-            flat[0, pl.ds(k, CHUNKS, stride=length), :] = filt[0, k] * total
-            grad_ext[0, k] = flat_cot[pl.ds(k, CHUNKS, stride=length), :] * total
+            flat[0, pl.ds(k, CHUNKS, stride=apart), :] = filt[0, k] * total
+            grad_ext[0, k] = flat_cot[pl.ds(k, CHUNKS, stride=apart), :] * total
 
         def finish_backward(k, total):
             grad_ext[1, k] = total * filt[2, k]
             grad_ext[2, k] = total * filt[1, k]
 
         long_filter(drive, True, finish_forward)
-        mixed_own_ref[:, some] = flat[0, own_rows].astype(bf16)
-        mixed_send_ref[:, some] = flat[0, other_rows].astype(bf16)
+        for s in range(CHUNKS // 2):
+            rows = slice(s * length, (s + 1) * length)
+            own_at = pl.multiple_of((core * (CHUNKS // 2) + s) * apart, 8)
+            other_at = pl.multiple_of(((1 - core) * (CHUNKS // 2) + s) * apart, 8)
+            mixed_own_ref[rows, some] = flat[0, pl.ds(own_at, length)].astype(bf16)
+            mixed_send_ref[rows, some] = flat[0, pl.ds(other_at, length)].astype(bf16)
         long_filter(back, False, finish_backward)
 
         for g in range(groups):
@@ -462,12 +477,13 @@
                 total = tap[0][g] * grad_ext[g, k]
                 for j in range(1, short):
                     total = total + tap[j][g] * grad_ext[g, k + j]
-                flat[g, pl.ds(k, CHUNKS, stride=length), :] = total
+                flat[g, pl.ds(k, CHUNKS, stride=apart), :] = total
             return _
 
         lax.fori_loop(0, length, adjoint_step, 0, unroll=4)
         for g in range(groups):
-            grad_ref[g, some, :] = flat[g].T.astype(bf16)
+            chunks = [flat[g, s * apart : s * apart + length] for s in range(CHUNKS)]
+            grad_ref[g, some, :] = jnp.concatenate(chunks, axis=0).T.astype(bf16)
         return _
 
     lax.fori_loop(0, chans // lanes, column, 0)
@@ -490,49 +506,54 @@
         "mixer",
         12 * modes * toks * chans,
         [
-            pltpu.VMEM((groups, toks, lanes), f32),
-            pltpu.VMEM((toks, lanes), f32),
+            pltpu.VMEM((groups, toks + 8 * CHUNKS, lanes), f32),
+            pltpu.VMEM((toks + 8 * CHUNKS, lanes), f32),
             pltpu.VMEM((groups, length + rim, CHUNKS, lanes), f32),
             pltpu.VMEM((groups, length, CHUNKS, lanes), f32),
             pltpu.VMEM((length, CHUNKS, lanes), f32),
             pltpu.VMEM((length, CHUNKS, lanes), f32),
             pltpu.VMEM((groups, length + rim, CHUNKS, lanes), f32),
+            pltpu.VMEM((modes, CHUNKS, lanes), f32),
+            pltpu.VMEM((modes, CHUNKS, lanes), f32),
         ],
     )
 
 
-def back_kernel(outs, w_ref, own_ref, other_ref, *out_refs):
-    groups, half, _ = own_ref.shape
+def back_kernel(outs, count, base, w_ref, *refs):
+    grads, out_refs = refs[: len(count)], refs[len(count) + base :]
+    groups, half, _ = grads[0].shape
     core = here()[3]
-    own_at = pl.multiple_of(core * half, half)
-    other_at = pl.multiple_of((1 - core) * half, half)
+    sides = [pl.multiple_of((1 - core if other else core) * half, half) for other in count]
     for blocks, out in zip(outs, out_refs):
         width = out.shape[0] // len(blocks)
         for n, block in enumerate(blocks):
+            rows = slice(n * width, (n + 1) * width)
             start = pl.multiple_of(block_at(*block) * width, width)
-            total = None
+            total = refs[len(count)][rows] if base else None
             for g in range(groups):
-                for ref, at in ((own_ref, own_at), (other_ref, other_at)):
+                for ref, at in zip(grads, sides):
                     term = jnp.dot(
                         w_ref[g, pl.ds(start, width), pl.ds(at, half)],
                         ref[g],
                         preferred_element_type=f32,
                     )
                     total = term if total is None else total + term
-            out[n * width : (n + 1) * width] = total.astype(out.dtype)
-
-
-def back_project(outs, dtypes, w, own, other, width):
-    groups, half, toks = own.shape
+            out[rows] = total.astype(out.dtype)
+
+
+def back_project(outs, dtypes, w, own, other, width, base=None):
+    grads = [(side, grad) for side, grad in enumerate((own, other)) if grad is not None]
+    groups, half, toks = grads[0][1].shape
+    extra = [] if base is None else [base]
     return small_call(
-        functools.partial(back_kernel, outs),
+        functools.partial(back_kernel, outs, [side for side, _ in grads], len(extra)),
         [
             jax.ShapeDtypeStruct((width * len(blocks), toks), dtype)
             for blocks, dtype in zip(outs, dtypes)
         ],
-        [w, own, other],
+        [w] + [grad for _, grad in grads] + extra,
         "back_project",
-        4 * sum(len(blocks) for blocks in outs) * groups * width * half * toks,
+        2 * sum(len(blocks) for blocks in outs) * groups * width * half * toks * len(grads),
         (),
         16,
     )
@@ -638,7 +659,6 @@
     first, other = first_way(came), other_way(came)
     x_2 = lax.ppermute(more, BOTH, OUTER_X)
     y_2 = lax.ppermute(more, BOTH, OUTER_Y)
-    d_2 = lax.ppermute(more, BOTH, OUTER_XY)
     sums = project(
         [embedded, more, near_y, near_d, came],
         [(0, 1, None), (1, 1, "x"), (2, 1, "y"), (3, 1, 2), (4, 2, None)],
@@ -647,8 +667,9 @@
         None,
         False,
     )
-    first, other, sums = lax.optimization_barrier((first, other, sums))
+    first, other, more, sums = lax.optimization_barrier((first, other, more, sums))
     both = other_way(first)
+    d_2 = lax.ppermute(more, BOTH, OUTER_XY)
     sums = project(
         [first, other], [(0, 2, 0), (1, 2, 1)], [(0, 1, 0), (1, 1, 1)], w, sums, False
     )
@@ -667,7 +688,9 @@
     grad_other = swap(grad_own)
     mixed_other = swap(mixed_send)
 
-    (across,) = back_project([[(1, 2), (2, 2)]], [bf16], w, grad_own, grad_other, width)
+    (part,) = back_project([[(1, 2), (2, 2)]], [f32], w, grad_own, None, width)
+    grad_other, part = lax.optimization_barrier((grad_other, part))
+    (across,) = back_project([[(1, 2), (2, 2)]], [bf16], w, None, grad_other, width, part)
     across = other_way(across)
     (other,) = back_project([[(1, 1), (2, 1)]], [bf16], w, grad_own, grad_other, width)
     other = other_way(other)

time: 82.1 us -> 81.7 us (level)
    ppermute x4, waiting for transfers between devices: 9.25 us -> 10.2 us  [chip_plan(): lax.ppermute(a, BOTH, pairs)]
    pallas_call x13 -> x14, Pallas kernels: 14.4 us -> 13.7 us  [small_call(): pl.pallas_call(kernel, in_specs=[IN_VMEM] * len(operands), out_specs=jax....]
  transfers between devices with their start and end apart: 23 -> 23, of which waited for: 10 -> 11; matrix products, arithmetic and copies ran while one was open for 0% -> 0% of each run, Pallas kernels for 16% -> 17%
where the time goes in v8:
time: 81.7 us; the launch traced here: 80.6 us
  waiting for transfers between devices  33.7 us (41%)
  starting transfers between devices  26.7 us (33%)
  Pallas kernels  19.3 us (24%)
  between operations  0.9 us (1%)
    ppermute x4, waiting for transfers between devices, other_way(): return lax.ppermute(array, BOTH, OTHER_WAY)  18.8 us
    pallas_call x14, Pallas kernels, small_call(): pl.pallas_call(kernel, in_specs=[IN_VMEM] * len(operands), out_specs=jax....  13.7 us
    ppermute x4, waiting for transfers between devices, chip_plan(): lax.ppermute(a, BOTH, pairs)  10.2 us
    ppermute x4, starting transfers between devices, chip_plan(): lax.ppermute(a, BOTH, pairs)  5.16 us
    ppermute x4, starting transfers between devices, other_way(): return lax.ppermute(array, BOTH, OTHER_WAY)  4.69 us
    ppermute x5, waiting for transfers between devices, swap(): return lax.ppermute(array, BOTH, OTHER_CORE)  4.64 us
    pallas_call x1, Pallas kernels, load(): pl.pallas_call(load_kernel, in_specs=[pl.BlockSpec(memory_space=pltpu.HBM...  4.59 us
    ppermute x3, starting transfers between devices, first_way(): return lax.ppermute(array, BOTH, FIRST_WAY)  3.65 us
  transfers between devices with their start and end apart: 23, of which 11 were waited for; matrix products, arithmetic and copies ran while one was open for 0% of the time, Pallas kernels for 17%

profile of v8, /device:TPU:0, one launch (start us, length us, event | category | flops | bytes accessed | tf_op | source)
XLA Modules:
  0.0 80.6 jit_solution(16871272313058055933)
XLA Ops:
  1.2 1.1 %fetch.1 = (s32[1,128]{1,0:T(1,128)S(1)}, bf16[512,512]{1,0:T(8,128)(2,1)S(1)}) custom-call(s32[1,128]{1,0:T(1,128)} %bitcast.6, bf16[512,512]{1,0:T(8,128)(2,1)} %table_ref.1), custom_call_target="tpu_custom_call" | custom-call | bytes 1048576 | tf_op jit(solution)/shard_map/fetch/pallas_call | solution.py:251
  2.8 3.0 %collective-permute-start.2 = (bf16[256,512]{1,0:T(8,128)(2,1)S(1)}, bf16[256,512]{1,0:T(8,128)(2,1)S(1)}, u32[]{:S(2)}, u32[]{:S(2)}) collective-permute-start(bf16[256,512]{1,0:T(8,128)(2,1)S(1)} %embed_rows.1.refs_0_), channel_id=1, source_target_pairs={{0,8},{2,10},{4,12},{6,14},{8,0},{10,2},{12,4},{14,6},{1,16},{3,18... | collective-permute-start | bytes 786440 | tf_op jit(solution)/shard_map/ppermute | solution.py:653
  5.7 1.5 %collective-permute-start.5 = (bf16[256,512]{1,0:T(8,128)(2,1)S(1)}, bf16[256,512]{1,0:T(8,128)(2,1)S(1)}, u32[]{:S(2)}, u32[]{:S(2)}) collective-permute-start(bf16[256,512]{1,0:T(8,128)(2,1)S(1)} %embed_rows.1.refs_0_), channel_id=1, source_target_pairs={{9,16},{11,18},{13,20},{15,22},{1,24},{3,26},{5,28},{7,30},{16,9},... | collective-permute-start | bytes 786440 | tf_op jit(solution)/shard_map/ppermute | solution.py:654
  7.2 3.4 %collective-permute-start.6 = (bf16[256,512]{1,0:T(8,128)(2,1)S(1)}, bf16[256,512]{1,0:T(8,128)(2,1)S(1)}, u32[]{:S(2)}, u32[]{:S(2)}) collective-permute-start(bf16[256,512]{1,0:T(8,128)(2,1)S(1)} %embed_rows.1.refs_0_), channel_id=1, source_target_pairs={{0,4},{1,1},{2,6},{3,3},{4,0},{5,5},{6,2},{7,7},{8,12},{9,9},{10,1... | collective-permute-start | bytes 786440 | tf_op jit(solution)/shard_map/ppermute | solution.py:655
  10.7 2.4 %collective-permute-start.7 = (bf16[256,512]{1,0:T(8,128)(2,1)S(1)}, bf16[256,512]{1,0:T(8,128)(2,1)S(1)}, u32[]{:S(2)}, u32[]{:S(2)}) collective-permute-start(bf16[256,512]{1,0:T(8,128)(2,1)S(1)} %embed_rows.1.refs_0_), channel_id=1, source_target_pairs={{0,6},{1,1},{2,4},{3,3},{4,2},{5,5},{6,0},{7,7},{8,14},{9,9},{10,1... | collective-permute-start | bytes 786440 | tf_op jit(solution)/shard_map/ppermute | solution.py:656
  13.1 4.6 %load.1.w_ref = bf16[3,4096,512]{2,1,0:T(8,128)(2,1)S(1)} custom-call(bf16[3,4096,512]{2,1,0:T(8,128)(2,1)} %bitcast.4), custom_call_target="tpu_custom_call" | custom-call | bytes 25165824 | tf_op jit(solution)/shard_map/load/pallas_call | solution.py:273
  17.7 1.6 %collective-permute-start.3 = (bf16[256,512]{1,0:T(8,128)(2,1)S(1)}, bf16[256,512]{1,0:T(8,128)(2,1)S(1)}, u32[]{:S(2)}, u32[]{:S(2)}) collective-permute-start(bf16[256,512]{1,0:T(8,128)(2,1)S(1)} %collective-permute-done.2.refs_4_), channel_id=1, source_target_pairs={{0,2},{1,5},{2,0},{3,7},{4,6},{5,1},{6,4},{7,3},{8,10},{9,13},{10,... | collective-permute-start | bytes 786440 | tf_op jit(solution)/shard_map/ppermute | solution.py:641
  19.2 1.5 %collective-permute-start.4 = (bf16[256,512]{1,0:T(8,128)(2,1)S(1)}, bf16[256,512]{1,0:T(8,128)(2,1)S(1)}, u32[]{:S(2)}, u32[]{:S(2)}) collective-permute-start(bf16[256,512]{1,0:T(8,128)(2,1)S(1)} %collective-permute-done.2.refs_4_), channel_id=1, source_target_pairs={{0,4},{1,3},{2,6},{3,1},{4,0},{5,7},{6,2},{7,5},{8,12},{9,11},{10,... | collective-permute-start | bytes 786440 | tf_op jit(solution)/shard_map/ppermute | solution.py:644
  22.1 2.2 %project.3.refs_2_ = f32[3,256,512]{2,1,0:T(8,128)S(1)} custom-call(bf16[3,4096,512]{2,1,0:T(8,128)(2,1)S(1)} %load.1.w_ref, bf16[256,512]{1,0:T(8,128)(2,1)S(1)} %embed_rows.1.refs_0_, bf16[256,512]{1,0:T(8,128)(2,1)S(1)} %collective-permute-done.5.refs_1_, bf16[256,512]{1,0:T(8,128)(2,1)S(1)} %collective-permute-done.6.refs_2_, ...), custom_call_target="tpu_custom_call" | custom-call | flops 31457280 | bytes 217088 | tf_op jit(solution)/shard_map/project/pallas_call | solution.py:174
  24.5 3.4 %collective-permute-done.4.refs_1_ = bf16[256,512]{1,0:T(8,128)(2,1)S(1)} collective-permute-done((bf16[256,512]{1,0:T(8,128)(2,1)S(1)}, bf16[256,512]{1,0:T(8,128)(2,1)S(1)}, u32[]{:S(2)}, u32[]{:S(2)}) %collective-permute-start.4) | collective-permute-done | bytes 262176 | tf_op jit(solution)/shard_map/ppermute | solution.py:644
  27.8 1.0 %collective-permute-start.8 = (bf16[256,512]{1,0:T(8,128)(2,1)S(1)}, bf16[256,512]{1,0:T(8,128)(2,1)S(1)}, u32[]{:S(2)}, u32[]{:S(2)}) collective-permute-start(bf16[256,512]{1,0:T(8,128)(2,1)S(1)} %collective-permute-done.3.refs_0_), channel_id=1, source_target_pairs={{0,4},{1,3},{2,6},{3,1},{4,0},{5,7},{6,2},{7,5},{8,12},{9,11},{10,... | collective-permute-start | bytes 786440 | tf_op jit(solution)/shard_map/ppermute | solution.py:644
  30.6 6.1 %collective-permute-done.8.refs_0_ = bf16[256,512]{1,0:T(8,128)(2,1)S(1)} collective-permute-done((bf16[256,512]{1,0:T(8,128)(2,1)S(1)}, bf16[256,512]{1,0:T(8,128)(2,1)S(1)}, u32[]{:S(2)}, u32[]{:S(2)}) %collective-permute-start.8) | collective-permute-done | bytes 262176 | tf_op jit(solution)/shard_map/ppermute | solution.py:644
  37.5 2.3 %collective-permute-done.12.other_ref = f32[3,256,256]{2,1,0:T(8,128)S(1)} collective-permute-done((f32[3,256,256]{2,1,0:T(8,128)S(1)}, f32[3,256,256]{2,1,0:T(8,128)S(1)}, u32[]{:S(2)}, u32[]{:S(2)}) %collective-permute-start.12) | collective-permute-done | bytes 786464 | tf_op jit(solution)/shard_map/ppermute | solution.py:638
  39.7 3.7 %mixer.1 = (bf16[128,256]{1,0:T(8,128)(2,1)S(1)}, bf16[128,256]{1,0:T(8,128)(2,1)S(1)}, bf16[3,256,256]{2,1,0:T(8,128)(2,1)S(1)}) custom-call(f32[3,256,256]{2,1,0:T(8,128)S(1)} %get-tuple-element.51.keep_ref, f32[3,256,256]{2,1,0:T(8,128)S(1)} %collective-permute-done.12.other_ref, f32[3,7,512]{2,1,0:T(8,128)S(1)} %bitcast.3, f32[16,512]{1,0:T(8,128)S(1)} %copy-done.2, ...), custom_call_target="tpu_custom_call" | custom-call | flops 196608 | bytes 30368 | tf_op jit(solution)/shard_map/mixer/pallas_call | solution.py:174
  44.2 1.0 %collective-permute-done.13.refs_0_.refs_1_ = bf16[3,256,256]{2,1,0:T(8,128)(2,1)S(1)} collective-permute-done((bf16[3,256,256]{2,1,0:T(8,128)(2,1)S(1)}, bf16[3,256,256]{2,1,0:T(8,128)(2,1)S(1)}, u32[]{:S(2)}, u32[]{:S(2)}) %collective-permute-start.13) | collective-permute-done | bytes 393248 | tf_op jit(solution)/shard_map/ppermute | solution.py:638
  47.7 1.2 %collective-permute-start.16 = (bf16[1024,256]{1,0:T(8,128)(2,1)S(1)}, bf16[1024,256]{1,0:T(8,128)(2,1)S(1)}, u32[]{:S(2)}, u32[]{:S(2)}) collective-permute-start(bf16[1024,256]{1,0:T(8,128)(2,1)S(1)} %back_project.7), channel_id=1, source_target_pairs={{0,4},{1,3},{2,6},{3,1},{4,0},{5,7},{6,2},{7,5},{8,12},{9,11},{10,... | collective-permute-start | bytes 1572872 | tf_op jit(solution)/shard_map/ppermute | solution.py:644
  48.9 1.3 %collective-permute-done.15.other_ref = bf16[128,256]{1,0:T(8,128)(2,1)S(1)} collective-permute-done((bf16[128,256]{1,0:T(8,128)(2,1)S(1)}, bf16[128,256]{1,0:T(8,128)(2,1)S(1)}, u32[]{:S(2)}, u32[]{:S(2)}) %collective-permute-start.15) | collective-permute-done | bytes 65568 | tf_op jit(solution)/shard_map/ppermute | solution.py:638
  50.9 1.8 %back_project.6 = (f32[512,256]{1,0:T(8,128)S(1)}, f32[512,256]{1,0:T(8,128)S(1)}, f32[512,256]{1,0:T(8,128)S(1)}, f32[512,256]{1,0:T(8,128)S(1)}) custom-call(bf16[3,4096,512]{2,1,0:T(8,128)(2,1)S(1)} %load.1.w_ref, bf16[3,256,256]{2,1,0:T(8,128)(2,1)S(1)} %get-tuple-element.54.refs_0_, bf16[3,256,256]{2,1,0:T(8,128)(2,1)S(1)} %collective-permute-done.13.refs_0_.refs_1_), custom_call_target="tpu_custom_call" | custom-call | flops 25165824 | bytes 208896 | tf_op jit(solution)/shard_map/back_project/pallas_call | solution.py:174
  52.6 2.4 %collective-permute-done.14.got_ref = bf16[1024,256]{1,0:T(8,128)(2,1)S(1)} collective-permute-done((bf16[1024,256]{1,0:T(8,128)(2,1)S(1)}, bf16[1024,256]{1,0:T(8,128)(2,1)S(1)}, u32[]{:S(2)}, u32[]{:S(2)}) %collective-permute-start.14) | collective-permute-done | bytes 524320 | tf_op jit(solution)/shard_map/ppermute | solution.py:644
  55.1 1.2 %collective-permute-start.18 = (bf16[512,256]{1,0:T(8,128)(2,1)S(1)}, bf16[512,256]{1,0:T(8,128)(2,1)S(1)}, u32[]{:S(2)}, u32[]{:S(2)}) collective-permute-start(bf16[512,256]{1,0:T(8,128)(2,1)S(1)} %get-tuple-element.67), channel_id=1, source_target_pairs={{0,2},{1,5},{2,0},{3,7},{4,6},{5,1},{6,4},{7,3},{8,10},{9,13},{10,... | collective-permute-start | bytes 786440 | tf_op jit(solution)/shard_map/ppermute | solution.py:641
  57.2 6.9 %collective-permute-done.16.other_ref = bf16[1024,256]{1,0:T(8,128)(2,1)S(1)} collective-permute-done((bf16[1024,256]{1,0:T(8,128)(2,1)S(1)}, bf16[1024,256]{1,0:T(8,128)(2,1)S(1)}, u32[]{:S(2)}, u32[]{:S(2)}) %collective-permute-start.16) | collective-permute-done | bytes 524320 | tf_op jit(solution)/shard_map/ppermute | solution.py:644
  64.5 4.2 %collective-permute-start.20 = (bf16[512,128]{1,0:T(8,128)(2,1)S(1)}, bf16[512,128]{1,0:T(8,128)(2,1)S(1)}, u32[]{:S(2)}, u32[]{:S(2)}) collective-permute-start(bf16[512,128]{1,0:T(8,128)(2,1)S(1)} %get-tuple-element.69), channel_id=1, source_target_pairs={{0,9},{2,11},{4,13},{6,15},{8,1},{10,3},{12,5},{14,7},{16,8},{18,1... | collective-permute-start | bytes 393224 | tf_op jit(solution)/shard_map/ppermute | solution.py:705
  69.7 5.2 %collective-permute-done.20.b_ref = bf16[512,128]{1,0:T(8,128)(2,1)S(1)} collective-permute-done((bf16[512,128]{1,0:T(8,128)(2,1)S(1)}, bf16[512,128]{1,0:T(8,128)(2,1)S(1)}, u32[]{:S(2)}, u32[]{:S(2)}) %collective-permute-start.20) | collective-permute-done | bytes 131104 | tf_op jit(solution)/shard_map/ppermute | solution.py:705
  74.9 4.9 %collective-permute-done.21.c_ref = bf16[512,128]{1,0:T(8,128)(2,1)S(1)} collective-permute-done((bf16[512,128]{1,0:T(8,128)(2,1)S(1)}, bf16[512,128]{1,0:T(8,128)(2,1)S(1)}, u32[]{:S(2)}, u32[]{:S(2)}) %collective-permute-start.21) | collective-permute-done | bytes 131104 | tf_op jit(solution)/shard_map/ppermute | solution.py:707
  (46 shorter events, 11.9 us)
Async XLA Ops:
  0.6 2.1 %collective-permute-start.1 = (bf16[128,512]{1,0:T(8,128)(2,1)}, bf16[128,512]{1,0:T(8,128)(2,1)S(1)}, u32[]{:S(2)}, u32[]{:S(2)}) collective-permute-start(bf16[128,512]{1,0:T(8,128)(2,1)} %cot_own_ref.1), channel_id=1, source_target_pairs={{0,1},{1,0},{2,3},{3,2},{4,5},{5,4},{6,7},{7,6},{8,9},{9,8},{10,11... | collective-permute-start | bytes 393224 | tf_op jit(solution)/shard_map/ppermute | solution.py:638
  1.1 1.3 %collective-permute-start = (s32[1,128]{1,0:T(1,128)}, s32[1,128]{1,0:T(1,128)S(1)}, u32[]{:S(2)}, u32[]{:S(2)}) collective-permute-start(s32[1,128]{1,0:T(1,128)} %bitcast.5), channel_id=1, source_target_pairs={{0,1},{1,0},{2,3},{3,2},{4,5},{5,4},{6,7},{7,6},{8,9},{9,8},{10,11... | collective-permute-start | bytes 1544 | tf_op jit(solution)/shard_map/ppermute | solution.py:638
  2.8 14.9 %collective-permute-start.2 = (bf16[256,512]{1,0:T(8,128)(2,1)S(1)}, bf16[256,512]{1,0:T(8,128)(2,1)S(1)}, u32[]{:S(2)}, u32[]{:S(2)}) collective-permute-start(bf16[256,512]{1,0:T(8,128)(2,1)S(1)} %embed_rows.1.refs_0_), channel_id=1, source_target_pairs={{0,8},{2,10},{4,12},{6,14},{8,0},{10,2},{12,4},{14,6},{1,16},{3,18... | collective-permute-start | bytes 786440 | tf_op jit(solution)/shard_map/ppermute | solution.py:653
  5.7 15.0 %collective-permute-start.5 = (bf16[256,512]{1,0:T(8,128)(2,1)S(1)}, bf16[256,512]{1,0:T(8,128)(2,1)S(1)}, u32[]{:S(2)}, u32[]{:S(2)}) collective-permute-start(bf16[256,512]{1,0:T(8,128)(2,1)S(1)} %embed_rows.1.refs_0_), channel_id=1, source_target_pairs={{9,16},{11,18},{13,20},{15,22},{1,24},{3,26},{5,28},{7,30},{16,9},... | collective-permute-start | bytes 786440 | tf_op jit(solution)/shard_map/ppermute | solution.py:654
  7.2 14.2 %collective-permute-start.6 = (bf16[256,512]{1,0:T(8,128)(2,1)S(1)}, bf16[256,512]{1,0:T(8,128)(2,1)S(1)}, u32[]{:S(2)}, u32[]{:S(2)}) collective-permute-start(bf16[256,512]{1,0:T(8,128)(2,1)S(1)} %embed_rows.1.refs_0_), channel_id=1, source_target_pairs={{0,4},{1,1},{2,6},{3,3},{4,0},{5,5},{6,2},{7,7},{8,12},{9,9},{10,1... | collective-permute-start | bytes 786440 | tf_op jit(solution)/shard_map/ppermute | solution.py:655
  10.7 11.5 %collective-permute-start.7 = (bf16[256,512]{1,0:T(8,128)(2,1)S(1)}, bf16[256,512]{1,0:T(8,128)(2,1)S(1)}, u32[]{:S(2)}, u32[]{:S(2)}) collective-permute-start(bf16[256,512]{1,0:T(8,128)(2,1)S(1)} %embed_rows.1.refs_0_), channel_id=1, source_target_pairs={{0,6},{1,1},{2,4},{3,3},{4,2},{5,5},{6,0},{7,7},{8,14},{9,9},{10,1... | collective-permute-start | bytes 786440 | tf_op jit(solution)/shard_map/ppermute | solution.py:656
  17.7 6.8 %collective-permute-start.3 = (bf16[256,512]{1,0:T(8,128)(2,1)S(1)}, bf16[256,512]{1,0:T(8,128)(2,1)S(1)}, u32[]{:S(2)}, u32[]{:S(2)}) collective-permute-start(bf16[256,512]{1,0:T(8,128)(2,1)S(1)} %collective-permute-done.2.refs_4_), channel_id=1, source_target_pairs={{0,2},{1,5},{2,0},{3,7},{4,6},{5,1},{6,4},{7,3},{8,10},{9,13},{10,... | collective-permute-start | bytes 786440 | tf_op jit(solution)/shard_map/ppermute | solution.py:641
  19.2 8.6 %collective-permute-start.4 = (bf16[256,512]{1,0:T(8,128)(2,1)S(1)}, bf16[256,512]{1,0:T(8,128)(2,1)S(1)}, u32[]{:S(2)}, u32[]{:S(2)}) collective-permute-start(bf16[256,512]{1,0:T(8,128)(2,1)S(1)} %collective-permute-done.2.refs_4_), channel_id=1, source_target_pairs={{0,4},{1,3},{2,6},{3,1},{4,0},{5,7},{6,2},{7,5},{8,12},{9,11},{10,... | collective-permute-start | bytes 786440 | tf_op jit(solution)/shard_map/ppermute | solution.py:644
  20.7 9.8 %collective-permute-start.10 = (bf16[256,512]{1,0:T(8,128)(2,1)S(1)}, bf16[256,512]{1,0:T(8,128)(2,1)S(1)}, u32[]{:S(2)}, u32[]{:S(2)}) collective-permute-start(bf16[256,512]{1,0:T(8,128)(2,1)S(1)} %collective-permute-done.5.refs_1_), channel_id=1, source_target_pairs={{0,0},{1,5},{2,2},{3,7},{4,4},{5,1},{6,6},{7,3},{8,8},{9,13},{10,1... | collective-permute-start | bytes 786440 | tf_op jit(solution)/shard_map/ppermute | solution.py:661
  21.4 9.1 %collective-permute-start.9 = (bf16[256,512]{1,0:T(8,128)(2,1)S(1)}, bf16[256,512]{1,0:T(8,128)(2,1)S(1)}, u32[]{:S(2)}, u32[]{:S(2)}) collective-permute-start(bf16[256,512]{1,0:T(8,128)(2,1)S(1)} %collective-permute-done.5.refs_1_), channel_id=1, source_target_pairs={{0,0},{1,3},{2,2},{3,1},{4,4},{5,7},{6,6},{7,5},{8,8},{9,11},{10,1... | collective-permute-start | bytes 786440 | tf_op jit(solution)/shard_map/ppermute | solution.py:660
  24.3 15.4 %copy-start = (bf16[128,512]{1,0:T(8,128)(2,1)S(1)}, bf16[128,512]{1,0:T(8,128)(2,1)}, u32[]{:S(2)}) copy-start(bf16[128,512]{1,0:T(8,128)(2,1)} %cot_own_ref.1) | copy-start | bytes 393220
  27.8 8.8 %collective-permute-start.8 = (bf16[256,512]{1,0:T(8,128)(2,1)S(1)}, bf16[256,512]{1,0:T(8,128)(2,1)S(1)}, u32[]{:S(2)}, u32[]{:S(2)}) collective-permute-start(bf16[256,512]{1,0:T(8,128)(2,1)S(1)} %collective-permute-done.3.refs_0_), channel_id=1, source_target_pairs={{0,4},{1,3},{2,6},{3,1},{4,0},{5,7},{6,2},{7,5},{8,12},{9,11},{10,... | collective-permute-start | bytes 786440 | tf_op jit(solution)/shard_map/ppermute | solution.py:644
  28.9 7.8 %collective-permute-start.11 = (bf16[256,512]{1,0:T(8,128)(2,1)S(1)}, bf16[256,512]{1,0:T(8,128)(2,1)S(1)}, u32[]{:S(2)}, u32[]{:S(2)}) collective-permute-start(bf16[256,512]{1,0:T(8,128)(2,1)S(1)} %collective-permute-done.5.refs_1_), channel_id=1, source_target_pairs={{0,0},{1,7},{2,2},{3,5},{4,4},{5,3},{6,6},{7,1},{8,8},{9,15},{10,1... | collective-permute-start | bytes 786440 | tf_op jit(solution)/shard_map/ppermute | solution.py:672
  37.4 2.4 %collective-permute-start.12 = (f32[3,256,256]{2,1,0:T(8,128)S(1)}, f32[3,256,256]{2,1,0:T(8,128)S(1)}, u32[]{:S(2)}, u32[]{:S(2)}) collective-permute-start(f32[3,256,256]{2,1,0:T(8,128)S(1)} %get-tuple-element.52), channel_id=1, source_target_pairs={{0,1},{1,0},{2,3},{3,2},{4,5},{5,4},{6,7},{7,6},{8,9},{9,8},{10,11... | collective-permute-start | bytes 2359304 | tf_op jit(solution)/shard_map/ppermute | solution.py:638
  43.4 1.8 %collective-permute-start.13 = (bf16[3,256,256]{2,1,0:T(8,128)(2,1)S(1)}, bf16[3,256,256]{2,1,0:T(8,128)(2,1)S(1)}, u32[]{:S(2)}, u32[]{:S(2)}) collective-permute-start(bf16[3,256,256]{2,1,0:T(8,128)(2,1)S(1)} %get-tuple-element.54.refs_0_), channel_id=1, source_target_pairs={{0,1},{1,0},{2,3},{3,2},{4,5},{5,4},{6,7},{7,6},{8,9},{9,8},{10,11... | collective-permute-start | bytes 1179656 | tf_op jit(solution)/shard_map/ppermute | solution.py:638
  45.8 9.2 %collective-permute-start.14 = (bf16[1024,256]{1,0:T(8,128)(2,1)S(1)}, bf16[1024,256]{1,0:T(8,128)(2,1)S(1)}, u32[]{:S(2)}, u32[]{:S(2)}) collective-permute-start(bf16[1024,256]{1,0:T(8,128)(2,1)S(1)} %back_project.5), channel_id=1, source_target_pairs={{0,4},{1,3},{2,6},{3,1},{4,0},{5,7},{6,2},{7,5},{8,12},{9,11},{10,... | collective-permute-start | bytes 1572872 | tf_op jit(solution)/shard_map/ppermute | solution.py:644
  47.7 16.4 %collective-permute-start.16 = (bf16[1024,256]{1,0:T(8,128)(2,1)S(1)}, bf16[1024,256]{1,0:T(8,128)(2,1)S(1)}, u32[]{:S(2)}, u32[]{:S(2)}) collective-permute-start(bf16[1024,256]{1,0:T(8,128)(2,1)S(1)} %back_project.7), channel_id=1, source_target_pairs={{0,4},{1,3},{2,6},{3,1},{4,0},{5,7},{6,2},{7,5},{8,12},{9,11},{10,... | collective-permute-start | bytes 1572872 | tf_op jit(solution)/shard_map/ppermute | solution.py:644
  48.9 1.3 %collective-permute-start.15 = (bf16[128,256]{1,0:T(8,128)(2,1)S(1)}, bf16[128,256]{1,0:T(8,128)(2,1)S(1)}, u32[]{:S(2)}, u32[]{:S(2)}) collective-permute-start(bf16[128,256]{1,0:T(8,128)(2,1)S(1)} %get-tuple-element.58), channel_id=1, source_target_pairs={{0,1},{1,0},{2,3},{3,2},{4,5},{5,4},{6,7},{7,6},{8,9},{9,8},{10,11... | collective-permute-start | bytes 196616 | tf_op jit(solution)/shard_map/ppermute | solution.py:638
  55.1 9.0 %collective-permute-start.18 = (bf16[512,256]{1,0:T(8,128)(2,1)S(1)}, bf16[512,256]{1,0:T(8,128)(2,1)S(1)}, u32[]{:S(2)}, u32[]{:S(2)}) collective-permute-start(bf16[512,256]{1,0:T(8,128)(2,1)S(1)} %get-tuple-element.67), channel_id=1, source_target_pairs={{0,2},{1,5},{2,0},{3,7},{4,6},{5,1},{6,4},{7,3},{8,10},{9,13},{10,... | collective-permute-start | bytes 786440 | tf_op jit(solution)/shard_map/ppermute | solution.py:641
  56.3 12.4 %collective-permute-start.17 = (bf16[512,256]{1,0:T(8,128)(2,1)S(1)}, bf16[512,256]{1,0:T(8,128)(2,1)S(1)}, u32[]{:S(2)}, u32[]{:S(2)}) collective-permute-start(bf16[512,256]{1,0:T(8,128)(2,1)S(1)} %get-tuple-element.64), channel_id=1, source_target_pairs={{0,2},{1,5},{2,0},{3,7},{4,6},{5,1},{6,4},{7,3},{8,10},{9,13},{10,... | collective-permute-start | bytes 786440 | tf_op jit(solution)/shard_map/ppermute | solution.py:641
  64.3 5.3 %collective-permute-start.19 = (bf16[512,128]{1,0:T(8,128)(2,1)S(1)}, bf16[512,128]{1,0:T(8,128)(2,1)S(1)}, u32[]{:S(2)}, u32[]{:S(2)}) collective-permute-start(bf16[512,128]{1,0:T(8,128)(2,1)S(1)} %get-tuple-element.68), channel_id=1, source_target_pairs={{0,8},{2,10},{4,12},{6,14},{8,0},{10,2},{12,4},{14,6},{16,9},{18,1... | collective-permute-start | bytes 393224 | tf_op jit(solution)/shard_map/ppermute | solution.py:705
  64.5 10.4 %collective-permute-start.20 = (bf16[512,128]{1,0:T(8,128)(2,1)S(1)}, bf16[512,128]{1,0:T(8,128)(2,1)S(1)}, u32[]{:S(2)}, u32[]{:S(2)}) collective-permute-start(bf16[512,128]{1,0:T(8,128)(2,1)S(1)} %get-tuple-element.69), channel_id=1, source_target_pairs={{0,9},{2,11},{4,13},{6,15},{8,1},{10,3},{12,5},{14,7},{16,8},{18,1... | collective-permute-start | bytes 393224 | tf_op jit(solution)/shard_map/ppermute | solution.py:705
  68.9 10.9 %collective-permute-start.21 = (bf16[512,128]{1,0:T(8,128)(2,1)S(1)}, bf16[512,128]{1,0:T(8,128)(2,1)S(1)}, u32[]{:S(2)}, u32[]{:S(2)}) collective-permute-start(bf16[512,128]{1,0:T(8,128)(2,1)S(1)} %get-tuple-element.70), channel_id=1, source_target_pairs={{0,1},{2,3},{4,5},{6,7},{8,9},{10,11},{12,13},{14,15},{16,0},{18,2... | collective-permute-start | bytes 393224 | tf_op jit(solution)/shard_map/ppermute | solution.py:707
  69.0 10.8 %collective-permute-start.22 = (bf16[512,128]{1,0:T(8,128)(2,1)S(1)}, bf16[512,128]{1,0:T(8,128)(2,1)S(1)}, u32[]{:S(2)}, u32[]{:S(2)}) collective-permute-start(bf16[512,128]{1,0:T(8,128)(2,1)S(1)} %get-tuple-element.71), channel_id=1, source_target_pairs={{16,1},{18,3},{20,5},{22,7},{24,9},{26,11},{28,13},{30,15},{9,24},... | collective-permute-start | bytes 393224 | tf_op jit(solution)/shard_map/ppermute | solution.py:707
  (3 other events, 46.1 us)

commit v9 on v8

--- a/solution.py
+++ b/solution.py
@@ -290,9 +290,14 @@
     groups, _, chans = w_ref.shape
     width = acts[0].shape[1]
     if last:
-        keep_ref, send_ref, total_ref = refs[-3:]
+        half = chans // 2
+        core = here()[3]
+        outs = [
+            (refs[-2], pl.ds(pl.multiple_of(core * half, half), half)),
+            (refs[-1], pl.ds(pl.multiple_of((1 - core) * half, half), half)),
+        ]
     else:
-        total_ref = refs[-1]
+        outs = [(refs[-1], slice(None))]
 
     def add(entries):
         spans = [
@@ -300,19 +305,17 @@
             for _, slot, way in entries
         ]
         for g in range(groups):
-            total = refs[count][g] if has_base else None
-            for (which, _, _), span in zip(entries, spans):
-                term = jnp.dot(acts[which][...], w_ref[g, span, :], preferred_element_type=f32)
-                total = term if total is None else total + term
-            total_ref[g] = total
+            for out, some in outs:
+                total = refs[count][g, :, some] if has_base else None
+                for (which, _, _), span in zip(entries, spans):
+                    term = jnp.dot(
+                        acts[which][...], w_ref[g, span, some], preferred_element_type=f32
+                    )
+                    total = term if total is None else total + term
+                out[g] = total
 
     pl.when(is_inner())(lambda: add(inner))
     pl.when(jnp.logical_not(is_inner()))(lambda: add(outer))
-    if last:
-        half = chans // 2
-        core = here()[3]
-        keep_ref[...] = total_ref[:, :, pl.ds(pl.multiple_of(core * half, half), half)]
-        send_ref[...] = total_ref[:, :, pl.ds(pl.multiple_of((1 - core) * half, half), half)]
 
 
 def project(acts, inner, outer, w, base, last):
@@ -326,7 +329,7 @@
         [w] + list(acts) + ([] if base is None else [base]),
         "project",
         2 * max(len(inner), len(outer)) * groups * width * chans * toks,
-        [pltpu.VMEM(total.shape, f32)] if last else [],
+        (),
         16,
     )
 
@@ -482,8 +485,8 @@
 
         lax.fori_loop(0, length, adjoint_step, 0, unroll=4)
         for g in range(groups):
-            chunks = [flat[g, s * apart : s * apart + length] for s in range(CHUNKS)]
-            grad_ref[g, some, :] = jnp.concatenate(chunks, axis=0).T.astype(bf16)
+            chunks = [flat[g, s * apart : s * apart + length].astype(bf16) for s in range(CHUNKS)]
+            grad_ref[g, some, :] = jnp.concatenate(chunks, axis=0).T
         return _
 
     lax.fori_loop(0, chans // lanes, column, 0)
@@ -673,11 +676,12 @@
     sums = project(
         [first, other], [(0, 2, 0), (1, 2, 1)], [(0, 1, 0), (1, 1, 1)], w, sums, False
     )
-    both, x_2, y_2, d_2, sums = lax.optimization_barrier((both, x_2, y_2, d_2, sums))
+    sums = project([x_2, y_2], [], [(0, 2, "x"), (1, 2, "y")], w, sums, False)
+    both, d_2, sums = lax.optimization_barrier((both, d_2, sums))
     keep, send = project(
-        [both, x_2, y_2, d_2],
+        [both, d_2],
         [(0, 2, 2)],
-        [(0, 1, 2), (1, 2, "x"), (2, 2, "y"), (3, 2, 2)],
+        [(0, 1, 2), (1, 2, 2)],
         w,
         sums,
         True,

time: 81.7 us -> 80.7 us (0.988)
  waiting for transfers between devices: 33.7 us -> 32.6 us
    ppermute x4, waiting for transfers between devices: 18.8 us -> 15.1 us  [other_way(): return lax.ppermute(array, BOTH, OTHER_WAY)]
    ppermute x3, waiting for transfers between devices: 0.11 us -> 2.64 us  [first_way(): return lax.ppermute(array, BOTH, FIRST_WAY)]
    pallas_call x14 -> x15, Pallas kernels: 13.7 us -> 13.6 us  [small_call(): pl.pallas_call(kernel, in_specs=[IN_VMEM] * len(operands), out_specs=jax....]
  transfers between devices with their start and end apart: 23 -> 23, of which waited for: 11 -> 10; matrix products, arithmetic and copies ran while one was open for 0% -> 0% of each run, Pallas kernels for 17% -> 17%
where the time goes in v9:
time: 80.7 us; the launch traced here: 79.6 us
  waiting for transfers between devices  32.6 us (40%)
  starting transfers between devices  26.8 us (33%)
  Pallas kernels  19.3 us (24%)
  between operations  0.91 us (1%)
    ppermute x4, waiting for transfers between devices, other_way(): return lax.ppermute(array, BOTH, OTHER_WAY)  15.1 us
    pallas_call x15, Pallas kernels, small_call(): pl.pallas_call(kernel, in_specs=[IN_VMEM] * len(operands), out_specs=jax....  13.6 us
    ppermute x4, waiting for transfers between devices, chip_plan(): lax.ppermute(a, BOTH, pairs)  10.2 us
    ppermute x4, starting transfers between devices, other_way(): return lax.ppermute(array, BOTH, OTHER_WAY)  5.2 us
    ppermute x4, starting transfers between devices, chip_plan(): lax.ppermute(a, BOTH, pairs)  4.84 us
    ppermute x5, waiting for transfers between devices, swap(): return lax.ppermute(array, BOTH, OTHER_CORE)  4.64 us
    pallas_call x1, Pallas kernels, load(): pl.pallas_call(load_kernel, in_specs=[pl.BlockSpec(memory_space=pltpu.HBM...  4.59 us
    ppermute x3, starting transfers between devices, first_way(): return lax.ppermute(array, BOTH, FIRST_WAY)  3.65 us
  transfers between devices with their start and end apart: 23, of which 10 were waited for; matrix products, arithmetic and copies ran while one was open for 0% of the time, Pallas kernels for 17%

profile of v9, /device:TPU:0, one launch (start us, length us, event | category | flops | bytes accessed | tf_op | source)
XLA Modules:
  0.0 79.6 jit_solution(2498983635856782756)
XLA Ops:
  1.2 1.1 %fetch.1 = (s32[1,128]{1,0:T(1,128)S(1)}, bf16[512,512]{1,0:T(8,128)(2,1)S(1)}) custom-call(s32[1,128]{1,0:T(1,128)} %bitcast.6, bf16[512,512]{1,0:T(8,128)(2,1)} %table_ref.1), custom_call_target="tpu_custom_call" | custom-call | bytes 1048576 | tf_op jit(solution)/shard_map/fetch/pallas_call | solution.py:251
  2.8 3.0 %collective-permute-start.2 = (bf16[256,512]{1,0:T(8,128)(2,1)S(1)}, bf16[256,512]{1,0:T(8,128)(2,1)S(1)}, u32[]{:S(2)}, u32[]{:S(2)}) collective-permute-start(bf16[256,512]{1,0:T(8,128)(2,1)S(1)} %embed_rows.1.refs_0_), channel_id=1, source_target_pairs={{0,8},{2,10},{4,12},{6,14},{8,0},{10,2},{12,4},{14,6},{1,16},{3,18... | collective-permute-start | bytes 786440 | tf_op jit(solution)/shard_map/ppermute | solution.py:656
  5.7 1.5 %collective-permute-start.5 = (bf16[256,512]{1,0:T(8,128)(2,1)S(1)}, bf16[256,512]{1,0:T(8,128)(2,1)S(1)}, u32[]{:S(2)}, u32[]{:S(2)}) collective-permute-start(bf16[256,512]{1,0:T(8,128)(2,1)S(1)} %embed_rows.1.refs_0_), channel_id=1, source_target_pairs={{9,16},{11,18},{13,20},{15,22},{1,24},{3,26},{5,28},{7,30},{16,9},... | collective-permute-start | bytes 786440 | tf_op jit(solution)/shard_map/ppermute | solution.py:657
  7.2 3.4 %collective-permute-start.6 = (bf16[256,512]{1,0:T(8,128)(2,1)S(1)}, bf16[256,512]{1,0:T(8,128)(2,1)S(1)}, u32[]{:S(2)}, u32[]{:S(2)}) collective-permute-start(bf16[256,512]{1,0:T(8,128)(2,1)S(1)} %embed_rows.1.refs_0_), channel_id=1, source_target_pairs={{0,4},{1,1},{2,6},{3,3},{4,0},{5,5},{6,2},{7,7},{8,12},{9,9},{10,1... | collective-permute-start | bytes 786440 | tf_op jit(solution)/shard_map/ppermute | solution.py:658
  10.7 2.4 %collective-permute-start.7 = (bf16[256,512]{1,0:T(8,128)(2,1)S(1)}, bf16[256,512]{1,0:T(8,128)(2,1)S(1)}, u32[]{:S(2)}, u32[]{:S(2)}) collective-permute-start(bf16[256,512]{1,0:T(8,128)(2,1)S(1)} %embed_rows.1.refs_0_), channel_id=1, source_target_pairs={{0,6},{1,1},{2,4},{3,3},{4,2},{5,5},{6,0},{7,7},{8,14},{9,9},{10,1... | collective-permute-start | bytes 786440 | tf_op jit(solution)/shard_map/ppermute | solution.py:659
  13.1 4.6 %load.1.w_ref = bf16[3,4096,512]{2,1,0:T(8,128)(2,1)S(1)} custom-call(bf16[3,4096,512]{2,1,0:T(8,128)(2,1)} %bitcast.4), custom_call_target="tpu_custom_call" | custom-call | bytes 25165824 | tf_op jit(solution)/shard_map/load/pallas_call | solution.py:273
  17.7 1.6 %collective-permute-start.3 = (bf16[256,512]{1,0:T(8,128)(2,1)S(1)}, bf16[256,512]{1,0:T(8,128)(2,1)S(1)}, u32[]{:S(2)}, u32[]{:S(2)}) collective-permute-start(bf16[256,512]{1,0:T(8,128)(2,1)S(1)} %collective-permute-done.2.refs_4_), channel_id=1, source_target_pairs={{0,2},{1,5},{2,0},{3,7},{4,6},{5,1},{6,4},{7,3},{8,10},{9,13},{10,... | collective-permute-start | bytes 786440 | tf_op jit(solution)/shard_map/ppermute | solution.py:644
  19.2 1.5 %collective-permute-start.4 = (bf16[256,512]{1,0:T(8,128)(2,1)S(1)}, bf16[256,512]{1,0:T(8,128)(2,1)S(1)}, u32[]{:S(2)}, u32[]{:S(2)}) collective-permute-start(bf16[256,512]{1,0:T(8,128)(2,1)S(1)} %collective-permute-done.2.refs_4_), channel_id=1, source_target_pairs={{0,4},{1,3},{2,6},{3,1},{4,0},{5,7},{6,2},{7,5},{8,12},{9,11},{10,... | collective-permute-start | bytes 786440 | tf_op jit(solution)/shard_map/ppermute | solution.py:647
  22.1 2.2 %project.4.refs_2_ = f32[3,256,512]{2,1,0:T(8,128)S(1)} custom-call(bf16[3,4096,512]{2,1,0:T(8,128)(2,1)S(1)} %load.1.w_ref, bf16[256,512]{1,0:T(8,128)(2,1)S(1)} %embed_rows.1.refs_0_, bf16[256,512]{1,0:T(8,128)(2,1)S(1)} %collective-permute-done.5.refs_1_, bf16[256,512]{1,0:T(8,128)(2,1)S(1)} %collective-permute-done.6.refs_2_, ...), custom_call_target="tpu_custom_call" | custom-call | flops 31457280 | bytes 217088 | tf_op jit(solution)/shard_map/project/pallas_call | solution.py:174
  24.3 2.6 %collective-permute-done.3.refs_0_ = bf16[256,512]{1,0:T(8,128)(2,1)S(1)} collective-permute-done((bf16[256,512]{1,0:T(8,128)(2,1)S(1)}, bf16[256,512]{1,0:T(8,128)(2,1)S(1)}, u32[]{:S(2)}, u32[]{:S(2)}) %collective-permute-start.3) | collective-permute-done | bytes 262176 | tf_op jit(solution)/shard_map/ppermute | solution.py:644
  27.0 1.5 %collective-permute-start.8 = (bf16[256,512]{1,0:T(8,128)(2,1)S(1)}, bf16[256,512]{1,0:T(8,128)(2,1)S(1)}, u32[]{:S(2)}, u32[]{:S(2)}) collective-permute-start(bf16[256,512]{1,0:T(8,128)(2,1)S(1)} %collective-permute-done.3.refs_0_), channel_id=1, source_target_pairs={{0,4},{1,3},{2,6},{3,1},{4,0},{5,7},{6,2},{7,5},{8,12},{9,11},{10,... | collective-permute-start | bytes 786440 | tf_op jit(solution)/shard_map/ppermute | solution.py:647
  30.4 5.8 %collective-permute-done.8.refs_0_ = bf16[256,512]{1,0:T(8,128)(2,1)S(1)} collective-permute-done((bf16[256,512]{1,0:T(8,128)(2,1)S(1)}, bf16[256,512]{1,0:T(8,128)(2,1)S(1)}, u32[]{:S(2)}, u32[]{:S(2)}) %collective-permute-start.8) | collective-permute-done | bytes 262176 | tf_op jit(solution)/shard_map/ppermute | solution.py:647
  36.8 2.3 %collective-permute-done.12.other_ref = f32[3,256,256]{2,1,0:T(8,128)S(1)} collective-permute-done((f32[3,256,256]{2,1,0:T(8,128)S(1)}, f32[3,256,256]{2,1,0:T(8,128)S(1)}, u32[]{:S(2)}, u32[]{:S(2)}) %collective-permute-start.12) | collective-permute-done | bytes 786464 | tf_op jit(solution)/shard_map/ppermute | solution.py:641
  39.1 3.6 %mixer.1 = (bf16[128,256]{1,0:T(8,128)(2,1)S(1)}, bf16[128,256]{1,0:T(8,128)(2,1)S(1)}, bf16[3,256,256]{2,1,0:T(8,128)(2,1)S(1)}) custom-call(f32[3,256,256]{2,1,0:T(8,128)S(1)} %get-tuple-element.47.keep_ref, f32[3,256,256]{2,1,0:T(8,128)S(1)} %collective-permute-done.12.other_ref, f32[3,7,512]{2,1,0:T(8,128)S(1)} %bitcast.3, f32[16,512]{1,0:T(8,128)S(1)} %copy-done.2, ...), custom_call_target="tpu_custom_call" | custom-call | flops 196608 | bytes 30368 | tf_op jit(solution)/shard_map/mixer/pallas_call | solution.py:174
  45.1 1.1 %collective-permute-start.14 = (bf16[1024,256]{1,0:T(8,128)(2,1)S(1)}, bf16[1024,256]{1,0:T(8,128)(2,1)S(1)}, u32[]{:S(2)}, u32[]{:S(2)}) collective-permute-start(bf16[1024,256]{1,0:T(8,128)(2,1)S(1)} %back_project.5), channel_id=1, source_target_pairs={{0,4},{1,3},{2,6},{3,1},{4,0},{5,7},{6,2},{7,5},{8,12},{9,11},{10,... | collective-permute-start | bytes 1572872 | tf_op jit(solution)/shard_map/ppermute | solution.py:647
  47.2 1.1 %collective-permute-start.16 = (bf16[1024,256]{1,0:T(8,128)(2,1)S(1)}, bf16[1024,256]{1,0:T(8,128)(2,1)S(1)}, u32[]{:S(2)}, u32[]{:S(2)}) collective-permute-start(bf16[1024,256]{1,0:T(8,128)(2,1)S(1)} %back_project.7), channel_id=1, source_target_pairs={{0,4},{1,3},{2,6},{3,1},{4,0},{5,7},{6,2},{7,5},{8,12},{9,11},{10,... | collective-permute-start | bytes 1572872 | tf_op jit(solution)/shard_map/ppermute | solution.py:647
  48.2 1.3 %collective-permute-done.15.other_ref = bf16[128,256]{1,0:T(8,128)(2,1)S(1)} collective-permute-done((bf16[128,256]{1,0:T(8,128)(2,1)S(1)}, bf16[128,256]{1,0:T(8,128)(2,1)S(1)}, u32[]{:S(2)}, u32[]{:S(2)}) %collective-permute-start.15) | collective-permute-done | bytes 65568 | tf_op jit(solution)/shard_map/ppermute | solution.py:641
  50.2 1.8 %back_project.6 = (f32[512,256]{1,0:T(8,128)S(1)}, f32[512,256]{1,0:T(8,128)S(1)}, f32[512,256]{1,0:T(8,128)S(1)}, f32[512,256]{1,0:T(8,128)S(1)}) custom-call(bf16[3,4096,512]{2,1,0:T(8,128)(2,1)S(1)} %load.1.w_ref, bf16[3,256,256]{2,1,0:T(8,128)(2,1)S(1)} %get-tuple-element.50.refs_0_, bf16[3,256,256]{2,1,0:T(8,128)(2,1)S(1)} %collective-permute-done.13.refs_0_.refs_1_), custom_call_target="tpu_custom_call" | custom-call | flops 25165824 | bytes 208896 | tf_op jit(solution)/shard_map/back_project/pallas_call | solution.py:174
  52.0 2.4 %collective-permute-done.14.got_ref = bf16[1024,256]{1,0:T(8,128)(2,1)S(1)} collective-permute-done((bf16[1024,256]{1,0:T(8,128)(2,1)S(1)}, bf16[1024,256]{1,0:T(8,128)(2,1)S(1)}, u32[]{:S(2)}, u32[]{:S(2)}) %collective-permute-start.14) | collective-permute-done | bytes 524320 | tf_op jit(solution)/shard_map/ppermute | solution.py:647
  54.4 1.1 %collective-permute-start.18 = (bf16[512,256]{1,0:T(8,128)(2,1)S(1)}, bf16[512,256]{1,0:T(8,128)(2,1)S(1)}, u32[]{:S(2)}, u32[]{:S(2)}) collective-permute-start(bf16[512,256]{1,0:T(8,128)(2,1)S(1)} %get-tuple-element.63), channel_id=1, source_target_pairs={{0,2},{1,5},{2,0},{3,7},{4,6},{5,1},{6,4},{7,3},{8,10},{9,13},{10,... | collective-permute-start | bytes 786440 | tf_op jit(solution)/shard_map/ppermute | solution.py:644
  56.5 6.9 %collective-permute-done.16.other_ref = bf16[1024,256]{1,0:T(8,128)(2,1)S(1)} collective-permute-done((bf16[1024,256]{1,0:T(8,128)(2,1)S(1)}, bf16[1024,256]{1,0:T(8,128)(2,1)S(1)}, u32[]{:S(2)}, u32[]{:S(2)}) %collective-permute-start.16) | collective-permute-done | bytes 524320 | tf_op jit(solution)/shard_map/ppermute | solution.py:647
  63.7 4.0 %collective-permute-start.20 = (bf16[512,128]{1,0:T(8,128)(2,1)S(1)}, bf16[512,128]{1,0:T(8,128)(2,1)S(1)}, u32[]{:S(2)}, u32[]{:S(2)}) collective-permute-start(bf16[512,128]{1,0:T(8,128)(2,1)S(1)} %get-tuple-element.65), channel_id=1, source_target_pairs={{0,9},{2,11},{4,13},{6,15},{8,1},{10,3},{12,5},{14,7},{16,8},{18,1... | collective-permute-start | bytes 393224 | tf_op jit(solution)/shard_map/ppermute | solution.py:709
  68.7 5.2 %collective-permute-done.20.b_ref = bf16[512,128]{1,0:T(8,128)(2,1)S(1)} collective-permute-done((bf16[512,128]{1,0:T(8,128)(2,1)S(1)}, bf16[512,128]{1,0:T(8,128)(2,1)S(1)}, u32[]{:S(2)}, u32[]{:S(2)}) %collective-permute-start.20) | collective-permute-done | bytes 131104 | tf_op jit(solution)/shard_map/ppermute | solution.py:709
  73.9 4.9 %collective-permute-done.21.c_ref = bf16[512,128]{1,0:T(8,128)(2,1)S(1)} collective-permute-done((bf16[512,128]{1,0:T(8,128)(2,1)S(1)}, bf16[512,128]{1,0:T(8,128)(2,1)S(1)}, u32[]{:S(2)}, u32[]{:S(2)}) %collective-permute-start.21) | collective-permute-done | bytes 131104 | tf_op jit(solution)/shard_map/ppermute | solution.py:711
  (47 shorter events, 11.8 us)
Async XLA Ops:
  0.6 2.1 %collective-permute-start.1 = (bf16[128,512]{1,0:T(8,128)(2,1)}, bf16[128,512]{1,0:T(8,128)(2,1)S(1)}, u32[]{:S(2)}, u32[]{:S(2)}) collective-permute-start(bf16[128,512]{1,0:T(8,128)(2,1)} %cot_own_ref.1), channel_id=1, source_target_pairs={{0,1},{1,0},{2,3},{3,2},{4,5},{5,4},{6,7},{7,6},{8,9},{9,8},{10,11... | collective-permute-start | bytes 393224 | tf_op jit(solution)/shard_map/ppermute | solution.py:641
  1.1 1.3 %collective-permute-start = (s32[1,128]{1,0:T(1,128)}, s32[1,128]{1,0:T(1,128)S(1)}, u32[]{:S(2)}, u32[]{:S(2)}) collective-permute-start(s32[1,128]{1,0:T(1,128)} %bitcast.5), channel_id=1, source_target_pairs={{0,1},{1,0},{2,3},{3,2},{4,5},{5,4},{6,7},{7,6},{8,9},{9,8},{10,11... | collective-permute-start | bytes 1544 | tf_op jit(solution)/shard_map/ppermute | solution.py:641
  2.8 14.9 %collective-permute-start.2 = (bf16[256,512]{1,0:T(8,128)(2,1)S(1)}, bf16[256,512]{1,0:T(8,128)(2,1)S(1)}, u32[]{:S(2)}, u32[]{:S(2)}) collective-permute-start(bf16[256,512]{1,0:T(8,128)(2,1)S(1)} %embed_rows.1.refs_0_), channel_id=1, source_target_pairs={{0,8},{2,10},{4,12},{6,14},{8,0},{10,2},{12,4},{14,6},{1,16},{3,18... | collective-permute-start | bytes 786440 | tf_op jit(solution)/shard_map/ppermute | solution.py:656
  5.7 15.0 %collective-permute-start.5 = (bf16[256,512]{1,0:T(8,128)(2,1)S(1)}, bf16[256,512]{1,0:T(8,128)(2,1)S(1)}, u32[]{:S(2)}, u32[]{:S(2)}) collective-permute-start(bf16[256,512]{1,0:T(8,128)(2,1)S(1)} %embed_rows.1.refs_0_), channel_id=1, source_target_pairs={{9,16},{11,18},{13,20},{15,22},{1,24},{3,26},{5,28},{7,30},{16,9},... | collective-permute-start | bytes 786440 | tf_op jit(solution)/shard_map/ppermute | solution.py:657
  7.2 14.2 %collective-permute-start.6 = (bf16[256,512]{1,0:T(8,128)(2,1)S(1)}, bf16[256,512]{1,0:T(8,128)(2,1)S(1)}, u32[]{:S(2)}, u32[]{:S(2)}) collective-permute-start(bf16[256,512]{1,0:T(8,128)(2,1)S(1)} %embed_rows.1.refs_0_), channel_id=1, source_target_pairs={{0,4},{1,1},{2,6},{3,3},{4,0},{5,5},{6,2},{7,7},{8,12},{9,9},{10,1... | collective-permute-start | bytes 786440 | tf_op jit(solution)/shard_map/ppermute | solution.py:658
  10.7 11.5 %collective-permute-start.7 = (bf16[256,512]{1,0:T(8,128)(2,1)S(1)}, bf16[256,512]{1,0:T(8,128)(2,1)S(1)}, u32[]{:S(2)}, u32[]{:S(2)}) collective-permute-start(bf16[256,512]{1,0:T(8,128)(2,1)S(1)} %embed_rows.1.refs_0_), channel_id=1, source_target_pairs={{0,6},{1,1},{2,4},{3,3},{4,2},{5,5},{6,0},{7,7},{8,14},{9,9},{10,1... | collective-permute-start | bytes 786440 | tf_op jit(solution)/shard_map/ppermute | solution.py:659
  17.7 9.3 %collective-permute-start.3 = (bf16[256,512]{1,0:T(8,128)(2,1)S(1)}, bf16[256,512]{1,0:T(8,128)(2,1)S(1)}, u32[]{:S(2)}, u32[]{:S(2)}) collective-permute-start(bf16[256,512]{1,0:T(8,128)(2,1)S(1)} %collective-permute-done.2.refs_4_), channel_id=1, source_target_pairs={{0,2},{1,5},{2,0},{3,7},{4,6},{5,1},{6,4},{7,3},{8,10},{9,13},{10,... | collective-permute-start | bytes 786440 | tf_op jit(solution)/shard_map/ppermute | solution.py:644
  19.2 7.8 %collective-permute-start.4 = (bf16[256,512]{1,0:T(8,128)(2,1)S(1)}, bf16[256,512]{1,0:T(8,128)(2,1)S(1)}, u32[]{:S(2)}, u32[]{:S(2)}) collective-permute-start(bf16[256,512]{1,0:T(8,128)(2,1)S(1)} %collective-permute-done.2.refs_4_), channel_id=1, source_target_pairs={{0,4},{1,3},{2,6},{3,1},{4,0},{5,7},{6,2},{7,5},{8,12},{9,11},{10,... | collective-permute-start | bytes 786440 | tf_op jit(solution)/shard_map/ppermute | solution.py:647
  20.7 9.4 %collective-permute-start.10 = (bf16[256,512]{1,0:T(8,128)(2,1)S(1)}, bf16[256,512]{1,0:T(8,128)(2,1)S(1)}, u32[]{:S(2)}, u32[]{:S(2)}) collective-permute-start(bf16[256,512]{1,0:T(8,128)(2,1)S(1)} %collective-permute-done.5.refs_1_), channel_id=1, source_target_pairs={{0,0},{1,3},{2,2},{3,1},{4,4},{5,7},{6,6},{7,5},{8,8},{9,11},{10,1... | collective-permute-start | bytes 786440 | tf_op jit(solution)/shard_map/ppermute | solution.py:663
  21.4 8.8 %collective-permute-start.11 = (bf16[256,512]{1,0:T(8,128)(2,1)S(1)}, bf16[256,512]{1,0:T(8,128)(2,1)S(1)}, u32[]{:S(2)}, u32[]{:S(2)}) collective-permute-start(bf16[256,512]{1,0:T(8,128)(2,1)S(1)} %collective-permute-done.5.refs_1_), channel_id=1, source_target_pairs={{0,0},{1,5},{2,2},{3,7},{4,4},{5,1},{6,6},{7,3},{8,8},{9,13},{10,1... | collective-permute-start | bytes 786440 | tf_op jit(solution)/shard_map/ppermute | solution.py:664
  27.0 9.2 %collective-permute-start.8 = (bf16[256,512]{1,0:T(8,128)(2,1)S(1)}, bf16[256,512]{1,0:T(8,128)(2,1)S(1)}, u32[]{:S(2)}, u32[]{:S(2)}) collective-permute-start(bf16[256,512]{1,0:T(8,128)(2,1)S(1)} %collective-permute-done.3.refs_0_), channel_id=1, source_target_pairs={{0,4},{1,3},{2,6},{3,1},{4,0},{5,7},{6,2},{7,5},{8,12},{9,11},{10,... | collective-permute-start | bytes 786440 | tf_op jit(solution)/shard_map/ppermute | solution.py:647
  28.5 7.7 %collective-permute-start.9 = (bf16[256,512]{1,0:T(8,128)(2,1)S(1)}, bf16[256,512]{1,0:T(8,128)(2,1)S(1)}, u32[]{:S(2)}, u32[]{:S(2)}) collective-permute-start(bf16[256,512]{1,0:T(8,128)(2,1)S(1)} %collective-permute-done.5.refs_1_), channel_id=1, source_target_pairs={{0,0},{1,7},{2,2},{3,5},{4,4},{5,3},{6,6},{7,1},{8,8},{9,15},{10,1... | collective-permute-start | bytes 786440 | tf_op jit(solution)/shard_map/ppermute | solution.py:675
  30.3 8.8 %copy-start = (bf16[128,512]{1,0:T(8,128)(2,1)S(1)}, bf16[128,512]{1,0:T(8,128)(2,1)}, u32[]{:S(2)}) copy-start(bf16[128,512]{1,0:T(8,128)(2,1)} %cot_own_ref.1) | copy-start | bytes 393220
  36.8 2.4 %collective-permute-start.12 = (f32[3,256,256]{2,1,0:T(8,128)S(1)}, f32[3,256,256]{2,1,0:T(8,128)S(1)}, u32[]{:S(2)}, u32[]{:S(2)}) collective-permute-start(f32[3,256,256]{2,1,0:T(8,128)S(1)} %get-tuple-element.48), channel_id=1, source_target_pairs={{0,1},{1,0},{2,3},{3,2},{4,5},{5,4},{6,7},{7,6},{8,9},{9,8},{10,11... | collective-permute-start | bytes 2359304 | tf_op jit(solution)/shard_map/ppermute | solution.py:641
  42.7 1.8 %collective-permute-start.13 = (bf16[3,256,256]{2,1,0:T(8,128)(2,1)S(1)}, bf16[3,256,256]{2,1,0:T(8,128)(2,1)S(1)}, u32[]{:S(2)}, u32[]{:S(2)}) collective-permute-start(bf16[3,256,256]{2,1,0:T(8,128)(2,1)S(1)} %get-tuple-element.50.refs_0_), channel_id=1, source_target_pairs={{0,1},{1,0},{2,3},{3,2},{4,5},{5,4},{6,7},{7,6},{8,9},{9,8},{10,11... | collective-permute-start | bytes 1179656 | tf_op jit(solution)/shard_map/ppermute | solution.py:641
  45.1 9.2 %collective-permute-start.14 = (bf16[1024,256]{1,0:T(8,128)(2,1)S(1)}, bf16[1024,256]{1,0:T(8,128)(2,1)S(1)}, u32[]{:S(2)}, u32[]{:S(2)}) collective-permute-start(bf16[1024,256]{1,0:T(8,128)(2,1)S(1)} %back_project.5), channel_id=1, source_target_pairs={{0,4},{1,3},{2,6},{3,1},{4,0},{5,7},{6,2},{7,5},{8,12},{9,11},{10,... | collective-permute-start | bytes 1572872 | tf_op jit(solution)/shard_map/ppermute | solution.py:647
  47.2 16.3 %collective-permute-start.16 = (bf16[1024,256]{1,0:T(8,128)(2,1)S(1)}, bf16[1024,256]{1,0:T(8,128)(2,1)S(1)}, u32[]{:S(2)}, u32[]{:S(2)}) collective-permute-start(bf16[1024,256]{1,0:T(8,128)(2,1)S(1)} %back_project.7), channel_id=1, source_target_pairs={{0,4},{1,3},{2,6},{3,1},{4,0},{5,7},{6,2},{7,5},{8,12},{9,11},{10,... | collective-permute-start | bytes 1572872 | tf_op jit(solution)/shard_map/ppermute | solution.py:647
  48.2 1.3 %collective-permute-start.15 = (bf16[128,256]{1,0:T(8,128)(2,1)S(1)}, bf16[128,256]{1,0:T(8,128)(2,1)S(1)}, u32[]{:S(2)}, u32[]{:S(2)}) collective-permute-start(bf16[128,256]{1,0:T(8,128)(2,1)S(1)} %get-tuple-element.54), channel_id=1, source_target_pairs={{0,1},{1,0},{2,3},{3,2},{4,5},{5,4},{6,7},{7,6},{8,9},{9,8},{10,11... | collective-permute-start | bytes 196616 | tf_op jit(solution)/shard_map/ppermute | solution.py:641
  54.4 9.0 %collective-permute-start.18 = (bf16[512,256]{1,0:T(8,128)(2,1)S(1)}, bf16[512,256]{1,0:T(8,128)(2,1)S(1)}, u32[]{:S(2)}, u32[]{:S(2)}) collective-permute-start(bf16[512,256]{1,0:T(8,128)(2,1)S(1)} %get-tuple-element.63), channel_id=1, source_target_pairs={{0,2},{1,5},{2,0},{3,7},{4,6},{5,1},{6,4},{7,3},{8,10},{9,13},{10,... | collective-permute-start | bytes 786440 | tf_op jit(solution)/shard_map/ppermute | solution.py:644
  55.6 12.2 %collective-permute-start.17 = (bf16[512,256]{1,0:T(8,128)(2,1)S(1)}, bf16[512,256]{1,0:T(8,128)(2,1)S(1)}, u32[]{:S(2)}, u32[]{:S(2)}) collective-permute-start(bf16[512,256]{1,0:T(8,128)(2,1)S(1)} %get-tuple-element.60), channel_id=1, source_target_pairs={{0,2},{1,5},{2,0},{3,7},{4,6},{5,1},{6,4},{7,3},{8,10},{9,13},{10,... | collective-permute-start | bytes 786440 | tf_op jit(solution)/shard_map/ppermute | solution.py:644
  63.6 5.0 %collective-permute-start.19 = (bf16[512,128]{1,0:T(8,128)(2,1)S(1)}, bf16[512,128]{1,0:T(8,128)(2,1)S(1)}, u32[]{:S(2)}, u32[]{:S(2)}) collective-permute-start(bf16[512,128]{1,0:T(8,128)(2,1)S(1)} %get-tuple-element.64), channel_id=1, source_target_pairs={{0,8},{2,10},{4,12},{6,14},{8,0},{10,2},{12,4},{14,6},{16,9},{18,1... | collective-permute-start | bytes 393224 | tf_op jit(solution)/shard_map/ppermute | solution.py:709
  63.7 10.2 %collective-permute-start.20 = (bf16[512,128]{1,0:T(8,128)(2,1)S(1)}, bf16[512,128]{1,0:T(8,128)(2,1)S(1)}, u32[]{:S(2)}, u32[]{:S(2)}) collective-permute-start(bf16[512,128]{1,0:T(8,128)(2,1)S(1)} %get-tuple-element.65), channel_id=1, source_target_pairs={{0,9},{2,11},{4,13},{6,15},{8,1},{10,3},{12,5},{14,7},{16,8},{18,1... | collective-permute-start | bytes 393224 | tf_op jit(solution)/shard_map/ppermute | solution.py:709
  67.9 10.9 %collective-permute-start.21 = (bf16[512,128]{1,0:T(8,128)(2,1)S(1)}, bf16[512,128]{1,0:T(8,128)(2,1)S(1)}, u32[]{:S(2)}, u32[]{:S(2)}) collective-permute-start(bf16[512,128]{1,0:T(8,128)(2,1)S(1)} %get-tuple-element.66), channel_id=1, source_target_pairs={{0,1},{2,3},{4,5},{6,7},{8,9},{10,11},{12,13},{14,15},{16,0},{18,2... | collective-permute-start | bytes 393224 | tf_op jit(solution)/shard_map/ppermute | solution.py:711
  68.0 10.8 %collective-permute-start.22 = (bf16[512,128]{1,0:T(8,128)(2,1)S(1)}, bf16[512,128]{1,0:T(8,128)(2,1)S(1)}, u32[]{:S(2)}, u32[]{:S(2)}) collective-permute-start(bf16[512,128]{1,0:T(8,128)(2,1)S(1)} %get-tuple-element.67), channel_id=1, source_target_pairs={{16,1},{18,3},{20,5},{22,7},{24,9},{26,11},{28,13},{30,15},{9,24},... | collective-permute-start | bytes 393224 | tf_op jit(solution)/shard_map/ppermute | solution.py:711
  (3 other events, 26.3 us)

commit v10 on v9

--- a/solution.py
+++ b/solution.py
@@ -660,21 +660,27 @@
     w = load(jnp.transpose(w_in, (1, 0, 2)))
     came, w = lax.optimization_barrier((came, w))
     first, other = first_way(came), other_way(came)
-    x_2 = lax.ppermute(more, BOTH, OUTER_X)
-    y_2 = lax.ppermute(more, BOTH, OUTER_Y)
     sums = project(
-        [embedded, more, near_y, near_d, came],
-        [(0, 1, None), (1, 1, "x"), (2, 1, "y"), (3, 1, 2), (4, 2, None)],
-        [(4, 1, None), (1, 2, None)],
+        [embedded, near_y, near_d, came],
+        [(0, 1, None), (1, 1, "y"), (2, 1, 2), (3, 2, None)],
+        [(3, 1, None)],
         w,
         None,
         False,
     )
-    first, other, more, sums = lax.optimization_barrier((first, other, more, sums))
+    more, sums = lax.optimization_barrier((more, sums))
+    x_2 = lax.ppermute(more, BOTH, OUTER_X)
+    y_2 = lax.ppermute(more, BOTH, OUTER_Y)
+    first, other, more = lax.optimization_barrier((first, other, more))
     both = other_way(first)
     d_2 = lax.ppermute(more, BOTH, OUTER_XY)
     sums = project(
-        [first, other], [(0, 2, 0), (1, 2, 1)], [(0, 1, 0), (1, 1, 1)], w, sums, False
+        [first, other, more],
+        [(0, 2, 0), (1, 2, 1), (2, 1, "x")],
+        [(0, 1, 0), (1, 1, 1), (2, 2, None)],
+        w,
+        sums,
+        False,
     )
     sums = project([x_2, y_2], [], [(0, 2, "x"), (1, 2, "y")], w, sums, False)
     both, d_2, sums = lax.optimization_barrier((both, d_2, sums))

time: 80.7 us -> 79.6 us (0.986)
  waiting for transfers between devices: 32.6 us -> 30 us
  starting transfers between devices: 26.8 us -> 29.2 us
    ppermute x4, waiting for transfers between devices: 10.2 us -> 7.54 us  [chip_plan(): lax.ppermute(a, BOTH, pairs)]
    ppermute x3, waiting for transfers between devices: 2.64 us -> 0.35 us  [first_way(): return lax.ppermute(array, BOTH, FIRST_WAY)]
    ppermute x4, waiting for transfers between devices: 15.1 us -> 17.4 us  [other_way(): return lax.ppermute(array, BOTH, OTHER_WAY)]
    ppermute x4, starting transfers between devices: 4.84 us -> 7.09 us  [chip_plan(): lax.ppermute(a, BOTH, pairs)]
    ppermute x1, starting transfers between devices: 2.39 us -> 4.34 us  [chip_plan(): near_d = lax.ppermute(embedded, BOTH, INNER_XY)]
    ppermute x1, starting transfers between devices: 3.42 us -> 2.41 us  [chip_plan(): near_y = lax.ppermute(embedded, BOTH, INNER_Y)]
    ppermute x1, starting transfers between devices: 1.49 us -> 0.6 us  [chip_plan(): more = lax.ppermute(embedded, BOTH, OUTER_Z_INNER_X)]
where the time goes in v10:
time: 79.6 us; the launch traced here: 79.3 us
  waiting for transfers between devices  30 us (38%)
  starting transfers between devices  29.2 us (37%)
  Pallas kernels  19.3 us (24%)
  between operations  0.89 us (1%)
    ppermute x4, waiting for transfers between devices, other_way(): return lax.ppermute(array, BOTH, OTHER_WAY)  17.4 us
    pallas_call x15, Pallas kernels, small_call(): pl.pallas_call(kernel, in_specs=[IN_VMEM] * len(operands), out_specs=jax....  13.6 us
    ppermute x4, waiting for transfers between devices, chip_plan(): lax.ppermute(a, BOTH, pairs)  7.54 us
    ppermute x4, starting transfers between devices, chip_plan(): lax.ppermute(a, BOTH, pairs)  7.09 us
    ppermute x4, starting transfers between devices, other_way(): return lax.ppermute(array, BOTH, OTHER_WAY)  5.27 us
    ppermute x5, waiting for transfers between devices, swap(): return lax.ppermute(array, BOTH, OTHER_CORE)  4.64 us
    pallas_call x1, Pallas kernels, load(): pl.pallas_call(load_kernel, in_specs=[pl.BlockSpec(memory_space=pltpu.HBM...  4.58 us
    ppermute x1, starting transfers between devices, chip_plan(): near_d = lax.ppermute(embedded, BOTH, INNER_XY)  4.34 us
  transfers between devices with their start and end apart: 23, of which 10 were waited for; matrix products, arithmetic and copies ran while one was open for 0% of the time, Pallas kernels for 17%

profile of v10, /device:TPU:0, one launch (start us, length us, event | category | flops | bytes accessed | tf_op | source)
XLA Modules:
  0.0 79.3 jit_solution(5446975566860946352)
XLA Ops:
  1.2 1.1 %fetch.1 = (s32[1,128]{1,0:T(1,128)S(1)}, bf16[512,512]{1,0:T(8,128)(2,1)S(1)}) custom-call(s32[1,128]{1,0:T(1,128)} %bitcast.6, bf16[512,512]{1,0:T(8,128)(2,1)} %table_ref.1), custom_call_target="tpu_custom_call" | custom-call | bytes 1048576 | tf_op jit(solution)/shard_map/fetch/pallas_call | solution.py:251
  2.8 3.0 %collective-permute-start.2 = (bf16[256,512]{1,0:T(8,128)(2,1)S(1)}, bf16[256,512]{1,0:T(8,128)(2,1)S(1)}, u32[]{:S(2)}, u32[]{:S(2)}) collective-permute-start(bf16[256,512]{1,0:T(8,128)(2,1)S(1)} %embed_rows.1.refs_0_), channel_id=1, source_target_pairs={{0,8},{2,10},{4,12},{6,14},{8,0},{10,2},{12,4},{14,6},{1,16},{3,18... | collective-permute-start | bytes 786440 | tf_op jit(solution)/shard_map/ppermute | solution.py:656
  5.7 4.3 %collective-permute-start.7 = (bf16[256,512]{1,0:T(8,128)(2,1)S(1)}, bf16[256,512]{1,0:T(8,128)(2,1)S(1)}, u32[]{:S(2)}, u32[]{:S(2)}) collective-permute-start(bf16[256,512]{1,0:T(8,128)(2,1)S(1)} %embed_rows.1.refs_0_), channel_id=1, source_target_pairs={{0,6},{1,1},{2,4},{3,3},{4,2},{5,5},{6,0},{7,7},{8,14},{9,9},{10,1... | collective-permute-start | bytes 786440 | tf_op jit(solution)/shard_map/ppermute | solution.py:659
  10.1 2.4 %collective-permute-start.6 = (bf16[256,512]{1,0:T(8,128)(2,1)S(1)}, bf16[256,512]{1,0:T(8,128)(2,1)S(1)}, u32[]{:S(2)}, u32[]{:S(2)}) collective-permute-start(bf16[256,512]{1,0:T(8,128)(2,1)S(1)} %embed_rows.1.refs_0_), channel_id=1, source_target_pairs={{0,4},{1,1},{2,6},{3,3},{4,0},{5,5},{6,2},{7,7},{8,12},{9,9},{10,1... | collective-permute-start | bytes 786440 | tf_op jit(solution)/shard_map/ppermute | solution.py:658
  13.1 4.6 %load.1.w_ref = bf16[3,4096,512]{2,1,0:T(8,128)(2,1)S(1)} custom-call(bf16[3,4096,512]{2,1,0:T(8,128)(2,1)} %bitcast.4), custom_call_target="tpu_custom_call" | custom-call | bytes 25165824 | tf_op jit(solution)/shard_map/load/pallas_call | solution.py:273
  17.7 1.6 %collective-permute-start.4 = (bf16[256,512]{1,0:T(8,128)(2,1)S(1)}, bf16[256,512]{1,0:T(8,128)(2,1)S(1)}, u32[]{:S(2)}, u32[]{:S(2)}) collective-permute-start(bf16[256,512]{1,0:T(8,128)(2,1)S(1)} %collective-permute-done.2.refs_3_), channel_id=1, source_target_pairs={{0,4},{1,3},{2,6},{3,1},{4,0},{5,7},{6,2},{7,5},{8,12},{9,11},{10,... | collective-permute-start | bytes 786440 | tf_op jit(solution)/shard_map/ppermute | solution.py:647
  19.3 1.5 %collective-permute-start.3 = (bf16[256,512]{1,0:T(8,128)(2,1)S(1)}, bf16[256,512]{1,0:T(8,128)(2,1)S(1)}, u32[]{:S(2)}, u32[]{:S(2)}) collective-permute-start(bf16[256,512]{1,0:T(8,128)(2,1)S(1)} %collective-permute-done.2.refs_3_), channel_id=1, source_target_pairs={{0,2},{1,5},{2,0},{3,7},{4,6},{5,1},{6,4},{7,3},{8,10},{9,13},{10,... | collective-permute-start | bytes 786440 | tf_op jit(solution)/shard_map/ppermute | solution.py:644
  20.8 1.8 %project.4.refs_3_ = f32[3,256,512]{2,1,0:T(8,128)S(1)} custom-call(bf16[3,4096,512]{2,1,0:T(8,128)(2,1)S(1)} %load.1.w_ref, bf16[256,512]{1,0:T(8,128)(2,1)S(1)} %embed_rows.1.refs_0_, bf16[256,512]{1,0:T(8,128)(2,1)S(1)} %collective-permute-done.6.refs_1_, bf16[256,512]{1,0:T(8,128)(2,1)S(1)} %collective-permute-done.7.refs_2_, ...), custom_call_target="tpu_custom_call" | custom-call | flops 25165824 | bytes 212992 | tf_op jit(solution)/shard_map/project/pallas_call | solution.py:174
  24.0 2.7 %collective-permute-done.4.refs_1_ = bf16[256,512]{1,0:T(8,128)(2,1)S(1)} collective-permute-done((bf16[256,512]{1,0:T(8,128)(2,1)S(1)}, bf16[256,512]{1,0:T(8,128)(2,1)S(1)}, u32[]{:S(2)}, u32[]{:S(2)}) %collective-permute-start.4) | collective-permute-done | bytes 262176 | tf_op jit(solution)/shard_map/ppermute | solution.py:647
  26.7 1.5 %collective-permute-start.8 = (bf16[256,512]{1,0:T(8,128)(2,1)S(1)}, bf16[256,512]{1,0:T(8,128)(2,1)S(1)}, u32[]{:S(2)}, u32[]{:S(2)}) collective-permute-start(bf16[256,512]{1,0:T(8,128)(2,1)S(1)} %collective-permute-done.3.refs_0_), channel_id=1, source_target_pairs={{0,4},{1,3},{2,6},{3,1},{4,0},{5,7},{6,2},{7,5},{8,12},{9,11},{10,... | collective-permute-start | bytes 786440 | tf_op jit(solution)/shard_map/ppermute | solution.py:647
  28.9 1.4 %project.5.refs_2_ = f32[3,256,512]{2,1,0:T(8,128)S(1)} custom-call(bf16[3,4096,512]{2,1,0:T(8,128)(2,1)S(1)} %load.1.w_ref, bf16[256,512]{1,0:T(8,128)(2,1)S(1)} %collective-permute-done.3.refs_0_, bf16[256,512]{1,0:T(8,128)(2,1)S(1)} %collective-permute-done.4.refs_1_, bf16[256,512]{1,0:T(8,128)(2,1)S(1)} %collective-permute-done.5.refs_2_, ...), custom_call_target="tpu_custom_call" | custom-call | flops 18874368 | bytes 233472 | tf_op jit(solution)/shard_map/project/pallas_call | solution.py:174
  30.5 5.4 %collective-permute-done.8.refs_0_ = bf16[256,512]{1,0:T(8,128)(2,1)S(1)} collective-permute-done((bf16[256,512]{1,0:T(8,128)(2,1)S(1)}, bf16[256,512]{1,0:T(8,128)(2,1)S(1)}, u32[]{:S(2)}, u32[]{:S(2)}) %collective-permute-start.8) | collective-permute-done | bytes 262176 | tf_op jit(solution)/shard_map/ppermute | solution.py:647
  36.5 2.3 %collective-permute-done.12.other_ref = f32[3,256,256]{2,1,0:T(8,128)S(1)} collective-permute-done((f32[3,256,256]{2,1,0:T(8,128)S(1)}, f32[3,256,256]{2,1,0:T(8,128)S(1)}, u32[]{:S(2)}, u32[]{:S(2)}) %collective-permute-start.12) | collective-permute-done | bytes 786464 | tf_op jit(solution)/shard_map/ppermute | solution.py:641
  38.8 3.6 %mixer.1 = (bf16[128,256]{1,0:T(8,128)(2,1)S(1)}, bf16[128,256]{1,0:T(8,128)(2,1)S(1)}, bf16[3,256,256]{2,1,0:T(8,128)(2,1)S(1)}) custom-call(f32[3,256,256]{2,1,0:T(8,128)S(1)} %get-tuple-element.49.keep_ref, f32[3,256,256]{2,1,0:T(8,128)S(1)} %collective-permute-done.12.other_ref, f32[3,7,512]{2,1,0:T(8,128)S(1)} %bitcast.3, f32[16,512]{1,0:T(8,128)S(1)} %copy-done.2, ...), custom_call_target="tpu_custom_call" | custom-call | flops 196608 | bytes 30368 | tf_op jit(solution)/shard_map/mixer/pallas_call | solution.py:174
  43.2 1.0 %collective-permute-done.13.refs_0_.refs_1_ = bf16[3,256,256]{2,1,0:T(8,128)(2,1)S(1)} collective-permute-done((bf16[3,256,256]{2,1,0:T(8,128)(2,1)S(1)}, bf16[3,256,256]{2,1,0:T(8,128)(2,1)S(1)}, u32[]{:S(2)}, u32[]{:S(2)}) %collective-permute-start.13) | collective-permute-done | bytes 393248 | tf_op jit(solution)/shard_map/ppermute | solution.py:641
  44.8 1.6 %collective-permute-start.14 = (bf16[1024,256]{1,0:T(8,128)(2,1)S(1)}, bf16[1024,256]{1,0:T(8,128)(2,1)S(1)}, u32[]{:S(2)}, u32[]{:S(2)}) collective-permute-start(bf16[1024,256]{1,0:T(8,128)(2,1)S(1)} %back_project.5), channel_id=1, source_target_pairs={{0,4},{1,3},{2,6},{3,1},{4,0},{5,7},{6,2},{7,5},{8,12},{9,11},{10,... | collective-permute-start | bytes 1572872 | tf_op jit(solution)/shard_map/ppermute | solution.py:647
  46.4 1.0 %back_project.7 = bf16[1024,256]{1,0:T(8,128)(2,1)S(1)} custom-call(bf16[3,4096,512]{2,1,0:T(8,128)(2,1)S(1)} %load.1.w_ref, bf16[3,256,256]{2,1,0:T(8,128)(2,1)S(1)} %get-tuple-element.52.refs_0_, bf16[3,256,256]{2,1,0:T(8,128)(2,1)S(1)} %collective-permute-done.13.refs_0_.refs_1_), custom_call_target="tpu_custom_call" | custom-call | flops 12582912 | bytes 208896 | tf_op jit(solution)/shard_map/back_project/pallas_call | solution.py:174
  47.9 1.3 %collective-permute-done.15.other_ref = bf16[128,256]{1,0:T(8,128)(2,1)S(1)} collective-permute-done((bf16[128,256]{1,0:T(8,128)(2,1)S(1)}, bf16[128,256]{1,0:T(8,128)(2,1)S(1)}, u32[]{:S(2)}, u32[]{:S(2)}) %collective-permute-start.15) | collective-permute-done | bytes 65568 | tf_op jit(solution)/shard_map/ppermute | solution.py:641
  49.9 1.8 %back_project.6 = (f32[512,256]{1,0:T(8,128)S(1)}, f32[512,256]{1,0:T(8,128)S(1)}, f32[512,256]{1,0:T(8,128)S(1)}, f32[512,256]{1,0:T(8,128)S(1)}) custom-call(bf16[3,4096,512]{2,1,0:T(8,128)(2,1)S(1)} %load.1.w_ref, bf16[3,256,256]{2,1,0:T(8,128)(2,1)S(1)} %get-tuple-element.52.refs_0_, bf16[3,256,256]{2,1,0:T(8,128)(2,1)S(1)} %collective-permute-done.13.refs_0_.refs_1_), custom_call_target="tpu_custom_call" | custom-call | flops 25165824 | bytes 208896 | tf_op jit(solution)/shard_map/back_project/pallas_call | solution.py:174
  51.7 2.4 %collective-permute-done.14.got_ref = bf16[1024,256]{1,0:T(8,128)(2,1)S(1)} collective-permute-done((bf16[1024,256]{1,0:T(8,128)(2,1)S(1)}, bf16[1024,256]{1,0:T(8,128)(2,1)S(1)}, u32[]{:S(2)}, u32[]{:S(2)}) %collective-permute-start.14) | collective-permute-done | bytes 524320 | tf_op jit(solution)/shard_map/ppermute | solution.py:647
  54.1 1.6 %collective-permute-start.17 = (bf16[512,256]{1,0:T(8,128)(2,1)S(1)}, bf16[512,256]{1,0:T(8,128)(2,1)S(1)}, u32[]{:S(2)}, u32[]{:S(2)}) collective-permute-start(bf16[512,256]{1,0:T(8,128)(2,1)S(1)} %get-tuple-element.62), channel_id=1, source_target_pairs={{0,2},{1,5},{2,0},{3,7},{4,6},{5,1},{6,4},{7,3},{8,10},{9,13},{10,... | collective-permute-start | bytes 786440 | tf_op jit(solution)/shard_map/ppermute | solution.py:644
  56.2 6.9 %collective-permute-done.16.other_ref = bf16[1024,256]{1,0:T(8,128)(2,1)S(1)} collective-permute-done((bf16[1024,256]{1,0:T(8,128)(2,1)S(1)}, bf16[1024,256]{1,0:T(8,128)(2,1)S(1)}, u32[]{:S(2)}, u32[]{:S(2)}) %collective-permute-start.16) | collective-permute-done | bytes 524320 | tf_op jit(solution)/shard_map/ppermute | solution.py:647
  65.2 5.7 %collective-permute-start.20 = (bf16[512,128]{1,0:T(8,128)(2,1)S(1)}, bf16[512,128]{1,0:T(8,128)(2,1)S(1)}, u32[]{:S(2)}, u32[]{:S(2)}) collective-permute-start(bf16[512,128]{1,0:T(8,128)(2,1)S(1)} %get-tuple-element.67), channel_id=1, source_target_pairs={{0,9},{2,11},{4,13},{6,15},{8,1},{10,3},{12,5},{14,7},{16,8},{18,1... | collective-permute-start | bytes 393224 | tf_op jit(solution)/shard_map/ppermute | solution.py:715
  71.0 7.5 %collective-permute-done.20.b_ref = bf16[512,128]{1,0:T(8,128)(2,1)S(1)} collective-permute-done((bf16[512,128]{1,0:T(8,128)(2,1)S(1)}, bf16[512,128]{1,0:T(8,128)(2,1)S(1)}, u32[]{:S(2)}, u32[]{:S(2)}) %collective-permute-start.20) | collective-permute-done | bytes 131104 | tf_op jit(solution)/shard_map/ppermute | solution.py:715
  (47 shorter events, 10.5 us)
Async XLA Ops:
  0.6 2.1 %collective-permute-start.1 = (bf16[128,512]{1,0:T(8,128)(2,1)}, bf16[128,512]{1,0:T(8,128)(2,1)S(1)}, u32[]{:S(2)}, u32[]{:S(2)}) collective-permute-start(bf16[128,512]{1,0:T(8,128)(2,1)} %cot_own_ref.1), channel_id=1, source_target_pairs={{0,1},{1,0},{2,3},{3,2},{4,5},{5,4},{6,7},{7,6},{8,9},{9,8},{10,11... | collective-permute-start | bytes 393224 | tf_op jit(solution)/shard_map/ppermute | solution.py:641
  1.1 1.3 %collective-permute-start = (s32[1,128]{1,0:T(1,128)}, s32[1,128]{1,0:T(1,128)S(1)}, u32[]{:S(2)}, u32[]{:S(2)}) collective-permute-start(s32[1,128]{1,0:T(1,128)} %bitcast.5), channel_id=1, source_target_pairs={{0,1},{1,0},{2,3},{3,2},{4,5},{5,4},{6,7},{7,6},{8,9},{9,8},{10,11... | collective-permute-start | bytes 1544 | tf_op jit(solution)/shard_map/ppermute | solution.py:641
  2.8 15.0 %collective-permute-start.2 = (bf16[256,512]{1,0:T(8,128)(2,1)S(1)}, bf16[256,512]{1,0:T(8,128)(2,1)S(1)}, u32[]{:S(2)}, u32[]{:S(2)}) collective-permute-start(bf16[256,512]{1,0:T(8,128)(2,1)S(1)} %embed_rows.1.refs_0_), channel_id=1, source_target_pairs={{0,8},{2,10},{4,12},{6,14},{8,0},{10,2},{12,4},{14,6},{1,16},{3,18... | collective-permute-start | bytes 786440 | tf_op jit(solution)/shard_map/ppermute | solution.py:656
  5.7 15.1 %collective-permute-start.7 = (bf16[256,512]{1,0:T(8,128)(2,1)S(1)}, bf16[256,512]{1,0:T(8,128)(2,1)S(1)}, u32[]{:S(2)}, u32[]{:S(2)}) collective-permute-start(bf16[256,512]{1,0:T(8,128)(2,1)S(1)} %embed_rows.1.refs_0_), channel_id=1, source_target_pairs={{0,6},{1,1},{2,4},{3,3},{4,2},{5,5},{6,0},{7,7},{8,14},{9,9},{10,1... | collective-permute-start | bytes 786440 | tf_op jit(solution)/shard_map/ppermute | solution.py:659
  10.1 10.7 %collective-permute-start.6 = (bf16[256,512]{1,0:T(8,128)(2,1)S(1)}, bf16[256,512]{1,0:T(8,128)(2,1)S(1)}, u32[]{:S(2)}, u32[]{:S(2)}) collective-permute-start(bf16[256,512]{1,0:T(8,128)(2,1)S(1)} %embed_rows.1.refs_0_), channel_id=1, source_target_pairs={{0,4},{1,1},{2,6},{3,3},{4,0},{5,5},{6,2},{7,7},{8,12},{9,9},{10,1... | collective-permute-start | bytes 786440 | tf_op jit(solution)/shard_map/ppermute | solution.py:658
  12.5 10.1 %collective-permute-start.5 = (bf16[256,512]{1,0:T(8,128)(2,1)S(1)}, bf16[256,512]{1,0:T(8,128)(2,1)S(1)}, u32[]{:S(2)}, u32[]{:S(2)}) collective-permute-start(bf16[256,512]{1,0:T(8,128)(2,1)S(1)} %embed_rows.1.refs_0_), channel_id=1, source_target_pairs={{9,16},{11,18},{13,20},{15,22},{1,24},{3,26},{5,28},{7,30},{16,9},... | collective-permute-start | bytes 786440 | tf_op jit(solution)/shard_map/ppermute | solution.py:657
  17.7 8.9 %collective-permute-start.4 = (bf16[256,512]{1,0:T(8,128)(2,1)S(1)}, bf16[256,512]{1,0:T(8,128)(2,1)S(1)}, u32[]{:S(2)}, u32[]{:S(2)}) collective-permute-start(bf16[256,512]{1,0:T(8,128)(2,1)S(1)} %collective-permute-done.2.refs_3_), channel_id=1, source_target_pairs={{0,4},{1,3},{2,6},{3,1},{4,0},{5,7},{6,2},{7,5},{8,12},{9,11},{10,... | collective-permute-start | bytes 786440 | tf_op jit(solution)/shard_map/ppermute | solution.py:647
  19.3 7.4 %collective-permute-start.3 = (bf16[256,512]{1,0:T(8,128)(2,1)S(1)}, bf16[256,512]{1,0:T(8,128)(2,1)S(1)}, u32[]{:S(2)}, u32[]{:S(2)}) collective-permute-start(bf16[256,512]{1,0:T(8,128)(2,1)S(1)} %collective-permute-done.2.refs_3_), channel_id=1, source_target_pairs={{0,2},{1,5},{2,0},{3,7},{4,6},{5,1},{6,4},{7,3},{8,10},{9,13},{10,... | collective-permute-start | bytes 786440 | tf_op jit(solution)/shard_map/ppermute | solution.py:644
  22.6 7.7 %collective-permute-start.11 = (bf16[256,512]{1,0:T(8,128)(2,1)S(1)}, bf16[256,512]{1,0:T(8,128)(2,1)S(1)}, u32[]{:S(2)}, u32[]{:S(2)}) collective-permute-start(bf16[256,512]{1,0:T(8,128)(2,1)S(1)} %collective-permute-done.5.refs_2_), channel_id=1, source_target_pairs={{0,0},{1,5},{2,2},{3,7},{4,4},{5,1},{6,6},{7,3},{8,8},{9,13},{10,1... | collective-permute-start | bytes 786440 | tf_op jit(solution)/shard_map/ppermute | solution.py:673
  23.3 7.0 %collective-permute-start.10 = (bf16[256,512]{1,0:T(8,128)(2,1)S(1)}, bf16[256,512]{1,0:T(8,128)(2,1)S(1)}, u32[]{:S(2)}, u32[]{:S(2)}) collective-permute-start(bf16[256,512]{1,0:T(8,128)(2,1)S(1)} %collective-permute-done.5.refs_2_), channel_id=1, source_target_pairs={{0,0},{1,3},{2,2},{3,1},{4,4},{5,7},{6,6},{7,5},{8,8},{9,11},{10,1... | collective-permute-start | bytes 786440 | tf_op jit(solution)/shard_map/ppermute | solution.py:672
  26.7 9.2 %collective-permute-start.8 = (bf16[256,512]{1,0:T(8,128)(2,1)S(1)}, bf16[256,512]{1,0:T(8,128)(2,1)S(1)}, u32[]{:S(2)}, u32[]{:S(2)}) collective-permute-start(bf16[256,512]{1,0:T(8,128)(2,1)S(1)} %collective-permute-done.3.refs_0_), channel_id=1, source_target_pairs={{0,4},{1,3},{2,6},{3,1},{4,0},{5,7},{6,2},{7,5},{8,12},{9,11},{10,... | collective-permute-start | bytes 786440 | tf_op jit(solution)/shard_map/ppermute | solution.py:647
  28.2 7.7 %collective-permute-start.9 = (bf16[256,512]{1,0:T(8,128)(2,1)S(1)}, bf16[256,512]{1,0:T(8,128)(2,1)S(1)}, u32[]{:S(2)}, u32[]{:S(2)}) collective-permute-start(bf16[256,512]{1,0:T(8,128)(2,1)S(1)} %collective-permute-done.5.refs_2_), channel_id=1, source_target_pairs={{0,0},{1,7},{2,2},{3,5},{4,4},{5,3},{6,6},{7,1},{8,8},{9,15},{10,1... | collective-permute-start | bytes 786440 | tf_op jit(solution)/shard_map/ppermute | solution.py:676
  30.4 8.4 %copy-start = (bf16[128,512]{1,0:T(8,128)(2,1)S(1)}, bf16[128,512]{1,0:T(8,128)(2,1)}, u32[]{:S(2)}) copy-start(bf16[128,512]{1,0:T(8,128)(2,1)} %cot_own_ref.1) | copy-start | bytes 393220
  36.5 2.4 %collective-permute-start.12 = (f32[3,256,256]{2,1,0:T(8,128)S(1)}, f32[3,256,256]{2,1,0:T(8,128)S(1)}, u32[]{:S(2)}, u32[]{:S(2)}) collective-permute-start(f32[3,256,256]{2,1,0:T(8,128)S(1)} %get-tuple-element.50), channel_id=1, source_target_pairs={{0,1},{1,0},{2,3},{3,2},{4,5},{5,4},{6,7},{7,6},{8,9},{9,8},{10,11... | collective-permute-start | bytes 2359304 | tf_op jit(solution)/shard_map/ppermute | solution.py:641
  42.4 1.8 %collective-permute-start.13 = (bf16[3,256,256]{2,1,0:T(8,128)(2,1)S(1)}, bf16[3,256,256]{2,1,0:T(8,128)(2,1)S(1)}, u32[]{:S(2)}, u32[]{:S(2)}) collective-permute-start(bf16[3,256,256]{2,1,0:T(8,128)(2,1)S(1)} %get-tuple-element.52.refs_0_), channel_id=1, source_target_pairs={{0,1},{1,0},{2,3},{3,2},{4,5},{5,4},{6,7},{7,6},{8,9},{9,8},{10,11... | collective-permute-start | bytes 1179656 | tf_op jit(solution)/shard_map/ppermute | solution.py:641
  44.8 9.2 %collective-permute-start.14 = (bf16[1024,256]{1,0:T(8,128)(2,1)S(1)}, bf16[1024,256]{1,0:T(8,128)(2,1)S(1)}, u32[]{:S(2)}, u32[]{:S(2)}) collective-permute-start(bf16[1024,256]{1,0:T(8,128)(2,1)S(1)} %back_project.5), channel_id=1, source_target_pairs={{0,4},{1,3},{2,6},{3,1},{4,0},{5,7},{6,2},{7,5},{8,12},{9,11},{10,... | collective-permute-start | bytes 1572872 | tf_op jit(solution)/shard_map/ppermute | solution.py:647
  47.4 15.8 %collective-permute-start.16 = (bf16[1024,256]{1,0:T(8,128)(2,1)S(1)}, bf16[1024,256]{1,0:T(8,128)(2,1)S(1)}, u32[]{:S(2)}, u32[]{:S(2)}) collective-permute-start(bf16[1024,256]{1,0:T(8,128)(2,1)S(1)} %back_project.7), channel_id=1, source_target_pairs={{0,4},{1,3},{2,6},{3,1},{4,0},{5,7},{6,2},{7,5},{8,12},{9,11},{10,... | collective-permute-start | bytes 1572872 | tf_op jit(solution)/shard_map/ppermute | solution.py:647
  47.9 1.3 %collective-permute-start.15 = (bf16[128,256]{1,0:T(8,128)(2,1)S(1)}, bf16[128,256]{1,0:T(8,128)(2,1)S(1)}, u32[]{:S(2)}, u32[]{:S(2)}) collective-permute-start(bf16[128,256]{1,0:T(8,128)(2,1)S(1)} %get-tuple-element.56), channel_id=1, source_target_pairs={{0,1},{1,0},{2,3},{3,2},{4,5},{5,4},{6,7},{7,6},{8,9},{9,8},{10,11... | collective-permute-start | bytes 196616 | tf_op jit(solution)/shard_map/ppermute | solution.py:641
  54.1 9.0 %collective-permute-start.17 = (bf16[512,256]{1,0:T(8,128)(2,1)S(1)}, bf16[512,256]{1,0:T(8,128)(2,1)S(1)}, u32[]{:S(2)}, u32[]{:S(2)}) collective-permute-start(bf16[512,256]{1,0:T(8,128)(2,1)S(1)} %get-tuple-element.62), channel_id=1, source_target_pairs={{0,2},{1,5},{2,0},{3,7},{4,6},{5,1},{6,4},{7,3},{8,10},{9,13},{10,... | collective-permute-start | bytes 786440 | tf_op jit(solution)/shard_map/ppermute | solution.py:644
  55.7 8.8 %collective-permute-start.18 = (bf16[512,256]{1,0:T(8,128)(2,1)S(1)}, bf16[512,256]{1,0:T(8,128)(2,1)S(1)}, u32[]{:S(2)}, u32[]{:S(2)}) collective-permute-start(bf16[512,256]{1,0:T(8,128)(2,1)S(1)} %get-tuple-element.65), channel_id=1, source_target_pairs={{0,2},{1,5},{2,0},{3,7},{4,6},{5,1},{6,4},{7,3},{8,10},{9,13},{10,... | collective-permute-start | bytes 786440 | tf_op jit(solution)/shard_map/ppermute | solution.py:644
  63.4 7.6 %collective-permute-start.21 = (bf16[512,128]{1,0:T(8,128)(2,1)S(1)}, bf16[512,128]{1,0:T(8,128)(2,1)S(1)}, u32[]{:S(2)}, u32[]{:S(2)}) collective-permute-start(bf16[512,128]{1,0:T(8,128)(2,1)S(1)} %get-tuple-element.68), channel_id=1, source_target_pairs={{0,1},{2,3},{4,5},{6,7},{8,9},{10,11},{12,13},{14,15},{16,0},{18,2... | collective-permute-start | bytes 393224 | tf_op jit(solution)/shard_map/ppermute | solution.py:717
  63.4 7.5 %collective-permute-start.22 = (bf16[512,128]{1,0:T(8,128)(2,1)S(1)}, bf16[512,128]{1,0:T(8,128)(2,1)S(1)}, u32[]{:S(2)}, u32[]{:S(2)}) collective-permute-start(bf16[512,128]{1,0:T(8,128)(2,1)S(1)} %get-tuple-element.69), channel_id=1, source_target_pairs={{16,1},{18,3},{20,5},{22,7},{24,9},{26,11},{28,13},{30,15},{9,24},... | collective-permute-start | bytes 393224 | tf_op jit(solution)/shard_map/ppermute | solution.py:717
  64.6 6.4 %collective-permute-start.19 = (bf16[512,128]{1,0:T(8,128)(2,1)S(1)}, bf16[512,128]{1,0:T(8,128)(2,1)S(1)}, u32[]{:S(2)}, u32[]{:S(2)}) collective-permute-start(bf16[512,128]{1,0:T(8,128)(2,1)S(1)} %get-tuple-element.66), channel_id=1, source_target_pairs={{0,8},{2,10},{4,12},{6,14},{8,0},{10,2},{12,4},{14,6},{16,9},{18,1... | collective-permute-start | bytes 393224 | tf_op jit(solution)/shard_map/ppermute | solution.py:715
  65.2 13.2 %collective-permute-start.20 = (bf16[512,128]{1,0:T(8,128)(2,1)S(1)}, bf16[512,128]{1,0:T(8,128)(2,1)S(1)}, u32[]{:S(2)}, u32[]{:S(2)}) collective-permute-start(bf16[512,128]{1,0:T(8,128)(2,1)S(1)} %get-tuple-element.67), channel_id=1, source_target_pairs={{0,9},{2,11},{4,13},{6,15},{8,1},{10,3},{12,5},{14,7},{16,8},{18,1... | collective-permute-start | bytes 393224 | tf_op jit(solution)/shard_map/ppermute | solution.py:715
  (3 other events, 25.1 us)

commit v11 on v10

--- a/solution.py
+++ b/solution.py
@@ -285,19 +285,18 @@
     return in_vmem(out)
 
 
-def project_kernel(inner, outer, count, has_base, last, w_ref, *refs):
+def project_kernel(inner, outer, count, has_base, part, w_ref, *refs):
     acts = refs[:count]
     groups, _, chans = w_ref.shape
     width = acts[0].shape[1]
-    if last:
+    out_ref = refs[-1]
+    if part is None:
+        some = slice(None)
+    else:
         half = chans // 2
         core = here()[3]
-        outs = [
-            (refs[-2], pl.ds(pl.multiple_of(core * half, half), half)),
-            (refs[-1], pl.ds(pl.multiple_of((1 - core) * half, half), half)),
-        ]
-    else:
-        outs = [(refs[-1], slice(None))]
+        side = core if part == "keep" else 1 - core
+        some = pl.ds(pl.multiple_of(side * half, half), half)
 
     def add(entries):
         spans = [
@@ -305,27 +304,24 @@
             for _, slot, way in entries
         ]
         for g in range(groups):
-            for out, some in outs:
-                total = refs[count][g, :, some] if has_base else None
-                for (which, _, _), span in zip(entries, spans):
-                    term = jnp.dot(
-                        acts[which][...], w_ref[g, span, some], preferred_element_type=f32
-                    )
-                    total = term if total is None else total + term
-                out[g] = total
+            total = refs[count][g, :, some] if has_base else None
+            for (which, _, _), span in zip(entries, spans):
+                term = jnp.dot(acts[which][...], w_ref[g, span, some], preferred_element_type=f32)
+                total = term if total is None else total + term
+            out_ref[g] = total
 
     pl.when(is_inner())(lambda: add(inner))
     pl.when(jnp.logical_not(is_inner()))(lambda: add(outer))
 
 
-def project(acts, inner, outer, w, base, last):
+def project(acts, inner, outer, w, base, part=None):
     groups, _, chans = w.shape
     toks, width = acts[0].shape
-    total = jax.ShapeDtypeStruct((groups, toks, chans), f32)
-    half = jax.ShapeDtypeStruct((groups, toks, chans // 2), f32)
+    if part is not None:
+        chans //= 2
     return small_call(
-        functools.partial(project_kernel, inner, outer, len(acts), base is not None, last),
-        [half, half] if last else total,
+        functools.partial(project_kernel, inner, outer, len(acts), base is not None, part),
+        jax.ShapeDtypeStruct((groups, toks, chans), f32),
         [w] + list(acts) + ([] if base is None else [base]),
         "project",
         2 * max(len(inner), len(outer)) * groups * width * chans * toks,
@@ -413,7 +409,7 @@
             back[k] = parts[0] * flat_cot[pl.ds(k, CHUNKS, stride=apart), :]
             return _
 
-        lax.fori_loop(0, length, filter_step, 0, unroll=4)
+        lax.fori_loop(0, length, filter_step, 0, unroll=8)
 
         rates = rates_ref[:, whole]
         decay_rows = jnp.exp(-rates)
@@ -434,7 +430,7 @@
                 return tuple(decay[m] * states[m] + value for m in range(modes))
 
             zero = jnp.zeros(wide, f32)
-            ends = lax.fori_loop(0, length, end_step, (zero,) * modes, unroll=8)
+            ends = lax.fori_loop(0, length, end_step, (zero,) * modes, unroll=16)
             entering = []
             sign = 1 if forward else -1
             for m in range(modes):
@@ -452,7 +448,7 @@
                 finish(place(k), terms[0])
                 return states
 
-            lax.fori_loop(0, length, out_step, tuple(entering), unroll=4)
+            lax.fori_loop(0, length, out_step, tuple(entering), unroll=8)
 
         def finish_forward(k, total):
             flat[0, pl.ds(k, CHUNKS, stride=apart), :] = filt[0, k] * total
@@ -483,7 +479,7 @@
                 flat[g, pl.ds(k, CHUNKS, stride=apart), :] = total
             return _
 
-        lax.fori_loop(0, length, adjoint_step, 0, unroll=4)
+        lax.fori_loop(0, length, adjoint_step, 0, unroll=8)
         for g in range(groups):
             chunks = [flat[g, s * apart : s * apart + length].astype(bf16) for s in range(CHUNKS)]
             grad_ref[g, some, :] = jnp.concatenate(chunks, axis=0).T
@@ -666,34 +662,30 @@
         [(3, 1, None)],
         w,
         None,
-        False,
     )
     more, sums = lax.optimization_barrier((more, sums))
     x_2 = lax.ppermute(more, BOTH, OUTER_X)
-    y_2 = lax.ppermute(more, BOTH, OUTER_Y)
+    d_2 = lax.ppermute(more, BOTH, OUTER_XY)
     first, other, more = lax.optimization_barrier((first, other, more))
     both = other_way(first)
-    d_2 = lax.ppermute(more, BOTH, OUTER_XY)
+    y_2 = lax.ppermute(more, BOTH, OUTER_Y)
     sums = project(
         [first, other, more],
         [(0, 2, 0), (1, 2, 1), (2, 1, "x")],
         [(0, 1, 0), (1, 1, 1), (2, 2, None)],
         w,
         sums,
-        False,
-    )
-    sums = project([x_2, y_2], [], [(0, 2, "x"), (1, 2, "y")], w, sums, False)
-    both, d_2, sums = lax.optimization_barrier((both, d_2, sums))
-    keep, send = project(
-        [both, d_2],
-        [(0, 2, 2)],
-        [(0, 1, 2), (1, 2, 2)],
-        w,
-        sums,
-        True,
-    )
+    )
+    sums = project([x_2, d_2], [], [(0, 2, "x"), (1, 2, 2)], w, sums)
+    both, y_2, sums = lax.optimization_barrier((both, y_2, sums))
+    inner, outer = [(0, 2, 2)], [(0, 1, 2), (1, 2, "y")]
+    send = project([both, y_2], inner, outer, w, sums, "send")
+    sums, send = lax.optimization_barrier((sums, send))
+    keep = project([both, y_2], inner, outer, w, sums, "keep")
+    got = swap(send)
+    keep, got = lax.optimization_barrier((keep, got))
     mixed_own, mixed_send, grad_own = mixer(
-        keep, swap(send), jnp.transpose(taps, (1, 0, 2)), rates, residues, cotangent, cot_other
+        keep, got, jnp.transpose(taps, (1, 0, 2)), rates, residues, cotangent, cot_other
     )
     grad_other = swap(grad_own)
     mixed_other = swap(mixed_send)

time: 79.6 us -> 78.4 us (0.985)
  starting transfers between devices: 29.2 us -> 28.4 us
    ppermute x3, waiting for transfers between devices: 0.35 us -> 3.08 us  [first_way(): return lax.ppermute(array, BOTH, FIRST_WAY)]
    ppermute x4, waiting for transfers between devices: 17.4 us -> 14.7 us  [other_way(): return lax.ppermute(array, BOTH, OTHER_WAY)]
    ppermute x4, starting transfers between devices: 5.27 us -> 4.31 us  [other_way(): return lax.ppermute(array, BOTH, OTHER_WAY)]
    pallas_call x15 -> x16, Pallas kernels: 13.6 us -> 13.6 us  [small_call(): pl.pallas_call(kernel, in_specs=[IN_VMEM] * len(operands), out_specs=jax....]
  transfers between devices with their start and end apart: 23 -> 23, of which waited for: 10 -> 12; matrix products, arithmetic and copies ran while one was open for 0% -> 0% of each run, Pallas kernels for 17% -> 18%
where the time goes in v11:
time: 78.4 us; the launch traced here: 78.1 us
  waiting for transfers between devices  29.6 us (38%)
  starting transfers between devices  28.4 us (36%)
  Pallas kernels  19.2 us (24%)
  between operations  0.9 us (1%)
    ppermute x4, waiting for transfers between devices, other_way(): return lax.ppermute(array, BOTH, OTHER_WAY)  14.7 us
    pallas_call x16, Pallas kernels, small_call(): pl.pallas_call(kernel, in_specs=[IN_VMEM] * len(operands), out_specs=jax....  13.6 us
    ppermute x4, waiting for transfers between devices, chip_plan(): lax.ppermute(a, BOTH, pairs)  7.58 us
    ppermute x4, starting transfers between devices, chip_plan(): lax.ppermute(a, BOTH, pairs)  7.25 us
    pallas_call x1, Pallas kernels, load(): pl.pallas_call(load_kernel, in_specs=[pl.BlockSpec(memory_space=pltpu.HBM...  4.58 us
    ppermute x1, starting transfers between devices, chip_plan(): near_d = lax.ppermute(embedded, BOTH, INNER_XY)  4.34 us
    ppermute x4, starting transfers between devices, other_way(): return lax.ppermute(array, BOTH, OTHER_WAY)  4.31 us
    ppermute x5, waiting for transfers between devices, swap(): return lax.ppermute(array, BOTH, OTHER_CORE)  4.24 us
  transfers between devices with their start and end apart: 23, of which 12 were waited for; matrix products, arithmetic and copies ran while one was open for 0% of the time, Pallas kernels for 18%

profile of v11, /device:TPU:0, one launch (start us, length us, event | category | flops | bytes accessed | tf_op | source)
XLA Modules:
  0.0 78.1 jit_solution(15795297860380529293)
XLA Ops:
  1.2 1.1 %fetch.1 = (s32[1,128]{1,0:T(1,128)S(1)}, bf16[512,512]{1,0:T(8,128)(2,1)S(1)}) custom-call(s32[1,128]{1,0:T(1,128)} %bitcast.6, bf16[512,512]{1,0:T(8,128)(2,1)} %table_ref.1), custom_call_target="tpu_custom_call" | custom-call | bytes 1048576 | tf_op jit(solution)/shard_map/fetch/pallas_call | solution.py:251
  2.8 3.0 %collective-permute-start.2 = (bf16[256,512]{1,0:T(8,128)(2,1)S(1)}, bf16[256,512]{1,0:T(8,128)(2,1)S(1)}, u32[]{:S(2)}, u32[]{:S(2)}) collective-permute-start(bf16[256,512]{1,0:T(8,128)(2,1)S(1)} %embed_rows.1.refs_0_), channel_id=1, source_target_pairs={{0,8},{2,10},{4,12},{6,14},{8,0},{10,2},{12,4},{14,6},{1,16},{3,18... | collective-permute-start | bytes 786440 | tf_op jit(solution)/shard_map/ppermute | solution.py:652
  5.7 4.3 %collective-permute-start.7 = (bf16[256,512]{1,0:T(8,128)(2,1)S(1)}, bf16[256,512]{1,0:T(8,128)(2,1)S(1)}, u32[]{:S(2)}, u32[]{:S(2)}) collective-permute-start(bf16[256,512]{1,0:T(8,128)(2,1)S(1)} %embed_rows.1.refs_0_), channel_id=1, source_target_pairs={{0,6},{1,1},{2,4},{3,3},{4,2},{5,5},{6,0},{7,7},{8,14},{9,9},{10,1... | collective-permute-start | bytes 786440 | tf_op jit(solution)/shard_map/ppermute | solution.py:655
  10.1 2.4 %collective-permute-start.6 = (bf16[256,512]{1,0:T(8,128)(2,1)S(1)}, bf16[256,512]{1,0:T(8,128)(2,1)S(1)}, u32[]{:S(2)}, u32[]{:S(2)}) collective-permute-start(bf16[256,512]{1,0:T(8,128)(2,1)S(1)} %embed_rows.1.refs_0_), channel_id=1, source_target_pairs={{0,4},{1,1},{2,6},{3,3},{4,0},{5,5},{6,2},{7,7},{8,12},{9,9},{10,1... | collective-permute-start | bytes 786440 | tf_op jit(solution)/shard_map/ppermute | solution.py:654
  13.1 4.6 %load.1.w_ref = bf16[3,4096,512]{2,1,0:T(8,128)(2,1)S(1)} custom-call(bf16[3,4096,512]{2,1,0:T(8,128)(2,1)} %bitcast.4), custom_call_target="tpu_custom_call" | custom-call | bytes 25165824 | tf_op jit(solution)/shard_map/load/pallas_call | solution.py:273
  17.7 1.6 %collective-permute-start.4 = (bf16[256,512]{1,0:T(8,128)(2,1)S(1)}, bf16[256,512]{1,0:T(8,128)(2,1)S(1)}, u32[]{:S(2)}, u32[]{:S(2)}) collective-permute-start(bf16[256,512]{1,0:T(8,128)(2,1)S(1)} %collective-permute-done.2.refs_3_), channel_id=1, source_target_pairs={{0,4},{1,3},{2,6},{3,1},{4,0},{5,7},{6,2},{7,5},{8,12},{9,11},{10,... | collective-permute-start | bytes 786440 | tf_op jit(solution)/shard_map/ppermute | solution.py:643
  19.3 1.5 %collective-permute-start.3 = (bf16[256,512]{1,0:T(8,128)(2,1)S(1)}, bf16[256,512]{1,0:T(8,128)(2,1)S(1)}, u32[]{:S(2)}, u32[]{:S(2)}) collective-permute-start(bf16[256,512]{1,0:T(8,128)(2,1)S(1)} %collective-permute-done.2.refs_3_), channel_id=1, source_target_pairs={{0,2},{1,5},{2,0},{3,7},{4,6},{5,1},{6,4},{7,3},{8,10},{9,13},{10,... | collective-permute-start | bytes 786440 | tf_op jit(solution)/shard_map/ppermute | solution.py:640
  20.8 1.8 %project.5.refs_3_ = f32[3,256,512]{2,1,0:T(8,128)S(1)} custom-call(bf16[3,4096,512]{2,1,0:T(8,128)(2,1)S(1)} %load.1.w_ref, bf16[256,512]{1,0:T(8,128)(2,1)S(1)} %embed_rows.1.refs_0_, bf16[256,512]{1,0:T(8,128)(2,1)S(1)} %collective-permute-done.6.refs_1_, bf16[256,512]{1,0:T(8,128)(2,1)S(1)} %collective-permute-done.7.refs_2_, ...), custom_call_target="tpu_custom_call" | custom-call | flops 25165824 | bytes 212992 | tf_op jit(solution)/shard_map/project/pallas_call | solution.py:174
  24.0 1.8 %collective-permute-done.4.refs_1_ = bf16[256,512]{1,0:T(8,128)(2,1)S(1)} collective-permute-done((bf16[256,512]{1,0:T(8,128)(2,1)S(1)}, bf16[256,512]{1,0:T(8,128)(2,1)S(1)}, u32[]{:S(2)}, u32[]{:S(2)}) %collective-permute-start.4) | collective-permute-done | bytes 262176 | tf_op jit(solution)/shard_map/ppermute | solution.py:643
  25.8 2.7 %collective-permute-done.3.refs_0_ = bf16[256,512]{1,0:T(8,128)(2,1)S(1)} collective-permute-done((bf16[256,512]{1,0:T(8,128)(2,1)S(1)}, bf16[256,512]{1,0:T(8,128)(2,1)S(1)}, u32[]{:S(2)}, u32[]{:S(2)}) %collective-permute-start.3) | collective-permute-done | bytes 262176 | tf_op jit(solution)/shard_map/ppermute | solution.py:640
  29.7 1.4 %project.6.refs_2_ = f32[3,256,512]{2,1,0:T(8,128)S(1)} custom-call(bf16[3,4096,512]{2,1,0:T(8,128)(2,1)S(1)} %load.1.w_ref, bf16[256,512]{1,0:T(8,128)(2,1)S(1)} %collective-permute-done.3.refs_0_, bf16[256,512]{1,0:T(8,128)(2,1)S(1)} %collective-permute-done.4.refs_1_, bf16[256,512]{1,0:T(8,128)(2,1)S(1)} %collective-permute-done.5.refs_2_, ...), custom_call_target="tpu_custom_call" | custom-call | flops 18874368 | bytes 233472 | tf_op jit(solution)/shard_map/project/pallas_call | solution.py:174
  31.3 3.6 %collective-permute-done.8.refs_0_ = bf16[256,512]{1,0:T(8,128)(2,1)S(1)} collective-permute-done((bf16[256,512]{1,0:T(8,128)(2,1)S(1)}, bf16[256,512]{1,0:T(8,128)(2,1)S(1)}, u32[]{:S(2)}, u32[]{:S(2)}) %collective-permute-start.8) | collective-permute-done | bytes 262176 | tf_op jit(solution)/shard_map/ppermute | solution.py:643
  35.8 1.9 %collective-permute-done.12.other_ref = f32[3,256,256]{2,1,0:T(8,128)S(1)} collective-permute-done((f32[3,256,256]{2,1,0:T(8,128)S(1)}, f32[3,256,256]{2,1,0:T(8,128)S(1)}, u32[]{:S(2)}, u32[]{:S(2)}) %collective-permute-start.12) | collective-permute-done | bytes 786464 | tf_op jit(solution)/shard_map/ppermute | solution.py:637
  37.7 3.4 %mixer.1 = (bf16[128,256]{1,0:T(8,128)(2,1)S(1)}, bf16[128,256]{1,0:T(8,128)(2,1)S(1)}, bf16[3,256,256]{2,1,0:T(8,128)(2,1)S(1)}) custom-call(f32[3,256,256]{2,1,0:T(8,128)S(1)} %project.9.keep_ref, f32[3,256,256]{2,1,0:T(8,128)S(1)} %collective-permute-done.12.other_ref, f32[3,7,512]{2,1,0:T(8,128)S(1)} %bitcast.3, f32[16,512]{1,0:T(8,128)S(1)} %copy-done.2, ...), custom_call_target="tpu_custom_call" | custom-call | flops 196608 | bytes 30368 | tf_op jit(solution)/shard_map/mixer/pallas_call | solution.py:174
  41.9 1.0 %collective-permute-done.13.refs_0_.refs_1_ = bf16[3,256,256]{2,1,0:T(8,128)(2,1)S(1)} collective-permute-done((bf16[3,256,256]{2,1,0:T(8,128)(2,1)S(1)}, bf16[3,256,256]{2,1,0:T(8,128)(2,1)S(1)}, u32[]{:S(2)}, u32[]{:S(2)}) %collective-permute-start.13) | collective-permute-done | bytes 393248 | tf_op jit(solution)/shard_map/ppermute | solution.py:637
  45.0 1.6 %collective-permute-start.16 = (bf16[1024,256]{1,0:T(8,128)(2,1)S(1)}, bf16[1024,256]{1,0:T(8,128)(2,1)S(1)}, u32[]{:S(2)}, u32[]{:S(2)}) collective-permute-start(bf16[1024,256]{1,0:T(8,128)(2,1)S(1)} %back_project.7), channel_id=1, source_target_pairs={{0,4},{1,3},{2,6},{3,1},{4,0},{5,7},{6,2},{7,5},{8,12},{9,11},{10,... | collective-permute-start | bytes 1572872 | tf_op jit(solution)/shard_map/ppermute | solution.py:643
  46.6 1.3 %collective-permute-done.15.other_ref = bf16[128,256]{1,0:T(8,128)(2,1)S(1)} collective-permute-done((bf16[128,256]{1,0:T(8,128)(2,1)S(1)}, bf16[128,256]{1,0:T(8,128)(2,1)S(1)}, u32[]{:S(2)}, u32[]{:S(2)}) %collective-permute-start.15) | collective-permute-done | bytes 65568 | tf_op jit(solution)/shard_map/ppermute | solution.py:637
  48.5 1.8 %back_project.6 = (f32[512,256]{1,0:T(8,128)S(1)}, f32[512,256]{1,0:T(8,128)S(1)}, f32[512,256]{1,0:T(8,128)S(1)}, f32[512,256]{1,0:T(8,128)S(1)}) custom-call(bf16[3,4096,512]{2,1,0:T(8,128)(2,1)S(1)} %load.1.w_ref, bf16[3,256,256]{2,1,0:T(8,128)(2,1)S(1)} %get-tuple-element.56.refs_0_, bf16[3,256,256]{2,1,0:T(8,128)(2,1)S(1)} %collective-permute-done.13.refs_0_.refs_1_), custom_call_target="tpu_custom_call" | custom-call | flops 25165824 | bytes 208896 | tf_op jit(solution)/shard_map/back_project/pallas_call | solution.py:174
  50.3 2.4 %collective-permute-done.14.got_ref = bf16[1024,256]{1,0:T(8,128)(2,1)S(1)} collective-permute-done((bf16[1024,256]{1,0:T(8,128)(2,1)S(1)}, bf16[1024,256]{1,0:T(8,128)(2,1)S(1)}, u32[]{:S(2)}, u32[]{:S(2)}) %collective-permute-start.14) | collective-permute-done | bytes 524320 | tf_op jit(solution)/shard_map/ppermute | solution.py:643
  52.8 1.5 %collective-permute-start.17 = (bf16[512,256]{1,0:T(8,128)(2,1)S(1)}, bf16[512,256]{1,0:T(8,128)(2,1)S(1)}, u32[]{:S(2)}, u32[]{:S(2)}) collective-permute-start(bf16[512,256]{1,0:T(8,128)(2,1)S(1)} %get-tuple-element.66), channel_id=1, source_target_pairs={{0,2},{1,5},{2,0},{3,7},{4,6},{5,1},{6,4},{7,3},{8,10},{9,13},{10,... | collective-permute-start | bytes 786440 | tf_op jit(solution)/shard_map/ppermute | solution.py:640
  54.9 6.9 %collective-permute-done.16.other_ref = bf16[1024,256]{1,0:T(8,128)(2,1)S(1)} collective-permute-done((bf16[1024,256]{1,0:T(8,128)(2,1)S(1)}, bf16[1024,256]{1,0:T(8,128)(2,1)S(1)}, u32[]{:S(2)}, u32[]{:S(2)}) %collective-permute-start.16) | collective-permute-done | bytes 524320 | tf_op jit(solution)/shard_map/ppermute | solution.py:643
  63.2 2.9 %collective-permute-start.19 = (bf16[512,128]{1,0:T(8,128)(2,1)S(1)}, bf16[512,128]{1,0:T(8,128)(2,1)S(1)}, u32[]{:S(2)}, u32[]{:S(2)}) collective-permute-start(bf16[512,128]{1,0:T(8,128)(2,1)S(1)} %get-tuple-element.70), channel_id=1, source_target_pairs={{0,8},{2,10},{4,12},{6,14},{8,0},{10,2},{12,4},{14,6},{16,9},{18,1... | collective-permute-start | bytes 393224 | tf_op jit(solution)/shard_map/ppermute | solution.py:707
  66.2 3.6 %collective-permute-start.20 = (bf16[512,128]{1,0:T(8,128)(2,1)S(1)}, bf16[512,128]{1,0:T(8,128)(2,1)S(1)}, u32[]{:S(2)}, u32[]{:S(2)}) collective-permute-start(bf16[512,128]{1,0:T(8,128)(2,1)S(1)} %get-tuple-element.71), channel_id=1, source_target_pairs={{0,9},{2,11},{4,13},{6,15},{8,1},{10,3},{12,5},{14,7},{16,8},{18,1... | collective-permute-start | bytes 393224 | tf_op jit(solution)/shard_map/ppermute | solution.py:707
  69.9 7.5 %collective-permute-done.20.b_ref = bf16[512,128]{1,0:T(8,128)(2,1)S(1)} collective-permute-done((bf16[512,128]{1,0:T(8,128)(2,1)S(1)}, bf16[512,128]{1,0:T(8,128)(2,1)S(1)}, u32[]{:S(2)}, u32[]{:S(2)}) %collective-permute-start.20) | collective-permute-done | bytes 131104 | tf_op jit(solution)/shard_map/ppermute | solution.py:707
  (48 shorter events, 11.8 us)
Async XLA Ops:
  0.6 2.1 %collective-permute-start.1 = (bf16[128,512]{1,0:T(8,128)(2,1)}, bf16[128,512]{1,0:T(8,128)(2,1)S(1)}, u32[]{:S(2)}, u32[]{:S(2)}) collective-permute-start(bf16[128,512]{1,0:T(8,128)(2,1)} %cot_own_ref.1), channel_id=1, source_target_pairs={{0,1},{1,0},{2,3},{3,2},{4,5},{5,4},{6,7},{7,6},{8,9},{9,8},{10,11... | collective-permute-start | bytes 393224 | tf_op jit(solution)/shard_map/ppermute | solution.py:637
  1.1 1.3 %collective-permute-start = (s32[1,128]{1,0:T(1,128)}, s32[1,128]{1,0:T(1,128)S(1)}, u32[]{:S(2)}, u32[]{:S(2)}) collective-permute-start(s32[1,128]{1,0:T(1,128)} %bitcast.5), channel_id=1, source_target_pairs={{0,1},{1,0},{2,3},{3,2},{4,5},{5,4},{6,7},{7,6},{8,9},{9,8},{10,11... | collective-permute-start | bytes 1544 | tf_op jit(solution)/shard_map/ppermute | solution.py:637
  2.8 15.0 %collective-permute-start.2 = (bf16[256,512]{1,0:T(8,128)(2,1)S(1)}, bf16[256,512]{1,0:T(8,128)(2,1)S(1)}, u32[]{:S(2)}, u32[]{:S(2)}) collective-permute-start(bf16[256,512]{1,0:T(8,128)(2,1)S(1)} %embed_rows.1.refs_0_), channel_id=1, source_target_pairs={{0,8},{2,10},{4,12},{6,14},{8,0},{10,2},{12,4},{14,6},{1,16},{3,18... | collective-permute-start | bytes 786440 | tf_op jit(solution)/shard_map/ppermute | solution.py:652
  5.7 15.1 %collective-permute-start.7 = (bf16[256,512]{1,0:T(8,128)(2,1)S(1)}, bf16[256,512]{1,0:T(8,128)(2,1)S(1)}, u32[]{:S(2)}, u32[]{:S(2)}) collective-permute-start(bf16[256,512]{1,0:T(8,128)(2,1)S(1)} %embed_rows.1.refs_0_), channel_id=1, source_target_pairs={{0,6},{1,1},{2,4},{3,3},{4,2},{5,5},{6,0},{7,7},{8,14},{9,9},{10,1... | collective-permute-start | bytes 786440 | tf_op jit(solution)/shard_map/ppermute | solution.py:655
  10.1 10.7 %collective-permute-start.6 = (bf16[256,512]{1,0:T(8,128)(2,1)S(1)}, bf16[256,512]{1,0:T(8,128)(2,1)S(1)}, u32[]{:S(2)}, u32[]{:S(2)}) collective-permute-start(bf16[256,512]{1,0:T(8,128)(2,1)S(1)} %embed_rows.1.refs_0_), channel_id=1, source_target_pairs={{0,4},{1,1},{2,6},{3,3},{4,0},{5,5},{6,2},{7,7},{8,12},{9,9},{10,1... | collective-permute-start | bytes 786440 | tf_op jit(solution)/shard_map/ppermute | solution.py:654
  12.5 10.1 %collective-permute-start.5 = (bf16[256,512]{1,0:T(8,128)(2,1)S(1)}, bf16[256,512]{1,0:T(8,128)(2,1)S(1)}, u32[]{:S(2)}, u32[]{:S(2)}) collective-permute-start(bf16[256,512]{1,0:T(8,128)(2,1)S(1)} %embed_rows.1.refs_0_), channel_id=1, source_target_pairs={{9,16},{11,18},{13,20},{15,22},{1,24},{3,26},{5,28},{7,30},{16,9},... | collective-permute-start | bytes 786440 | tf_op jit(solution)/shard_map/ppermute | solution.py:653
  17.7 8.0 %collective-permute-start.4 = (bf16[256,512]{1,0:T(8,128)(2,1)S(1)}, bf16[256,512]{1,0:T(8,128)(2,1)S(1)}, u32[]{:S(2)}, u32[]{:S(2)}) collective-permute-start(bf16[256,512]{1,0:T(8,128)(2,1)S(1)} %collective-permute-done.2.refs_3_), channel_id=1, source_target_pairs={{0,4},{1,3},{2,6},{3,1},{4,0},{5,7},{6,2},{7,5},{8,12},{9,11},{10,... | collective-permute-start | bytes 786440 | tf_op jit(solution)/shard_map/ppermute | solution.py:643
  19.3 9.2 %collective-permute-start.3 = (bf16[256,512]{1,0:T(8,128)(2,1)S(1)}, bf16[256,512]{1,0:T(8,128)(2,1)S(1)}, u32[]{:S(2)}, u32[]{:S(2)}) collective-permute-start(bf16[256,512]{1,0:T(8,128)(2,1)S(1)} %collective-permute-done.2.refs_3_), channel_id=1, source_target_pairs={{0,2},{1,5},{2,0},{3,7},{4,6},{5,1},{6,4},{7,3},{8,10},{9,13},{10,... | collective-permute-start | bytes 786440 | tf_op jit(solution)/shard_map/ppermute | solution.py:640
  22.6 8.5 %collective-permute-start.11 = (bf16[256,512]{1,0:T(8,128)(2,1)S(1)}, bf16[256,512]{1,0:T(8,128)(2,1)S(1)}, u32[]{:S(2)}, u32[]{:S(2)}) collective-permute-start(bf16[256,512]{1,0:T(8,128)(2,1)S(1)} %collective-permute-done.5.refs_2_), channel_id=1, source_target_pairs={{0,0},{1,7},{2,2},{3,5},{4,4},{5,3},{6,6},{7,1},{8,8},{9,15},{10,1... | collective-permute-start | bytes 786440 | tf_op jit(solution)/shard_map/ppermute | solution.py:668
  23.3 7.9 %collective-permute-start.10 = (bf16[256,512]{1,0:T(8,128)(2,1)S(1)}, bf16[256,512]{1,0:T(8,128)(2,1)S(1)}, u32[]{:S(2)}, u32[]{:S(2)}) collective-permute-start(bf16[256,512]{1,0:T(8,128)(2,1)S(1)} %collective-permute-done.5.refs_2_), channel_id=1, source_target_pairs={{0,0},{1,3},{2,2},{3,1},{4,4},{5,7},{6,6},{7,5},{8,8},{9,11},{10,1... | collective-permute-start | bytes 786440 | tf_op jit(solution)/shard_map/ppermute | solution.py:667
  28.5 6.4 %collective-permute-start.8 = (bf16[256,512]{1,0:T(8,128)(2,1)S(1)}, bf16[256,512]{1,0:T(8,128)(2,1)S(1)}, u32[]{:S(2)}, u32[]{:S(2)}) collective-permute-start(bf16[256,512]{1,0:T(8,128)(2,1)S(1)} %collective-permute-done.3.refs_0_), channel_id=1, source_target_pairs={{0,4},{1,3},{2,6},{3,1},{4,0},{5,7},{6,2},{7,5},{8,12},{9,11},{10,... | collective-permute-start | bytes 786440 | tf_op jit(solution)/shard_map/ppermute | solution.py:643
  29.1 5.8 %collective-permute-start.9 = (bf16[256,512]{1,0:T(8,128)(2,1)S(1)}, bf16[256,512]{1,0:T(8,128)(2,1)S(1)}, u32[]{:S(2)}, u32[]{:S(2)}) collective-permute-start(bf16[256,512]{1,0:T(8,128)(2,1)S(1)} %collective-permute-done.5.refs_2_), channel_id=1, source_target_pairs={{0,0},{1,5},{2,2},{3,7},{4,4},{5,1},{6,6},{7,3},{8,8},{9,13},{10,1... | collective-permute-start | bytes 786440 | tf_op jit(solution)/shard_map/ppermute | solution.py:671
  35.3 2.4 %copy-start = (bf16[128,512]{1,0:T(8,128)(2,1)S(1)}, bf16[128,512]{1,0:T(8,128)(2,1)}, u32[]{:S(2)}) copy-start(bf16[128,512]{1,0:T(8,128)(2,1)} %cot_own_ref.1) | copy-start | bytes 393220
  35.3 2.4 %collective-permute-start.12 = (f32[3,256,256]{2,1,0:T(8,128)S(1)}, f32[3,256,256]{2,1,0:T(8,128)S(1)}, u32[]{:S(2)}, u32[]{:S(2)}) collective-permute-start(f32[3,256,256]{2,1,0:T(8,128)S(1)} %project.8), channel_id=1, source_target_pairs={{0,1},{1,0},{2,3},{3,2},{4,5},{5,4},{6,7},{7,6},{8,9},{9,8},{10,11... | collective-permute-start | bytes 2359304 | tf_op jit(solution)/shard_map/ppermute | solution.py:637
  41.1 1.8 %collective-permute-start.13 = (bf16[3,256,256]{2,1,0:T(8,128)(2,1)S(1)}, bf16[3,256,256]{2,1,0:T(8,128)(2,1)S(1)}, u32[]{:S(2)}, u32[]{:S(2)}) collective-permute-start(bf16[3,256,256]{2,1,0:T(8,128)(2,1)S(1)} %get-tuple-element.56.refs_0_), channel_id=1, source_target_pairs={{0,1},{1,0},{2,3},{3,2},{4,5},{5,4},{6,7},{7,6},{8,9},{9,8},{10,11... | collective-permute-start | bytes 1179656 | tf_op jit(solution)/shard_map/ppermute | solution.py:637
  43.5 9.2 %collective-permute-start.14 = (bf16[1024,256]{1,0:T(8,128)(2,1)S(1)}, bf16[1024,256]{1,0:T(8,128)(2,1)S(1)}, u32[]{:S(2)}, u32[]{:S(2)}) collective-permute-start(bf16[1024,256]{1,0:T(8,128)(2,1)S(1)} %back_project.5), channel_id=1, source_target_pairs={{0,4},{1,3},{2,6},{3,1},{4,0},{5,7},{6,2},{7,5},{8,12},{9,11},{10,... | collective-permute-start | bytes 1572872 | tf_op jit(solution)/shard_map/ppermute | solution.py:643
  45.0 16.8 %collective-permute-start.16 = (bf16[1024,256]{1,0:T(8,128)(2,1)S(1)}, bf16[1024,256]{1,0:T(8,128)(2,1)S(1)}, u32[]{:S(2)}, u32[]{:S(2)}) collective-permute-start(bf16[1024,256]{1,0:T(8,128)(2,1)S(1)} %back_project.7), channel_id=1, source_target_pairs={{0,4},{1,3},{2,6},{3,1},{4,0},{5,7},{6,2},{7,5},{8,12},{9,11},{10,... | collective-permute-start | bytes 1572872 | tf_op jit(solution)/shard_map/ppermute | solution.py:643
  46.6 1.3 %collective-permute-start.15 = (bf16[128,256]{1,0:T(8,128)(2,1)S(1)}, bf16[128,256]{1,0:T(8,128)(2,1)S(1)}, u32[]{:S(2)}, u32[]{:S(2)}) collective-permute-start(bf16[128,256]{1,0:T(8,128)(2,1)S(1)} %get-tuple-element.60), channel_id=1, source_target_pairs={{0,1},{1,0},{2,3},{3,2},{4,5},{5,4},{6,7},{7,6},{8,9},{9,8},{10,11... | collective-permute-start | bytes 196616 | tf_op jit(solution)/shard_map/ppermute | solution.py:637
  52.8 9.0 %collective-permute-start.17 = (bf16[512,256]{1,0:T(8,128)(2,1)S(1)}, bf16[512,256]{1,0:T(8,128)(2,1)S(1)}, u32[]{:S(2)}, u32[]{:S(2)}) collective-permute-start(bf16[512,256]{1,0:T(8,128)(2,1)S(1)} %get-tuple-element.66), channel_id=1, source_target_pairs={{0,2},{1,5},{2,0},{3,7},{4,6},{5,1},{6,4},{7,3},{8,10},{9,13},{10,... | collective-permute-start | bytes 786440 | tf_op jit(solution)/shard_map/ppermute | solution.py:640
  54.3 8.8 %collective-permute-start.18 = (bf16[512,256]{1,0:T(8,128)(2,1)S(1)}, bf16[512,256]{1,0:T(8,128)(2,1)S(1)}, u32[]{:S(2)}, u32[]{:S(2)}) collective-permute-start(bf16[512,256]{1,0:T(8,128)(2,1)S(1)} %get-tuple-element.69), channel_id=1, source_target_pairs={{0,2},{1,5},{2,0},{3,7},{4,6},{5,1},{6,4},{7,3},{8,10},{9,13},{10,... | collective-permute-start | bytes 786440 | tf_op jit(solution)/shard_map/ppermute | solution.py:640
  62.0 7.8 %collective-permute-start.21 = (bf16[512,128]{1,0:T(8,128)(2,1)S(1)}, bf16[512,128]{1,0:T(8,128)(2,1)S(1)}, u32[]{:S(2)}, u32[]{:S(2)}) collective-permute-start(bf16[512,128]{1,0:T(8,128)(2,1)S(1)} %get-tuple-element.72), channel_id=1, source_target_pairs={{0,1},{2,3},{4,5},{6,7},{8,9},{10,11},{12,13},{14,15},{16,0},{18,2... | collective-permute-start | bytes 393224 | tf_op jit(solution)/shard_map/ppermute | solution.py:709
  62.1 7.7 %collective-permute-start.22 = (bf16[512,128]{1,0:T(8,128)(2,1)S(1)}, bf16[512,128]{1,0:T(8,128)(2,1)S(1)}, u32[]{:S(2)}, u32[]{:S(2)}) collective-permute-start(bf16[512,128]{1,0:T(8,128)(2,1)S(1)} %get-tuple-element.73), channel_id=1, source_target_pairs={{16,1},{18,3},{20,5},{22,7},{24,9},{26,11},{28,13},{30,15},{9,24},... | collective-permute-start | bytes 393224 | tf_op jit(solution)/shard_map/ppermute | solution.py:709
  63.2 6.6 %collective-permute-start.19 = (bf16[512,128]{1,0:T(8,128)(2,1)S(1)}, bf16[512,128]{1,0:T(8,128)(2,1)S(1)}, u32[]{:S(2)}, u32[]{:S(2)}) collective-permute-start(bf16[512,128]{1,0:T(8,128)(2,1)S(1)} %get-tuple-element.70), channel_id=1, source_target_pairs={{0,8},{2,10},{4,12},{6,14},{8,0},{10,2},{12,4},{14,6},{16,9},{18,1... | collective-permute-start | bytes 393224 | tf_op jit(solution)/shard_map/ppermute | solution.py:707
  66.2 11.2 %collective-permute-start.20 = (bf16[512,128]{1,0:T(8,128)(2,1)S(1)}, bf16[512,128]{1,0:T(8,128)(2,1)S(1)}, u32[]{:S(2)}, u32[]{:S(2)}) collective-permute-start(bf16[512,128]{1,0:T(8,128)(2,1)S(1)} %get-tuple-element.71), channel_id=1, source_target_pairs={{0,9},{2,11},{4,13},{6,15},{8,1},{10,3},{12,5},{14,7},{16,8},{18,1... | collective-permute-start | bytes 393224 | tf_op jit(solution)/shard_map/ppermute | solution.py:707
  (3 other events, 7.2 us)

commit v12 on v11

--- a/solution.py
+++ b/solution.py
@@ -409,7 +409,7 @@
             back[k] = parts[0] * flat_cot[pl.ds(k, CHUNKS, stride=apart), :]
             return _
 
-        lax.fori_loop(0, length, filter_step, 0, unroll=8)
+        lax.fori_loop(0, length, filter_step, 0, unroll=16)
 
         rates = rates_ref[:, whole]
         decay_rows = jnp.exp(-rates)
@@ -430,7 +430,7 @@
                 return tuple(decay[m] * states[m] + value for m in range(modes))
 
             zero = jnp.zeros(wide, f32)
-            ends = lax.fori_loop(0, length, end_step, (zero,) * modes, unroll=16)
+            ends = lax.fori_loop(0, length, end_step, (zero,) * modes, unroll=32)
             entering = []
             sign = 1 if forward else -1
             for m in range(modes):
@@ -448,7 +448,7 @@
                 finish(place(k), terms[0])
                 return states
 
-            lax.fori_loop(0, length, out_step, tuple(entering), unroll=8)
+            lax.fori_loop(0, length, out_step, tuple(entering), unroll=16)
 
         def finish_forward(k, total):
             flat[0, pl.ds(k, CHUNKS, stride=apart), :] = filt[0, k] * total
@@ -479,7 +479,7 @@
                 flat[g, pl.ds(k, CHUNKS, stride=apart), :] = total
             return _
 
-        lax.fori_loop(0, length, adjoint_step, 0, unroll=8)
+        lax.fori_loop(0, length, adjoint_step, 0, unroll=16)
         for g in range(groups):
             chunks = [flat[g, s * apart : s * apart + length].astype(bf16) for s in range(CHUNKS)]
             grad_ref[g, some, :] = jnp.concatenate(chunks, axis=0).T
@@ -676,12 +676,13 @@
         w,
         sums,
     )
-    sums = project([x_2, d_2], [], [(0, 2, "x"), (1, 2, 2)], w, sums)
-    both, y_2, sums = lax.optimization_barrier((both, y_2, sums))
-    inner, outer = [(0, 2, 2)], [(0, 1, 2), (1, 2, "y")]
-    send = project([both, y_2], inner, outer, w, sums, "send")
+    sums = project([x_2], [], [(0, 2, "x")], w, sums)
+    both, y_2, d_2, sums = lax.optimization_barrier((both, y_2, d_2, sums))
+    acts = [both, y_2, d_2]
+    inner, outer = [(0, 2, 2)], [(0, 1, 2), (1, 2, "y"), (2, 2, 2)]
+    send = project(acts, inner, outer, w, sums, "send")
     sums, send = lax.optimization_barrier((sums, send))
-    keep = project([both, y_2], inner, outer, w, sums, "keep")
+    keep = project(acts, inner, outer, w, sums, "keep")
     got = swap(send)
     keep, got = lax.optimization_barrier((keep, got))
     mixed_own, mixed_send, grad_own = mixer(

time: 78.4 us -> 80.3 us (1.024)
  waiting for transfers between devices: 29.6 us -> 31.7 us
    ppermute x3, waiting for transfers between devices: 3.08 us -> 4.74 us  [first_way(): return lax.ppermute(array, BOTH, FIRST_WAY)]
where the time goes in v12:
time: 80.3 us; the launch traced here: 80.1 us
  waiting for transfers between devices  31.7 us (39%)
  starting transfers between devices  28.4 us (35%)
  Pallas kernels  19.1 us (24%)
  between operations  0.9 us (1%)
    ppermute x4, waiting for transfers between devices, other_way(): return lax.ppermute(array, BOTH, OTHER_WAY)  15 us
    pallas_call x16, Pallas kernels, small_call(): pl.pallas_call(kernel, in_specs=[IN_VMEM] * len(operands), out_specs=jax....  13.4 us
    ppermute x4, waiting for transfers between devices, chip_plan(): lax.ppermute(a, BOTH, pairs)  7.7 us
    ppermute x4, starting transfers between devices, chip_plan(): lax.ppermute(a, BOTH, pairs)  7.33 us
    ppermute x3, waiting for transfers between devices, first_way(): return lax.ppermute(array, BOTH, FIRST_WAY)  4.74 us
    pallas_call x1, Pallas kernels, load(): pl.pallas_call(load_kernel, in_specs=[pl.BlockSpec(memory_space=pltpu.HBM...  4.58 us
    ppermute x1, starting transfers between devices, chip_plan(): near_d = lax.ppermute(embedded, BOTH, INNER_XY)  4.34 us
    ppermute x4, starting transfers between devices, other_way(): return lax.ppermute(array, BOTH, OTHER_WAY)  4.24 us
  transfers between devices with their start and end apart: 23, of which 12 were waited for; matrix products, arithmetic and copies ran while one was open for 0% of the time, Pallas kernels for 18%

profile of v12, /device:TPU:0, one launch (start us, length us, event | category | flops | bytes accessed | tf_op | source)
XLA Modules:
  0.0 80.1 jit_solution(14813402364371910920)
XLA Ops:
  1.2 1.1 %fetch.1 = (s32[1,128]{1,0:T(1,128)S(1)}, bf16[512,512]{1,0:T(8,128)(2,1)S(1)}) custom-call(s32[1,128]{1,0:T(1,128)} %bitcast.6, bf16[512,512]{1,0:T(8,128)(2,1)} %table_ref.1), custom_call_target="tpu_custom_call" | custom-call | bytes 1048576 | tf_op jit(solution)/shard_map/fetch/pallas_call | solution.py:251
  2.8 3.0 %collective-permute-start.2 = (bf16[256,512]{1,0:T(8,128)(2,1)S(1)}, bf16[256,512]{1,0:T(8,128)(2,1)S(1)}, u32[]{:S(2)}, u32[]{:S(2)}) collective-permute-start(bf16[256,512]{1,0:T(8,128)(2,1)S(1)} %embed_rows.1.refs_0_), channel_id=1, source_target_pairs={{0,8},{2,10},{4,12},{6,14},{8,0},{10,2},{12,4},{14,6},{1,16},{3,18... | collective-permute-start | bytes 786440 | tf_op jit(solution)/shard_map/ppermute | solution.py:652
  5.7 4.3 %collective-permute-start.7 = (bf16[256,512]{1,0:T(8,128)(2,1)S(1)}, bf16[256,512]{1,0:T(8,128)(2,1)S(1)}, u32[]{:S(2)}, u32[]{:S(2)}) collective-permute-start(bf16[256,512]{1,0:T(8,128)(2,1)S(1)} %embed_rows.1.refs_0_), channel_id=1, source_target_pairs={{0,6},{1,1},{2,4},{3,3},{4,2},{5,5},{6,0},{7,7},{8,14},{9,9},{10,1... | collective-permute-start | bytes 786440 | tf_op jit(solution)/shard_map/ppermute | solution.py:655
  10.1 2.4 %collective-permute-start.6 = (bf16[256,512]{1,0:T(8,128)(2,1)S(1)}, bf16[256,512]{1,0:T(8,128)(2,1)S(1)}, u32[]{:S(2)}, u32[]{:S(2)}) collective-permute-start(bf16[256,512]{1,0:T(8,128)(2,1)S(1)} %embed_rows.1.refs_0_), channel_id=1, source_target_pairs={{0,4},{1,1},{2,6},{3,3},{4,0},{5,5},{6,2},{7,7},{8,12},{9,9},{10,1... | collective-permute-start | bytes 786440 | tf_op jit(solution)/shard_map/ppermute | solution.py:654
  13.1 4.6 %load.1.w_ref = bf16[3,4096,512]{2,1,0:T(8,128)(2,1)S(1)} custom-call(bf16[3,4096,512]{2,1,0:T(8,128)(2,1)} %bitcast.4), custom_call_target="tpu_custom_call" | custom-call | bytes 25165824 | tf_op jit(solution)/shard_map/load/pallas_call | solution.py:273
  17.7 1.6 %collective-permute-start.4 = (bf16[256,512]{1,0:T(8,128)(2,1)S(1)}, bf16[256,512]{1,0:T(8,128)(2,1)S(1)}, u32[]{:S(2)}, u32[]{:S(2)}) collective-permute-start(bf16[256,512]{1,0:T(8,128)(2,1)S(1)} %collective-permute-done.2.refs_3_), channel_id=1, source_target_pairs={{0,4},{1,3},{2,6},{3,1},{4,0},{5,7},{6,2},{7,5},{8,12},{9,11},{10,... | collective-permute-start | bytes 786440 | tf_op jit(solution)/shard_map/ppermute | solution.py:643
  19.3 1.5 %collective-permute-start.3 = (bf16[256,512]{1,0:T(8,128)(2,1)S(1)}, bf16[256,512]{1,0:T(8,128)(2,1)S(1)}, u32[]{:S(2)}, u32[]{:S(2)}) collective-permute-start(bf16[256,512]{1,0:T(8,128)(2,1)S(1)} %collective-permute-done.2.refs_3_), channel_id=1, source_target_pairs={{0,2},{1,5},{2,0},{3,7},{4,6},{5,1},{6,4},{7,3},{8,10},{9,13},{10,... | collective-permute-start | bytes 786440 | tf_op jit(solution)/shard_map/ppermute | solution.py:640
  20.8 1.8 %project.5.refs_3_ = f32[3,256,512]{2,1,0:T(8,128)S(1)} custom-call(bf16[3,4096,512]{2,1,0:T(8,128)(2,1)S(1)} %load.1.w_ref, bf16[256,512]{1,0:T(8,128)(2,1)S(1)} %embed_rows.1.refs_0_, bf16[256,512]{1,0:T(8,128)(2,1)S(1)} %collective-permute-done.6.refs_1_, bf16[256,512]{1,0:T(8,128)(2,1)S(1)} %collective-permute-done.7.refs_2_, ...), custom_call_target="tpu_custom_call" | custom-call | flops 25165824 | bytes 212992 | tf_op jit(solution)/shard_map/project/pallas_call | solution.py:174
  24.2 4.4 %collective-permute-done.3.refs_0_ = bf16[256,512]{1,0:T(8,128)(2,1)S(1)} collective-permute-done((bf16[256,512]{1,0:T(8,128)(2,1)S(1)}, bf16[256,512]{1,0:T(8,128)(2,1)S(1)}, u32[]{:S(2)}, u32[]{:S(2)}) %collective-permute-start.3) | collective-permute-done | bytes 262176 | tf_op jit(solution)/shard_map/ppermute | solution.py:640
  29.7 1.4 %project.6.refs_1_ = f32[3,256,512]{2,1,0:T(8,128)S(1)} custom-call(bf16[3,4096,512]{2,1,0:T(8,128)(2,1)S(1)} %load.1.w_ref, bf16[256,512]{1,0:T(8,128)(2,1)S(1)} %collective-permute-done.3.refs_0_, bf16[256,512]{1,0:T(8,128)(2,1)S(1)} %collective-permute-done.4.refs_1_, bf16[256,512]{1,0:T(8,128)(2,1)S(1)} %collective-permute-done.5.refs_2_, ...), custom_call_target="tpu_custom_call" | custom-call | flops 18874368 | bytes 233472 | tf_op jit(solution)/shard_map/project/pallas_call | solution.py:174
  31.3 5.5 %collective-permute-done.8.refs_0_ = bf16[256,512]{1,0:T(8,128)(2,1)S(1)} collective-permute-done((bf16[256,512]{1,0:T(8,128)(2,1)S(1)}, bf16[256,512]{1,0:T(8,128)(2,1)S(1)}, u32[]{:S(2)}, u32[]{:S(2)}) %collective-permute-start.8) | collective-permute-done | bytes 262176 | tf_op jit(solution)/shard_map/ppermute | solution.py:643
  37.7 1.9 %collective-permute-done.12.other_ref = f32[3,256,256]{2,1,0:T(8,128)S(1)} collective-permute-done((f32[3,256,256]{2,1,0:T(8,128)S(1)}, f32[3,256,256]{2,1,0:T(8,128)S(1)}, u32[]{:S(2)}, u32[]{:S(2)}) %collective-permute-start.12) | collective-permute-done | bytes 786464 | tf_op jit(solution)/shard_map/ppermute | solution.py:637
  39.6 3.2 %mixer.1 = (bf16[128,256]{1,0:T(8,128)(2,1)S(1)}, bf16[128,256]{1,0:T(8,128)(2,1)S(1)}, bf16[3,256,256]{2,1,0:T(8,128)(2,1)S(1)}) custom-call(f32[3,256,256]{2,1,0:T(8,128)S(1)} %project.9.keep_ref, f32[3,256,256]{2,1,0:T(8,128)S(1)} %collective-permute-done.12.other_ref, f32[3,7,512]{2,1,0:T(8,128)S(1)} %bitcast.3, f32[16,512]{1,0:T(8,128)S(1)} %copy-done.2, ...), custom_call_target="tpu_custom_call" | custom-call | flops 196608 | bytes 30368 | tf_op jit(solution)/shard_map/mixer/pallas_call | solution.py:174
  43.6 1.0 %collective-permute-done.13.refs_0_.refs_1_ = bf16[3,256,256]{2,1,0:T(8,128)(2,1)S(1)} collective-permute-done((bf16[3,256,256]{2,1,0:T(8,128)(2,1)S(1)}, bf16[3,256,256]{2,1,0:T(8,128)(2,1)S(1)}, u32[]{:S(2)}, u32[]{:S(2)}) %collective-permute-start.13) | collective-permute-done | bytes 393248 | tf_op jit(solution)/shard_map/ppermute | solution.py:637
  46.6 1.7 %collective-permute-start.16 = (bf16[1024,256]{1,0:T(8,128)(2,1)S(1)}, bf16[1024,256]{1,0:T(8,128)(2,1)S(1)}, u32[]{:S(2)}, u32[]{:S(2)}) collective-permute-start(bf16[1024,256]{1,0:T(8,128)(2,1)S(1)} %back_project.7), channel_id=1, source_target_pairs={{0,4},{1,3},{2,6},{3,1},{4,0},{5,7},{6,2},{7,5},{8,12},{9,11},{10,... | collective-permute-start | bytes 1572872 | tf_op jit(solution)/shard_map/ppermute | solution.py:643
  48.3 1.3 %collective-permute-done.15.other_ref = bf16[128,256]{1,0:T(8,128)(2,1)S(1)} collective-permute-done((bf16[128,256]{1,0:T(8,128)(2,1)S(1)}, bf16[128,256]{1,0:T(8,128)(2,1)S(1)}, u32[]{:S(2)}, u32[]{:S(2)}) %collective-permute-start.15) | collective-permute-done | bytes 65568 | tf_op jit(solution)/shard_map/ppermute | solution.py:637
  50.3 1.8 %back_project.6 = (f32[512,256]{1,0:T(8,128)S(1)}, f32[512,256]{1,0:T(8,128)S(1)}, f32[512,256]{1,0:T(8,128)S(1)}, f32[512,256]{1,0:T(8,128)S(1)}) custom-call(bf16[3,4096,512]{2,1,0:T(8,128)(2,1)S(1)} %load.1.w_ref, bf16[3,256,256]{2,1,0:T(8,128)(2,1)S(1)} %get-tuple-element.58.refs_0_, bf16[3,256,256]{2,1,0:T(8,128)(2,1)S(1)} %collective-permute-done.13.refs_0_.refs_1_), custom_call_target="tpu_custom_call" | custom-call | flops 25165824 | bytes 208896 | tf_op jit(solution)/shard_map/back_project/pallas_call | solution.py:174
  52.0 2.4 %collective-permute-done.14.got_ref = bf16[1024,256]{1,0:T(8,128)(2,1)S(1)} collective-permute-done((bf16[1024,256]{1,0:T(8,128)(2,1)S(1)}, bf16[1024,256]{1,0:T(8,128)(2,1)S(1)}, u32[]{:S(2)}, u32[]{:S(2)}) %collective-permute-start.14) | collective-permute-done | bytes 524320 | tf_op jit(solution)/shard_map/ppermute | solution.py:643
  54.5 1.5 %collective-permute-start.17 = (bf16[512,256]{1,0:T(8,128)(2,1)S(1)}, bf16[512,256]{1,0:T(8,128)(2,1)S(1)}, u32[]{:S(2)}, u32[]{:S(2)}) collective-permute-start(bf16[512,256]{1,0:T(8,128)(2,1)S(1)} %get-tuple-element.68), channel_id=1, source_target_pairs={{0,2},{1,5},{2,0},{3,7},{4,6},{5,1},{6,4},{7,3},{8,10},{9,13},{10,... | collective-permute-start | bytes 786440 | tf_op jit(solution)/shard_map/ppermute | solution.py:640
  56.6 6.9 %collective-permute-done.16.other_ref = bf16[1024,256]{1,0:T(8,128)(2,1)S(1)} collective-permute-done((bf16[1024,256]{1,0:T(8,128)(2,1)S(1)}, bf16[1024,256]{1,0:T(8,128)(2,1)S(1)}, u32[]{:S(2)}, u32[]{:S(2)}) %collective-permute-start.16) | collective-permute-done | bytes 524320 | tf_op jit(solution)/shard_map/ppermute | solution.py:643
  65.0 1.3 %collective-permute-start.19 = (bf16[512,128]{1,0:T(8,128)(2,1)S(1)}, bf16[512,128]{1,0:T(8,128)(2,1)S(1)}, u32[]{:S(2)}, u32[]{:S(2)}) collective-permute-start(bf16[512,128]{1,0:T(8,128)(2,1)S(1)} %get-tuple-element.72), channel_id=1, source_target_pairs={{0,8},{2,10},{4,12},{6,14},{8,0},{10,2},{12,4},{14,6},{16,9},{18,1... | collective-permute-start | bytes 393224 | tf_op jit(solution)/shard_map/ppermute | solution.py:708
  66.2 5.3 %collective-permute-start.20 = (bf16[512,128]{1,0:T(8,128)(2,1)S(1)}, bf16[512,128]{1,0:T(8,128)(2,1)S(1)}, u32[]{:S(2)}, u32[]{:S(2)}) collective-permute-start(bf16[512,128]{1,0:T(8,128)(2,1)S(1)} %get-tuple-element.73), channel_id=1, source_target_pairs={{0,9},{2,11},{4,13},{6,15},{8,1},{10,3},{12,5},{14,7},{16,8},{18,1... | collective-permute-start | bytes 393224 | tf_op jit(solution)/shard_map/ppermute | solution.py:708
  71.6 1.0 %collective-permute-done.21.c_ref = bf16[512,128]{1,0:T(8,128)(2,1)S(1)} collective-permute-done((bf16[512,128]{1,0:T(8,128)(2,1)S(1)}, bf16[512,128]{1,0:T(8,128)(2,1)S(1)}, u32[]{:S(2)}, u32[]{:S(2)}) %collective-permute-start.21) | collective-permute-done | bytes 131104 | tf_op jit(solution)/shard_map/ppermute | solution.py:710
  72.6 6.7 %collective-permute-done.20.b_ref = bf16[512,128]{1,0:T(8,128)(2,1)S(1)} collective-permute-done((bf16[512,128]{1,0:T(8,128)(2,1)S(1)}, bf16[512,128]{1,0:T(8,128)(2,1)S(1)}, u32[]{:S(2)}, u32[]{:S(2)}) %collective-permute-start.20) | collective-permute-done | bytes 131104 | tf_op jit(solution)/shard_map/ppermute | solution.py:708
  (48 shorter events, 11.7 us)
Async XLA Ops:
  0.6 2.1 %collective-permute-start.1 = (bf16[128,512]{1,0:T(8,128)(2,1)}, bf16[128,512]{1,0:T(8,128)(2,1)S(1)}, u32[]{:S(2)}, u32[]{:S(2)}) collective-permute-start(bf16[128,512]{1,0:T(8,128)(2,1)} %cot_own_ref.1), channel_id=1, source_target_pairs={{0,1},{1,0},{2,3},{3,2},{4,5},{5,4},{6,7},{7,6},{8,9},{9,8},{10,11... | collective-permute-start | bytes 393224 | tf_op jit(solution)/shard_map/ppermute | solution.py:637
  1.1 1.3 %collective-permute-start = (s32[1,128]{1,0:T(1,128)}, s32[1,128]{1,0:T(1,128)S(1)}, u32[]{:S(2)}, u32[]{:S(2)}) collective-permute-start(s32[1,128]{1,0:T(1,128)} %bitcast.5), channel_id=1, source_target_pairs={{0,1},{1,0},{2,3},{3,2},{4,5},{5,4},{6,7},{7,6},{8,9},{9,8},{10,11... | collective-permute-start | bytes 1544 | tf_op jit(solution)/shard_map/ppermute | solution.py:637
  2.8 15.0 %collective-permute-start.2 = (bf16[256,512]{1,0:T(8,128)(2,1)S(1)}, bf16[256,512]{1,0:T(8,128)(2,1)S(1)}, u32[]{:S(2)}, u32[]{:S(2)}) collective-permute-start(bf16[256,512]{1,0:T(8,128)(2,1)S(1)} %embed_rows.1.refs_0_), channel_id=1, source_target_pairs={{0,8},{2,10},{4,12},{6,14},{8,0},{10,2},{12,4},{14,6},{1,16},{3,18... | collective-permute-start | bytes 786440 | tf_op jit(solution)/shard_map/ppermute | solution.py:652
  5.7 15.1 %collective-permute-start.7 = (bf16[256,512]{1,0:T(8,128)(2,1)S(1)}, bf16[256,512]{1,0:T(8,128)(2,1)S(1)}, u32[]{:S(2)}, u32[]{:S(2)}) collective-permute-start(bf16[256,512]{1,0:T(8,128)(2,1)S(1)} %embed_rows.1.refs_0_), channel_id=1, source_target_pairs={{0,6},{1,1},{2,4},{3,3},{4,2},{5,5},{6,0},{7,7},{8,14},{9,9},{10,1... | collective-permute-start | bytes 786440 | tf_op jit(solution)/shard_map/ppermute | solution.py:655
  10.1 10.7 %collective-permute-start.6 = (bf16[256,512]{1,0:T(8,128)(2,1)S(1)}, bf16[256,512]{1,0:T(8,128)(2,1)S(1)}, u32[]{:S(2)}, u32[]{:S(2)}) collective-permute-start(bf16[256,512]{1,0:T(8,128)(2,1)S(1)} %embed_rows.1.refs_0_), channel_id=1, source_target_pairs={{0,4},{1,1},{2,6},{3,3},{4,0},{5,5},{6,2},{7,7},{8,12},{9,9},{10,1... | collective-permute-start | bytes 786440 | tf_op jit(solution)/shard_map/ppermute | solution.py:654
  12.5 10.1 %collective-permute-start.5 = (bf16[256,512]{1,0:T(8,128)(2,1)S(1)}, bf16[256,512]{1,0:T(8,128)(2,1)S(1)}, u32[]{:S(2)}, u32[]{:S(2)}) collective-permute-start(bf16[256,512]{1,0:T(8,128)(2,1)S(1)} %embed_rows.1.refs_0_), channel_id=1, source_target_pairs={{9,16},{11,18},{13,20},{15,22},{1,24},{3,26},{5,28},{7,30},{16,9},... | collective-permute-start | bytes 786440 | tf_op jit(solution)/shard_map/ppermute | solution.py:653
  17.7 6.4 %collective-permute-start.4 = (bf16[256,512]{1,0:T(8,128)(2,1)S(1)}, bf16[256,512]{1,0:T(8,128)(2,1)S(1)}, u32[]{:S(2)}, u32[]{:S(2)}) collective-permute-start(bf16[256,512]{1,0:T(8,128)(2,1)S(1)} %collective-permute-done.2.refs_3_), channel_id=1, source_target_pairs={{0,4},{1,3},{2,6},{3,1},{4,0},{5,7},{6,2},{7,5},{8,12},{9,11},{10,... | collective-permute-start | bytes 786440 | tf_op jit(solution)/shard_map/ppermute | solution.py:643
  19.3 9.2 %collective-permute-start.3 = (bf16[256,512]{1,0:T(8,128)(2,1)S(1)}, bf16[256,512]{1,0:T(8,128)(2,1)S(1)}, u32[]{:S(2)}, u32[]{:S(2)}) collective-permute-start(bf16[256,512]{1,0:T(8,128)(2,1)S(1)} %collective-permute-done.2.refs_3_), channel_id=1, source_target_pairs={{0,2},{1,5},{2,0},{3,7},{4,6},{5,1},{6,4},{7,3},{8,10},{9,13},{10,... | collective-permute-start | bytes 786440 | tf_op jit(solution)/shard_map/ppermute | solution.py:640
  22.6 8.5 %collective-permute-start.11 = (bf16[256,512]{1,0:T(8,128)(2,1)S(1)}, bf16[256,512]{1,0:T(8,128)(2,1)S(1)}, u32[]{:S(2)}, u32[]{:S(2)}) collective-permute-start(bf16[256,512]{1,0:T(8,128)(2,1)S(1)} %collective-permute-done.5.refs_2_), channel_id=1, source_target_pairs={{0,0},{1,3},{2,2},{3,1},{4,4},{5,7},{6,6},{7,5},{8,8},{9,11},{10,1... | collective-permute-start | bytes 786440 | tf_op jit(solution)/shard_map/ppermute | solution.py:667
  23.3 8.0 %collective-permute-start.10 = (bf16[256,512]{1,0:T(8,128)(2,1)S(1)}, bf16[256,512]{1,0:T(8,128)(2,1)S(1)}, u32[]{:S(2)}, u32[]{:S(2)}) collective-permute-start(bf16[256,512]{1,0:T(8,128)(2,1)S(1)} %collective-permute-done.5.refs_2_), channel_id=1, source_target_pairs={{0,0},{1,7},{2,2},{3,5},{4,4},{5,3},{6,6},{7,1},{8,8},{9,15},{10,1... | collective-permute-start | bytes 786440 | tf_op jit(solution)/shard_map/ppermute | solution.py:668
  28.6 8.2 %collective-permute-start.8 = (bf16[256,512]{1,0:T(8,128)(2,1)S(1)}, bf16[256,512]{1,0:T(8,128)(2,1)S(1)}, u32[]{:S(2)}, u32[]{:S(2)}) collective-permute-start(bf16[256,512]{1,0:T(8,128)(2,1)S(1)} %collective-permute-done.3.refs_0_), channel_id=1, source_target_pairs={{0,4},{1,3},{2,6},{3,1},{4,0},{5,7},{6,2},{7,5},{8,12},{9,11},{10,... | collective-permute-start | bytes 786440 | tf_op jit(solution)/shard_map/ppermute | solution.py:643
  29.1 7.7 %collective-permute-start.9 = (bf16[256,512]{1,0:T(8,128)(2,1)S(1)}, bf16[256,512]{1,0:T(8,128)(2,1)S(1)}, u32[]{:S(2)}, u32[]{:S(2)}) collective-permute-start(bf16[256,512]{1,0:T(8,128)(2,1)S(1)} %collective-permute-done.5.refs_2_), channel_id=1, source_target_pairs={{0,0},{1,5},{2,2},{3,7},{4,4},{5,1},{6,6},{7,3},{8,8},{9,13},{10,1... | collective-permute-start | bytes 786440 | tf_op jit(solution)/shard_map/ppermute | solution.py:671
  37.2 2.4 %copy-start = (bf16[128,512]{1,0:T(8,128)(2,1)S(1)}, bf16[128,512]{1,0:T(8,128)(2,1)}, u32[]{:S(2)}) copy-start(bf16[128,512]{1,0:T(8,128)(2,1)} %cot_own_ref.1) | copy-start | bytes 393220
  37.2 2.4 %collective-permute-start.12 = (f32[3,256,256]{2,1,0:T(8,128)S(1)}, f32[3,256,256]{2,1,0:T(8,128)S(1)}, u32[]{:S(2)}, u32[]{:S(2)}) collective-permute-start(f32[3,256,256]{2,1,0:T(8,128)S(1)} %project.8), channel_id=1, source_target_pairs={{0,1},{1,0},{2,3},{3,2},{4,5},{5,4},{6,7},{7,6},{8,9},{9,8},{10,11... | collective-permute-start | bytes 2359304 | tf_op jit(solution)/shard_map/ppermute | solution.py:637
  42.8 1.8 %collective-permute-start.13 = (bf16[3,256,256]{2,1,0:T(8,128)(2,1)S(1)}, bf16[3,256,256]{2,1,0:T(8,128)(2,1)S(1)}, u32[]{:S(2)}, u32[]{:S(2)}) collective-permute-start(bf16[3,256,256]{2,1,0:T(8,128)(2,1)S(1)} %get-tuple-element.58.refs_0_), channel_id=1, source_target_pairs={{0,1},{1,0},{2,3},{3,2},{4,5},{5,4},{6,7},{7,6},{8,9},{9,8},{10,11... | collective-permute-start | bytes 1179656 | tf_op jit(solution)/shard_map/ppermute | solution.py:637
  45.2 9.2 %collective-permute-start.14 = (bf16[1024,256]{1,0:T(8,128)(2,1)S(1)}, bf16[1024,256]{1,0:T(8,128)(2,1)S(1)}, u32[]{:S(2)}, u32[]{:S(2)}) collective-permute-start(bf16[1024,256]{1,0:T(8,128)(2,1)S(1)} %back_project.5), channel_id=1, source_target_pairs={{0,4},{1,3},{2,6},{3,1},{4,0},{5,7},{6,2},{7,5},{8,12},{9,11},{10,... | collective-permute-start | bytes 1572872 | tf_op jit(solution)/shard_map/ppermute | solution.py:643
  46.6 16.9 %collective-permute-start.16 = (bf16[1024,256]{1,0:T(8,128)(2,1)S(1)}, bf16[1024,256]{1,0:T(8,128)(2,1)S(1)}, u32[]{:S(2)}, u32[]{:S(2)}) collective-permute-start(bf16[1024,256]{1,0:T(8,128)(2,1)S(1)} %back_project.7), channel_id=1, source_target_pairs={{0,4},{1,3},{2,6},{3,1},{4,0},{5,7},{6,2},{7,5},{8,12},{9,11},{10,... | collective-permute-start | bytes 1572872 | tf_op jit(solution)/shard_map/ppermute | solution.py:643
  48.3 1.3 %collective-permute-start.15 = (bf16[128,256]{1,0:T(8,128)(2,1)S(1)}, bf16[128,256]{1,0:T(8,128)(2,1)S(1)}, u32[]{:S(2)}, u32[]{:S(2)}) collective-permute-start(bf16[128,256]{1,0:T(8,128)(2,1)S(1)} %get-tuple-element.62), channel_id=1, source_target_pairs={{0,1},{1,0},{2,3},{3,2},{4,5},{5,4},{6,7},{7,6},{8,9},{9,8},{10,11... | collective-permute-start | bytes 196616 | tf_op jit(solution)/shard_map/ppermute | solution.py:637
  54.5 9.0 %collective-permute-start.17 = (bf16[512,256]{1,0:T(8,128)(2,1)S(1)}, bf16[512,256]{1,0:T(8,128)(2,1)S(1)}, u32[]{:S(2)}, u32[]{:S(2)}) collective-permute-start(bf16[512,256]{1,0:T(8,128)(2,1)S(1)} %get-tuple-element.68), channel_id=1, source_target_pairs={{0,2},{1,5},{2,0},{3,7},{4,6},{5,1},{6,4},{7,3},{8,10},{9,13},{10,... | collective-permute-start | bytes 786440 | tf_op jit(solution)/shard_map/ppermute | solution.py:640
  56.0 8.8 %collective-permute-start.18 = (bf16[512,256]{1,0:T(8,128)(2,1)S(1)}, bf16[512,256]{1,0:T(8,128)(2,1)S(1)}, u32[]{:S(2)}, u32[]{:S(2)}) collective-permute-start(bf16[512,256]{1,0:T(8,128)(2,1)S(1)} %get-tuple-element.71), channel_id=1, source_target_pairs={{0,2},{1,5},{2,0},{3,7},{4,6},{5,1},{6,4},{7,3},{8,10},{9,13},{10,... | collective-permute-start | bytes 786440 | tf_op jit(solution)/shard_map/ppermute | solution.py:640
  63.7 8.8 %collective-permute-start.21 = (bf16[512,128]{1,0:T(8,128)(2,1)S(1)}, bf16[512,128]{1,0:T(8,128)(2,1)S(1)}, u32[]{:S(2)}, u32[]{:S(2)}) collective-permute-start(bf16[512,128]{1,0:T(8,128)(2,1)S(1)} %get-tuple-element.74), channel_id=1, source_target_pairs={{0,1},{2,3},{4,5},{6,7},{8,9},{10,11},{12,13},{14,15},{16,0},{18,2... | collective-permute-start | bytes 393224 | tf_op jit(solution)/shard_map/ppermute | solution.py:710
  63.8 8.8 %collective-permute-start.22 = (bf16[512,128]{1,0:T(8,128)(2,1)S(1)}, bf16[512,128]{1,0:T(8,128)(2,1)S(1)}, u32[]{:S(2)}, u32[]{:S(2)}) collective-permute-start(bf16[512,128]{1,0:T(8,128)(2,1)S(1)} %get-tuple-element.75), channel_id=1, source_target_pairs={{16,1},{18,3},{20,5},{22,7},{24,9},{26,11},{28,13},{30,15},{9,24},... | collective-permute-start | bytes 393224 | tf_op jit(solution)/shard_map/ppermute | solution.py:710
  65.0 7.6 %collective-permute-start.19 = (bf16[512,128]{1,0:T(8,128)(2,1)S(1)}, bf16[512,128]{1,0:T(8,128)(2,1)S(1)}, u32[]{:S(2)}, u32[]{:S(2)}) collective-permute-start(bf16[512,128]{1,0:T(8,128)(2,1)S(1)} %get-tuple-element.72), channel_id=1, source_target_pairs={{0,8},{2,10},{4,12},{6,14},{8,0},{10,2},{12,4},{14,6},{16,9},{18,1... | collective-permute-start | bytes 393224 | tf_op jit(solution)/shard_map/ppermute | solution.py:708
  66.2 13.0 %collective-permute-start.20 = (bf16[512,128]{1,0:T(8,128)(2,1)S(1)}, bf16[512,128]{1,0:T(8,128)(2,1)S(1)}, u32[]{:S(2)}, u32[]{:S(2)}) collective-permute-start(bf16[512,128]{1,0:T(8,128)(2,1)S(1)} %get-tuple-element.73), channel_id=1, source_target_pairs={{0,9},{2,11},{4,13},{6,15},{8,1},{10,3},{12,5},{14,7},{16,8},{18,1... | collective-permute-start | bytes 393224 | tf_op jit(solution)/shard_map/ppermute | solution.py:708
  (3 other events, 7.2 us)

commit v13 on v12

--- a/solution.py
+++ b/solution.py
@@ -676,10 +676,10 @@
         w,
         sums,
     )
-    sums = project([x_2], [], [(0, 2, "x")], w, sums)
-    both, y_2, d_2, sums = lax.optimization_barrier((both, y_2, d_2, sums))
-    acts = [both, y_2, d_2]
-    inner, outer = [(0, 2, 2)], [(0, 1, 2), (1, 2, "y"), (2, 2, 2)]
+    sums = project([d_2], [], [(0, 2, 2)], w, sums)
+    both, y_2, x_2, sums = lax.optimization_barrier((both, y_2, x_2, sums))
+    acts = [both, y_2, x_2]
+    inner, outer = [(0, 2, 2)], [(0, 1, 2), (1, 2, "y"), (2, 2, "x")]
     send = project(acts, inner, outer, w, sums, "send")
     sums, send = lax.optimization_barrier((sums, send))
     keep = project(acts, inner, outer, w, sums, "keep")

time: 80.3 us -> 78.3 us (0.975)
  waiting for transfers between devices: 31.7 us -> 29.7 us
    ppermute x3, waiting for transfers between devices: 4.74 us -> 3.08 us  [first_way(): return lax.ppermute(array, BOTH, FIRST_WAY)]
where the time goes in v13:
time: 78.3 us; the launch traced here: 78 us
  waiting for transfers between devices  29.7 us (38%)
  starting transfers between devices  28.4 us (36%)
  Pallas kernels  19.1 us (24%)
  between operations  0.9 us (1%)
    ppermute x4, waiting for transfers between devices, other_way(): return lax.ppermute(array, BOTH, OTHER_WAY)  14.7 us
    pallas_call x16, Pallas kernels, small_call(): pl.pallas_call(kernel, in_specs=[IN_VMEM] * len(operands), out_specs=jax....  13.4 us
    ppermute x4, waiting for transfers between devices, chip_plan(): lax.ppermute(a, BOTH, pairs)  7.61 us
    ppermute x4, starting transfers between devices, chip_plan(): lax.ppermute(a, BOTH, pairs)  7.25 us
    pallas_call x1, Pallas kernels, load(): pl.pallas_call(load_kernel, in_specs=[pl.BlockSpec(memory_space=pltpu.HBM...  4.58 us
    ppermute x1, starting transfers between devices, chip_plan(): near_d = lax.ppermute(embedded, BOTH, INNER_XY)  4.34 us
    ppermute x4, starting transfers between devices, other_way(): return lax.ppermute(array, BOTH, OTHER_WAY)  4.31 us
    ppermute x5, waiting for transfers between devices, swap(): return lax.ppermute(array, BOTH, OTHER_CORE)  4.24 us
  transfers between devices with their start and end apart: 23, of which 12 were waited for; matrix products, arithmetic and copies ran while one was open for 0% of the time, Pallas kernels for 18%

profile of v13, /device:TPU:0, one launch (start us, length us, event | category | flops | bytes accessed | tf_op | source)
XLA Modules:
  0.0 78.0 jit_solution(3288934239032292075)
XLA Ops:
  1.2 1.1 %fetch.1 = (s32[1,128]{1,0:T(1,128)S(1)}, bf16[512,512]{1,0:T(8,128)(2,1)S(1)}) custom-call(s32[1,128]{1,0:T(1,128)} %bitcast.6, bf16[512,512]{1,0:T(8,128)(2,1)} %table_ref.1), custom_call_target="tpu_custom_call" | custom-call | bytes 1048576 | tf_op jit(solution)/shard_map/fetch/pallas_call | solution.py:251
  2.8 3.0 %collective-permute-start.2 = (bf16[256,512]{1,0:T(8,128)(2,1)S(1)}, bf16[256,512]{1,0:T(8,128)(2,1)S(1)}, u32[]{:S(2)}, u32[]{:S(2)}) collective-permute-start(bf16[256,512]{1,0:T(8,128)(2,1)S(1)} %embed_rows.1.refs_0_), channel_id=1, source_target_pairs={{0,8},{2,10},{4,12},{6,14},{8,0},{10,2},{12,4},{14,6},{1,16},{3,18... | collective-permute-start | bytes 786440 | tf_op jit(solution)/shard_map/ppermute | solution.py:652
  5.7 4.3 %collective-permute-start.7 = (bf16[256,512]{1,0:T(8,128)(2,1)S(1)}, bf16[256,512]{1,0:T(8,128)(2,1)S(1)}, u32[]{:S(2)}, u32[]{:S(2)}) collective-permute-start(bf16[256,512]{1,0:T(8,128)(2,1)S(1)} %embed_rows.1.refs_0_), channel_id=1, source_target_pairs={{0,6},{1,1},{2,4},{3,3},{4,2},{5,5},{6,0},{7,7},{8,14},{9,9},{10,1... | collective-permute-start | bytes 786440 | tf_op jit(solution)/shard_map/ppermute | solution.py:655
  10.1 2.4 %collective-permute-start.6 = (bf16[256,512]{1,0:T(8,128)(2,1)S(1)}, bf16[256,512]{1,0:T(8,128)(2,1)S(1)}, u32[]{:S(2)}, u32[]{:S(2)}) collective-permute-start(bf16[256,512]{1,0:T(8,128)(2,1)S(1)} %embed_rows.1.refs_0_), channel_id=1, source_target_pairs={{0,4},{1,1},{2,6},{3,3},{4,0},{5,5},{6,2},{7,7},{8,12},{9,9},{10,1... | collective-permute-start | bytes 786440 | tf_op jit(solution)/shard_map/ppermute | solution.py:654
  13.1 4.6 %load.1.w_ref = bf16[3,4096,512]{2,1,0:T(8,128)(2,1)S(1)} custom-call(bf16[3,4096,512]{2,1,0:T(8,128)(2,1)} %bitcast.4), custom_call_target="tpu_custom_call" | custom-call | bytes 25165824 | tf_op jit(solution)/shard_map/load/pallas_call | solution.py:273
  17.7 1.6 %collective-permute-start.4 = (bf16[256,512]{1,0:T(8,128)(2,1)S(1)}, bf16[256,512]{1,0:T(8,128)(2,1)S(1)}, u32[]{:S(2)}, u32[]{:S(2)}) collective-permute-start(bf16[256,512]{1,0:T(8,128)(2,1)S(1)} %collective-permute-done.2.refs_3_), channel_id=1, source_target_pairs={{0,4},{1,3},{2,6},{3,1},{4,0},{5,7},{6,2},{7,5},{8,12},{9,11},{10,... | collective-permute-start | bytes 786440 | tf_op jit(solution)/shard_map/ppermute | solution.py:643
  19.3 1.5 %collective-permute-start.3 = (bf16[256,512]{1,0:T(8,128)(2,1)S(1)}, bf16[256,512]{1,0:T(8,128)(2,1)S(1)}, u32[]{:S(2)}, u32[]{:S(2)}) collective-permute-start(bf16[256,512]{1,0:T(8,128)(2,1)S(1)} %collective-permute-done.2.refs_3_), channel_id=1, source_target_pairs={{0,2},{1,5},{2,0},{3,7},{4,6},{5,1},{6,4},{7,3},{8,10},{9,13},{10,... | collective-permute-start | bytes 786440 | tf_op jit(solution)/shard_map/ppermute | solution.py:640
  20.8 1.8 %project.5.refs_3_ = f32[3,256,512]{2,1,0:T(8,128)S(1)} custom-call(bf16[3,4096,512]{2,1,0:T(8,128)(2,1)S(1)} %load.1.w_ref, bf16[256,512]{1,0:T(8,128)(2,1)S(1)} %embed_rows.1.refs_0_, bf16[256,512]{1,0:T(8,128)(2,1)S(1)} %collective-permute-done.6.refs_1_, bf16[256,512]{1,0:T(8,128)(2,1)S(1)} %collective-permute-done.7.refs_2_, ...), custom_call_target="tpu_custom_call" | custom-call | flops 25165824 | bytes 212992 | tf_op jit(solution)/shard_map/project/pallas_call | solution.py:174
  24.0 1.8 %collective-permute-done.4.refs_1_ = bf16[256,512]{1,0:T(8,128)(2,1)S(1)} collective-permute-done((bf16[256,512]{1,0:T(8,128)(2,1)S(1)}, bf16[256,512]{1,0:T(8,128)(2,1)S(1)}, u32[]{:S(2)}, u32[]{:S(2)}) %collective-permute-start.4) | collective-permute-done | bytes 262176 | tf_op jit(solution)/shard_map/ppermute | solution.py:643
  25.8 2.7 %collective-permute-done.3.refs_0_ = bf16[256,512]{1,0:T(8,128)(2,1)S(1)} collective-permute-done((bf16[256,512]{1,0:T(8,128)(2,1)S(1)}, bf16[256,512]{1,0:T(8,128)(2,1)S(1)}, u32[]{:S(2)}, u32[]{:S(2)}) %collective-permute-start.3) | collective-permute-done | bytes 262176 | tf_op jit(solution)/shard_map/ppermute | solution.py:640
  29.7 1.4 %project.6.refs_1_ = f32[3,256,512]{2,1,0:T(8,128)S(1)} custom-call(bf16[3,4096,512]{2,1,0:T(8,128)(2,1)S(1)} %load.1.w_ref, bf16[256,512]{1,0:T(8,128)(2,1)S(1)} %collective-permute-done.3.refs_0_, bf16[256,512]{1,0:T(8,128)(2,1)S(1)} %collective-permute-done.4.refs_1_, bf16[256,512]{1,0:T(8,128)(2,1)S(1)} %collective-permute-done.5.refs_2_, ...), custom_call_target="tpu_custom_call" | custom-call | flops 18874368 | bytes 233472 | tf_op jit(solution)/shard_map/project/pallas_call | solution.py:174
  31.3 3.6 %collective-permute-done.8.refs_0_ = bf16[256,512]{1,0:T(8,128)(2,1)S(1)} collective-permute-done((bf16[256,512]{1,0:T(8,128)(2,1)S(1)}, bf16[256,512]{1,0:T(8,128)(2,1)S(1)}, u32[]{:S(2)}, u32[]{:S(2)}) %collective-permute-start.8) | collective-permute-done | bytes 262176 | tf_op jit(solution)/shard_map/ppermute | solution.py:643
  35.8 1.9 %collective-permute-done.12.other_ref = f32[3,256,256]{2,1,0:T(8,128)S(1)} collective-permute-done((f32[3,256,256]{2,1,0:T(8,128)S(1)}, f32[3,256,256]{2,1,0:T(8,128)S(1)}, u32[]{:S(2)}, u32[]{:S(2)}) %collective-permute-start.12) | collective-permute-done | bytes 786464 | tf_op jit(solution)/shard_map/ppermute | solution.py:637
  37.7 3.2 %mixer.1 = (bf16[128,256]{1,0:T(8,128)(2,1)S(1)}, bf16[128,256]{1,0:T(8,128)(2,1)S(1)}, bf16[3,256,256]{2,1,0:T(8,128)(2,1)S(1)}) custom-call(f32[3,256,256]{2,1,0:T(8,128)S(1)} %project.9.keep_ref, f32[3,256,256]{2,1,0:T(8,128)S(1)} %collective-permute-done.12.other_ref, f32[3,7,512]{2,1,0:T(8,128)S(1)} %bitcast.3, f32[16,512]{1,0:T(8,128)S(1)} %copy-done.2, ...), custom_call_target="tpu_custom_call" | custom-call | flops 196608 | bytes 30368 | tf_op jit(solution)/shard_map/mixer/pallas_call | solution.py:174
  41.7 1.0 %collective-permute-done.13.refs_0_.refs_1_ = bf16[3,256,256]{2,1,0:T(8,128)(2,1)S(1)} collective-permute-done((bf16[3,256,256]{2,1,0:T(8,128)(2,1)S(1)}, bf16[3,256,256]{2,1,0:T(8,128)(2,1)S(1)}, u32[]{:S(2)}, u32[]{:S(2)}) %collective-permute-start.13) | collective-permute-done | bytes 393248 | tf_op jit(solution)/shard_map/ppermute | solution.py:637
  44.9 1.6 %collective-permute-start.16 = (bf16[1024,256]{1,0:T(8,128)(2,1)S(1)}, bf16[1024,256]{1,0:T(8,128)(2,1)S(1)}, u32[]{:S(2)}, u32[]{:S(2)}) collective-permute-start(bf16[1024,256]{1,0:T(8,128)(2,1)S(1)} %back_project.7), channel_id=1, source_target_pairs={{0,4},{1,3},{2,6},{3,1},{4,0},{5,7},{6,2},{7,5},{8,12},{9,11},{10,... | collective-permute-start | bytes 1572872 | tf_op jit(solution)/shard_map/ppermute | solution.py:643
  46.5 1.3 %collective-permute-done.15.other_ref = bf16[128,256]{1,0:T(8,128)(2,1)S(1)} collective-permute-done((bf16[128,256]{1,0:T(8,128)(2,1)S(1)}, bf16[128,256]{1,0:T(8,128)(2,1)S(1)}, u32[]{:S(2)}, u32[]{:S(2)}) %collective-permute-start.15) | collective-permute-done | bytes 65568 | tf_op jit(solution)/shard_map/ppermute | solution.py:637
  48.4 1.8 %back_project.6 = (f32[512,256]{1,0:T(8,128)S(1)}, f32[512,256]{1,0:T(8,128)S(1)}, f32[512,256]{1,0:T(8,128)S(1)}, f32[512,256]{1,0:T(8,128)S(1)}) custom-call(bf16[3,4096,512]{2,1,0:T(8,128)(2,1)S(1)} %load.1.w_ref, bf16[3,256,256]{2,1,0:T(8,128)(2,1)S(1)} %get-tuple-element.58.refs_0_, bf16[3,256,256]{2,1,0:T(8,128)(2,1)S(1)} %collective-permute-done.13.refs_0_.refs_1_), custom_call_target="tpu_custom_call" | custom-call | flops 25165824 | bytes 208896 | tf_op jit(solution)/shard_map/back_project/pallas_call | solution.py:174
  50.2 2.4 %collective-permute-done.14.got_ref = bf16[1024,256]{1,0:T(8,128)(2,1)S(1)} collective-permute-done((bf16[1024,256]{1,0:T(8,128)(2,1)S(1)}, bf16[1024,256]{1,0:T(8,128)(2,1)S(1)}, u32[]{:S(2)}, u32[]{:S(2)}) %collective-permute-start.14) | collective-permute-done | bytes 524320 | tf_op jit(solution)/shard_map/ppermute | solution.py:643
  52.7 1.5 %collective-permute-start.17 = (bf16[512,256]{1,0:T(8,128)(2,1)S(1)}, bf16[512,256]{1,0:T(8,128)(2,1)S(1)}, u32[]{:S(2)}, u32[]{:S(2)}) collective-permute-start(bf16[512,256]{1,0:T(8,128)(2,1)S(1)} %get-tuple-element.68), channel_id=1, source_target_pairs={{0,2},{1,5},{2,0},{3,7},{4,6},{5,1},{6,4},{7,3},{8,10},{9,13},{10,... | collective-permute-start | bytes 786440 | tf_op jit(solution)/shard_map/ppermute | solution.py:640
  54.7 6.9 %collective-permute-done.16.other_ref = bf16[1024,256]{1,0:T(8,128)(2,1)S(1)} collective-permute-done((bf16[1024,256]{1,0:T(8,128)(2,1)S(1)}, bf16[1024,256]{1,0:T(8,128)(2,1)S(1)}, u32[]{:S(2)}, u32[]{:S(2)}) %collective-permute-start.16) | collective-permute-done | bytes 524320 | tf_op jit(solution)/shard_map/ppermute | solution.py:643
  63.1 2.9 %collective-permute-start.19 = (bf16[512,128]{1,0:T(8,128)(2,1)S(1)}, bf16[512,128]{1,0:T(8,128)(2,1)S(1)}, u32[]{:S(2)}, u32[]{:S(2)}) collective-permute-start(bf16[512,128]{1,0:T(8,128)(2,1)S(1)} %get-tuple-element.72), channel_id=1, source_target_pairs={{0,8},{2,10},{4,12},{6,14},{8,0},{10,2},{12,4},{14,6},{16,9},{18,1... | collective-permute-start | bytes 393224 | tf_op jit(solution)/shard_map/ppermute | solution.py:708
  66.0 3.6 %collective-permute-start.20 = (bf16[512,128]{1,0:T(8,128)(2,1)S(1)}, bf16[512,128]{1,0:T(8,128)(2,1)S(1)}, u32[]{:S(2)}, u32[]{:S(2)}) collective-permute-start(bf16[512,128]{1,0:T(8,128)(2,1)S(1)} %get-tuple-element.73), channel_id=1, source_target_pairs={{0,9},{2,11},{4,13},{6,15},{8,1},{10,3},{12,5},{14,7},{16,8},{18,1... | collective-permute-start | bytes 393224 | tf_op jit(solution)/shard_map/ppermute | solution.py:708
  69.9 7.3 %collective-permute-done.20.b_ref = bf16[512,128]{1,0:T(8,128)(2,1)S(1)} collective-permute-done((bf16[512,128]{1,0:T(8,128)(2,1)S(1)}, bf16[512,128]{1,0:T(8,128)(2,1)S(1)}, u32[]{:S(2)}, u32[]{:S(2)}) %collective-permute-start.20) | collective-permute-done | bytes 131104 | tf_op jit(solution)/shard_map/ppermute | solution.py:708
  (48 shorter events, 12.0 us)
Async XLA Ops:
  0.6 2.1 %collective-permute-start.1 = (bf16[128,512]{1,0:T(8,128)(2,1)}, bf16[128,512]{1,0:T(8,128)(2,1)S(1)}, u32[]{:S(2)}, u32[]{:S(2)}) collective-permute-start(bf16[128,512]{1,0:T(8,128)(2,1)} %cot_own_ref.1), channel_id=1, source_target_pairs={{0,1},{1,0},{2,3},{3,2},{4,5},{5,4},{6,7},{7,6},{8,9},{9,8},{10,11... | collective-permute-start | bytes 393224 | tf_op jit(solution)/shard_map/ppermute | solution.py:637
  1.1 1.3 %collective-permute-start = (s32[1,128]{1,0:T(1,128)}, s32[1,128]{1,0:T(1,128)S(1)}, u32[]{:S(2)}, u32[]{:S(2)}) collective-permute-start(s32[1,128]{1,0:T(1,128)} %bitcast.5), channel_id=1, source_target_pairs={{0,1},{1,0},{2,3},{3,2},{4,5},{5,4},{6,7},{7,6},{8,9},{9,8},{10,11... | collective-permute-start | bytes 1544 | tf_op jit(solution)/shard_map/ppermute | solution.py:637
  2.8 15.0 %collective-permute-start.2 = (bf16[256,512]{1,0:T(8,128)(2,1)S(1)}, bf16[256,512]{1,0:T(8,128)(2,1)S(1)}, u32[]{:S(2)}, u32[]{:S(2)}) collective-permute-start(bf16[256,512]{1,0:T(8,128)(2,1)S(1)} %embed_rows.1.refs_0_), channel_id=1, source_target_pairs={{0,8},{2,10},{4,12},{6,14},{8,0},{10,2},{12,4},{14,6},{1,16},{3,18... | collective-permute-start | bytes 786440 | tf_op jit(solution)/shard_map/ppermute | solution.py:652
  5.7 15.1 %collective-permute-start.7 = (bf16[256,512]{1,0:T(8,128)(2,1)S(1)}, bf16[256,512]{1,0:T(8,128)(2,1)S(1)}, u32[]{:S(2)}, u32[]{:S(2)}) collective-permute-start(bf16[256,512]{1,0:T(8,128)(2,1)S(1)} %embed_rows.1.refs_0_), channel_id=1, source_target_pairs={{0,6},{1,1},{2,4},{3,3},{4,2},{5,5},{6,0},{7,7},{8,14},{9,9},{10,1... | collective-permute-start | bytes 786440 | tf_op jit(solution)/shard_map/ppermute | solution.py:655
  10.1 10.7 %collective-permute-start.6 = (bf16[256,512]{1,0:T(8,128)(2,1)S(1)}, bf16[256,512]{1,0:T(8,128)(2,1)S(1)}, u32[]{:S(2)}, u32[]{:S(2)}) collective-permute-start(bf16[256,512]{1,0:T(8,128)(2,1)S(1)} %embed_rows.1.refs_0_), channel_id=1, source_target_pairs={{0,4},{1,1},{2,6},{3,3},{4,0},{5,5},{6,2},{7,7},{8,12},{9,9},{10,1... | collective-permute-start | bytes 786440 | tf_op jit(solution)/shard_map/ppermute | solution.py:654
  12.5 10.1 %collective-permute-start.5 = (bf16[256,512]{1,0:T(8,128)(2,1)S(1)}, bf16[256,512]{1,0:T(8,128)(2,1)S(1)}, u32[]{:S(2)}, u32[]{:S(2)}) collective-permute-start(bf16[256,512]{1,0:T(8,128)(2,1)S(1)} %embed_rows.1.refs_0_), channel_id=1, source_target_pairs={{9,16},{11,18},{13,20},{15,22},{1,24},{3,26},{5,28},{7,30},{16,9},... | collective-permute-start | bytes 786440 | tf_op jit(solution)/shard_map/ppermute | solution.py:653
  17.7 8.0 %collective-permute-start.4 = (bf16[256,512]{1,0:T(8,128)(2,1)S(1)}, bf16[256,512]{1,0:T(8,128)(2,1)S(1)}, u32[]{:S(2)}, u32[]{:S(2)}) collective-permute-start(bf16[256,512]{1,0:T(8,128)(2,1)S(1)} %collective-permute-done.2.refs_3_), channel_id=1, source_target_pairs={{0,4},{1,3},{2,6},{3,1},{4,0},{5,7},{6,2},{7,5},{8,12},{9,11},{10,... | collective-permute-start | bytes 786440 | tf_op jit(solution)/shard_map/ppermute | solution.py:643
  19.3 9.2 %collective-permute-start.3 = (bf16[256,512]{1,0:T(8,128)(2,1)S(1)}, bf16[256,512]{1,0:T(8,128)(2,1)S(1)}, u32[]{:S(2)}, u32[]{:S(2)}) collective-permute-start(bf16[256,512]{1,0:T(8,128)(2,1)S(1)} %collective-permute-done.2.refs_3_), channel_id=1, source_target_pairs={{0,2},{1,5},{2,0},{3,7},{4,6},{5,1},{6,4},{7,3},{8,10},{9,13},{10,... | collective-permute-start | bytes 786440 | tf_op jit(solution)/shard_map/ppermute | solution.py:640
  22.6 8.5 %collective-permute-start.11 = (bf16[256,512]{1,0:T(8,128)(2,1)S(1)}, bf16[256,512]{1,0:T(8,128)(2,1)S(1)}, u32[]{:S(2)}, u32[]{:S(2)}) collective-permute-start(bf16[256,512]{1,0:T(8,128)(2,1)S(1)} %collective-permute-done.5.refs_2_), channel_id=1, source_target_pairs={{0,0},{1,7},{2,2},{3,5},{4,4},{5,3},{6,6},{7,1},{8,8},{9,15},{10,1... | collective-permute-start | bytes 786440 | tf_op jit(solution)/shard_map/ppermute | solution.py:668
  23.3 8.0 %collective-permute-start.10 = (bf16[256,512]{1,0:T(8,128)(2,1)S(1)}, bf16[256,512]{1,0:T(8,128)(2,1)S(1)}, u32[]{:S(2)}, u32[]{:S(2)}) collective-permute-start(bf16[256,512]{1,0:T(8,128)(2,1)S(1)} %collective-permute-done.5.refs_2_), channel_id=1, source_target_pairs={{0,0},{1,3},{2,2},{3,1},{4,4},{5,7},{6,6},{7,5},{8,8},{9,11},{10,1... | collective-permute-start | bytes 786440 | tf_op jit(solution)/shard_map/ppermute | solution.py:667
  28.5 6.4 %collective-permute-start.8 = (bf16[256,512]{1,0:T(8,128)(2,1)S(1)}, bf16[256,512]{1,0:T(8,128)(2,1)S(1)}, u32[]{:S(2)}, u32[]{:S(2)}) collective-permute-start(bf16[256,512]{1,0:T(8,128)(2,1)S(1)} %collective-permute-done.3.refs_0_), channel_id=1, source_target_pairs={{0,4},{1,3},{2,6},{3,1},{4,0},{5,7},{6,2},{7,5},{8,12},{9,11},{10,... | collective-permute-start | bytes 786440 | tf_op jit(solution)/shard_map/ppermute | solution.py:643
  29.1 5.8 %collective-permute-start.9 = (bf16[256,512]{1,0:T(8,128)(2,1)S(1)}, bf16[256,512]{1,0:T(8,128)(2,1)S(1)}, u32[]{:S(2)}, u32[]{:S(2)}) collective-permute-start(bf16[256,512]{1,0:T(8,128)(2,1)S(1)} %collective-permute-done.5.refs_2_), channel_id=1, source_target_pairs={{0,0},{1,5},{2,2},{3,7},{4,4},{5,1},{6,6},{7,3},{8,8},{9,13},{10,1... | collective-permute-start | bytes 786440 | tf_op jit(solution)/shard_map/ppermute | solution.py:671
  35.3 2.4 %copy-start = (bf16[128,512]{1,0:T(8,128)(2,1)S(1)}, bf16[128,512]{1,0:T(8,128)(2,1)}, u32[]{:S(2)}) copy-start(bf16[128,512]{1,0:T(8,128)(2,1)} %cot_own_ref.1) | copy-start | bytes 393220
  35.3 2.4 %collective-permute-start.12 = (f32[3,256,256]{2,1,0:T(8,128)S(1)}, f32[3,256,256]{2,1,0:T(8,128)S(1)}, u32[]{:S(2)}, u32[]{:S(2)}) collective-permute-start(f32[3,256,256]{2,1,0:T(8,128)S(1)} %project.8), channel_id=1, source_target_pairs={{0,1},{1,0},{2,3},{3,2},{4,5},{5,4},{6,7},{7,6},{8,9},{9,8},{10,11... | collective-permute-start | bytes 2359304 | tf_op jit(solution)/shard_map/ppermute | solution.py:637
  40.9 1.8 %collective-permute-start.13 = (bf16[3,256,256]{2,1,0:T(8,128)(2,1)S(1)}, bf16[3,256,256]{2,1,0:T(8,128)(2,1)S(1)}, u32[]{:S(2)}, u32[]{:S(2)}) collective-permute-start(bf16[3,256,256]{2,1,0:T(8,128)(2,1)S(1)} %get-tuple-element.58.refs_0_), channel_id=1, source_target_pairs={{0,1},{1,0},{2,3},{3,2},{4,5},{5,4},{6,7},{7,6},{8,9},{9,8},{10,11... | collective-permute-start | bytes 1179656 | tf_op jit(solution)/shard_map/ppermute | solution.py:637
  43.3 9.2 %collective-permute-start.14 = (bf16[1024,256]{1,0:T(8,128)(2,1)S(1)}, bf16[1024,256]{1,0:T(8,128)(2,1)S(1)}, u32[]{:S(2)}, u32[]{:S(2)}) collective-permute-start(bf16[1024,256]{1,0:T(8,128)(2,1)S(1)} %back_project.5), channel_id=1, source_target_pairs={{0,4},{1,3},{2,6},{3,1},{4,0},{5,7},{6,2},{7,5},{8,12},{9,11},{10,... | collective-permute-start | bytes 1572872 | tf_op jit(solution)/shard_map/ppermute | solution.py:643
  44.9 16.8 %collective-permute-start.16 = (bf16[1024,256]{1,0:T(8,128)(2,1)S(1)}, bf16[1024,256]{1,0:T(8,128)(2,1)S(1)}, u32[]{:S(2)}, u32[]{:S(2)}) collective-permute-start(bf16[1024,256]{1,0:T(8,128)(2,1)S(1)} %back_project.7), channel_id=1, source_target_pairs={{0,4},{1,3},{2,6},{3,1},{4,0},{5,7},{6,2},{7,5},{8,12},{9,11},{10,... | collective-permute-start | bytes 1572872 | tf_op jit(solution)/shard_map/ppermute | solution.py:643
  46.4 1.3 %collective-permute-start.15 = (bf16[128,256]{1,0:T(8,128)(2,1)S(1)}, bf16[128,256]{1,0:T(8,128)(2,1)S(1)}, u32[]{:S(2)}, u32[]{:S(2)}) collective-permute-start(bf16[128,256]{1,0:T(8,128)(2,1)S(1)} %get-tuple-element.62), channel_id=1, source_target_pairs={{0,1},{1,0},{2,3},{3,2},{4,5},{5,4},{6,7},{7,6},{8,9},{9,8},{10,11... | collective-permute-start | bytes 196616 | tf_op jit(solution)/shard_map/ppermute | solution.py:637
  52.7 9.0 %collective-permute-start.17 = (bf16[512,256]{1,0:T(8,128)(2,1)S(1)}, bf16[512,256]{1,0:T(8,128)(2,1)S(1)}, u32[]{:S(2)}, u32[]{:S(2)}) collective-permute-start(bf16[512,256]{1,0:T(8,128)(2,1)S(1)} %get-tuple-element.68), channel_id=1, source_target_pairs={{0,2},{1,5},{2,0},{3,7},{4,6},{5,1},{6,4},{7,3},{8,10},{9,13},{10,... | collective-permute-start | bytes 786440 | tf_op jit(solution)/shard_map/ppermute | solution.py:640
  54.2 8.8 %collective-permute-start.18 = (bf16[512,256]{1,0:T(8,128)(2,1)S(1)}, bf16[512,256]{1,0:T(8,128)(2,1)S(1)}, u32[]{:S(2)}, u32[]{:S(2)}) collective-permute-start(bf16[512,256]{1,0:T(8,128)(2,1)S(1)} %get-tuple-element.71), channel_id=1, source_target_pairs={{0,2},{1,5},{2,0},{3,7},{4,6},{5,1},{6,4},{7,3},{8,10},{9,13},{10,... | collective-permute-start | bytes 786440 | tf_op jit(solution)/shard_map/ppermute | solution.py:640
  61.9 7.8 %collective-permute-start.21 = (bf16[512,128]{1,0:T(8,128)(2,1)S(1)}, bf16[512,128]{1,0:T(8,128)(2,1)S(1)}, u32[]{:S(2)}, u32[]{:S(2)}) collective-permute-start(bf16[512,128]{1,0:T(8,128)(2,1)S(1)} %get-tuple-element.74), channel_id=1, source_target_pairs={{0,1},{2,3},{4,5},{6,7},{8,9},{10,11},{12,13},{14,15},{16,0},{18,2... | collective-permute-start | bytes 393224 | tf_op jit(solution)/shard_map/ppermute | solution.py:710
  61.9 7.7 %collective-permute-start.22 = (bf16[512,128]{1,0:T(8,128)(2,1)S(1)}, bf16[512,128]{1,0:T(8,128)(2,1)S(1)}, u32[]{:S(2)}, u32[]{:S(2)}) collective-permute-start(bf16[512,128]{1,0:T(8,128)(2,1)S(1)} %get-tuple-element.75), channel_id=1, source_target_pairs={{16,1},{18,3},{20,5},{22,7},{24,9},{26,11},{28,13},{30,15},{9,24},... | collective-permute-start | bytes 393224 | tf_op jit(solution)/shard_map/ppermute | solution.py:710
  63.1 6.8 %collective-permute-start.19 = (bf16[512,128]{1,0:T(8,128)(2,1)S(1)}, bf16[512,128]{1,0:T(8,128)(2,1)S(1)}, u32[]{:S(2)}, u32[]{:S(2)}) collective-permute-start(bf16[512,128]{1,0:T(8,128)(2,1)S(1)} %get-tuple-element.72), channel_id=1, source_target_pairs={{0,8},{2,10},{4,12},{6,14},{8,0},{10,2},{12,4},{14,6},{16,9},{18,1... | collective-permute-start | bytes 393224 | tf_op jit(solution)/shard_map/ppermute | solution.py:708
  66.0 11.2 %collective-permute-start.20 = (bf16[512,128]{1,0:T(8,128)(2,1)S(1)}, bf16[512,128]{1,0:T(8,128)(2,1)S(1)}, u32[]{:S(2)}, u32[]{:S(2)}) collective-permute-start(bf16[512,128]{1,0:T(8,128)(2,1)S(1)} %get-tuple-element.73), channel_id=1, source_target_pairs={{0,9},{2,11},{4,13},{6,15},{8,1},{10,3},{12,5},{14,7},{16,8},{18,1... | collective-permute-start | bytes 393224 | tf_op jit(solution)/shard_map/ppermute | solution.py:708
  (3 other events, 7.2 us)

commit v14 on v13

--- a/solution.py
+++ b/solution.py
@@ -677,12 +677,12 @@
         sums,
     )
     sums = project([d_2], [], [(0, 2, 2)], w, sums)
-    both, y_2, x_2, sums = lax.optimization_barrier((both, y_2, x_2, sums))
-    acts = [both, y_2, x_2]
-    inner, outer = [(0, 2, 2)], [(0, 1, 2), (1, 2, "y"), (2, 2, "x")]
-    send = project(acts, inner, outer, w, sums, "send")
+    both, x_2, sums = lax.optimization_barrier((both, x_2, sums))
+    sums = project([both, x_2], [(0, 2, 2)], [(0, 1, 2), (1, 2, "x")], w, sums)
+    y_2, sums = lax.optimization_barrier((y_2, sums))
+    send = project([y_2], [], [(0, 2, "y")], w, sums, "send")
     sums, send = lax.optimization_barrier((sums, send))
-    keep = project(acts, inner, outer, w, sums, "keep")
+    keep = project([y_2], [], [(0, 2, "y")], w, sums, "keep")
     got = swap(send)
     keep, got = lax.optimization_barrier((keep, got))
     mixed_own, mixed_send, grad_own = mixer(

time: 78.3 us -> 78.5 us (level)
    pallas_call x16 -> x17, Pallas kernels: 13.4 us -> 13.4 us  [small_call(): pl.pallas_call(kernel, in_specs=[IN_VMEM] * len(operands), out_specs=jax....]
where the time goes in v14:
time: 78.5 us; the launch traced here: 78.3 us
  waiting for transfers between devices  30 us (38%)
  starting transfers between devices  28.4 us (36%)
  Pallas kernels  19 us (24%)
  between operations  0.91 us (1%)
    ppermute x4, waiting for transfers between devices, other_way(): return lax.ppermute(array, BOTH, OTHER_WAY)  14.7 us
    pallas_call x17, Pallas kernels, small_call(): pl.pallas_call(kernel, in_specs=[IN_VMEM] * len(operands), out_specs=jax....  13.4 us
    ppermute x4, waiting for transfers between devices, chip_plan(): lax.ppermute(a, BOTH, pairs)  7.57 us
    ppermute x4, starting transfers between devices, chip_plan(): lax.ppermute(a, BOTH, pairs)  7.25 us
    pallas_call x1, Pallas kernels, load(): pl.pallas_call(load_kernel, in_specs=[pl.BlockSpec(memory_space=pltpu.HBM...  4.58 us
    ppermute x5, waiting for transfers between devices, swap(): return lax.ppermute(array, BOTH, OTHER_CORE)  4.56 us
    ppermute x1, starting transfers between devices, chip_plan(): near_d = lax.ppermute(embedded, BOTH, INNER_XY)  4.34 us
    ppermute x4, starting transfers between devices, other_way(): return lax.ppermute(array, BOTH, OTHER_WAY)  4.31 us
  transfers between devices with their start and end apart: 23, of which 12 were waited for; matrix products, arithmetic and copies ran while one was open for 0% of the time, Pallas kernels for 18%

profile of v14, /device:TPU:0, one launch (start us, length us, event | category | flops | bytes accessed | tf_op | source)
XLA Modules:
  0.0 78.3 jit_solution(14913487909322157988)
XLA Ops:
  1.2 1.1 %fetch.1 = (s32[1,128]{1,0:T(1,128)S(1)}, bf16[512,512]{1,0:T(8,128)(2,1)S(1)}) custom-call(s32[1,128]{1,0:T(1,128)} %bitcast.6, bf16[512,512]{1,0:T(8,128)(2,1)} %table_ref.1), custom_call_target="tpu_custom_call" | custom-call | bytes 1048576 | tf_op jit(solution)/shard_map/fetch/pallas_call | solution.py:251
  2.8 3.0 %collective-permute-start.2 = (bf16[256,512]{1,0:T(8,128)(2,1)S(1)}, bf16[256,512]{1,0:T(8,128)(2,1)S(1)}, u32[]{:S(2)}, u32[]{:S(2)}) collective-permute-start(bf16[256,512]{1,0:T(8,128)(2,1)S(1)} %embed_rows.1.refs_0_), channel_id=1, source_target_pairs={{0,8},{2,10},{4,12},{6,14},{8,0},{10,2},{12,4},{14,6},{1,16},{3,18... | collective-permute-start | bytes 786440 | tf_op jit(solution)/shard_map/ppermute | solution.py:652
  5.7 4.3 %collective-permute-start.7 = (bf16[256,512]{1,0:T(8,128)(2,1)S(1)}, bf16[256,512]{1,0:T(8,128)(2,1)S(1)}, u32[]{:S(2)}, u32[]{:S(2)}) collective-permute-start(bf16[256,512]{1,0:T(8,128)(2,1)S(1)} %embed_rows.1.refs_0_), channel_id=1, source_target_pairs={{0,6},{1,1},{2,4},{3,3},{4,2},{5,5},{6,0},{7,7},{8,14},{9,9},{10,1... | collective-permute-start | bytes 786440 | tf_op jit(solution)/shard_map/ppermute | solution.py:655
  10.1 2.4 %collective-permute-start.6 = (bf16[256,512]{1,0:T(8,128)(2,1)S(1)}, bf16[256,512]{1,0:T(8,128)(2,1)S(1)}, u32[]{:S(2)}, u32[]{:S(2)}) collective-permute-start(bf16[256,512]{1,0:T(8,128)(2,1)S(1)} %embed_rows.1.refs_0_), channel_id=1, source_target_pairs={{0,4},{1,1},{2,6},{3,3},{4,0},{5,5},{6,2},{7,7},{8,12},{9,9},{10,1... | collective-permute-start | bytes 786440 | tf_op jit(solution)/shard_map/ppermute | solution.py:654
  13.1 4.6 %load.1.w_ref = bf16[3,4096,512]{2,1,0:T(8,128)(2,1)S(1)} custom-call(bf16[3,4096,512]{2,1,0:T(8,128)(2,1)} %bitcast.4), custom_call_target="tpu_custom_call" | custom-call | bytes 25165824 | tf_op jit(solution)/shard_map/load/pallas_call | solution.py:273
  17.7 1.6 %collective-permute-start.4 = (bf16[256,512]{1,0:T(8,128)(2,1)S(1)}, bf16[256,512]{1,0:T(8,128)(2,1)S(1)}, u32[]{:S(2)}, u32[]{:S(2)}) collective-permute-start(bf16[256,512]{1,0:T(8,128)(2,1)S(1)} %collective-permute-done.2.refs_3_), channel_id=1, source_target_pairs={{0,4},{1,3},{2,6},{3,1},{4,0},{5,7},{6,2},{7,5},{8,12},{9,11},{10,... | collective-permute-start | bytes 786440 | tf_op jit(solution)/shard_map/ppermute | solution.py:643
  19.3 1.5 %collective-permute-start.3 = (bf16[256,512]{1,0:T(8,128)(2,1)S(1)}, bf16[256,512]{1,0:T(8,128)(2,1)S(1)}, u32[]{:S(2)}, u32[]{:S(2)}) collective-permute-start(bf16[256,512]{1,0:T(8,128)(2,1)S(1)} %collective-permute-done.2.refs_3_), channel_id=1, source_target_pairs={{0,2},{1,5},{2,0},{3,7},{4,6},{5,1},{6,4},{7,3},{8,10},{9,13},{10,... | collective-permute-start | bytes 786440 | tf_op jit(solution)/shard_map/ppermute | solution.py:640
  20.8 1.8 %project.6.refs_3_ = f32[3,256,512]{2,1,0:T(8,128)S(1)} custom-call(bf16[3,4096,512]{2,1,0:T(8,128)(2,1)S(1)} %load.1.w_ref, bf16[256,512]{1,0:T(8,128)(2,1)S(1)} %embed_rows.1.refs_0_, bf16[256,512]{1,0:T(8,128)(2,1)S(1)} %collective-permute-done.6.refs_1_, bf16[256,512]{1,0:T(8,128)(2,1)S(1)} %collective-permute-done.7.refs_2_, ...), custom_call_target="tpu_custom_call" | custom-call | flops 25165824 | bytes 212992 | tf_op jit(solution)/shard_map/project/pallas_call | solution.py:174
  24.0 1.8 %collective-permute-done.4.refs_1_ = bf16[256,512]{1,0:T(8,128)(2,1)S(1)} collective-permute-done((bf16[256,512]{1,0:T(8,128)(2,1)S(1)}, bf16[256,512]{1,0:T(8,128)(2,1)S(1)}, u32[]{:S(2)}, u32[]{:S(2)}) %collective-permute-start.4) | collective-permute-done | bytes 262176 | tf_op jit(solution)/shard_map/ppermute | solution.py:643
  25.8 2.7 %collective-permute-done.3.refs_0_ = bf16[256,512]{1,0:T(8,128)(2,1)S(1)} collective-permute-done((bf16[256,512]{1,0:T(8,128)(2,1)S(1)}, bf16[256,512]{1,0:T(8,128)(2,1)S(1)}, u32[]{:S(2)}, u32[]{:S(2)}) %collective-permute-start.3) | collective-permute-done | bytes 262176 | tf_op jit(solution)/shard_map/ppermute | solution.py:640
  29.7 1.4 %project.7.refs_1_ = f32[3,256,512]{2,1,0:T(8,128)S(1)} custom-call(bf16[3,4096,512]{2,1,0:T(8,128)(2,1)S(1)} %load.1.w_ref, bf16[256,512]{1,0:T(8,128)(2,1)S(1)} %collective-permute-done.3.refs_0_, bf16[256,512]{1,0:T(8,128)(2,1)S(1)} %collective-permute-done.4.refs_1_, bf16[256,512]{1,0:T(8,128)(2,1)S(1)} %collective-permute-done.5.refs_2_, ...), custom_call_target="tpu_custom_call" | custom-call | flops 18874368 | bytes 233472 | tf_op jit(solution)/shard_map/project/pallas_call | solution.py:174
  31.3 3.6 %collective-permute-done.9.refs_0_ = bf16[256,512]{1,0:T(8,128)(2,1)S(1)} collective-permute-done((bf16[256,512]{1,0:T(8,128)(2,1)S(1)}, bf16[256,512]{1,0:T(8,128)(2,1)S(1)}, u32[]{:S(2)}, u32[]{:S(2)}) %collective-permute-start.9) | collective-permute-done | bytes 262176 | tf_op jit(solution)/shard_map/ppermute | solution.py:643
  35.8 2.2 %collective-permute-done.12.other_ref = f32[3,256,256]{2,1,0:T(8,128)S(1)} collective-permute-done((f32[3,256,256]{2,1,0:T(8,128)S(1)}, f32[3,256,256]{2,1,0:T(8,128)S(1)}, u32[]{:S(2)}, u32[]{:S(2)}) %collective-permute-start.12) | collective-permute-done | bytes 786464 | tf_op jit(solution)/shard_map/ppermute | solution.py:637
  38.0 3.2 %mixer.1 = (bf16[128,256]{1,0:T(8,128)(2,1)S(1)}, bf16[128,256]{1,0:T(8,128)(2,1)S(1)}, bf16[3,256,256]{2,1,0:T(8,128)(2,1)S(1)}) custom-call(f32[3,256,256]{2,1,0:T(8,128)S(1)} %project.11.keep_ref, f32[3,256,256]{2,1,0:T(8,128)S(1)} %collective-permute-done.12.other_ref, f32[3,7,512]{2,1,0:T(8,128)S(1)} %bitcast.3, f32[16,512]{1,0:T(8,128)S(1)} %copy-done.2, ...), custom_call_target="tpu_custom_call" | custom-call | flops 196608 | bytes 30368 | tf_op jit(solution)/shard_map/mixer/pallas_call | solution.py:174
  42.0 1.0 %collective-permute-done.13.refs_0_.refs_1_ = bf16[3,256,256]{2,1,0:T(8,128)(2,1)S(1)} collective-permute-done((bf16[3,256,256]{2,1,0:T(8,128)(2,1)S(1)}, bf16[3,256,256]{2,1,0:T(8,128)(2,1)S(1)}, u32[]{:S(2)}, u32[]{:S(2)}) %collective-permute-start.13) | collective-permute-done | bytes 393248 | tf_op jit(solution)/shard_map/ppermute | solution.py:637
  45.2 1.6 %collective-permute-start.16 = (bf16[1024,256]{1,0:T(8,128)(2,1)S(1)}, bf16[1024,256]{1,0:T(8,128)(2,1)S(1)}, u32[]{:S(2)}, u32[]{:S(2)}) collective-permute-start(bf16[1024,256]{1,0:T(8,128)(2,1)S(1)} %back_project.7), channel_id=1, source_target_pairs={{0,4},{1,3},{2,6},{3,1},{4,0},{5,7},{6,2},{7,5},{8,12},{9,11},{10,... | collective-permute-start | bytes 1572872 | tf_op jit(solution)/shard_map/ppermute | solution.py:643
  46.7 1.3 %collective-permute-done.15.other_ref = bf16[128,256]{1,0:T(8,128)(2,1)S(1)} collective-permute-done((bf16[128,256]{1,0:T(8,128)(2,1)S(1)}, bf16[128,256]{1,0:T(8,128)(2,1)S(1)}, u32[]{:S(2)}, u32[]{:S(2)}) %collective-permute-start.15) | collective-permute-done | bytes 65568 | tf_op jit(solution)/shard_map/ppermute | solution.py:637
  48.7 1.8 %back_project.6 = (f32[512,256]{1,0:T(8,128)S(1)}, f32[512,256]{1,0:T(8,128)S(1)}, f32[512,256]{1,0:T(8,128)S(1)}, f32[512,256]{1,0:T(8,128)S(1)}) custom-call(bf16[3,4096,512]{2,1,0:T(8,128)(2,1)S(1)} %load.1.w_ref, bf16[3,256,256]{2,1,0:T(8,128)(2,1)S(1)} %get-tuple-element.60.refs_0_, bf16[3,256,256]{2,1,0:T(8,128)(2,1)S(1)} %collective-permute-done.13.refs_0_.refs_1_), custom_call_target="tpu_custom_call" | custom-call | flops 25165824 | bytes 208896 | tf_op jit(solution)/shard_map/back_project/pallas_call | solution.py:174
  50.4 2.4 %collective-permute-done.14.got_ref = bf16[1024,256]{1,0:T(8,128)(2,1)S(1)} collective-permute-done((bf16[1024,256]{1,0:T(8,128)(2,1)S(1)}, bf16[1024,256]{1,0:T(8,128)(2,1)S(1)}, u32[]{:S(2)}, u32[]{:S(2)}) %collective-permute-start.14) | collective-permute-done | bytes 524320 | tf_op jit(solution)/shard_map/ppermute | solution.py:643
  52.9 1.5 %collective-permute-start.17 = (bf16[512,256]{1,0:T(8,128)(2,1)S(1)}, bf16[512,256]{1,0:T(8,128)(2,1)S(1)}, u32[]{:S(2)}, u32[]{:S(2)}) collective-permute-start(bf16[512,256]{1,0:T(8,128)(2,1)S(1)} %get-tuple-element.70), channel_id=1, source_target_pairs={{0,2},{1,5},{2,0},{3,7},{4,6},{5,1},{6,4},{7,3},{8,10},{9,13},{10,... | collective-permute-start | bytes 786440 | tf_op jit(solution)/shard_map/ppermute | solution.py:640
  55.0 6.9 %collective-permute-done.16.other_ref = bf16[1024,256]{1,0:T(8,128)(2,1)S(1)} collective-permute-done((bf16[1024,256]{1,0:T(8,128)(2,1)S(1)}, bf16[1024,256]{1,0:T(8,128)(2,1)S(1)}, u32[]{:S(2)}, u32[]{:S(2)}) %collective-permute-start.16) | collective-permute-done | bytes 524320 | tf_op jit(solution)/shard_map/ppermute | solution.py:643
  63.4 2.9 %collective-permute-start.19 = (bf16[512,128]{1,0:T(8,128)(2,1)S(1)}, bf16[512,128]{1,0:T(8,128)(2,1)S(1)}, u32[]{:S(2)}, u32[]{:S(2)}) collective-permute-start(bf16[512,128]{1,0:T(8,128)(2,1)S(1)} %get-tuple-element.74), channel_id=1, source_target_pairs={{0,8},{2,10},{4,12},{6,14},{8,0},{10,2},{12,4},{14,6},{16,9},{18,1... | collective-permute-start | bytes 393224 | tf_op jit(solution)/shard_map/ppermute | solution.py:708
  66.3 3.6 %collective-permute-start.20 = (bf16[512,128]{1,0:T(8,128)(2,1)S(1)}, bf16[512,128]{1,0:T(8,128)(2,1)S(1)}, u32[]{:S(2)}, u32[]{:S(2)}) collective-permute-start(bf16[512,128]{1,0:T(8,128)(2,1)S(1)} %get-tuple-element.75), channel_id=1, source_target_pairs={{0,9},{2,11},{4,13},{6,15},{8,1},{10,3},{12,5},{14,7},{16,8},{18,1... | collective-permute-start | bytes 393224 | tf_op jit(solution)/shard_map/ppermute | solution.py:708
  70.0 7.5 %collective-permute-done.20.b_ref = bf16[512,128]{1,0:T(8,128)(2,1)S(1)} collective-permute-done((bf16[512,128]{1,0:T(8,128)(2,1)S(1)}, bf16[512,128]{1,0:T(8,128)(2,1)S(1)}, u32[]{:S(2)}, u32[]{:S(2)}) %collective-permute-start.20) | collective-permute-done | bytes 131104 | tf_op jit(solution)/shard_map/ppermute | solution.py:708
  (49 shorter events, 11.7 us)
Async XLA Ops:
  0.6 2.1 %collective-permute-start.1 = (bf16[128,512]{1,0:T(8,128)(2,1)}, bf16[128,512]{1,0:T(8,128)(2,1)S(1)}, u32[]{:S(2)}, u32[]{:S(2)}) collective-permute-start(bf16[128,512]{1,0:T(8,128)(2,1)} %cot_own_ref.1), channel_id=1, source_target_pairs={{0,1},{1,0},{2,3},{3,2},{4,5},{5,4},{6,7},{7,6},{8,9},{9,8},{10,11... | collective-permute-start | bytes 393224 | tf_op jit(solution)/shard_map/ppermute | solution.py:637
  1.1 1.3 %collective-permute-start = (s32[1,128]{1,0:T(1,128)}, s32[1,128]{1,0:T(1,128)S(1)}, u32[]{:S(2)}, u32[]{:S(2)}) collective-permute-start(s32[1,128]{1,0:T(1,128)} %bitcast.5), channel_id=1, source_target_pairs={{0,1},{1,0},{2,3},{3,2},{4,5},{5,4},{6,7},{7,6},{8,9},{9,8},{10,11... | collective-permute-start | bytes 1544 | tf_op jit(solution)/shard_map/ppermute | solution.py:637
  2.8 15.0 %collective-permute-start.2 = (bf16[256,512]{1,0:T(8,128)(2,1)S(1)}, bf16[256,512]{1,0:T(8,128)(2,1)S(1)}, u32[]{:S(2)}, u32[]{:S(2)}) collective-permute-start(bf16[256,512]{1,0:T(8,128)(2,1)S(1)} %embed_rows.1.refs_0_), channel_id=1, source_target_pairs={{0,8},{2,10},{4,12},{6,14},{8,0},{10,2},{12,4},{14,6},{1,16},{3,18... | collective-permute-start | bytes 786440 | tf_op jit(solution)/shard_map/ppermute | solution.py:652
  5.7 15.1 %collective-permute-start.7 = (bf16[256,512]{1,0:T(8,128)(2,1)S(1)}, bf16[256,512]{1,0:T(8,128)(2,1)S(1)}, u32[]{:S(2)}, u32[]{:S(2)}) collective-permute-start(bf16[256,512]{1,0:T(8,128)(2,1)S(1)} %embed_rows.1.refs_0_), channel_id=1, source_target_pairs={{0,6},{1,1},{2,4},{3,3},{4,2},{5,5},{6,0},{7,7},{8,14},{9,9},{10,1... | collective-permute-start | bytes 786440 | tf_op jit(solution)/shard_map/ppermute | solution.py:655
  10.1 10.7 %collective-permute-start.6 = (bf16[256,512]{1,0:T(8,128)(2,1)S(1)}, bf16[256,512]{1,0:T(8,128)(2,1)S(1)}, u32[]{:S(2)}, u32[]{:S(2)}) collective-permute-start(bf16[256,512]{1,0:T(8,128)(2,1)S(1)} %embed_rows.1.refs_0_), channel_id=1, source_target_pairs={{0,4},{1,1},{2,6},{3,3},{4,0},{5,5},{6,2},{7,7},{8,12},{9,9},{10,1... | collective-permute-start | bytes 786440 | tf_op jit(solution)/shard_map/ppermute | solution.py:654
  12.5 10.1 %collective-permute-start.5 = (bf16[256,512]{1,0:T(8,128)(2,1)S(1)}, bf16[256,512]{1,0:T(8,128)(2,1)S(1)}, u32[]{:S(2)}, u32[]{:S(2)}) collective-permute-start(bf16[256,512]{1,0:T(8,128)(2,1)S(1)} %embed_rows.1.refs_0_), channel_id=1, source_target_pairs={{9,16},{11,18},{13,20},{15,22},{1,24},{3,26},{5,28},{7,30},{16,9},... | collective-permute-start | bytes 786440 | tf_op jit(solution)/shard_map/ppermute | solution.py:653
  17.7 8.0 %collective-permute-start.4 = (bf16[256,512]{1,0:T(8,128)(2,1)S(1)}, bf16[256,512]{1,0:T(8,128)(2,1)S(1)}, u32[]{:S(2)}, u32[]{:S(2)}) collective-permute-start(bf16[256,512]{1,0:T(8,128)(2,1)S(1)} %collective-permute-done.2.refs_3_), channel_id=1, source_target_pairs={{0,4},{1,3},{2,6},{3,1},{4,0},{5,7},{6,2},{7,5},{8,12},{9,11},{10,... | collective-permute-start | bytes 786440 | tf_op jit(solution)/shard_map/ppermute | solution.py:643
  19.3 9.2 %collective-permute-start.3 = (bf16[256,512]{1,0:T(8,128)(2,1)S(1)}, bf16[256,512]{1,0:T(8,128)(2,1)S(1)}, u32[]{:S(2)}, u32[]{:S(2)}) collective-permute-start(bf16[256,512]{1,0:T(8,128)(2,1)S(1)} %collective-permute-done.2.refs_3_), channel_id=1, source_target_pairs={{0,2},{1,5},{2,0},{3,7},{4,6},{5,1},{6,4},{7,3},{8,10},{9,13},{10,... | collective-permute-start | bytes 786440 | tf_op jit(solution)/shard_map/ppermute | solution.py:640
  22.6 8.5 %collective-permute-start.11 = (bf16[256,512]{1,0:T(8,128)(2,1)S(1)}, bf16[256,512]{1,0:T(8,128)(2,1)S(1)}, u32[]{:S(2)}, u32[]{:S(2)}) collective-permute-start(bf16[256,512]{1,0:T(8,128)(2,1)S(1)} %collective-permute-done.5.refs_2_), channel_id=1, source_target_pairs={{0,0},{1,7},{2,2},{3,5},{4,4},{5,3},{6,6},{7,1},{8,8},{9,15},{10,1... | collective-permute-start | bytes 786440 | tf_op jit(solution)/shard_map/ppermute | solution.py:668
  23.3 8.0 %collective-permute-start.10 = (bf16[256,512]{1,0:T(8,128)(2,1)S(1)}, bf16[256,512]{1,0:T(8,128)(2,1)S(1)}, u32[]{:S(2)}, u32[]{:S(2)}) collective-permute-start(bf16[256,512]{1,0:T(8,128)(2,1)S(1)} %collective-permute-done.5.refs_2_), channel_id=1, source_target_pairs={{0,0},{1,3},{2,2},{3,1},{4,4},{5,7},{6,6},{7,5},{8,8},{9,11},{10,1... | collective-permute-start | bytes 786440 | tf_op jit(solution)/shard_map/ppermute | solution.py:667
  28.5 6.4 %collective-permute-start.9 = (bf16[256,512]{1,0:T(8,128)(2,1)S(1)}, bf16[256,512]{1,0:T(8,128)(2,1)S(1)}, u32[]{:S(2)}, u32[]{:S(2)}) collective-permute-start(bf16[256,512]{1,0:T(8,128)(2,1)S(1)} %collective-permute-done.3.refs_0_), channel_id=1, source_target_pairs={{0,4},{1,3},{2,6},{3,1},{4,0},{5,7},{6,2},{7,5},{8,12},{9,11},{10,... | collective-permute-start | bytes 786440 | tf_op jit(solution)/shard_map/ppermute | solution.py:643
  29.1 6.4 %collective-permute-start.8 = (bf16[256,512]{1,0:T(8,128)(2,1)S(1)}, bf16[256,512]{1,0:T(8,128)(2,1)S(1)}, u32[]{:S(2)}, u32[]{:S(2)}) collective-permute-start(bf16[256,512]{1,0:T(8,128)(2,1)S(1)} %collective-permute-done.5.refs_2_), channel_id=1, source_target_pairs={{0,0},{1,5},{2,2},{3,7},{4,4},{5,1},{6,6},{7,3},{8,8},{9,13},{10,1... | collective-permute-start | bytes 786440 | tf_op jit(solution)/shard_map/ppermute | solution.py:671
  35.6 2.4 %copy-start = (bf16[128,512]{1,0:T(8,128)(2,1)S(1)}, bf16[128,512]{1,0:T(8,128)(2,1)}, u32[]{:S(2)}) copy-start(bf16[128,512]{1,0:T(8,128)(2,1)} %cot_own_ref.1) | copy-start | bytes 393220
  35.6 2.4 %collective-permute-start.12 = (f32[3,256,256]{2,1,0:T(8,128)S(1)}, f32[3,256,256]{2,1,0:T(8,128)S(1)}, u32[]{:S(2)}, u32[]{:S(2)}) collective-permute-start(f32[3,256,256]{2,1,0:T(8,128)S(1)} %project.10), channel_id=1, source_target_pairs={{0,1},{1,0},{2,3},{3,2},{4,5},{5,4},{6,7},{7,6},{8,9},{9,8},{10,11... | collective-permute-start | bytes 2359304 | tf_op jit(solution)/shard_map/ppermute | solution.py:637
  41.2 1.8 %collective-permute-start.13 = (bf16[3,256,256]{2,1,0:T(8,128)(2,1)S(1)}, bf16[3,256,256]{2,1,0:T(8,128)(2,1)S(1)}, u32[]{:S(2)}, u32[]{:S(2)}) collective-permute-start(bf16[3,256,256]{2,1,0:T(8,128)(2,1)S(1)} %get-tuple-element.60.refs_0_), channel_id=1, source_target_pairs={{0,1},{1,0},{2,3},{3,2},{4,5},{5,4},{6,7},{7,6},{8,9},{9,8},{10,11... | collective-permute-start | bytes 1179656 | tf_op jit(solution)/shard_map/ppermute | solution.py:637
  43.6 9.2 %collective-permute-start.14 = (bf16[1024,256]{1,0:T(8,128)(2,1)S(1)}, bf16[1024,256]{1,0:T(8,128)(2,1)S(1)}, u32[]{:S(2)}, u32[]{:S(2)}) collective-permute-start(bf16[1024,256]{1,0:T(8,128)(2,1)S(1)} %back_project.5), channel_id=1, source_target_pairs={{0,4},{1,3},{2,6},{3,1},{4,0},{5,7},{6,2},{7,5},{8,12},{9,11},{10,... | collective-permute-start | bytes 1572872 | tf_op jit(solution)/shard_map/ppermute | solution.py:643
  45.2 16.8 %collective-permute-start.16 = (bf16[1024,256]{1,0:T(8,128)(2,1)S(1)}, bf16[1024,256]{1,0:T(8,128)(2,1)S(1)}, u32[]{:S(2)}, u32[]{:S(2)}) collective-permute-start(bf16[1024,256]{1,0:T(8,128)(2,1)S(1)} %back_project.7), channel_id=1, source_target_pairs={{0,4},{1,3},{2,6},{3,1},{4,0},{5,7},{6,2},{7,5},{8,12},{9,11},{10,... | collective-permute-start | bytes 1572872 | tf_op jit(solution)/shard_map/ppermute | solution.py:643
  46.7 1.3 %collective-permute-start.15 = (bf16[128,256]{1,0:T(8,128)(2,1)S(1)}, bf16[128,256]{1,0:T(8,128)(2,1)S(1)}, u32[]{:S(2)}, u32[]{:S(2)}) collective-permute-start(bf16[128,256]{1,0:T(8,128)(2,1)S(1)} %get-tuple-element.64), channel_id=1, source_target_pairs={{0,1},{1,0},{2,3},{3,2},{4,5},{5,4},{6,7},{7,6},{8,9},{9,8},{10,11... | collective-permute-start | bytes 196616 | tf_op jit(solution)/shard_map/ppermute | solution.py:637
  52.9 9.0 %collective-permute-start.17 = (bf16[512,256]{1,0:T(8,128)(2,1)S(1)}, bf16[512,256]{1,0:T(8,128)(2,1)S(1)}, u32[]{:S(2)}, u32[]{:S(2)}) collective-permute-start(bf16[512,256]{1,0:T(8,128)(2,1)S(1)} %get-tuple-element.70), channel_id=1, source_target_pairs={{0,2},{1,5},{2,0},{3,7},{4,6},{5,1},{6,4},{7,3},{8,10},{9,13},{10,... | collective-permute-start | bytes 786440 | tf_op jit(solution)/shard_map/ppermute | solution.py:640
  54.5 8.8 %collective-permute-start.18 = (bf16[512,256]{1,0:T(8,128)(2,1)S(1)}, bf16[512,256]{1,0:T(8,128)(2,1)S(1)}, u32[]{:S(2)}, u32[]{:S(2)}) collective-permute-start(bf16[512,256]{1,0:T(8,128)(2,1)S(1)} %get-tuple-element.73), channel_id=1, source_target_pairs={{0,2},{1,5},{2,0},{3,7},{4,6},{5,1},{6,4},{7,3},{8,10},{9,13},{10,... | collective-permute-start | bytes 786440 | tf_op jit(solution)/shard_map/ppermute | solution.py:640
  62.1 7.8 %collective-permute-start.21 = (bf16[512,128]{1,0:T(8,128)(2,1)S(1)}, bf16[512,128]{1,0:T(8,128)(2,1)S(1)}, u32[]{:S(2)}, u32[]{:S(2)}) collective-permute-start(bf16[512,128]{1,0:T(8,128)(2,1)S(1)} %get-tuple-element.76), channel_id=1, source_target_pairs={{0,1},{2,3},{4,5},{6,7},{8,9},{10,11},{12,13},{14,15},{16,0},{18,2... | collective-permute-start | bytes 393224 | tf_op jit(solution)/shard_map/ppermute | solution.py:710
  62.2 7.7 %collective-permute-start.22 = (bf16[512,128]{1,0:T(8,128)(2,1)S(1)}, bf16[512,128]{1,0:T(8,128)(2,1)S(1)}, u32[]{:S(2)}, u32[]{:S(2)}) collective-permute-start(bf16[512,128]{1,0:T(8,128)(2,1)S(1)} %get-tuple-element.77), channel_id=1, source_target_pairs={{16,1},{18,3},{20,5},{22,7},{24,9},{26,11},{28,13},{30,15},{9,24},... | collective-permute-start | bytes 393224 | tf_op jit(solution)/shard_map/ppermute | solution.py:710
  63.4 6.6 %collective-permute-start.19 = (bf16[512,128]{1,0:T(8,128)(2,1)S(1)}, bf16[512,128]{1,0:T(8,128)(2,1)S(1)}, u32[]{:S(2)}, u32[]{:S(2)}) collective-permute-start(bf16[512,128]{1,0:T(8,128)(2,1)S(1)} %get-tuple-element.74), channel_id=1, source_target_pairs={{0,8},{2,10},{4,12},{6,14},{8,0},{10,2},{12,4},{14,6},{16,9},{18,1... | collective-permute-start | bytes 393224 | tf_op jit(solution)/shard_map/ppermute | solution.py:708
  66.3 11.2 %collective-permute-start.20 = (bf16[512,128]{1,0:T(8,128)(2,1)S(1)}, bf16[512,128]{1,0:T(8,128)(2,1)S(1)}, u32[]{:S(2)}, u32[]{:S(2)}) collective-permute-start(bf16[512,128]{1,0:T(8,128)(2,1)S(1)} %get-tuple-element.75), channel_id=1, source_target_pairs={{0,9},{2,11},{4,13},{6,15},{8,1},{10,3},{12,5},{14,7},{16,8},{18,1... | collective-permute-start | bytes 393224 | tf_op jit(solution)/shard_map/ppermute | solution.py:708
  (3 other events, 7.2 us)

commit v15 on v14

--- a/solution.py
+++ b/solution.py
@@ -606,9 +606,9 @@
     )
 
 
-def finish_kernel(own_ref, a_ref, b_ref, c_ref, d_ref, out_ref):
+def finish_kernel(own_ref, a_ref, b_ref, out_ref):
     total = own_ref[...]
-    for ref in (a_ref, b_ref, c_ref, d_ref):
+    for ref in (a_ref, b_ref):
         total = total + ref[...].astype(f32)
     out_ref[...] = total.T.astype(bf16)
 
@@ -616,6 +616,15 @@
 def finish(own, received):
     shape = jax.ShapeDtypeStruct((own.shape[1], own.shape[0]), bf16)
     return small_call(finish_kernel, shape, [own] + received, "finish")
+
+
+def presum_kernel(own_ref, a_ref, b_ref, out_ref):
+    out_ref[...] = own_ref[...] + a_ref[...].astype(f32) + b_ref[...].astype(f32)
+
+
+def presum(own, received):
+    shape = jax.ShapeDtypeStruct(own.shape, f32)
+    return small_call(presum_kernel, shape, [own] + received, "presum")
 
 
 def pair_kernel(own_ref, other_ref, out_ref):
@@ -708,7 +717,7 @@
     received = [lax.ppermute(a, BOTH, pairs) for a, pairs in zip(sends, SCATTER_Z[:2])]
     *sends, own = column(1, own_1, other, first_1)
     received += [lax.ppermute(a, BOTH, pairs) for a, pairs in zip(sends, SCATTER_Z[2:])]
-    return (mixed, finish(own, received))
+    return (mixed, finish(presum(own, received[2:]), received[:2]))
 
 
 def solution(mesh):

time: 78.5 us -> 78.5 us (level)
    pallas_call x17 -> x18, Pallas kernels: 13.4 us -> 13.4 us  [small_call(): pl.pallas_call(kernel, in_specs=[IN_VMEM] * len(operands), out_specs=jax....]
  transfers between devices with their start and end apart: 23 -> 23, of which waited for: 12 -> 11; matrix products, arithmetic and copies ran while one was open for 0% -> 0% of each run, Pallas kernels for 18% -> 18%
where the time goes in v15:
time: 78.5 us; the launch traced here: 78.2 us
  waiting for transfers between devices  29.9 us (38%)
  starting transfers between devices  28.4 us (36%)
  Pallas kernels  19 us (24%)
  between operations  0.92 us (1%)
    ppermute x4, waiting for transfers between devices, other_way(): return lax.ppermute(array, BOTH, OTHER_WAY)  14.7 us
    pallas_call x18, Pallas kernels, small_call(): pl.pallas_call(kernel, in_specs=[IN_VMEM] * len(operands), out_specs=jax....  13.4 us
    ppermute x4, waiting for transfers between devices, chip_plan(): lax.ppermute(a, BOTH, pairs)  7.53 us
    ppermute x4, starting transfers between devices, chip_plan(): lax.ppermute(a, BOTH, pairs)  7.25 us
    pallas_call x1, Pallas kernels, load(): pl.pallas_call(load_kernel, in_specs=[pl.BlockSpec(memory_space=pltpu.HBM...  4.58 us
    ppermute x5, waiting for transfers between devices, swap(): return lax.ppermute(array, BOTH, OTHER_CORE)  4.56 us
    ppermute x1, starting transfers between devices, chip_plan(): near_d = lax.ppermute(embedded, BOTH, INNER_XY)  4.34 us
    ppermute x4, starting transfers between devices, other_way(): return lax.ppermute(array, BOTH, OTHER_WAY)  4.31 us
  transfers between devices with their start and end apart: 23, of which 11 were waited for; matrix products, arithmetic and copies ran while one was open for 0% of the time, Pallas kernels for 18%

profile of v15, /device:TPU:0, one launch (start us, length us, event | category | flops | bytes accessed | tf_op | source)
XLA Modules:
  0.0 78.2 jit_solution(13774719242266242445)
XLA Ops:
  1.2 1.1 %fetch.1 = (s32[1,128]{1,0:T(1,128)S(1)}, bf16[512,512]{1,0:T(8,128)(2,1)S(1)}) custom-call(s32[1,128]{1,0:T(1,128)} %bitcast.6, bf16[512,512]{1,0:T(8,128)(2,1)} %table_ref.1), custom_call_target="tpu_custom_call" | custom-call | bytes 1048576 | tf_op jit(solution)/shard_map/fetch/pallas_call | solution.py:251
  2.8 3.0 %collective-permute-start.2 = (bf16[256,512]{1,0:T(8,128)(2,1)S(1)}, bf16[256,512]{1,0:T(8,128)(2,1)S(1)}, u32[]{:S(2)}, u32[]{:S(2)}) collective-permute-start(bf16[256,512]{1,0:T(8,128)(2,1)S(1)} %embed_rows.1.refs_0_), channel_id=1, source_target_pairs={{0,8},{2,10},{4,12},{6,14},{8,0},{10,2},{12,4},{14,6},{1,16},{3,18... | collective-permute-start | bytes 786440 | tf_op jit(solution)/shard_map/ppermute | solution.py:661
  5.7 4.3 %collective-permute-start.7 = (bf16[256,512]{1,0:T(8,128)(2,1)S(1)}, bf16[256,512]{1,0:T(8,128)(2,1)S(1)}, u32[]{:S(2)}, u32[]{:S(2)}) collective-permute-start(bf16[256,512]{1,0:T(8,128)(2,1)S(1)} %embed_rows.1.refs_0_), channel_id=1, source_target_pairs={{0,6},{1,1},{2,4},{3,3},{4,2},{5,5},{6,0},{7,7},{8,14},{9,9},{10,1... | collective-permute-start | bytes 786440 | tf_op jit(solution)/shard_map/ppermute | solution.py:664
  10.1 2.4 %collective-permute-start.6 = (bf16[256,512]{1,0:T(8,128)(2,1)S(1)}, bf16[256,512]{1,0:T(8,128)(2,1)S(1)}, u32[]{:S(2)}, u32[]{:S(2)}) collective-permute-start(bf16[256,512]{1,0:T(8,128)(2,1)S(1)} %embed_rows.1.refs_0_), channel_id=1, source_target_pairs={{0,4},{1,1},{2,6},{3,3},{4,0},{5,5},{6,2},{7,7},{8,12},{9,9},{10,1... | collective-permute-start | bytes 786440 | tf_op jit(solution)/shard_map/ppermute | solution.py:663
  13.1 4.6 %load.1.w_ref = bf16[3,4096,512]{2,1,0:T(8,128)(2,1)S(1)} custom-call(bf16[3,4096,512]{2,1,0:T(8,128)(2,1)} %bitcast.4), custom_call_target="tpu_custom_call" | custom-call | bytes 25165824 | tf_op jit(solution)/shard_map/load/pallas_call | solution.py:273
  17.7 1.6 %collective-permute-start.4 = (bf16[256,512]{1,0:T(8,128)(2,1)S(1)}, bf16[256,512]{1,0:T(8,128)(2,1)S(1)}, u32[]{:S(2)}, u32[]{:S(2)}) collective-permute-start(bf16[256,512]{1,0:T(8,128)(2,1)S(1)} %collective-permute-done.2.refs_3_), channel_id=1, source_target_pairs={{0,4},{1,3},{2,6},{3,1},{4,0},{5,7},{6,2},{7,5},{8,12},{9,11},{10,... | collective-permute-start | bytes 786440 | tf_op jit(solution)/shard_map/ppermute | solution.py:652
  19.3 1.5 %collective-permute-start.3 = (bf16[256,512]{1,0:T(8,128)(2,1)S(1)}, bf16[256,512]{1,0:T(8,128)(2,1)S(1)}, u32[]{:S(2)}, u32[]{:S(2)}) collective-permute-start(bf16[256,512]{1,0:T(8,128)(2,1)S(1)} %collective-permute-done.2.refs_3_), channel_id=1, source_target_pairs={{0,2},{1,5},{2,0},{3,7},{4,6},{5,1},{6,4},{7,3},{8,10},{9,13},{10,... | collective-permute-start | bytes 786440 | tf_op jit(solution)/shard_map/ppermute | solution.py:649
  20.8 1.8 %project.6.refs_3_ = f32[3,256,512]{2,1,0:T(8,128)S(1)} custom-call(bf16[3,4096,512]{2,1,0:T(8,128)(2,1)S(1)} %load.1.w_ref, bf16[256,512]{1,0:T(8,128)(2,1)S(1)} %embed_rows.1.refs_0_, bf16[256,512]{1,0:T(8,128)(2,1)S(1)} %collective-permute-done.6.refs_1_, bf16[256,512]{1,0:T(8,128)(2,1)S(1)} %collective-permute-done.7.refs_2_, ...), custom_call_target="tpu_custom_call" | custom-call | flops 25165824 | bytes 212992 | tf_op jit(solution)/shard_map/project/pallas_call | solution.py:174
  24.0 1.8 %collective-permute-done.4.refs_1_ = bf16[256,512]{1,0:T(8,128)(2,1)S(1)} collective-permute-done((bf16[256,512]{1,0:T(8,128)(2,1)S(1)}, bf16[256,512]{1,0:T(8,128)(2,1)S(1)}, u32[]{:S(2)}, u32[]{:S(2)}) %collective-permute-start.4) | collective-permute-done | bytes 262176 | tf_op jit(solution)/shard_map/ppermute | solution.py:652
  25.8 2.7 %collective-permute-done.3.refs_0_ = bf16[256,512]{1,0:T(8,128)(2,1)S(1)} collective-permute-done((bf16[256,512]{1,0:T(8,128)(2,1)S(1)}, bf16[256,512]{1,0:T(8,128)(2,1)S(1)}, u32[]{:S(2)}, u32[]{:S(2)}) %collective-permute-start.3) | collective-permute-done | bytes 262176 | tf_op jit(solution)/shard_map/ppermute | solution.py:649
  29.7 1.4 %project.7.refs_1_ = f32[3,256,512]{2,1,0:T(8,128)S(1)} custom-call(bf16[3,4096,512]{2,1,0:T(8,128)(2,1)S(1)} %load.1.w_ref, bf16[256,512]{1,0:T(8,128)(2,1)S(1)} %collective-permute-done.3.refs_0_, bf16[256,512]{1,0:T(8,128)(2,1)S(1)} %collective-permute-done.4.refs_1_, bf16[256,512]{1,0:T(8,128)(2,1)S(1)} %collective-permute-done.5.refs_2_, ...), custom_call_target="tpu_custom_call" | custom-call | flops 18874368 | bytes 233472 | tf_op jit(solution)/shard_map/project/pallas_call | solution.py:174
  31.3 3.6 %collective-permute-done.9.refs_0_ = bf16[256,512]{1,0:T(8,128)(2,1)S(1)} collective-permute-done((bf16[256,512]{1,0:T(8,128)(2,1)S(1)}, bf16[256,512]{1,0:T(8,128)(2,1)S(1)}, u32[]{:S(2)}, u32[]{:S(2)}) %collective-permute-start.9) | collective-permute-done | bytes 262176 | tf_op jit(solution)/shard_map/ppermute | solution.py:652
  35.8 2.2 %collective-permute-done.12.other_ref = f32[3,256,256]{2,1,0:T(8,128)S(1)} collective-permute-done((f32[3,256,256]{2,1,0:T(8,128)S(1)}, f32[3,256,256]{2,1,0:T(8,128)S(1)}, u32[]{:S(2)}, u32[]{:S(2)}) %collective-permute-start.12) | collective-permute-done | bytes 786464 | tf_op jit(solution)/shard_map/ppermute | solution.py:646
  38.0 3.2 %mixer.1 = (bf16[128,256]{1,0:T(8,128)(2,1)S(1)}, bf16[128,256]{1,0:T(8,128)(2,1)S(1)}, bf16[3,256,256]{2,1,0:T(8,128)(2,1)S(1)}) custom-call(f32[3,256,256]{2,1,0:T(8,128)S(1)} %project.11.keep_ref, f32[3,256,256]{2,1,0:T(8,128)S(1)} %collective-permute-done.12.other_ref, f32[3,7,512]{2,1,0:T(8,128)S(1)} %bitcast.3, f32[16,512]{1,0:T(8,128)S(1)} %copy-done.2, ...), custom_call_target="tpu_custom_call" | custom-call | flops 196608 | bytes 30368 | tf_op jit(solution)/shard_map/mixer/pallas_call | solution.py:174
  42.0 1.0 %collective-permute-done.13.refs_0_.refs_1_ = bf16[3,256,256]{2,1,0:T(8,128)(2,1)S(1)} collective-permute-done((bf16[3,256,256]{2,1,0:T(8,128)(2,1)S(1)}, bf16[3,256,256]{2,1,0:T(8,128)(2,1)S(1)}, u32[]{:S(2)}, u32[]{:S(2)}) %collective-permute-start.13) | collective-permute-done | bytes 393248 | tf_op jit(solution)/shard_map/ppermute | solution.py:646
  45.2 1.6 %collective-permute-start.16 = (bf16[1024,256]{1,0:T(8,128)(2,1)S(1)}, bf16[1024,256]{1,0:T(8,128)(2,1)S(1)}, u32[]{:S(2)}, u32[]{:S(2)}) collective-permute-start(bf16[1024,256]{1,0:T(8,128)(2,1)S(1)} %back_project.7), channel_id=1, source_target_pairs={{0,4},{1,3},{2,6},{3,1},{4,0},{5,7},{6,2},{7,5},{8,12},{9,11},{10,... | collective-permute-start | bytes 1572872 | tf_op jit(solution)/shard_map/ppermute | solution.py:652
  46.7 1.3 %collective-permute-done.15.other_ref = bf16[128,256]{1,0:T(8,128)(2,1)S(1)} collective-permute-done((bf16[128,256]{1,0:T(8,128)(2,1)S(1)}, bf16[128,256]{1,0:T(8,128)(2,1)S(1)}, u32[]{:S(2)}, u32[]{:S(2)}) %collective-permute-start.15) | collective-permute-done | bytes 65568 | tf_op jit(solution)/shard_map/ppermute | solution.py:646
  48.7 1.8 %back_project.6 = (f32[512,256]{1,0:T(8,128)S(1)}, f32[512,256]{1,0:T(8,128)S(1)}, f32[512,256]{1,0:T(8,128)S(1)}, f32[512,256]{1,0:T(8,128)S(1)}) custom-call(bf16[3,4096,512]{2,1,0:T(8,128)(2,1)S(1)} %load.1.w_ref, bf16[3,256,256]{2,1,0:T(8,128)(2,1)S(1)} %get-tuple-element.60.refs_0_, bf16[3,256,256]{2,1,0:T(8,128)(2,1)S(1)} %collective-permute-done.13.refs_0_.refs_1_), custom_call_target="tpu_custom_call" | custom-call | flops 25165824 | bytes 208896 | tf_op jit(solution)/shard_map/back_project/pallas_call | solution.py:174
  50.4 2.4 %collective-permute-done.14.got_ref = bf16[1024,256]{1,0:T(8,128)(2,1)S(1)} collective-permute-done((bf16[1024,256]{1,0:T(8,128)(2,1)S(1)}, bf16[1024,256]{1,0:T(8,128)(2,1)S(1)}, u32[]{:S(2)}, u32[]{:S(2)}) %collective-permute-start.14) | collective-permute-done | bytes 524320 | tf_op jit(solution)/shard_map/ppermute | solution.py:652
  52.9 1.5 %collective-permute-start.17 = (bf16[512,256]{1,0:T(8,128)(2,1)S(1)}, bf16[512,256]{1,0:T(8,128)(2,1)S(1)}, u32[]{:S(2)}, u32[]{:S(2)}) collective-permute-start(bf16[512,256]{1,0:T(8,128)(2,1)S(1)} %get-tuple-element.70), channel_id=1, source_target_pairs={{0,2},{1,5},{2,0},{3,7},{4,6},{5,1},{6,4},{7,3},{8,10},{9,13},{10,... | collective-permute-start | bytes 786440 | tf_op jit(solution)/shard_map/ppermute | solution.py:649
  55.0 6.9 %collective-permute-done.16.other_ref = bf16[1024,256]{1,0:T(8,128)(2,1)S(1)} collective-permute-done((bf16[1024,256]{1,0:T(8,128)(2,1)S(1)}, bf16[1024,256]{1,0:T(8,128)(2,1)S(1)}, u32[]{:S(2)}, u32[]{:S(2)}) %collective-permute-start.16) | collective-permute-done | bytes 524320 | tf_op jit(solution)/shard_map/ppermute | solution.py:652
  63.4 2.9 %collective-permute-start.21 = (bf16[512,128]{1,0:T(8,128)(2,1)S(1)}, bf16[512,128]{1,0:T(8,128)(2,1)S(1)}, u32[]{:S(2)}, u32[]{:S(2)}) collective-permute-start(bf16[512,128]{1,0:T(8,128)(2,1)S(1)} %get-tuple-element.76), channel_id=1, source_target_pairs={{0,8},{2,10},{4,12},{6,14},{8,0},{10,2},{12,4},{14,6},{16,9},{18,1... | collective-permute-start | bytes 393224 | tf_op jit(solution)/shard_map/ppermute | solution.py:717
  66.3 3.6 %collective-permute-start.22 = (bf16[512,128]{1,0:T(8,128)(2,1)S(1)}, bf16[512,128]{1,0:T(8,128)(2,1)S(1)}, u32[]{:S(2)}, u32[]{:S(2)}) collective-permute-start(bf16[512,128]{1,0:T(8,128)(2,1)S(1)} %get-tuple-element.77), channel_id=1, source_target_pairs={{0,9},{2,11},{4,13},{6,15},{8,1},{10,3},{12,5},{14,7},{16,8},{18,1... | collective-permute-start | bytes 393224 | tf_op jit(solution)/shard_map/ppermute | solution.py:717
  70.0 7.5 %collective-permute-done.22.b_ref = bf16[512,128]{1,0:T(8,128)(2,1)S(1)} collective-permute-done((bf16[512,128]{1,0:T(8,128)(2,1)S(1)}, bf16[512,128]{1,0:T(8,128)(2,1)S(1)}, u32[]{:S(2)}, u32[]{:S(2)}) %collective-permute-start.22) | collective-permute-done | bytes 131104 | tf_op jit(solution)/shard_map/ppermute | solution.py:717
  (50 shorter events, 11.6 us)
Async XLA Ops:
  0.6 2.1 %collective-permute-start.1 = (bf16[128,512]{1,0:T(8,128)(2,1)}, bf16[128,512]{1,0:T(8,128)(2,1)S(1)}, u32[]{:S(2)}, u32[]{:S(2)}) collective-permute-start(bf16[128,512]{1,0:T(8,128)(2,1)} %cot_own_ref.1), channel_id=1, source_target_pairs={{0,1},{1,0},{2,3},{3,2},{4,5},{5,4},{6,7},{7,6},{8,9},{9,8},{10,11... | collective-permute-start | bytes 393224 | tf_op jit(solution)/shard_map/ppermute | solution.py:646
  1.1 1.3 %collective-permute-start = (s32[1,128]{1,0:T(1,128)}, s32[1,128]{1,0:T(1,128)S(1)}, u32[]{:S(2)}, u32[]{:S(2)}) collective-permute-start(s32[1,128]{1,0:T(1,128)} %bitcast.5), channel_id=1, source_target_pairs={{0,1},{1,0},{2,3},{3,2},{4,5},{5,4},{6,7},{7,6},{8,9},{9,8},{10,11... | collective-permute-start | bytes 1544 | tf_op jit(solution)/shard_map/ppermute | solution.py:646
  2.8 15.0 %collective-permute-start.2 = (bf16[256,512]{1,0:T(8,128)(2,1)S(1)}, bf16[256,512]{1,0:T(8,128)(2,1)S(1)}, u32[]{:S(2)}, u32[]{:S(2)}) collective-permute-start(bf16[256,512]{1,0:T(8,128)(2,1)S(1)} %embed_rows.1.refs_0_), channel_id=1, source_target_pairs={{0,8},{2,10},{4,12},{6,14},{8,0},{10,2},{12,4},{14,6},{1,16},{3,18... | collective-permute-start | bytes 786440 | tf_op jit(solution)/shard_map/ppermute | solution.py:661
  5.7 15.1 %collective-permute-start.7 = (bf16[256,512]{1,0:T(8,128)(2,1)S(1)}, bf16[256,512]{1,0:T(8,128)(2,1)S(1)}, u32[]{:S(2)}, u32[]{:S(2)}) collective-permute-start(bf16[256,512]{1,0:T(8,128)(2,1)S(1)} %embed_rows.1.refs_0_), channel_id=1, source_target_pairs={{0,6},{1,1},{2,4},{3,3},{4,2},{5,5},{6,0},{7,7},{8,14},{9,9},{10,1... | collective-permute-start | bytes 786440 | tf_op jit(solution)/shard_map/ppermute | solution.py:664
  10.1 10.7 %collective-permute-start.6 = (bf16[256,512]{1,0:T(8,128)(2,1)S(1)}, bf16[256,512]{1,0:T(8,128)(2,1)S(1)}, u32[]{:S(2)}, u32[]{:S(2)}) collective-permute-start(bf16[256,512]{1,0:T(8,128)(2,1)S(1)} %embed_rows.1.refs_0_), channel_id=1, source_target_pairs={{0,4},{1,1},{2,6},{3,3},{4,0},{5,5},{6,2},{7,7},{8,12},{9,9},{10,1... | collective-permute-start | bytes 786440 | tf_op jit(solution)/shard_map/ppermute | solution.py:663
  12.5 10.1 %collective-permute-start.5 = (bf16[256,512]{1,0:T(8,128)(2,1)S(1)}, bf16[256,512]{1,0:T(8,128)(2,1)S(1)}, u32[]{:S(2)}, u32[]{:S(2)}) collective-permute-start(bf16[256,512]{1,0:T(8,128)(2,1)S(1)} %embed_rows.1.refs_0_), channel_id=1, source_target_pairs={{9,16},{11,18},{13,20},{15,22},{1,24},{3,26},{5,28},{7,30},{16,9},... | collective-permute-start | bytes 786440 | tf_op jit(solution)/shard_map/ppermute | solution.py:662
  17.7 8.0 %collective-permute-start.4 = (bf16[256,512]{1,0:T(8,128)(2,1)S(1)}, bf16[256,512]{1,0:T(8,128)(2,1)S(1)}, u32[]{:S(2)}, u32[]{:S(2)}) collective-permute-start(bf16[256,512]{1,0:T(8,128)(2,1)S(1)} %collective-permute-done.2.refs_3_), channel_id=1, source_target_pairs={{0,4},{1,3},{2,6},{3,1},{4,0},{5,7},{6,2},{7,5},{8,12},{9,11},{10,... | collective-permute-start | bytes 786440 | tf_op jit(solution)/shard_map/ppermute | solution.py:652
  19.3 9.2 %collective-permute-start.3 = (bf16[256,512]{1,0:T(8,128)(2,1)S(1)}, bf16[256,512]{1,0:T(8,128)(2,1)S(1)}, u32[]{:S(2)}, u32[]{:S(2)}) collective-permute-start(bf16[256,512]{1,0:T(8,128)(2,1)S(1)} %collective-permute-done.2.refs_3_), channel_id=1, source_target_pairs={{0,2},{1,5},{2,0},{3,7},{4,6},{5,1},{6,4},{7,3},{8,10},{9,13},{10,... | collective-permute-start | bytes 786440 | tf_op jit(solution)/shard_map/ppermute | solution.py:649
  22.6 8.5 %collective-permute-start.11 = (bf16[256,512]{1,0:T(8,128)(2,1)S(1)}, bf16[256,512]{1,0:T(8,128)(2,1)S(1)}, u32[]{:S(2)}, u32[]{:S(2)}) collective-permute-start(bf16[256,512]{1,0:T(8,128)(2,1)S(1)} %collective-permute-done.5.refs_2_), channel_id=1, source_target_pairs={{0,0},{1,7},{2,2},{3,5},{4,4},{5,3},{6,6},{7,1},{8,8},{9,15},{10,1... | collective-permute-start | bytes 786440 | tf_op jit(solution)/shard_map/ppermute | solution.py:677
  23.3 8.0 %collective-permute-start.10 = (bf16[256,512]{1,0:T(8,128)(2,1)S(1)}, bf16[256,512]{1,0:T(8,128)(2,1)S(1)}, u32[]{:S(2)}, u32[]{:S(2)}) collective-permute-start(bf16[256,512]{1,0:T(8,128)(2,1)S(1)} %collective-permute-done.5.refs_2_), channel_id=1, source_target_pairs={{0,0},{1,3},{2,2},{3,1},{4,4},{5,7},{6,6},{7,5},{8,8},{9,11},{10,1... | collective-permute-start | bytes 786440 | tf_op jit(solution)/shard_map/ppermute | solution.py:676
  28.5 6.4 %collective-permute-start.9 = (bf16[256,512]{1,0:T(8,128)(2,1)S(1)}, bf16[256,512]{1,0:T(8,128)(2,1)S(1)}, u32[]{:S(2)}, u32[]{:S(2)}) collective-permute-start(bf16[256,512]{1,0:T(8,128)(2,1)S(1)} %collective-permute-done.3.refs_0_), channel_id=1, source_target_pairs={{0,4},{1,3},{2,6},{3,1},{4,0},{5,7},{6,2},{7,5},{8,12},{9,11},{10,... | collective-permute-start | bytes 786440 | tf_op jit(solution)/shard_map/ppermute | solution.py:652
  29.1 6.4 %collective-permute-start.8 = (bf16[256,512]{1,0:T(8,128)(2,1)S(1)}, bf16[256,512]{1,0:T(8,128)(2,1)S(1)}, u32[]{:S(2)}, u32[]{:S(2)}) collective-permute-start(bf16[256,512]{1,0:T(8,128)(2,1)S(1)} %collective-permute-done.5.refs_2_), channel_id=1, source_target_pairs={{0,0},{1,5},{2,2},{3,7},{4,4},{5,1},{6,6},{7,3},{8,8},{9,13},{10,1... | collective-permute-start | bytes 786440 | tf_op jit(solution)/shard_map/ppermute | solution.py:680
  35.6 2.4 %copy-start = (bf16[128,512]{1,0:T(8,128)(2,1)S(1)}, bf16[128,512]{1,0:T(8,128)(2,1)}, u32[]{:S(2)}) copy-start(bf16[128,512]{1,0:T(8,128)(2,1)} %cot_own_ref.1) | copy-start | bytes 393220
  35.6 2.4 %collective-permute-start.12 = (f32[3,256,256]{2,1,0:T(8,128)S(1)}, f32[3,256,256]{2,1,0:T(8,128)S(1)}, u32[]{:S(2)}, u32[]{:S(2)}) collective-permute-start(f32[3,256,256]{2,1,0:T(8,128)S(1)} %project.10), channel_id=1, source_target_pairs={{0,1},{1,0},{2,3},{3,2},{4,5},{5,4},{6,7},{7,6},{8,9},{9,8},{10,11... | collective-permute-start | bytes 2359304 | tf_op jit(solution)/shard_map/ppermute | solution.py:646
  41.2 1.8 %collective-permute-start.13 = (bf16[3,256,256]{2,1,0:T(8,128)(2,1)S(1)}, bf16[3,256,256]{2,1,0:T(8,128)(2,1)S(1)}, u32[]{:S(2)}, u32[]{:S(2)}) collective-permute-start(bf16[3,256,256]{2,1,0:T(8,128)(2,1)S(1)} %get-tuple-element.60.refs_0_), channel_id=1, source_target_pairs={{0,1},{1,0},{2,3},{3,2},{4,5},{5,4},{6,7},{7,6},{8,9},{9,8},{10,11... | collective-permute-start | bytes 1179656 | tf_op jit(solution)/shard_map/ppermute | solution.py:646
  43.6 9.2 %collective-permute-start.14 = (bf16[1024,256]{1,0:T(8,128)(2,1)S(1)}, bf16[1024,256]{1,0:T(8,128)(2,1)S(1)}, u32[]{:S(2)}, u32[]{:S(2)}) collective-permute-start(bf16[1024,256]{1,0:T(8,128)(2,1)S(1)} %back_project.5), channel_id=1, source_target_pairs={{0,4},{1,3},{2,6},{3,1},{4,0},{5,7},{6,2},{7,5},{8,12},{9,11},{10,... | collective-permute-start | bytes 1572872 | tf_op jit(solution)/shard_map/ppermute | solution.py:652
  45.2 16.8 %collective-permute-start.16 = (bf16[1024,256]{1,0:T(8,128)(2,1)S(1)}, bf16[1024,256]{1,0:T(8,128)(2,1)S(1)}, u32[]{:S(2)}, u32[]{:S(2)}) collective-permute-start(bf16[1024,256]{1,0:T(8,128)(2,1)S(1)} %back_project.7), channel_id=1, source_target_pairs={{0,4},{1,3},{2,6},{3,1},{4,0},{5,7},{6,2},{7,5},{8,12},{9,11},{10,... | collective-permute-start | bytes 1572872 | tf_op jit(solution)/shard_map/ppermute | solution.py:652
  46.7 1.3 %collective-permute-start.15 = (bf16[128,256]{1,0:T(8,128)(2,1)S(1)}, bf16[128,256]{1,0:T(8,128)(2,1)S(1)}, u32[]{:S(2)}, u32[]{:S(2)}) collective-permute-start(bf16[128,256]{1,0:T(8,128)(2,1)S(1)} %get-tuple-element.64), channel_id=1, source_target_pairs={{0,1},{1,0},{2,3},{3,2},{4,5},{5,4},{6,7},{7,6},{8,9},{9,8},{10,11... | collective-permute-start | bytes 196616 | tf_op jit(solution)/shard_map/ppermute | solution.py:646
  52.9 9.0 %collective-permute-start.17 = (bf16[512,256]{1,0:T(8,128)(2,1)S(1)}, bf16[512,256]{1,0:T(8,128)(2,1)S(1)}, u32[]{:S(2)}, u32[]{:S(2)}) collective-permute-start(bf16[512,256]{1,0:T(8,128)(2,1)S(1)} %get-tuple-element.70), channel_id=1, source_target_pairs={{0,2},{1,5},{2,0},{3,7},{4,6},{5,1},{6,4},{7,3},{8,10},{9,13},{10,... | collective-permute-start | bytes 786440 | tf_op jit(solution)/shard_map/ppermute | solution.py:649
  54.5 8.8 %collective-permute-start.20 = (bf16[512,256]{1,0:T(8,128)(2,1)S(1)}, bf16[512,256]{1,0:T(8,128)(2,1)S(1)}, u32[]{:S(2)}, u32[]{:S(2)}) collective-permute-start(bf16[512,256]{1,0:T(8,128)(2,1)S(1)} %get-tuple-element.75), channel_id=1, source_target_pairs={{0,2},{1,5},{2,0},{3,7},{4,6},{5,1},{6,4},{7,3},{8,10},{9,13},{10,... | collective-permute-start | bytes 786440 | tf_op jit(solution)/shard_map/ppermute | solution.py:649
  62.1 7.8 %collective-permute-start.18 = (bf16[512,128]{1,0:T(8,128)(2,1)S(1)}, bf16[512,128]{1,0:T(8,128)(2,1)S(1)}, u32[]{:S(2)}, u32[]{:S(2)}) collective-permute-start(bf16[512,128]{1,0:T(8,128)(2,1)S(1)} %get-tuple-element.72), channel_id=1, source_target_pairs={{0,1},{2,3},{4,5},{6,7},{8,9},{10,11},{12,13},{14,15},{16,0},{18,2... | collective-permute-start | bytes 393224 | tf_op jit(solution)/shard_map/ppermute | solution.py:719
  62.2 7.7 %collective-permute-start.19 = (bf16[512,128]{1,0:T(8,128)(2,1)S(1)}, bf16[512,128]{1,0:T(8,128)(2,1)S(1)}, u32[]{:S(2)}, u32[]{:S(2)}) collective-permute-start(bf16[512,128]{1,0:T(8,128)(2,1)S(1)} %get-tuple-element.73), channel_id=1, source_target_pairs={{16,1},{18,3},{20,5},{22,7},{24,9},{26,11},{28,13},{30,15},{9,24},... | collective-permute-start | bytes 393224 | tf_op jit(solution)/shard_map/ppermute | solution.py:719
  63.4 6.6 %collective-permute-start.21 = (bf16[512,128]{1,0:T(8,128)(2,1)S(1)}, bf16[512,128]{1,0:T(8,128)(2,1)S(1)}, u32[]{:S(2)}, u32[]{:S(2)}) collective-permute-start(bf16[512,128]{1,0:T(8,128)(2,1)S(1)} %get-tuple-element.76), channel_id=1, source_target_pairs={{0,8},{2,10},{4,12},{6,14},{8,0},{10,2},{12,4},{14,6},{16,9},{18,1... | collective-permute-start | bytes 393224 | tf_op jit(solution)/shard_map/ppermute | solution.py:717
  66.3 11.2 %collective-permute-start.22 = (bf16[512,128]{1,0:T(8,128)(2,1)S(1)}, bf16[512,128]{1,0:T(8,128)(2,1)S(1)}, u32[]{:S(2)}, u32[]{:S(2)}) collective-permute-start(bf16[512,128]{1,0:T(8,128)(2,1)S(1)} %get-tuple-element.77), channel_id=1, source_target_pairs={{0,9},{2,11},{4,13},{6,15},{8,1},{10,3},{12,5},{14,7},{16,8},{18,1... | collective-permute-start | bytes 393224 | tf_op jit(solution)/shard_map/ppermute | solution.py:717
  (3 other events, 7.2 us)
